TPU v7x, 32 devices: a whole 2x2x4 slice. The times are simulated.
32 devices in a mesh: replica: 4 (over z), shard: 4 (over y, core), tensor: 2 (over x).
Axes of the slice: x: 2, y: 2, z: 4, core: 2. Of those that a mesh axis runs over, the one named last changes fastest.
Arguments:
- trained_up: bfloat16 [4, 1024, 4096], P('replica', None, 'tensor'), may hold values from -6 to 6
- trained_down: bfloat16 [4, 4096, 1024], P('replica', 'tensor'), may hold values from -6 to 6
- trained_embed: bfloat16 [4, 8192, 1024], P('replica', ('shard', 'tensor')), may hold values from -6 to 6
- trained_norm: bfloat16 [4, 2, 1024], P('replica'), may hold values from 0.099609375 to 1.8984375
- master_up: float32 [1024, 4096], P(('replica', 'shard', 'tensor')), may hold values from -6 to 6
- moment_up: float32 [1024, 4096], P(('replica', 'shard', 'tensor')), may hold values from -4 to 4
- master_down: float32 [2, 2048, 1024], P('tensor', ('replica', 'shard')), may hold values from -6 to 6
- moment_down: float32 [2, 2048, 1024], P('tensor', ('replica', 'shard')), may hold values from -4 to 4
- master_embed: float32 [8, 1024, 1024], P(('shard', 'tensor'), 'replica'), may hold values from -6 to 6
- moment_embed: float32 [8, 1024, 64], P(('shard', 'tensor'), 'replica'), may hold values from -4 to 4
- master_norm: float32 [2, 1024], replicated, may hold values from 0.1 to 1.9
- moment_norm: float32 [2, 1024], replicated, may hold values from -2 to 2
- embed_basis: float32 [1024, 64], replicated, may hold values from -0.1875 to 0.1875
Outputs:
- recast_up: bfloat16 [1024, 4096], P(None, 'tensor')
- recast_down: bfloat16 [4096, 1024], P('tensor')
- recast_embed: bfloat16 [8192, 1024], P(('shard', 'tensor'))
- recast_norm: bfloat16 [2, 1024], replicated
- stored_up: float32 [1024, 4096], P(('replica', 'shard', 'tensor'))
- velocity_up: float32 [1024, 4096], P(('replica', 'shard', 'tensor'))
- stored_down: float32 [2, 2048, 1024], P('tensor', ('replica', 'shard'))
- velocity_down: float32 [2, 2048, 1024], P('tensor', ('replica', 'shard'))
- stored_embed: float32 [8, 1024, 1024], P(('shard', 'tensor'), 'replica')
- velocity_embed: float32 [8, 1024, 64], P(('shard', 'tensor'), 'replica')
- stored_norm: float32 [2, 1024], replicated
- velocity_norm: float32 [2, 1024], replicated
All inputs are finite; a program needn't handle non-finite values.
Results may differ from a plain program's by a relative error of at most 0.012.
Values may be sent and summed in bfloat16 or wider, within the bound.
No kernel may reach another device: no remote copies, remote signals or barrier semaphores. Data moves between devices by JAX's collectives and lax.ppermute only.
A program may use at most 128 MiB of HBM per device.

v0:
```python
import functools

import jax
import jax.numpy as jnp
from jax import lax
from jax.experimental import pallas as pl
from jax.experimental.pallas import tpu as pltpu
from jax.sharding import PartitionSpec as P

F32 = jnp.float32
BF16 = jnp.bfloat16
HIGHEST = lax.Precision.HIGHEST
HBM = pl.BlockSpec(memory_space=pltpu.HBM)
ANY = pl.BlockSpec(memory_space=pl.ANY)
VMEM = pl.BlockSpec(memory_space=pltpu.VMEM)


def outer_step(master, moment, summed, groups):
    difference = master - summed / groups
    velocity = 0.5 * moment + difference
    return (master - 0.7 * (difference + 0.5 * velocity), velocity)


def call(kernel, name, out_shape, in_specs, out_specs, scratch, *operands, limit=24, aliases={}):
    size = sum(x.size * x.dtype.itemsize for x in jax.tree.leaves(out_shape))
    return pl.pallas_call(
        kernel,
        name=name,
        out_shape=out_shape,
        in_specs=in_specs,
        out_specs=out_specs,
        scratch_shapes=scratch,
        input_output_aliases=aliases,
        compiler_params=pltpu.CompilerParams(vmem_limit_bytes=limit * 2**20),
        cost_estimate=pl.CostEstimate(flops=0, bytes_accessed=3 * size, transcendentals=0),
    )(*operands)


def swap(x, axis, bit):
    return lax.ppermute(x, axis, [(i, i ^ bit) for i in range(lax.axis_size(axis))])


def bits_down(size):
    bit = size // 2
    while bit:
        yield bit
        bit //= 2


def project_kernel(trained, basis, norm, own, *refs):
    *outs, projected = refs
    rank, rows = basis.shape[0], own.shape[1]
    high = basis[...].astype(BF16)
    rest = basis[...] - high.astype(F32)
    middle = rest.astype(BF16)
    low = (rest - middle.astype(F32)).astype(BF16)
    split = jnp.concatenate([high, middle, low], axis=0)
    product = lax.dot_general(
        split, trained[...], (((1,), (1,)), ((), ())), preferred_element_type=F32
    )
    projected[...] = product[:rank] + (product[rank : 2 * rank] + product[2 * rank :])
    pos = lax.axis_index("replica")
    values = norm[...].astype(F32)
    per = norm.shape[1] // rows
    extra = outs[0].shape[0] - rank
    parts = [
        values[i // per : i // per + 1, (i % per) * rows : (i % per + 1) * rows]
        for i in range(norm.shape[0] * per)
    ]
    parts = jnp.concatenate((parts * extra)[:extra], axis=0).astype(BF16)
    own[...] = projected[:, pl.ds(pl.multiple_of(pos * rows, rows), rows)]
    for mask, out in enumerate(outs, 1):
        owner = jnp.bitwise_xor(pos, mask)
        block = projected[:, pl.ds(pl.multiple_of(owner * rows, rows), rows)]
        out[:rank, :] = block.astype(BF16)
        out[rank:, :] = parts


def embed_kernel(groups, n_came, *refs):
    refs = list(refs)
    own, base, master, moment, basis, norm, master_norm, moment_norm = refs[:8]
    came = refs[8 : 8 + n_came]
    stored, recast, velocity, norm_cast, norm_stored, norm_velocity = refs[-6:]
    rank, rows = own.shape
    total = own[...]
    for ref in came:
        total = total + ref[:rank, :].astype(F32)
    coefficient = base[...] - total / groups
    moved = 0.5 * moment[...] + coefficient
    velocity[...] = moved
    change = lax.dot_general(
        coefficient + 0.5 * moved,
        basis[...],
        (((0,), (0,)), ((), ())),
        precision=HIGHEST,
        preferred_element_type=F32,
    )
    new = master[...] - 0.7 * change
    stored[...] = new
    recast[...] = new.astype(BF16)
    per = norm.shape[1] // rows
    values = norm[...].astype(F32)
    tails = [ref[rank:, :].astype(F32) for ref in came]
    for i in range(norm.shape[0] * per):
        row, span = i // per, slice((i % per) * rows, (i % per + 1) * rows)
        summed = values[row : row + 1, span]
        for tail in tails:
            summed = summed + tail[i : i + 1, :]
        new_norm, moved_norm = outer_step(
            master_norm[row : row + 1, span], moment_norm[row : row + 1, span], summed, groups
        )
        norm_stored[row : row + 1, span] = new_norm
        norm_velocity[row : row + 1, span] = moved_norm
    norm_cast[...] = norm_stored[...].astype(BF16)


def pack_kernel(masks, down, up, *refs):
    *outs, sems = refs
    pos, shard = lax.axis_index("replica"), lax.axis_index("shard")
    rows, width = down.shape[2:]
    tall, cols = up.shape[2:]
    copies = []

    def bring(source, dest):
        copies.append(pltpu.make_async_copy(source, dest, sems.at[len(copies)]))
        copies[-1].start()

    for mask, out in zip(masks, outs):
        owner = jnp.bitwise_xor(pos, mask)
        bring(down.at[owner, shard], out.at[pl.ds(0, rows)])
        for chunk in range(cols // width):
            bring(
                up.at[owner, shard, :, pl.ds(chunk * width, width)],
                out.at[pl.ds(rows + chunk * tall, tall)],
            )
    for copy in copies:
        copy.wait()


def add_kernel(block, came, later, out, later_out):
    out[...] = (block[...].astype(F32) + came[...].astype(F32)).astype(BF16)
    later_out[...] = later[...]


def update_kernel(groups, tensors, n_came, *refs):
    refs = list(refs)
    master_down, moment_down, master_up, moment_up, embed = refs[:5]
    came, state_came = refs[5 : 5 + n_came], refs[5 + n_came : 4 + n_came + tensors]
    piece, embed_out, stored_down, velocity_down, *sums = refs[4 + n_came + tensors : -3]
    summed, master, moment = refs[-3:]
    me = lax.axis_index("tensor")
    rows_down, width = master_down.shape
    rows_up = master_up.shape[0]
    tall, cols = summed.shape

    def at(index):
        return pl.ds(pl.multiple_of(index * rows_up, rows_up), rows_up)

    own_cols = pl.ds(pl.multiple_of(me * cols, cols), cols)
    master[at(me), :] = master_up[:, own_cols]
    moment[at(me), :] = moment_up[:, own_cols]
    for shift in range(1, tensors):
        source = lax.rem(me + tensors - shift, tensors)
        master[at(source), :] = state_came[shift - 1][0]
        moment[at(source), :] = state_came[shift - 1][1]

    def total(lo, hi):
        value = came[0][lo:hi, :].astype(F32)
        for ref in came[1:]:
            value = value + ref[lo:hi, :].astype(F32)
        return value

    stored, velocity = outer_step(
        master_down[...], moment_down[...], total(0, rows_down), groups
    )
    stored_down[...] = stored
    velocity_down[...] = velocity
    piece[:rows_down, :] = stored.astype(BF16)
    for chunk in range(cols // width):
        lo = rows_down + chunk * tall
        part = total(lo, lo + tall)
        span = slice(chunk * width, (chunk + 1) * width)
        summed[:, span] = part
        stored, _ = outer_step(master[:, span], moment[:, span], part, groups)
        piece[lo : lo + tall, :] = stored.astype(BF16)
    for shift in range(tensors):
        sums[shift][...] = summed[at(lax.rem(me + shift, tensors)), :]
    embed_out[...] = embed[...]


def up_kernel(groups, tensors, master_up, moment_up, *refs):
    sums, (stored_up, velocity_up, token) = refs[:tensors], refs[tensors:]
    cols = sums[0].shape[1]
    me = lax.axis_index("tensor")
    for shift in range(tensors):
        source = lax.rem(me + tensors - shift, tensors)
        span = pl.ds(pl.multiple_of(source * cols, cols), cols)
        stored, velocity = outer_step(
            master_up[:, span], moment_up[:, span], sums[shift][...], groups
        )
        stored_up[:, span] = stored
        velocity_up[:, span] = velocity
    token[...] = jnp.zeros_like(token)


def state_kernel(tensors, master_up, moment_up, *outs):
    me = lax.axis_index("tensor")
    cols = outs[0].shape[2]
    for shift in range(1, tensors):
        target = lax.rem(me + shift, tensors)
        span = pl.ds(pl.multiple_of(target * cols, cols), cols)
        outs[shift - 1][0] = master_up[:, span]
        outs[shift - 1][1] = moment_up[:, span]


def gate_kernel(x, *refs):
    refs[-1][...] = x[...]


def gate(x, *after):
    return call(
        gate_kernel,
        "gate",
        jax.ShapeDtypeStruct(x.shape, x.dtype),
        [VMEM] + [ANY] * len(after),
        VMEM,
        [],
        x,
        *after,
    )


def place_kernel(far, masks, *refs):
    pieces, (down, up, token, sems) = refs[: len(masks)], refs[-4:]
    token[...] = jnp.zeros_like(token)
    pos, shard = lax.axis_index("replica"), lax.axis_index("shard")
    rows, width = down.shape[2:]
    tall, cols = up.shape[2:]
    copies = []

    def send(source, dest):
        copies.append(pltpu.make_async_copy(source, dest, sems.at[len(copies)]))
        copies[-1].start()

    owner = jnp.bitwise_xor(pos, far)
    for piece, mask in zip(pieces, masks):
        place = jnp.bitwise_xor(shard, mask)
        send(piece.at[pl.ds(0, rows)], down.at[owner, place])
        for chunk in range(cols // width):
            send(
                piece.at[pl.ds(rows + chunk * tall, tall)],
                up.at[owner, place, :, pl.ds(chunk * width, width)],
            )
    for copy in copies:
        copy.wait()


def place_embed_kernel(masks, *refs):
    pieces, (out, sems) = refs[: len(masks)], refs[-2:]
    pos = lax.axis_index("replica")
    copies = [
        pltpu.make_async_copy(piece, out.at[jnp.bitwise_xor(pos, mask)], sems.at[i])
        for i, (piece, mask) in enumerate(zip(pieces, masks))
    ]
    for copy in copies:
        copy.start()
    for copy in copies:
        copy.wait()


def spread(pieces, axis):
    for bit in bits_down(lax.axis_size(axis)):
        pieces.update({mask ^ bit: swap(x, axis, bit) for mask, x in list(pieces.items())})
    return pieces


def body(
    trained_up,
    trained_down,
    trained_embed,
    trained_norm,
    master_up,
    moment_up,
    master_down,
    moment_down,
    master_embed,
    moment_embed,
    master_norm,
    moment_norm,
    embed_basis,
):
    replicas = lax.axis_size("replica")
    shards = lax.axis_size("shard")
    tensors = lax.axis_size("tensor")
    width, rank = embed_basis.shape
    rows_up, half_cols = master_up.shape[0], trained_up.shape[2]
    rows_down, rows_embed = master_down.shape[1], master_embed.shape[1]
    tall = tensors * rows_up
    chunks = half_cols // width
    packed = jax.ShapeDtypeStruct((rows_down + chunks * tall, width), BF16)
    dma = pltpu.SemaphoreType.DMA

    basis_t = embed_basis.T
    rank_rows = jax.ShapeDtypeStruct((rank, rows_embed), F32)
    packet = jax.ShapeDtypeStruct((rank + 16, rows_embed), BF16)
    own_rows, *packets = call(
        project_kernel,
        "project_rows",
        [rank_rows] + [packet] * (replicas - 1),
        [VMEM] * 3,
        [VMEM] * replicas,
        [pltpu.VMEM((rank, replicas * rows_embed), F32)],
        trained_embed[0],
        basis_t,
        trained_norm[0],
    )
    packets_came = [swap(x, "replica", mask) for mask, x in enumerate(packets, 1)]

    down = trained_down[0].reshape(replicas, shards, rows_down, width)
    up = trained_up[0].reshape(replicas, shards, tall, half_cols)
    masks = [3, 2, 1, 0]
    block3, block2, block1, block0 = call(
        functools.partial(pack_kernel, masks),
        "pack_blocks",
        [packed] * replicas,
        [HBM] * 2,
        [VMEM] * replicas,
        [dma((replicas * (1 + chunks),))],
        down,
        up,
        limit=61,
    )
    came2 = swap(gate(block3, *packets_came), "replica", 1)

    state = jax.ShapeDtypeStruct((2, rows_up, half_cols), F32)
    states = call(
        functools.partial(state_kernel, tensors),
        "up_state",
        [state] * (tensors - 1),
        [VMEM] * 2,
        [VMEM] * (tensors - 1),
        [],
        master_up,
        moment_up,
    )
    states = [
        lax.ppermute(x, "tensor", [(i, (i + shift) % tensors) for i in range(tensors)])
        for shift, x in enumerate(states, 1)
    ]

    base = lax.dot_general(
        basis_t, master_embed[0], (((1,), (1,)), ((), ())), precision=HIGHEST
    )
    norm_state = jax.ShapeDtypeStruct(master_norm.shape, F32)
    embed_rows = jax.ShapeDtypeStruct((rows_embed, width), BF16)
    stored_rows, recast_rows, velocity_rows, norm_cast, stored_norm, velocity_norm = call(
        functools.partial(embed_kernel, replicas, replicas - 1),
        "embed_update",
        [
            jax.ShapeDtypeStruct((rows_embed, width), F32),
            embed_rows,
            rank_rows,
            jax.ShapeDtypeStruct(master_norm.shape, BF16),
            norm_state,
            norm_state,
        ],
        [VMEM] * (7 + replicas),
        [VMEM] * 6,
        [],
        own_rows,
        base,
        master_embed[0],
        moment_embed[0].T,
        basis_t,
        trained_norm[0],
        master_norm,
        moment_norm,
        *packets_came,
    )

    block2, block1 = call(
        add_kernel,
        "add_block",
        [packed] * 2,
        [VMEM] * 3,
        [VMEM] * 2,
        [],
        block2,
        came2,
        block1,
    )
    came0 = [block0, swap(block1, "replica", 1), swap(block2, "replica", 2)]
    half_sum = jax.ShapeDtypeStruct((rows_up, half_cols), F32)
    down_state = jax.ShapeDtypeStruct((rows_down, width), F32)
    piece, embed_late, stored_down, velocity_down, *sums = call(
        functools.partial(update_kernel, replicas, tensors, len(came0)),
        "update_rows",
        [packed, embed_rows, down_state, down_state] + [half_sum] * tensors,
        [VMEM] * (5 + len(came0) + len(states)),
        [VMEM] * (4 + tensors),
        [pltpu.VMEM((tall, half_cols), F32)] * 3,
        master_down[0],
        moment_down[0],
        master_up,
        moment_up,
        recast_rows,
        *came0,
        *states,
    )

    top = shards // 2
    pieces = {0: piece, 1: swap(piece, "replica", 1), 2: swap(piece, "replica", 2)}
    groups = {0: spread({0: piece}, "shard")}
    groups[1] = spread({0: gate(pieces[1], groups[0][top])}, "shard")
    groups[2] = spread({0: pieces[2]}, "shard")
    pieces[3] = swap(gate(pieces[2], groups[1][top]), "replica", 1)
    groups[3] = spread({0: pieces[3]}, "shard")
    last_far = groups[3][top]
    embed_near = swap(embed_late, "replica", 1)
    embed_far = swap(gate(embed_late, pieces[2]), "replica", 2)
    embed_last = swap(gate(embed_far, last_far), "replica", 1)

    sums = [sums[0]] + [
        lax.ppermute(
            gate(x, last_far), "tensor", [(i, (i + shift) % tensors) for i in range(tensors)]
        )
        for shift, x in enumerate(sums[1:], 1)
    ]
    token_shape = jax.ShapeDtypeStruct((8, 128), F32)
    stored_up, velocity_up, token = call(
        functools.partial(up_kernel, replicas, tensors),
        "update_up",
        [jax.ShapeDtypeStruct(master_up.shape, F32)] * 2 + [token_shape],
        [VMEM] * (2 + tensors),
        [VMEM] * 3,
        [],
        master_up,
        moment_up,
        *sums,
    )

    shapes = [jax.ShapeDtypeStruct(down.shape, BF16), jax.ShapeDtypeStruct(up.shape, BF16)]
    placed = ()
    for far, group in groups.items():
        extra = (token,) if far == replicas - 1 else ()
        count = len(group) + len(extra)
        *placed, placed_token = call(
            functools.partial(place_kernel, far, list(group)),
            "place_rows",
            shapes + [token_shape],
            [VMEM] * count + [HBM] * len(placed),
            [HBM] * 2 + [VMEM],
            [dma((len(group) * (1 + chunks),))],
            *group.values(),
            *extra,
            *placed,
            aliases={count: 0, count + 1: 1} if placed else {},
        )
    recast_down, recast_up = placed

    embed_shape = jax.ShapeDtypeStruct((replicas, rows_embed, width), BF16)
    recast_embed = call(
        functools.partial(place_embed_kernel, [0, 1]),
        "place_embed",
        embed_shape,
        [VMEM] * 2,
        HBM,
        [dma((2,))],
        embed_late,
        embed_near,
    )
    recast_embed = call(
        functools.partial(place_embed_kernel, [2, 3]),
        "place_embed",
        embed_shape,
        [VMEM] * 3 + [HBM],
        HBM,
        [dma((2,))],
        embed_far,
        embed_last,
        placed_token,
        recast_embed,
        aliases={3: 0},
    )

    return (
        recast_up.reshape(-1, half_cols),
        recast_down.reshape(-1, width),
        recast_embed.reshape(-1, width),
        norm_cast,
        stored_up,
        velocity_up,
        stored_down[None],
        velocity_down[None],
        stored_rows[None],
        velocity_rows.T[None],
        stored_norm,
        velocity_norm,
    )


def solution(mesh):
    in_specs = (
        P("replica", None, "tensor"),
        P("replica", "tensor", None),
        P("replica", ("shard", "tensor"), None),
        P("replica", None, None),
        P(("replica", "shard", "tensor"), None),
        P(("replica", "shard", "tensor"), None),
        P("tensor", ("replica", "shard"), None),
        P("tensor", ("replica", "shard"), None),
        P(("shard", "tensor"), "replica", None),
        P(("shard", "tensor"), "replica", None),
        P(),
        P(),
        P(),
    )
    out_specs = (
        P(None, "tensor"),
        P("tensor", None),
        P(("shard", "tensor"), None),
        P(),
        P(("replica", "shard", "tensor"), None),
        P(("replica", "shard", "tensor"), None),
        P("tensor", ("replica", "shard"), None),
        P("tensor", ("replica", "shard"), None),
        P(("shard", "tensor"), "replica", None),
        P(("shard", "tensor"), "replica", None),
        P(),
        P(),
    )
    return jax.shard_map(body, mesh=mesh, in_specs=in_specs, out_specs=out_specs, check_vma=False)
```

profile of v0, /device:TPU:0, one launch (start us, length us, event | category | flops | bytes accessed | tf_op | source)
XLA Modules:
  0.0 143.5 jit_solution(9736620014896155316)
XLA Ops:
  1.6 1.6 %copy-done.5 = bf16[1,1024,1024]{2,1,0:T(8,128)(2,1)S(1)} copy-done((bf16[1,1024,1024]{2,1,0:T(8,128)(2,1)S(1)}, bf16[1,1024,1024]{2,1,0:T(8,128)(2,1)}, u32[]{:S(2)}) %copy-start.5) | copy-done | bytes 2097176
  4.8 3.1 %collective-permute-start = (bf16[80,256]{1,0:T(8,128)(2,1)S(1)}, bf16[80,256]{1,0:T(8,128)(2,1)S(1)}, u32[]{:S(2)}, u32[]{:S(2)}) collective-permute-start(bf16[80,256]{1,0:T(8,128)(2,1)S(1)} %get-tuple-element.47), channel_id=1, source_target_pairs={{0,8},{8,0},{16,24},{24,16},{1,9},{9,1},{17,25},{25,17},{2,10},{10... | collective-permute-start | bytes 122888 | tf_op jit(solution)/shard_map/ppermute | solution.py:40
  7.8 2.6 %collective-permute-start.1 = (bf16[80,256]{1,0:T(8,128)(2,1)S(1)}, bf16[80,256]{1,0:T(8,128)(2,1)S(1)}, u32[]{:S(2)}, u32[]{:S(2)}) collective-permute-start(bf16[80,256]{1,0:T(8,128)(2,1)S(1)} %get-tuple-element.48), channel_id=1, source_target_pairs={{0,16},{8,24},{16,0},{24,8},{1,17},{9,25},{17,1},{25,9},{2,18},{10... | collective-permute-start | bytes 122888 | tf_op jit(solution)/shard_map/ppermute | solution.py:40
  10.5 3.0 %pack_blocks.1 = (bf16[256,1024]{1,0:T(8,128)(2,1)}, bf16[256,1024]{1,0:T(8,128)(2,1)}, bf16[256,1024]{1,0:T(8,128)(2,1)}, bf16[256,1024]{1,0:T(8,128)(2,1)}) custom-call(bf16[4,4,128,1024]{3,2,1,0:T(8,128)(2,1)} %bitcast.35, bf16[4,4,64,2048]{3,2,1,0:T(8,128)(2,1)} %bitcast.36), custom_call_target="tpu_custom_call" | custom-call | bytes 6291456 | tf_op jit(solution)/shard_map/pack_blocks/pallas_call | solution.py:26
  13.6 2.6 %collective-permute-done.2.refs_10_.refs_2_ = bf16[80,256]{1,0:T(8,128)(2,1)S(1)} collective-permute-done((bf16[80,256]{1,0:T(8,128)(2,1)S(1)}, bf16[80,256]{1,0:T(8,128)(2,1)S(1)}, u32[]{:S(2)}, u32[]{:S(2)}) %collective-permute-start.2) | collective-permute-done | bytes 40992 | tf_op jit(solution)/shard_map/ppermute | solution.py:40
  19.0 10.4 %collective-permute-done.3.came = bf16[256,1024]{1,0:T(8,128)(2,1)S(1)} collective-permute-done((bf16[256,1024]{1,0:T(8,128)(2,1)S(1)}, bf16[256,1024]{1,0:T(8,128)(2,1)S(1)}, u32[]{:S(2)}, u32[]{:S(2)}) %collective-permute-start.3) | collective-permute-done | bytes 524320 | tf_op jit(solution)/shard_map/ppermute | solution.py:40
  32.0 2.4 %collective-permute-start.5 = (bf16[256,1024]{1,0:T(8,128)(2,1)S(1)}, bf16[256,1024]{1,0:T(8,128)(2,1)S(1)}, u32[]{:S(2)}, u32[]{:S(2)}) collective-permute-start(bf16[256,1024]{1,0:T(8,128)(2,1)S(1)} %get-tuple-element.56), channel_id=1, source_target_pairs={{0,16},{8,24},{16,0},{24,8},{1,17},{9,25},{17,1},{25,9},{2,18},{10... | collective-permute-start | bytes 1572872 | tf_op jit(solution)/shard_map/ppermute | solution.py:40
  35.6 2.0 %embed_update.1 = (f32[256,1024]{1,0:T(8,128)}, bf16[256,1024]{1,0:T(8,128)(2,1)S(1)}, f32[64,256]{1,0:T(8,128)}, bf16[2,1024]{1,0:T(2,128)(2,1)}, f32[2,1024]{1,0:T(2,128)}, /*index=5*/f32[2,1024]{1,0:T(2,128)}) custom-call(f32[64,256]{1,0:T(8,128)S(1)} %get-tuple-element.46.refs_0_, f32[64,256]{1,0:T(8,128)S(1)} %fusion.refs_1_, f32[256,1024]{1,0:T(8,128)S(1)} %bitcast.23, ...), custom_call_target="tpu_custom_call" | custom-call | bytes 4976640 | tf_op jit(solution)/shard_map/embed_update/pallas_call | solution.py:26
  37.6 16.4 %collective-permute-done.4.refs_6_ = bf16[256,1024]{1,0:T(8,128)(2,1)S(1)} collective-permute-done((bf16[256,1024]{1,0:T(8,128)(2,1)S(1)}, bf16[256,1024]{1,0:T(8,128)(2,1)S(1)}, u32[]{:S(2)}, u32[]{:S(2)}) %collective-permute-start.4) | collective-permute-done | bytes 524320 | tf_op jit(solution)/shard_map/ppermute | solution.py:40
  54.0 1.6 %collective-permute-done.5.refs_7_ = bf16[256,1024]{1,0:T(8,128)(2,1)S(1)} collective-permute-done((bf16[256,1024]{1,0:T(8,128)(2,1)S(1)}, bf16[256,1024]{1,0:T(8,128)(2,1)S(1)}, u32[]{:S(2)}, u32[]{:S(2)}) %collective-permute-start.5) | collective-permute-done | bytes 524320 | tf_op jit(solution)/shard_map/ppermute | solution.py:40
  55.6 1.7 %update_rows.1 = (bf16[256,1024]{1,0:T(8,128)(2,1)S(1)}, bf16[256,1024]{1,0:T(8,128)(2,1)S(1)}, f32[128,1024]{1,0:T(8,128)}, f32[128,1024]{1,0:T(8,128)}, f32[32...) custom-call(f32[128,1024]{1,0:T(8,128)S(1)} %bitcast.27, f32[128,1024]{1,0:T(8,128)S(1)} %bitcast.28, f32[32,4096]{1,0:T(8,128)S(1)} %copy-done, ...), custom_call_target="tpu_custom_call" | custom-call | bytes 7864320 | tf_op jit(solution)/shard_map/update_rows/pallas_call | solution.py:26
  59.3 2.6 %collective-permute-start.7 = (bf16[256,1024]{1,0:T(8,128)(2,1)S(1)}, bf16[256,1024]{1,0:T(8,128)(2,1)S(1)}, u32[]{:S(2)}, u32[]{:S(2)}) collective-permute-start(bf16[256,1024]{1,0:T(8,128)(2,1)S(1)} %get-tuple-element.57.refs_0_), channel_id=1, source_target_pairs={{0,16},{8,24},{16,0},{24,8},{1,17},{9,25},{17,1},{25,9},{2,18},{10... | collective-permute-start | bytes 1572872 | tf_op jit(solution)/shard_map/ppermute | solution.py:40
  61.9 6.2 %collective-permute-done.9.refs_0_.refs_1_ = bf16[256,1024]{1,0:T(8,128)(2,1)S(1)} collective-permute-done((bf16[256,1024]{1,0:T(8,128)(2,1)S(1)}, bf16[256,1024]{1,0:T(8,128)(2,1)S(1)}, u32[]{:S(2)}, u32[]{:S(2)}) %collective-permute-start.9) | collective-permute-done | bytes 524320 | tf_op jit(solution)/shard_map/ppermute | solution.py:40
  68.1 11.4 %collective-permute-done.8.x = bf16[256,1024]{1,0:T(8,128)(2,1)S(1)} collective-permute-done((bf16[256,1024]{1,0:T(8,128)(2,1)S(1)}, bf16[256,1024]{1,0:T(8,128)(2,1)S(1)}, u32[]{:S(2)}, u32[]{:S(2)}) %collective-permute-start.8) | collective-permute-done | bytes 524320 | tf_op jit(solution)/shard_map/ppermute | solution.py:40
  80.0 1.9 %collective-permute-done.7.x.refs_0_ = bf16[256,1024]{1,0:T(8,128)(2,1)S(1)} collective-permute-done((bf16[256,1024]{1,0:T(8,128)(2,1)S(1)}, bf16[256,1024]{1,0:T(8,128)(2,1)S(1)}, u32[]{:S(2)}, u32[]{:S(2)}) %collective-permute-start.7) | collective-permute-done | bytes 524320 | tf_op jit(solution)/shard_map/ppermute | solution.py:40
  81.9 10.1 %collective-permute-done.10.refs_0_.refs_1_ = bf16[256,1024]{1,0:T(8,128)(2,1)S(1)} collective-permute-done((bf16[256,1024]{1,0:T(8,128)(2,1)S(1)}, bf16[256,1024]{1,0:T(8,128)(2,1)S(1)}, u32[]{:S(2)}, u32[]{:S(2)}) %collective-permute-start.10) | collective-permute-done | bytes 524320 | tf_op jit(solution)/shard_map/ppermute | solution.py:40
  94.8 2.2 %collective-permute-start.23 = (bf16[256,1024]{1,0:T(8,128)(2,1)S(1)}, bf16[256,1024]{1,0:T(8,128)(2,1)S(1)}, u32[]{:S(2)}, u32[]{:S(2)}) collective-permute-start(bf16[256,1024]{1,0:T(8,128)(2,1)S(1)} %gate.10), channel_id=1, source_target_pairs={{0,16},{8,24},{16,0},{24,8},{1,17},{9,25},{17,1},{25,9},{2,18},{10... | collective-permute-start | bytes 1572872 | tf_op jit(solution)/shard_map/ppermute | solution.py:40
  97.0 17.7 %collective-permute-done.11.refs_0_ = bf16[256,1024]{1,0:T(8,128)(2,1)S(1)} collective-permute-done((bf16[256,1024]{1,0:T(8,128)(2,1)S(1)}, bf16[256,1024]{1,0:T(8,128)(2,1)S(1)}, u32[]{:S(2)}, u32[]{:S(2)}) %collective-permute-start.11) | collective-permute-done | bytes 524320 | tf_op jit(solution)/shard_map/ppermute | solution.py:40
  116.8 3.3 %collective-permute-done.23.x.refs_0_ = bf16[256,1024]{1,0:T(8,128)(2,1)S(1)} collective-permute-done((bf16[256,1024]{1,0:T(8,128)(2,1)S(1)}, bf16[256,1024]{1,0:T(8,128)(2,1)S(1)}, u32[]{:S(2)}, u32[]{:S(2)}) %collective-permute-start.23) | collective-permute-done | bytes 524320 | tf_op jit(solution)/shard_map/ppermute | solution.py:40
  120.1 7.9 %collective-permute-done.12.refs_0_.refs_1_ = bf16[256,1024]{1,0:T(8,128)(2,1)S(1)} collective-permute-done((bf16[256,1024]{1,0:T(8,128)(2,1)S(1)}, bf16[256,1024]{1,0:T(8,128)(2,1)S(1)}, u32[]{:S(2)}, u32[]{:S(2)}) %collective-permute-start.12) | collective-permute-done | bytes 524320 | tf_op jit(solution)/shard_map/ppermute | solution.py:40
  130.8 2.0 %place_rows.4 = (bf16[4,4,128,1024]{3,2,1,0:T(8,128)(2,1)}, bf16[4,4,64,2048]{3,2,1,0:T(8,128)(2,1)}, f32[8,128]{1,0:T(8,128)}) custom-call(bf16[256,1024]{1,0:T(8,128)(2,1)S(1)} %get-tuple-element.57.refs_0_, bf16[256,1024]{1,0:T(8,128)(2,1)S(1)} %collective-permute-done.9.refs_0_.refs_1_, bf16[256,1024]{1,0:T(8,128)(2,1)S(1)} %collective-permute-done.21.refs_2_, ...), custom_call_target="tpu_custom_call" | custom-call | bytes 25178112 | tf_op jit(solution)/shard_map/place_rows/pallas_call | solution.py:26
  132.8 2.0 %place_rows.5 = (bf16[4,4,128,1024]{3,2,1,0:T(8,128)(2,1)}, bf16[4,4,64,2048]{3,2,1,0:T(8,128)(2,1)}, f32[8,128]{1,0:T(8,128)}) custom-call(bf16[256,1024]{1,0:T(8,128)(2,1)S(1)} %gate.7.refs_0_, bf16[256,1024]{1,0:T(8,128)(2,1)S(1)} %collective-permute-done.10.refs_0_.refs_1_, ...), custom_call_target="tpu_custom_call", output_to_operand_aliasing={{0}: (4, {}), {1}: (5, {})} | custom-call | bytes 25178112 | tf_op jit(solution)/shard_map/place_rows/pallas_call | solution.py:26
  134.8 2.0 %place_rows.6 = (bf16[4,4,128,1024]{3,2,1,0:T(8,128)(2,1)}, bf16[4,4,64,2048]{3,2,1,0:T(8,128)(2,1)}, f32[8,128]{1,0:T(8,128)}) custom-call(bf16[256,1024]{1,0:T(8,128)(2,1)S(1)} %collective-permute-done.7.x.refs_0_, bf16[256,1024]{1,0:T(8,128)(2,1)S(1)} %collective-permute-done.16.refs_1_, ...), custom_call_target="tpu_custom_call", output_to_operand_aliasing={{0}: (4, {}), {1}: (5, {})} | custom-call | bytes 25178112 | tf_op jit(solution)/shard_map/place_rows/pallas_call | solution.py:26
  139.6 3.0 %collective-permute-done.24.refs_1_ = bf16[256,1024]{1,0:T(8,128)(2,1)S(1)} collective-permute-done((bf16[256,1024]{1,0:T(8,128)(2,1)S(1)}, bf16[256,1024]{1,0:T(8,128)(2,1)S(1)}, u32[]{:S(2)}, u32[]{:S(2)}) %collective-permute-start.24) | collective-permute-done | bytes 524320 | tf_op jit(solution)/shard_map/ppermute | solution.py:40
  (82 shorter events, 22.8 us)
Async XLA Ops:
  4.8 8.9 %collective-permute-start = (bf16[80,256]{1,0:T(8,128)(2,1)S(1)}, bf16[80,256]{1,0:T(8,128)(2,1)S(1)}, u32[]{:S(2)}, u32[]{:S(2)}) collective-permute-start(bf16[80,256]{1,0:T(8,128)(2,1)S(1)} %get-tuple-element.47), channel_id=1, source_target_pairs={{0,8},{8,0},{16,24},{24,16},{1,9},{9,1},{17,25},{25,17},{2,10},{10... | collective-permute-start | bytes 122888 | tf_op jit(solution)/shard_map/ppermute | solution.py:40
  17.3 12.1 %collective-permute-start.3 = (bf16[256,1024]{1,0:T(8,128)(2,1)S(1)}, bf16[256,1024]{1,0:T(8,128)(2,1)S(1)}, u32[]{:S(2)}, u32[]{:S(2)}) collective-permute-start(bf16[256,1024]{1,0:T(8,128)(2,1)S(1)} %gate.6), channel_id=1, source_target_pairs={{0,8},{8,0},{16,24},{24,16},{1,9},{9,1},{17,25},{25,17},{2,10},{10... | collective-permute-start | bytes 1572872 | tf_op jit(solution)/shard_map/ppermute | solution.py:40
  17.5 20.1 %collective-permute-start.6 = (f32[2,32,2048]{2,1,0:T(8,128)S(1)}, f32[2,32,2048]{2,1,0:T(8,128)S(1)}, u32[]{:S(2)}, u32[]{:S(2)}) collective-permute-start(f32[2,32,2048]{2,1,0:T(8,128)S(1)} %up_state.1), channel_id=1, source_target_pairs={{0,1},{1,0},{2,3},{3,2},{4,5},{5,4},{6,7},{7,6},{8,9},{9,8},{10,11... | collective-permute-start | bytes 1572872 | tf_op jit(solution)/shard_map/ppermute | solution.py:347
  31.7 22.3 %collective-permute-start.4 = (bf16[256,1024]{1,0:T(8,128)(2,1)S(1)}, bf16[256,1024]{1,0:T(8,128)(2,1)S(1)}, u32[]{:S(2)}, u32[]{:S(2)}) collective-permute-start(bf16[256,1024]{1,0:T(8,128)(2,1)S(1)} %get-tuple-element.55), channel_id=1, source_target_pairs={{0,8},{8,0},{16,24},{24,16},{1,9},{9,1},{17,25},{25,17},{2,10},{10... | collective-permute-start | bytes 1572872 | tf_op jit(solution)/shard_map/ppermute | solution.py:40
  32.0 23.6 %collective-permute-start.5 = (bf16[256,1024]{1,0:T(8,128)(2,1)S(1)}, bf16[256,1024]{1,0:T(8,128)(2,1)S(1)}, u32[]{:S(2)}, u32[]{:S(2)}) collective-permute-start(bf16[256,1024]{1,0:T(8,128)(2,1)S(1)} %get-tuple-element.56), channel_id=1, source_target_pairs={{0,16},{8,24},{16,0},{24,8},{1,17},{9,25},{17,1},{25,9},{2,18},{10... | collective-permute-start | bytes 1572872 | tf_op jit(solution)/shard_map/ppermute | solution.py:40
  57.3 10.8 %collective-permute-start.9 = (bf16[256,1024]{1,0:T(8,128)(2,1)S(1)}, bf16[256,1024]{1,0:T(8,128)(2,1)S(1)}, u32[]{:S(2)}, u32[]{:S(2)}) collective-permute-start(bf16[256,1024]{1,0:T(8,128)(2,1)S(1)} %get-tuple-element.57.refs_0_), channel_id=1, source_target_pairs={{0,4},{2,6},{4,0},{6,2},{1,5},{3,7},{5,1},{7,3},{8,12},{10,14},{12... | collective-permute-start | bytes 1572872 | tf_op jit(solution)/shard_map/ppermute | solution.py:40
  58.8 20.6 %collective-permute-start.8 = (bf16[256,1024]{1,0:T(8,128)(2,1)S(1)}, bf16[256,1024]{1,0:T(8,128)(2,1)S(1)}, u32[]{:S(2)}, u32[]{:S(2)}) collective-permute-start(bf16[256,1024]{1,0:T(8,128)(2,1)S(1)} %get-tuple-element.57.refs_0_), channel_id=1, source_target_pairs={{0,8},{8,0},{16,24},{24,16},{1,9},{9,1},{17,25},{25,17},{2,10},{10... | collective-permute-start | bytes 1572872 | tf_op jit(solution)/shard_map/ppermute | solution.py:40
  59.3 22.7 %collective-permute-start.7 = (bf16[256,1024]{1,0:T(8,128)(2,1)S(1)}, bf16[256,1024]{1,0:T(8,128)(2,1)S(1)}, u32[]{:S(2)}, u32[]{:S(2)}) collective-permute-start(bf16[256,1024]{1,0:T(8,128)(2,1)S(1)} %get-tuple-element.57.refs_0_), channel_id=1, source_target_pairs={{0,16},{8,24},{16,0},{24,8},{1,17},{9,25},{17,1},{25,9},{2,18},{10... | collective-permute-start | bytes 1572872 | tf_op jit(solution)/shard_map/ppermute | solution.py:40
  79.5 12.5 %collective-permute-start.10 = (bf16[256,1024]{1,0:T(8,128)(2,1)S(1)}, bf16[256,1024]{1,0:T(8,128)(2,1)S(1)}, u32[]{:S(2)}, u32[]{:S(2)}) collective-permute-start(bf16[256,1024]{1,0:T(8,128)(2,1)S(1)} %gate.7.refs_0_), channel_id=1, source_target_pairs={{0,4},{2,6},{4,0},{6,2},{1,5},{3,7},{5,1},{7,3},{8,12},{10,14},{12... | collective-permute-start | bytes 1572872 | tf_op jit(solution)/shard_map/ppermute | solution.py:40
  80.0 12.6 %collective-permute-start.21 = (bf16[256,1024]{1,0:T(8,128)(2,1)S(1)}, bf16[256,1024]{1,0:T(8,128)(2,1)S(1)}, u32[]{:S(2)}, u32[]{:S(2)}) collective-permute-start(bf16[256,1024]{1,0:T(8,128)(2,1)S(1)} %get-tuple-element.57.refs_0_), channel_id=1, source_target_pairs={{0,2},{2,0},{4,6},{6,4},{1,3},{3,1},{5,7},{7,5},{8,10},{10,8},{12,... | collective-permute-start | bytes 1572872 | tf_op jit(solution)/shard_map/ppermute | solution.py:40
  80.0 14.7 %collective-permute-start.25 = (bf16[256,1024]{1,0:T(8,128)(2,1)S(1)}, bf16[256,1024]{1,0:T(8,128)(2,1)S(1)}, u32[]{:S(2)}, u32[]{:S(2)}) collective-permute-start(bf16[256,1024]{1,0:T(8,128)(2,1)S(1)} %get-tuple-element.69.x.refs_0_), channel_id=1, source_target_pairs={{0,8},{8,0},{16,24},{24,16},{1,9},{9,1},{17,25},{25,17},{2,10},{10... | collective-permute-start | bytes 1572872 | tf_op jit(solution)/shard_map/ppermute | solution.py:40
  92.0 22.7 %collective-permute-start.11 = (bf16[256,1024]{1,0:T(8,128)(2,1)S(1)}, bf16[256,1024]{1,0:T(8,128)(2,1)S(1)}, u32[]{:S(2)}, u32[]{:S(2)}) collective-permute-start(bf16[256,1024]{1,0:T(8,128)(2,1)S(1)} %gate.8), channel_id=1, source_target_pairs={{0,8},{8,0},{16,24},{24,16},{1,9},{9,1},{17,25},{25,17},{2,10},{10... | collective-permute-start | bytes 1572872 | tf_op jit(solution)/shard_map/ppermute | solution.py:40
  92.1 24.1 %collective-permute-start.22 = (bf16[256,1024]{1,0:T(8,128)(2,1)S(1)}, bf16[256,1024]{1,0:T(8,128)(2,1)S(1)}, u32[]{:S(2)}, u32[]{:S(2)}) collective-permute-start(bf16[256,1024]{1,0:T(8,128)(2,1)S(1)} %collective-permute-done.9.refs_0_.refs_1_), channel_id=1, source_target_pairs={{0,2},{2,0},{4,6},{6,4},{1,3},{3,1},{5,7},{7,5},{8,10},{10,8},{12,... | collective-permute-start | bytes 1572872 | tf_op jit(solution)/shard_map/ppermute | solution.py:40
  92.2 24.1 %collective-permute-start.19 = (bf16[256,1024]{1,0:T(8,128)(2,1)S(1)}, bf16[256,1024]{1,0:T(8,128)(2,1)S(1)}, u32[]{:S(2)}, u32[]{:S(2)}) collective-permute-start(bf16[256,1024]{1,0:T(8,128)(2,1)S(1)} %gate.7.refs_0_), channel_id=1, source_target_pairs={{0,2},{2,0},{4,6},{6,4},{1,3},{3,1},{5,7},{7,5},{8,10},{10,8},{12,... | collective-permute-start | bytes 1572872 | tf_op jit(solution)/shard_map/ppermute | solution.py:40
  92.7 24.1 %collective-permute-start.16 = (bf16[256,1024]{1,0:T(8,128)(2,1)S(1)}, bf16[256,1024]{1,0:T(8,128)(2,1)S(1)}, u32[]{:S(2)}, u32[]{:S(2)}) collective-permute-start(bf16[256,1024]{1,0:T(8,128)(2,1)S(1)} %collective-permute-done.7.x.refs_0_), channel_id=1, source_target_pairs={{0,4},{2,6},{4,0},{6,2},{1,5},{3,7},{5,1},{7,3},{8,12},{10,14},{12... | collective-permute-start | bytes 1572872 | tf_op jit(solution)/shard_map/ppermute | solution.py:40
  94.8 25.4 %collective-permute-start.23 = (bf16[256,1024]{1,0:T(8,128)(2,1)S(1)}, bf16[256,1024]{1,0:T(8,128)(2,1)S(1)}, u32[]{:S(2)}, u32[]{:S(2)}) collective-permute-start(bf16[256,1024]{1,0:T(8,128)(2,1)S(1)} %gate.10), channel_id=1, source_target_pairs={{0,16},{8,24},{16,0},{24,8},{1,17},{9,25},{17,1},{25,9},{2,18},{10... | collective-permute-start | bytes 1572872 | tf_op jit(solution)/shard_map/ppermute | solution.py:40
  114.7 13.3 %collective-permute-start.12 = (bf16[256,1024]{1,0:T(8,128)(2,1)S(1)}, bf16[256,1024]{1,0:T(8,128)(2,1)S(1)}, u32[]{:S(2)}, u32[]{:S(2)}) collective-permute-start(bf16[256,1024]{1,0:T(8,128)(2,1)S(1)} %collective-permute-done.11.refs_0_), channel_id=1, source_target_pairs={{0,4},{2,6},{4,0},{6,2},{1,5},{3,7},{5,1},{7,3},{8,12},{10,14},{12... | collective-permute-start | bytes 1572872 | tf_op jit(solution)/shard_map/ppermute | solution.py:40
  116.2 11.9 %collective-permute-start.17 = (bf16[256,1024]{1,0:T(8,128)(2,1)S(1)}, bf16[256,1024]{1,0:T(8,128)(2,1)S(1)}, u32[]{:S(2)}, u32[]{:S(2)}) collective-permute-start(bf16[256,1024]{1,0:T(8,128)(2,1)S(1)} %collective-permute-done.7.x.refs_0_), channel_id=1, source_target_pairs={{0,2},{2,0},{4,6},{6,4},{1,3},{3,1},{5,7},{7,5},{8,10},{10,8},{12,... | collective-permute-start | bytes 1572872 | tf_op jit(solution)/shard_map/ppermute | solution.py:40
  116.3 12.0 %collective-permute-start.20 = (bf16[256,1024]{1,0:T(8,128)(2,1)S(1)}, bf16[256,1024]{1,0:T(8,128)(2,1)S(1)}, u32[]{:S(2)}, u32[]{:S(2)}) collective-permute-start(bf16[256,1024]{1,0:T(8,128)(2,1)S(1)} %collective-permute-done.10.refs_0_.refs_1_), channel_id=1, source_target_pairs={{0,2},{2,0},{4,6},{6,4},{1,3},{3,1},{5,7},{7,5},{8,10},{10,8},{12,... | collective-permute-start | bytes 1572872 | tf_op jit(solution)/shard_map/ppermute | solution.py:40
  116.8 18.1 %collective-permute-start.18 = (bf16[256,1024]{1,0:T(8,128)(2,1)S(1)}, bf16[256,1024]{1,0:T(8,128)(2,1)S(1)}, u32[]{:S(2)}, u32[]{:S(2)}) collective-permute-start(bf16[256,1024]{1,0:T(8,128)(2,1)S(1)} %collective-permute-done.16.refs_1_), channel_id=1, source_target_pairs={{0,2},{2,0},{4,6},{6,4},{1,3},{3,1},{5,7},{7,5},{8,10},{10,8},{12,... | collective-permute-start | bytes 1572872 | tf_op jit(solution)/shard_map/ppermute | solution.py:40
  120.1 18.0 %collective-permute-start.13 = (bf16[256,1024]{1,0:T(8,128)(2,1)S(1)}, bf16[256,1024]{1,0:T(8,128)(2,1)S(1)}, u32[]{:S(2)}, u32[]{:S(2)}) collective-permute-start(bf16[256,1024]{1,0:T(8,128)(2,1)S(1)} %collective-permute-done.11.refs_0_), channel_id=1, source_target_pairs={{0,2},{2,0},{4,6},{6,4},{1,3},{3,1},{5,7},{7,5},{8,10},{10,8},{12,... | collective-permute-start | bytes 1572872 | tf_op jit(solution)/shard_map/ppermute | solution.py:40
  128.1 10.1 %collective-permute-start.14 = (bf16[256,1024]{1,0:T(8,128)(2,1)S(1)}, bf16[256,1024]{1,0:T(8,128)(2,1)S(1)}, u32[]{:S(2)}, u32[]{:S(2)}) collective-permute-start(bf16[256,1024]{1,0:T(8,128)(2,1)S(1)} %collective-permute-done.12.refs_0_.refs_1_), channel_id=1, source_target_pairs={{0,2},{2,0},{4,6},{6,4},{1,3},{3,1},{5,7},{7,5},{8,10},{10,8},{12,... | collective-permute-start | bytes 1572872 | tf_op jit(solution)/shard_map/ppermute | solution.py:40
  128.1 14.4 %collective-permute-start.24 = (bf16[256,1024]{1,0:T(8,128)(2,1)S(1)}, bf16[256,1024]{1,0:T(8,128)(2,1)S(1)}, u32[]{:S(2)}, u32[]{:S(2)}) collective-permute-start(bf16[256,1024]{1,0:T(8,128)(2,1)S(1)} %gate.11), channel_id=1, source_target_pairs={{0,8},{8,0},{16,24},{24,16},{1,9},{9,1},{17,25},{25,17},{2,10},{10... | collective-permute-start | bytes 1572872 | tf_op jit(solution)/shard_map/ppermute | solution.py:40
  128.2 8.8 %collective-permute-start.15 = (f32[32,2048]{1,0:T(8,128)S(1)}, f32[32,2048]{1,0:T(8,128)S(1)}, u32[]{:S(2)}, u32[]{:S(2)}) collective-permute-start(f32[32,2048]{1,0:T(8,128)S(1)} %gate.9), channel_id=1, source_target_pairs={{0,1},{1,0},{2,3},{3,2},{4,5},{5,4},{6,7},{7,6},{8,9},{9,8},{10,11... | collective-permute-start | bytes 786440 | tf_op jit(solution)/shard_map/ppermute | solution.py:424
  (19 other events, 299.9 us)
where the time goes:
time: 144 us; the launch traced here: 143 us
  waiting for transfers between devices  94.2 us (65%)
  starting transfers between devices  22.3 us (15%)
  Pallas kernels  18.5 us (13%)
  local copies, waits for them, and re-layouts  6.41 us (4%)
    ppermute x24, waiting for transfers between devices, swap(): lax.ppermute(x, axis, [(i, i ^ bit) for i in range(lax.axis_size(axis))])  94 us
    ppermute x24, starting transfers between devices, swap(): lax.ppermute(x, axis, [(i, i ^ bit) for i in range(lax.axis_size(axis))])  19.2 us
    pallas_call x19, Pallas kernels, call(): pl.pallas_call(kernel, name=name, out_shape=out_shape, in_specs=in_specs,...  18.5 us
    unnamed x34, local copies, waits for them, and re-layouts  6.41 us
  transfers between devices with their start and end apart: 26, of which 14 were waited for; matrix products, arithmetic and copies ran while one was open for 1% of the time, Pallas kernels for 10%

commit v1 on v0

--- a/solution.py
+++ b/solution.py
@@ -36,6 +36,22 @@
     )(*operands)
 
 
+OUTER = (0, 3)
+INWARD = ((0, 1), (3, 2))
+ACROSS = ((1, 2), (2, 1))
+OUTWARD = ((1, 0), (2, 3))
+
+
+def owners():
+    pos = lax.axis_index("replica")
+    low = pos < 2
+    return pos, jnp.bitwise_xor(pos, 1), jnp.where(low, 2, 1), jnp.where(low, 3, 0)
+
+
+def along(x, pairs):
+    return lax.ppermute(x, "replica", pairs)
+
+
 def swap(x, axis, bit):
     return lax.ppermute(x, axis, [(i, i ^ bit) for i in range(lax.axis_size(axis))])
 
@@ -48,7 +64,8 @@
 
 
 def project_kernel(trained, basis, norm, own, *refs):
-    *outs, projected = refs
+    *outs, token, projected = refs
+    token[...] = jnp.zeros_like(token)
     rank, rows = basis.shape[0], own.shape[1]
     high = basis[...].astype(BF16)
     rest = basis[...] - high.astype(F32)
@@ -114,9 +131,9 @@
     norm_cast[...] = norm_stored[...].astype(BF16)
 
 
-def pack_kernel(masks, down, up, *refs):
+def pack_kernel(down, up, _, *refs):
     *outs, sems = refs
-    pos, shard = lax.axis_index("replica"), lax.axis_index("shard")
+    shard = lax.axis_index("shard")
     rows, width = down.shape[2:]
     tall, cols = up.shape[2:]
     copies = []
@@ -125,8 +142,7 @@
         copies.append(pltpu.make_async_copy(source, dest, sems.at[len(copies)]))
         copies[-1].start()
 
-    for mask, out in zip(masks, outs):
-        owner = jnp.bitwise_xor(pos, mask)
+    for owner, out in reversed(list(zip(owners(), outs))):
         bring(down.at[owner, shard], out.at[pl.ds(0, rows)])
         for chunk in range(cols // width):
             bring(
@@ -137,16 +153,47 @@
         copy.wait()
 
 
-def add_kernel(block, came, later, out, later_out):
-    out[...] = (block[...].astype(F32) + came[...].astype(F32)).astype(BF16)
-    later_out[...] = later[...]
+def add_kernel(block, came, *refs):
+    refs[-1][...] = (block[...].astype(F32) + came[...].astype(F32)).astype(BF16)
+
+
+def add(block, came, *after):
+    return call(
+        add_kernel,
+        "add_block",
+        jax.ShapeDtypeStruct(block.shape, BF16),
+        [VMEM] * 2 + [ANY] * len(after),
+        VMEM,
+        [],
+        block,
+        came,
+        *after,
+    )
+
+
+def pick_kernel(middle, end, out):
+    pos = lax.axis_index("replica")
+    outer = jnp.logical_or(pos == OUTER[0], pos == OUTER[1])
+
+    @pl.when(outer)
+    def _():
+        out[...] = end[...]
+
+    @pl.when(jnp.logical_not(outer))
+    def _():
+        out[...] = middle[...]
+
+
+def pick(middle, end):
+    shape = jax.ShapeDtypeStruct(end.shape, end.dtype)
+    return call(pick_kernel, "pick", shape, [VMEM] * 2, VMEM, [], middle, end)
 
 
 def update_kernel(groups, tensors, n_came, *refs):
     refs = list(refs)
-    master_down, moment_down, master_up, moment_up, embed = refs[:5]
-    came, state_came = refs[5 : 5 + n_came], refs[5 + n_came : 4 + n_came + tensors]
-    piece, embed_out, stored_down, velocity_down, *sums = refs[4 + n_came + tensors : -3]
+    master_down, moment_down, master_up, moment_up = refs[:4]
+    came, state_came = refs[4 : 4 + n_came], refs[4 + n_came : 3 + n_came + tensors]
+    piece, stored_down, velocity_down, *sums = refs[3 + n_came + tensors : -3]
     summed, master, moment = refs[-3:]
     me = lax.axis_index("tensor")
     rows_down, width = master_down.shape
@@ -185,7 +232,6 @@
         piece[lo : lo + tall, :] = stored.astype(BF16)
     for shift in range(tensors):
         sums[shift][...] = summed[at(lax.rem(me + shift, tensors)), :]
-    embed_out[...] = embed[...]
 
 
 def up_kernel(groups, tensors, master_up, moment_up, *refs):
@@ -230,10 +276,10 @@
     )
 
 
-def place_kernel(far, masks, *refs):
+def place_kernel(slot, masks, *refs):
     pieces, (down, up, token, sems) = refs[: len(masks)], refs[-4:]
     token[...] = jnp.zeros_like(token)
-    pos, shard = lax.axis_index("replica"), lax.axis_index("shard")
+    shard = lax.axis_index("shard")
     rows, width = down.shape[2:]
     tall, cols = up.shape[2:]
     copies = []
@@ -242,7 +288,7 @@
         copies.append(pltpu.make_async_copy(source, dest, sems.at[len(copies)]))
         copies[-1].start()
 
-    owner = jnp.bitwise_xor(pos, far)
+    owner = owners()[slot]
     for piece, mask in zip(pieces, masks):
         place = jnp.bitwise_xor(shard, mask)
         send(piece.at[pl.ds(0, rows)], down.at[owner, place])
@@ -255,12 +301,11 @@
         copy.wait()
 
 
-def place_embed_kernel(masks, *refs):
-    pieces, (out, sems) = refs[: len(masks)], refs[-2:]
-    pos = lax.axis_index("replica")
+def place_embed_kernel(slots, *refs):
+    pieces, (out, sems) = refs[: len(slots)], refs[-2:]
     copies = [
-        pltpu.make_async_copy(piece, out.at[jnp.bitwise_xor(pos, mask)], sems.at[i])
-        for i, (piece, mask) in enumerate(zip(pieces, masks))
+        pltpu.make_async_copy(piece, out.at[owners()[slot]], sems.at[i])
+        for i, (piece, slot) in enumerate(zip(pieces, slots))
     ]
     for copy in copies:
         copy.start()
@@ -268,9 +313,14 @@
         copy.wait()
 
 
-def spread(pieces, axis):
-    for bit in bits_down(lax.axis_size(axis)):
-        pieces.update({mask ^ bit: swap(x, axis, bit) for mask, x in list(pieces.items())})
+def spread(piece):
+    top = lax.axis_size("shard") // 2
+    return spread_low({0: piece, top: swap(piece, "shard", top)})
+
+
+def spread_low(pieces):
+    for bit in bits_down(lax.axis_size("shard") // 2):
+        pieces.update({mask ^ bit: swap(x, "shard", bit) for mask, x in list(pieces.items())})
     return pieces
 
 
@@ -303,34 +353,35 @@
     basis_t = embed_basis.T
     rank_rows = jax.ShapeDtypeStruct((rank, rows_embed), F32)
     packet = jax.ShapeDtypeStruct((rank + 16, rows_embed), BF16)
-    own_rows, *packets = call(
+    token_shape = jax.ShapeDtypeStruct((8, 128), F32)
+    own_rows, *packets, projected = call(
         project_kernel,
         "project_rows",
-        [rank_rows] + [packet] * (replicas - 1),
+        [rank_rows] + [packet] * (replicas - 1) + [token_shape],
         [VMEM] * 3,
-        [VMEM] * replicas,
+        [VMEM] * (replicas + 1),
         [pltpu.VMEM((rank, replicas * rows_embed), F32)],
-        trained_embed[0],
-        basis_t,
-        trained_norm[0],
+        pltpu.with_memory_space_constraint(trained_embed[0], pltpu.HBM),
+        pltpu.with_memory_space_constraint(basis_t, pltpu.HBM),
+        pltpu.with_memory_space_constraint(trained_norm[0], pltpu.HBM),
     )
     packets_came = [swap(x, "replica", mask) for mask, x in enumerate(packets, 1)]
 
     down = trained_down[0].reshape(replicas, shards, rows_down, width)
     up = trained_up[0].reshape(replicas, shards, tall, half_cols)
-    masks = [3, 2, 1, 0]
-    block3, block2, block1, block0 = call(
-        functools.partial(pack_kernel, masks),
+    own, near, middle, end = call(
+        pack_kernel,
         "pack_blocks",
         [packed] * replicas,
-        [HBM] * 2,
+        [HBM] * 2 + [VMEM],
         [VMEM] * replicas,
         [dma((replicas * (1 + chunks),))],
-        down,
-        up,
-        limit=61,
-    )
-    came2 = swap(gate(block3, *packets_came), "replica", 1)
+        pltpu.with_memory_space_constraint(down, pltpu.HBM),
+        pltpu.with_memory_space_constraint(up, pltpu.HBM),
+        projected,
+    )
+    end = gate(end, packets_came[0])
+    from_end = [along(x, INWARD) for x in (end, middle, near)]
 
     state = jax.ShapeDtypeStruct((2, rows_up, half_cols), F32)
     states = call(
@@ -364,7 +415,7 @@
             norm_state,
             norm_state,
         ],
-        [VMEM] * (7 + replicas),
+        [VMEM] * (7 + replicas) + [ANY],
         [VMEM] * 6,
         [],
         own_rows,
@@ -376,57 +427,51 @@
         master_norm,
         moment_norm,
         *packets_came,
-    )
-
-    block2, block1 = call(
-        add_kernel,
-        "add_block",
-        [packed] * 2,
-        [VMEM] * 3,
-        [VMEM] * 2,
-        [],
-        block2,
-        came2,
-        block1,
-    )
-    came0 = [block0, swap(block1, "replica", 1), swap(block2, "replica", 2)]
+        end,
+    )
+
+    embed_out = along(recast_rows, OUTWARD)
+    embed_middle = along(recast_rows, ACROSS)
+    end_partial = along(add(end, from_end[0], embed_out, embed_middle), ACROSS)
+    middle_partial = along(add(middle, from_end[1]), ACROSS)
+    embed_middle_out = along(embed_middle, OUTWARD)
+    to_end = along(add(near, end_partial, embed_middle_out), OUTWARD)
+    came0 = [own, from_end[2], middle_partial, to_end]
     half_sum = jax.ShapeDtypeStruct((rows_up, half_cols), F32)
     down_state = jax.ShapeDtypeStruct((rows_down, width), F32)
-    piece, embed_late, stored_down, velocity_down, *sums = call(
+    piece, stored_down, velocity_down, *sums = call(
         functools.partial(update_kernel, replicas, tensors, len(came0)),
         "update_rows",
-        [packed, embed_rows, down_state, down_state] + [half_sum] * tensors,
-        [VMEM] * (5 + len(came0) + len(states)),
-        [VMEM] * (4 + tensors),
+        [packed, down_state, down_state] + [half_sum] * tensors,
+        [VMEM] * (4 + len(came0) + len(states)),
+        [VMEM] * (3 + tensors),
         [pltpu.VMEM((tall, half_cols), F32)] * 3,
         master_down[0],
         moment_down[0],
         master_up,
         moment_up,
-        recast_rows,
         *came0,
         *states,
     )
 
     top = shards // 2
-    pieces = {0: piece, 1: swap(piece, "replica", 1), 2: swap(piece, "replica", 2)}
-    groups = {0: spread({0: piece}, "shard")}
-    groups[1] = spread({0: gate(pieces[1], groups[0][top])}, "shard")
-    groups[2] = spread({0: pieces[2]}, "shard")
-    pieces[3] = swap(gate(pieces[2], groups[1][top]), "replica", 1)
-    groups[3] = spread({0: pieces[3]}, "shard")
-    last_far = groups[3][top]
-    embed_near = swap(embed_late, "replica", 1)
-    embed_far = swap(gate(embed_late, pieces[2]), "replica", 2)
-    embed_last = swap(gate(embed_far, last_far), "replica", 1)
+    near_piece = swap(piece, "replica", 1)
+    middle_piece = along(piece, ACROSS)
+    end_piece = along(near_piece, ACROSS)
+    second = pick(middle_piece, along(middle_piece, OUTWARD))
+    third = pick(end_piece, along(end_piece, OUTWARD))
+    groups = [spread(x) for x in (piece, near_piece, second)]
+
+    embed_in = along(gate(recast_rows, near_piece), INWARD)
+    embed_end = along(embed_in, ACROSS)
+    embed_last = along(embed_end, OUTWARD)
 
     sums = [sums[0]] + [
         lax.ppermute(
-            gate(x, last_far), "tensor", [(i, (i + shift) % tensors) for i in range(tensors)]
+            gate(x, second), "tensor", [(i, (i + shift) % tensors) for i in range(tensors)]
         )
         for shift, x in enumerate(sums[1:], 1)
     ]
-    token_shape = jax.ShapeDtypeStruct((8, 128), F32)
     stored_up, velocity_up, token = call(
         functools.partial(up_kernel, replicas, tensors),
         "update_up",
@@ -439,48 +484,54 @@
         *sums,
     )
 
+    embed_shape = jax.ShapeDtypeStruct((replicas, rows_embed, width), BF16)
+    recast_embed = call(
+        functools.partial(place_embed_kernel, [0, 1, 2]),
+        "place_embed",
+        embed_shape,
+        [VMEM] * 4,
+        HBM,
+        [dma((3,))],
+        recast_rows,
+        pick(embed_in, embed_out),
+        pick(embed_middle, embed_middle_out),
+        token,
+    )
+
     shapes = [jax.ShapeDtypeStruct(down.shape, BF16), jax.ShapeDtypeStruct(up.shape, BF16)]
-    placed = ()
-    for far, group in groups.items():
-        extra = (token,) if far == replicas - 1 else ()
-        count = len(group) + len(extra)
-        *placed, placed_token = call(
-            functools.partial(place_kernel, far, list(group)),
+
+    def place(slot, group, placed, *after):
+        count = len(group) + len(after)
+        return call(
+            functools.partial(place_kernel, slot, list(group)),
             "place_rows",
             shapes + [token_shape],
             [VMEM] * count + [HBM] * len(placed),
             [HBM] * 2 + [VMEM],
             [dma((len(group) * (1 + chunks),))],
             *group.values(),
-            *extra,
+            *after,
             *placed,
             aliases={count: 0, count + 1: 1} if placed else {},
         )
-    recast_down, recast_up = placed
-
-    embed_shape = jax.ShapeDtypeStruct((replicas, rows_embed, width), BF16)
+
+    placed = []
+    for slot, group in enumerate(groups):
+        *placed, token = place(slot, group, placed, token)
+    far = gate(swap(third, "shard", top), token)
+    *placed, token = place(3, spread_low({0: third}), placed)
+    recast_down, recast_up, token = place(3, spread_low({top: far}), placed)
     recast_embed = call(
-        functools.partial(place_embed_kernel, [0, 1]),
+        functools.partial(place_embed_kernel, [3]),
         "place_embed",
         embed_shape,
-        [VMEM] * 2,
+        [VMEM] * 2 + [HBM],
         HBM,
-        [dma((2,))],
-        embed_late,
-        embed_near,
-    )
-    recast_embed = call(
-        functools.partial(place_embed_kernel, [2, 3]),
-        "place_embed",
-        embed_shape,
-        [VMEM] * 3 + [HBM],
-        HBM,
-        [dma((2,))],
-        embed_far,
-        embed_last,
-        placed_token,
+        [dma((1,))],
+        pick(embed_end, embed_last),
+        token,
         recast_embed,
-        aliases={3: 0},
+        aliases={2: 0},
     )
 
     return (

time: 144 us -> 129 us (0.90)
  waiting for transfers between devices: 94.2 us -> 60.4 us
  starting transfers between devices: 22.3 us -> 45.5 us
  local copies, waits for them, and re-layouts: 6.41 us -> 0.06 us
    ppermute x24 -> x16, waiting for transfers between devices: 94 us -> 26.3 us  [swap(): lax.ppermute(x, axis, [(i, i ^ bit) for i in range(lax.axis_size(axis))])]
    ppermute x1 -> x17, waiting for transfers between devices: 0.16 us -> 34.1 us  [the longest x16 34.1 us: along(): return lax.ppermute(x, 'replica', pairs)]
    ppermute x1 -> x17, starting transfers between devices: 1.57 us -> 29.7 us  [the longest x16 28.2 us: along(): return lax.ppermute(x, 'replica', pairs)]
    unnamed x34 -> x20, local copies, waits for them, and re-layouts: 6.41 us -> 0.06 us
    ppermute x24 -> x16, starting transfers between devices: 19.2 us -> 14.2 us  [swap(): lax.ppermute(x, axis, [(i, i ^ bit) for i in range(lax.axis_size(axis))])]
    pallas_call x19 -> x25, Pallas kernels: 18.5 us -> 18.8 us  [call(): pl.pallas_call(kernel, name=name, out_shape=out_shape, in_specs=in_specs,...]
  transfers between devices with their start and end apart: 26 -> 34, of which waited for: 14 -> 14; matrix products, arithmetic and copies ran while one was open for 1% -> 2% of each run, Pallas kernels for 10% -> 8%
where the time goes in v1:
time: 129 us; the launch traced here: 128 us
  waiting for transfers between devices  60.4 us (47%)
  starting transfers between devices  45.5 us (35%)
  Pallas kernels  18.8 us (15%)
  matrix products  2.4 us (2%)
    ppermute x16, waiting for transfers between devices, along(): return lax.ppermute(x, 'replica', pairs)  34.1 us
    ppermute x16, starting transfers between devices, along(): return lax.ppermute(x, 'replica', pairs)  28.2 us
    ppermute x16, waiting for transfers between devices, swap(): lax.ppermute(x, axis, [(i, i ^ bit) for i in range(lax.axis_size(axis))])  26.3 us
    pallas_call x25, Pallas kernels, call(): pl.pallas_call(kernel, name=name, out_shape=out_shape, in_specs=in_specs,...  18.8 us
    ppermute x16, starting transfers between devices, swap(): lax.ppermute(x, axis, [(i, i ^ bit) for i in range(lax.axis_size(axis))])  14.2 us
  transfers between devices with their start and end apart: 34, of which 14 were waited for; matrix products, arithmetic and copies ran while one was open for 2% of the time, Pallas kernels for 8%

profile of v1, /device:TPU:0, one launch (start us, length us, event | category | flops | bytes accessed | tf_op | source)
XLA Modules:
  0.0 128.3 jit_solution(9961505212292735406)
XLA Ops:
  0.6 2.6 %project_rows.1 = (f32[64,256]{1,0:T(8,128)S(1)}, bf16[80,256]{1,0:T(8,128)(2,1)S(1)}, bf16[80,256]{1,0:T(8,128)(2,1)S(1)}, bf16[80,256]{1,0:T(8,128)(2,1)S(1)}, f32[8,128]{1,0:T(8,128)S(1)}) custom-call(bf16[1024,1024]{1,0:T(8,128)(2,1)} %bitcast.36, f32[64,1024]{1,0:T(8,128)} %bitcast.24, bf16[2,1024]{1,0:T(2,128)(2,1)} %bitcast.29), custom_call_target="tpu_custom_call" | custom-call | bytes 577536 | tf_op jit(solution)/shard_map/project_rows/pallas_call | solution.py:26
  3.2 3.1 %collective-permute-start.3 = (bf16[80,256]{1,0:T(8,128)(2,1)S(1)}, bf16[80,256]{1,0:T(8,128)(2,1)S(1)}, u32[]{:S(2)}, u32[]{:S(2)}) collective-permute-start(bf16[80,256]{1,0:T(8,128)(2,1)S(1)} %get-tuple-element.54), channel_id=1, source_target_pairs={{0,8},{8,0},{16,24},{24,16},{1,9},{9,1},{17,25},{25,17},{2,10},{10... | collective-permute-start | bytes 122888 | tf_op jit(solution)/shard_map/ppermute | solution.py:56
  6.3 2.6 %collective-permute-start.5 = (bf16[80,256]{1,0:T(8,128)(2,1)S(1)}, bf16[80,256]{1,0:T(8,128)(2,1)S(1)}, u32[]{:S(2)}, u32[]{:S(2)}) collective-permute-start(bf16[80,256]{1,0:T(8,128)(2,1)S(1)} %get-tuple-element.56), channel_id=1, source_target_pairs={{0,16},{8,24},{16,0},{24,8},{1,17},{9,25},{17,1},{25,9},{2,18},{10... | collective-permute-start | bytes 122888 | tf_op jit(solution)/shard_map/ppermute | solution.py:56
  8.9 2.4 %fusion.refs_1_ = f32[64,256]{1,0:T(8,128)S(1)} fusion(f32[1024,64]{0,1:T(8,128)} %param.25, f32[1,256,1024]{2,1,0:T(8,128)} %param.21), kind=kOutput, calls=%fused_computation | convolution fusion | flops 201326592 | bytes 1376256 | tf_op jit(solution)/shard_map/dot_general | solution.py:402
  11.4 1.8 %pack_blocks.1 = (bf16[256,1024]{1,0:T(8,128)(2,1)S(1)}, bf16[256,1024]{1,0:T(8,128)(2,1)S(1)}, bf16[256,1024]{1,0:T(8,128)(2,1)S(1)}, bf16[256,1024]{1,0:T(8,128)(2,1)S(1)}) custom-call(bf16[4,4,128,1024]{3,2,1,0:T(8,128)(2,1)} %bitcast.34, bf16[4,4,64,2048]{3,2,1,0:T(8,128)(2,1)} %bitcast.35, f32[8,128]{1,0:T(8,128)S(1)} %get-tuple-element.49._), custom_call_target="tpu_custom_call" | custom-call | bytes 6291456 | tf_op jit(solution)/shard_map/pack_blocks/pallas_call | solution.py:26
  14.7 2.0 %embed_update.1 = (f32[256,1024]{1,0:T(8,128)}, bf16[256,1024]{1,0:T(8,128)(2,1)S(1)}, f32[64,256]{1,0:T(8,128)}, bf16[2,1024]{1,0:T(2,128)(2,1)}, f32[2,1024]{1,0:T(2,128)}, /*index=5*/f32[2,1024]{1,0:T(2,128)}) custom-call(f32[64,256]{1,0:T(8,128)S(1)} %get-tuple-element.55.refs_0_, f32[64,256]{1,0:T(8,128)S(1)} %fusion.refs_1_, f32[256,1024]{1,0:T(8,128)S(1)} %bitcast.23, ...), custom_call_target="tpu_custom_call" | custom-call | bytes 4976640 | tf_op jit(solution)/shard_map/embed_update/pallas_call | solution.py:26
  18.9 4.6 %collective-permute-start.4 = (bf16[256,1024]{1,0:T(8,128)(2,1)S(1)}, bf16[256,1024]{1,0:T(8,128)(2,1)S(1)}, u32[]{:S(2)}, u32[]{:S(2)}) collective-permute-start(bf16[256,1024]{1,0:T(8,128)(2,1)S(1)} %gate.4.refs_11_.block), channel_id=1, source_target_pairs={{0,8},{24,16},{1,9},{25,17},{2,10},{26,18},{3,11},{27,19},{4,12},{... | collective-permute-start | bytes 1572872 | tf_op jit(solution)/shard_map/ppermute | solution.py:52
  24.8 7.1 %collective-permute-done.7.refs_0_.end = bf16[256,1024]{1,0:T(8,128)(2,1)S(1)} collective-permute-done((bf16[256,1024]{1,0:T(8,128)(2,1)S(1)}, bf16[256,1024]{1,0:T(8,128)(2,1)S(1)}, u32[]{:S(2)}, u32[]{:S(2)}) %collective-permute-start.7) | collective-permute-done | bytes 524320 | tf_op jit(solution)/shard_map/ppermute | solution.py:52
  31.9 3.9 %collective-permute-done.4.came = bf16[256,1024]{1,0:T(8,128)(2,1)S(1)} collective-permute-done((bf16[256,1024]{1,0:T(8,128)(2,1)S(1)}, bf16[256,1024]{1,0:T(8,128)(2,1)S(1)}, u32[]{:S(2)}, u32[]{:S(2)}) %collective-permute-start.4) | collective-permute-done | bytes 524320 | tf_op jit(solution)/shard_map/ppermute | solution.py:52
  38.0 7.1 %collective-permute-start = (bf16[256,1024]{1,0:T(8,128)(2,1)S(1)}, bf16[256,1024]{1,0:T(8,128)(2,1)S(1)}, u32[]{:S(2)}, u32[]{:S(2)}) collective-permute-start(bf16[256,1024]{1,0:T(8,128)(2,1)S(1)} %get-tuple-element.51.block), channel_id=1, source_target_pairs={{0,8},{24,16},{1,9},{25,17},{2,10},{26,18},{3,11},{27,19},{4,12},{... | collective-permute-start | bytes 1572872 | tf_op jit(solution)/shard_map/ppermute | solution.py:52
  47.9 2.5 %collective-permute-done.10.refs_0_.end = bf16[256,1024]{1,0:T(8,128)(2,1)S(1)} collective-permute-done((bf16[256,1024]{1,0:T(8,128)(2,1)S(1)}, bf16[256,1024]{1,0:T(8,128)(2,1)S(1)}, u32[]{:S(2)}, u32[]{:S(2)}) %collective-permute-start.10) | collective-permute-done | bytes 524320 | tf_op jit(solution)/shard_map/ppermute | solution.py:52
  51.8 3.8 %collective-permute-done.refs_5_ = bf16[256,1024]{1,0:T(8,128)(2,1)S(1)} collective-permute-done((bf16[256,1024]{1,0:T(8,128)(2,1)S(1)}, bf16[256,1024]{1,0:T(8,128)(2,1)S(1)}, u32[]{:S(2)}, u32[]{:S(2)}) %collective-permute-start) | collective-permute-done | bytes 524320 | tf_op jit(solution)/shard_map/ppermute | solution.py:52
  55.6 6.2 %collective-permute-done.11.refs_7_ = bf16[256,1024]{1,0:T(8,128)(2,1)S(1)} collective-permute-done((bf16[256,1024]{1,0:T(8,128)(2,1)S(1)}, bf16[256,1024]{1,0:T(8,128)(2,1)S(1)}, u32[]{:S(2)}, u32[]{:S(2)}) %collective-permute-start.11) | collective-permute-done | bytes 524320 | tf_op jit(solution)/shard_map/ppermute | solution.py:52
  61.8 1.7 %update_rows.1 = (bf16[256,1024]{1,0:T(8,128)(2,1)S(1)}, f32[128,1024]{1,0:T(8,128)}, f32[128,1024]{1,0:T(8,128)}, f32[32,2048]{1,0:T(8,128)S(1)}, f32[32,2048]{1,0:T(8,128)S(1)}) custom-call(f32[128,1024]{1,0:T(8,128)S(1)} %bitcast.26, f32[128,1024]{1,0:T(8,128)S(1)} %bitcast.27, f32[32,4096]{1,0:T(8,128)S(1)} %copy-done, f32[32,4096]{1,0:T(8,128)S(1)} %copy-done.1, ...), custom_call_target="tpu_custom_call" | custom-call | bytes 6291456 | tf_op jit(solution)/shard_map/update_rows/pallas_call | solution.py:26
  64.2 1.9 %collective-permute-start.13 = (bf16[256,1024]{1,0:T(8,128)(2,1)S(1)}, bf16[256,1024]{1,0:T(8,128)(2,1)S(1)}, u32[]{:S(2)}, u32[]{:S(2)}) collective-permute-start(bf16[256,1024]{1,0:T(8,128)(2,1)S(1)} %get-tuple-element.59.refs_0_), channel_id=1, source_target_pairs={{0,8},{8,0},{16,24},{24,16},{1,9},{9,1},{17,25},{25,17},{2,10},{10... | collective-permute-start | bytes 1572872 | tf_op jit(solution)/shard_map/ppermute | solution.py:56
  68.8 5.4 %collective-permute-done.13.refs_0_ = bf16[256,1024]{1,0:T(8,128)(2,1)S(1)} collective-permute-done((bf16[256,1024]{1,0:T(8,128)(2,1)S(1)}, bf16[256,1024]{1,0:T(8,128)(2,1)S(1)}, u32[]{:S(2)}, u32[]{:S(2)}) %collective-permute-start.13) | collective-permute-done | bytes 524320 | tf_op jit(solution)/shard_map/ppermute | solution.py:56
  74.3 3.1 %collective-permute-start.31 = (bf16[256,1024]{1,0:T(8,128)(2,1)S(1)}, bf16[256,1024]{1,0:T(8,128)(2,1)S(1)}, u32[]{:S(2)}, u32[]{:S(2)}) collective-permute-start(bf16[256,1024]{1,0:T(8,128)(2,1)S(1)} %gate.7), channel_id=1, source_target_pairs={{0,8},{24,16},{1,9},{25,17},{2,10},{26,18},{3,11},{27,19},{4,12},{... | collective-permute-start | bytes 1572872 | tf_op jit(solution)/shard_map/ppermute | solution.py:52
  78.2 1.6 %collective-permute-start.22 = (bf16[256,1024]{1,0:T(8,128)(2,1)S(1)}, bf16[256,1024]{1,0:T(8,128)(2,1)S(1)}, u32[]{:S(2)}, u32[]{:S(2)}) collective-permute-start(bf16[256,1024]{1,0:T(8,128)(2,1)S(1)} %collective-permute-done.13.refs_0_), channel_id=1, source_target_pairs={{0,4},{2,6},{4,0},{6,2},{1,5},{3,7},{5,1},{7,3},{8,12},{10,14},{12... | collective-permute-start | bytes 1572872 | tf_op jit(solution)/shard_map/ppermute | solution.py:56
  79.8 4.9 %collective-permute-done.18.end = bf16[256,1024]{1,0:T(8,128)(2,1)S(1)} collective-permute-done((bf16[256,1024]{1,0:T(8,128)(2,1)S(1)}, bf16[256,1024]{1,0:T(8,128)(2,1)S(1)}, u32[]{:S(2)}, u32[]{:S(2)}) %collective-permute-start.18) | collective-permute-done | bytes 524320 | tf_op jit(solution)/shard_map/ppermute | solution.py:52
  89.2 3.8 %collective-permute-done.22.refs_1_ = bf16[256,1024]{1,0:T(8,128)(2,1)S(1)} collective-permute-done((bf16[256,1024]{1,0:T(8,128)(2,1)S(1)}, bf16[256,1024]{1,0:T(8,128)(2,1)S(1)}, u32[]{:S(2)}, u32[]{:S(2)}) %collective-permute-start.22) | collective-permute-done | bytes 524320 | tf_op jit(solution)/shard_map/ppermute | solution.py:56
  93.7 10.1 %collective-permute-done.19.refs_1_ = bf16[256,1024]{1,0:T(8,128)(2,1)S(1)} collective-permute-done((bf16[256,1024]{1,0:T(8,128)(2,1)S(1)}, bf16[256,1024]{1,0:T(8,128)(2,1)S(1)}, u32[]{:S(2)}, u32[]{:S(2)}) %collective-permute-start.19) | collective-permute-done | bytes 524320 | tf_op jit(solution)/shard_map/ppermute | solution.py:56
  112.7 5.5 %collective-permute-done.16.x = bf16[256,1024]{1,0:T(8,128)(2,1)S(1)} collective-permute-done((bf16[256,1024]{1,0:T(8,128)(2,1)S(1)}, bf16[256,1024]{1,0:T(8,128)(2,1)S(1)}, u32[]{:S(2)}, u32[]{:S(2)}) %collective-permute-start.16) | collective-permute-done | bytes 524320 | tf_op jit(solution)/shard_map/ppermute | solution.py:56
  119.7 5.1 %collective-permute-done.33.end = bf16[256,1024]{1,0:T(8,128)(2,1)S(1)} collective-permute-done((bf16[256,1024]{1,0:T(8,128)(2,1)S(1)}, bf16[256,1024]{1,0:T(8,128)(2,1)S(1)}, u32[]{:S(2)}, u32[]{:S(2)}) %collective-permute-start.33) | collective-permute-done | bytes 524320 | tf_op jit(solution)/shard_map/ppermute | solution.py:52
  124.8 1.6 %place_rows.8 = (bf16[4,4,128,1024]{3,2,1,0:T(8,128)(2,1)}, bf16[4,4,64,2048]{3,2,1,0:T(8,128)(2,1)}, f32[8,128]{1,0:T(8,128)}) custom-call(bf16[256,1024]{1,0:T(8,128)(2,1)S(1)} %pick.5.refs_0_, bf16[256,1024]{1,0:T(8,128)(2,1)S(1)} %collective-permute-done.30.refs_1_, ...), custom_call_target="tpu_custom_call", output_to_operand_aliasing={{0}: (2, {}), {1}: (3, {})} | custom-call | bytes 25178112 | tf_op jit(solution)/shard_map/place_rows/pallas_call | solution.py:26
  (90 shorter events, 32.9 us)
Async XLA Ops:
  3.2 9.9 %collective-permute-start.3 = (bf16[80,256]{1,0:T(8,128)(2,1)S(1)}, bf16[80,256]{1,0:T(8,128)(2,1)S(1)}, u32[]{:S(2)}, u32[]{:S(2)}) collective-permute-start(bf16[80,256]{1,0:T(8,128)(2,1)S(1)} %get-tuple-element.54), channel_id=1, source_target_pairs={{0,8},{8,0},{16,24},{24,16},{1,9},{9,1},{17,25},{25,17},{2,10},{10... | collective-permute-start | bytes 122888 | tf_op jit(solution)/shard_map/ppermute | solution.py:56
  17.6 14.3 %collective-permute-start.7 = (bf16[256,1024]{1,0:T(8,128)(2,1)S(1)}, bf16[256,1024]{1,0:T(8,128)(2,1)S(1)}, u32[]{:S(2)}, u32[]{:S(2)}) collective-permute-start(bf16[256,1024]{1,0:T(8,128)(2,1)S(1)} %get-tuple-element.58.x.refs_0_), channel_id=1, source_target_pairs={{8,0},{16,24},{9,1},{17,25},{10,2},{18,26},{11,3},{19,27},{12,4},{... | collective-permute-start | bytes 1572872 | tf_op jit(solution)/shard_map/ppermute | solution.py:52
  18.9 16.9 %collective-permute-start.4 = (bf16[256,1024]{1,0:T(8,128)(2,1)S(1)}, bf16[256,1024]{1,0:T(8,128)(2,1)S(1)}, u32[]{:S(2)}, u32[]{:S(2)}) collective-permute-start(bf16[256,1024]{1,0:T(8,128)(2,1)S(1)} %gate.4.refs_11_.block), channel_id=1, source_target_pairs={{0,8},{24,16},{1,9},{25,17},{2,10},{26,18},{3,11},{27,19},{4,12},{... | collective-permute-start | bytes 1572872 | tf_op jit(solution)/shard_map/ppermute | solution.py:52
  23.5 23.6 %collective-permute-start.1 = (bf16[256,1024]{1,0:T(8,128)(2,1)S(1)}, bf16[256,1024]{1,0:T(8,128)(2,1)S(1)}, u32[]{:S(2)}, u32[]{:S(2)}) collective-permute-start(bf16[256,1024]{1,0:T(8,128)(2,1)S(1)} %get-tuple-element.52.block), channel_id=1, source_target_pairs={{0,8},{24,16},{1,9},{25,17},{2,10},{26,18},{3,11},{27,19},{4,12},{... | collective-permute-start | bytes 1572872 | tf_op jit(solution)/shard_map/ppermute | solution.py:52
  36.0 11.9 %collective-permute-start.9 = (bf16[256,1024]{1,0:T(8,128)(2,1)S(1)}, bf16[256,1024]{1,0:T(8,128)(2,1)S(1)}, u32[]{:S(2)}, u32[]{:S(2)}) collective-permute-start(bf16[256,1024]{1,0:T(8,128)(2,1)S(1)} %add_block.4), channel_id=1, source_target_pairs={{8,16},{16,8},{9,17},{17,9},{10,18},{18,10},{11,19},{19,11},{12,20... | collective-permute-start | bytes 1572872 | tf_op jit(solution)/shard_map/ppermute | solution.py:52
  36.7 13.7 %collective-permute-start.10 = (bf16[256,1024]{1,0:T(8,128)(2,1)S(1)}, bf16[256,1024]{1,0:T(8,128)(2,1)S(1)}, u32[]{:S(2)}, u32[]{:S(2)}) collective-permute-start(bf16[256,1024]{1,0:T(8,128)(2,1)S(1)} %collective-permute-done.8.refs_1_.middle), channel_id=1, source_target_pairs={{8,0},{16,24},{9,1},{17,25},{10,2},{18,26},{11,3},{19,27},{12,4},{... | collective-permute-start | bytes 1572872 | tf_op jit(solution)/shard_map/ppermute | solution.py:52
  38.0 17.6 %collective-permute-start = (bf16[256,1024]{1,0:T(8,128)(2,1)S(1)}, bf16[256,1024]{1,0:T(8,128)(2,1)S(1)}, u32[]{:S(2)}, u32[]{:S(2)}) collective-permute-start(bf16[256,1024]{1,0:T(8,128)(2,1)S(1)} %get-tuple-element.51.block), channel_id=1, source_target_pairs={{0,8},{24,16},{1,9},{25,17},{2,10},{26,18},{3,11},{27,19},{4,12},{... | collective-permute-start | bytes 1572872 | tf_op jit(solution)/shard_map/ppermute | solution.py:52
  45.2 10.4 %collective-permute-start.12 = (f32[2,32,2048]{2,1,0:T(8,128)S(1)}, f32[2,32,2048]{2,1,0:T(8,128)S(1)}, u32[]{:S(2)}, u32[]{:S(2)}) collective-permute-start(f32[2,32,2048]{2,1,0:T(8,128)S(1)} %up_state.1), channel_id=1, source_target_pairs={{0,1},{1,0},{2,3},{3,2},{4,5},{5,4},{6,7},{7,6},{8,9},{9,8},{10,11... | collective-permute-start | bytes 1572872 | tf_op jit(solution)/shard_map/ppermute | solution.py:398
  50.5 11.3 %collective-permute-start.11 = (bf16[256,1024]{1,0:T(8,128)(2,1)S(1)}, bf16[256,1024]{1,0:T(8,128)(2,1)S(1)}, u32[]{:S(2)}, u32[]{:S(2)}) collective-permute-start(bf16[256,1024]{1,0:T(8,128)(2,1)S(1)} %add_block.5), channel_id=1, source_target_pairs={{8,0},{16,24},{9,1},{17,25},{10,2},{18,26},{11,3},{19,27},{12,4},{... | collective-permute-start | bytes 1572872 | tf_op jit(solution)/shard_map/ppermute | solution.py:52
  64.2 10.1 %collective-permute-start.13 = (bf16[256,1024]{1,0:T(8,128)(2,1)S(1)}, bf16[256,1024]{1,0:T(8,128)(2,1)S(1)}, u32[]{:S(2)}, u32[]{:S(2)}) collective-permute-start(bf16[256,1024]{1,0:T(8,128)(2,1)S(1)} %get-tuple-element.59.refs_0_), channel_id=1, source_target_pairs={{0,8},{8,0},{16,24},{24,16},{1,9},{9,1},{17,25},{25,17},{2,10},{10... | collective-permute-start | bytes 1572872 | tf_op jit(solution)/shard_map/ppermute | solution.py:56
  66.0 12.1 %collective-permute-start.25 = (bf16[256,1024]{1,0:T(8,128)(2,1)S(1)}, bf16[256,1024]{1,0:T(8,128)(2,1)S(1)}, u32[]{:S(2)}, u32[]{:S(2)}) collective-permute-start(bf16[256,1024]{1,0:T(8,128)(2,1)S(1)} %get-tuple-element.59.refs_0_), channel_id=1, source_target_pairs={{0,4},{2,6},{4,0},{6,2},{1,5},{3,7},{5,1},{7,3},{8,12},{10,14},{12... | collective-permute-start | bytes 1572872 | tf_op jit(solution)/shard_map/ppermute | solution.py:56
  67.5 10.6 %collective-permute-start.26 = (bf16[256,1024]{1,0:T(8,128)(2,1)S(1)}, bf16[256,1024]{1,0:T(8,128)(2,1)S(1)}, u32[]{:S(2)}, u32[]{:S(2)}) collective-permute-start(bf16[256,1024]{1,0:T(8,128)(2,1)S(1)} %get-tuple-element.59.refs_0_), channel_id=1, source_target_pairs={{0,2},{2,0},{4,6},{6,4},{1,3},{3,1},{5,7},{7,5},{8,10},{10,8},{12,... | collective-permute-start | bytes 1572872 | tf_op jit(solution)/shard_map/ppermute | solution.py:56
  67.5 17.1 %collective-permute-start.18 = (bf16[256,1024]{1,0:T(8,128)(2,1)S(1)}, bf16[256,1024]{1,0:T(8,128)(2,1)S(1)}, u32[]{:S(2)}, u32[]{:S(2)}) collective-permute-start(bf16[256,1024]{1,0:T(8,128)(2,1)S(1)} %collective-permute-done.17.middle), channel_id=1, source_target_pairs={{8,0},{16,24},{9,1},{17,25},{10,2},{18,26},{11,3},{19,27},{12,4},{... | collective-permute-start | bytes 1572872 | tf_op jit(solution)/shard_map/ppermute | solution.py:52
  74.3 10.8 %collective-permute-start.31 = (bf16[256,1024]{1,0:T(8,128)(2,1)S(1)}, bf16[256,1024]{1,0:T(8,128)(2,1)S(1)}, u32[]{:S(2)}, u32[]{:S(2)}) collective-permute-start(bf16[256,1024]{1,0:T(8,128)(2,1)S(1)} %gate.7), channel_id=1, source_target_pairs={{0,8},{24,16},{1,9},{25,17},{2,10},{26,18},{3,11},{27,19},{4,12},{... | collective-permute-start | bytes 1572872 | tf_op jit(solution)/shard_map/ppermute | solution.py:52
  78.1 9.5 %collective-permute-start.27 = (bf16[256,1024]{1,0:T(8,128)(2,1)S(1)}, bf16[256,1024]{1,0:T(8,128)(2,1)S(1)}, u32[]{:S(2)}, u32[]{:S(2)}) collective-permute-start(bf16[256,1024]{1,0:T(8,128)(2,1)S(1)} %collective-permute-done.25.refs_1_), channel_id=1, source_target_pairs={{0,2},{2,0},{4,6},{6,4},{1,3},{3,1},{5,7},{7,5},{8,10},{10,8},{12,... | collective-permute-start | bytes 1572872 | tf_op jit(solution)/shard_map/ppermute | solution.py:56
  78.2 14.8 %collective-permute-start.22 = (bf16[256,1024]{1,0:T(8,128)(2,1)S(1)}, bf16[256,1024]{1,0:T(8,128)(2,1)S(1)}, u32[]{:S(2)}, u32[]{:S(2)}) collective-permute-start(bf16[256,1024]{1,0:T(8,128)(2,1)S(1)} %collective-permute-done.13.refs_0_), channel_id=1, source_target_pairs={{0,4},{2,6},{4,0},{6,2},{1,5},{3,7},{5,1},{7,3},{8,12},{10,14},{12... | collective-permute-start | bytes 1572872 | tf_op jit(solution)/shard_map/ppermute | solution.py:56
  85.0 18.7 %collective-permute-start.19 = (bf16[256,1024]{1,0:T(8,128)(2,1)S(1)}, bf16[256,1024]{1,0:T(8,128)(2,1)S(1)}, u32[]{:S(2)}, u32[]{:S(2)}) collective-permute-start(bf16[256,1024]{1,0:T(8,128)(2,1)S(1)} %pick.6.refs_0_), channel_id=1, source_target_pairs={{0,4},{2,6},{4,0},{6,2},{1,5},{3,7},{5,1},{7,3},{8,12},{10,14},{12... | collective-permute-start | bytes 1572872 | tf_op jit(solution)/shard_map/ppermute | solution.py:56
  86.3 17.5 %collective-permute-start.15 = (bf16[256,1024]{1,0:T(8,128)(2,1)S(1)}, bf16[256,1024]{1,0:T(8,128)(2,1)S(1)}, u32[]{:S(2)}, u32[]{:S(2)}) collective-permute-start(bf16[256,1024]{1,0:T(8,128)(2,1)S(1)} %collective-permute-done.14.middle), channel_id=1, source_target_pairs={{8,0},{16,24},{9,1},{17,25},{10,2},{18,26},{11,3},{19,27},{12,4},{... | collective-permute-start | bytes 1572872 | tf_op jit(solution)/shard_map/ppermute | solution.py:52
  87.6 16.7 %collective-permute-start.28 = (f32[32,2048]{1,0:T(8,128)S(1)}, f32[32,2048]{1,0:T(8,128)S(1)}, u32[]{:S(2)}, u32[]{:S(2)}) collective-permute-start(f32[32,2048]{1,0:T(8,128)S(1)} %gate.5), channel_id=1, source_target_pairs={{0,1},{1,0},{2,3},{3,2},{4,5},{5,4},{6,7},{7,6},{8,9},{9,8},{10,11... | collective-permute-start | bytes 786440 | tf_op jit(solution)/shard_map/ppermute | solution.py:470
  93.0 15.5 %collective-permute-start.24 = (bf16[256,1024]{1,0:T(8,128)(2,1)S(1)}, bf16[256,1024]{1,0:T(8,128)(2,1)S(1)}, u32[]{:S(2)}, u32[]{:S(2)}) collective-permute-start(bf16[256,1024]{1,0:T(8,128)(2,1)S(1)} %collective-permute-done.22.refs_1_), channel_id=1, source_target_pairs={{0,2},{2,0},{4,6},{6,4},{1,3},{3,1},{5,7},{7,5},{8,10},{10,8},{12,... | collective-permute-start | bytes 1572872 | tf_op jit(solution)/shard_map/ppermute | solution.py:56
  93.0 15.5 %collective-permute-start.32 = (bf16[256,1024]{1,0:T(8,128)(2,1)S(1)}, bf16[256,1024]{1,0:T(8,128)(2,1)S(1)}, u32[]{:S(2)}, u32[]{:S(2)}) collective-permute-start(bf16[256,1024]{1,0:T(8,128)(2,1)S(1)} %collective-permute-done.31.middle), channel_id=1, source_target_pairs={{8,16},{16,8},{9,17},{17,9},{10,18},{18,10},{11,19},{19,11},{12,20... | collective-permute-start | bytes 1572872 | tf_op jit(solution)/shard_map/ppermute | solution.py:52
  104.3 13.9 %collective-permute-start.16 = (bf16[256,1024]{1,0:T(8,128)(2,1)S(1)}, bf16[256,1024]{1,0:T(8,128)(2,1)S(1)}, u32[]{:S(2)}, u32[]{:S(2)}) collective-permute-start(bf16[256,1024]{1,0:T(8,128)(2,1)S(1)} %pick.5.refs_0_), channel_id=1, source_target_pairs={{0,4},{2,6},{4,0},{6,2},{1,5},{3,7},{5,1},{7,3},{8,12},{10,14},{12... | collective-permute-start | bytes 1572872 | tf_op jit(solution)/shard_map/ppermute | solution.py:56
  108.5 16.3 %collective-permute-start.30 = (bf16[256,1024]{1,0:T(8,128)(2,1)S(1)}, bf16[256,1024]{1,0:T(8,128)(2,1)S(1)}, u32[]{:S(2)}, u32[]{:S(2)}) collective-permute-start(bf16[256,1024]{1,0:T(8,128)(2,1)S(1)} %pick.5.refs_0_), channel_id=1, source_target_pairs={{0,2},{2,0},{4,6},{6,4},{1,3},{3,1},{5,7},{7,5},{8,10},{10,8},{12,... | collective-permute-start | bytes 1572872 | tf_op jit(solution)/shard_map/ppermute | solution.py:56
  108.5 16.2 %collective-permute-start.33 = (bf16[256,1024]{1,0:T(8,128)(2,1)S(1)}, bf16[256,1024]{1,0:T(8,128)(2,1)S(1)}, u32[]{:S(2)}, u32[]{:S(2)}) collective-permute-start(bf16[256,1024]{1,0:T(8,128)(2,1)S(1)} %collective-permute-done.32.middle), channel_id=1, source_target_pairs={{8,0},{16,24},{9,1},{17,25},{10,2},{18,26},{11,3},{19,27},{12,4},{... | collective-permute-start | bytes 1572872 | tf_op jit(solution)/shard_map/ppermute | solution.py:52
  (20 other events, 248.0 us)

commit v2 on v1

--- a/solution.py
+++ b/solution.py
@@ -64,8 +64,7 @@
 
 
 def project_kernel(trained, basis, norm, own, *refs):
-    *outs, token, projected = refs
-    token[...] = jnp.zeros_like(token)
+    *outs, projected = refs
     rank, rows = basis.shape[0], own.shape[1]
     high = basis[...].astype(BF16)
     rest = basis[...] - high.astype(F32)
@@ -95,14 +94,21 @@
 
 def embed_kernel(groups, n_came, *refs):
     refs = list(refs)
-    own, base, master, moment, basis, norm, master_norm, moment_norm = refs[:8]
-    came = refs[8 : 8 + n_came]
+    own, master, moment, basis, norm, master_norm, moment_norm = refs[:7]
+    came = refs[7 : 7 + n_came]
     stored, recast, velocity, norm_cast, norm_stored, norm_velocity = refs[-6:]
     rank, rows = own.shape
     total = own[...]
     for ref in came:
         total = total + ref[:rank, :].astype(F32)
-    coefficient = base[...] - total / groups
+    base = lax.dot_general(
+        basis[...],
+        master[...],
+        (((1,), (1,)), ((), ())),
+        precision=HIGHEST,
+        preferred_element_type=F32,
+    )
+    coefficient = base - total / groups
     moved = 0.5 * moment[...] + coefficient
     velocity[...] = moved
     change = lax.dot_general(
@@ -131,7 +137,7 @@
     norm_cast[...] = norm_stored[...].astype(BF16)
 
 
-def pack_kernel(down, up, _, *refs):
+def pack_kernel(down, up, *refs):
     *outs, sems = refs
     shard = lax.axis_index("shard")
     rows, width = down.shape[2:]
@@ -171,7 +177,8 @@
     )
 
 
-def pick_kernel(middle, end, out):
+def pick_kernel(middle, end, *refs):
+    out = refs[-1]
     pos = lax.axis_index("replica")
     outer = jnp.logical_or(pos == OUTER[0], pos == OUTER[1])
 
@@ -184,9 +191,10 @@
         out[...] = middle[...]
 
 
-def pick(middle, end):
+def pick(middle, end, *after):
+    specs = [VMEM] * 2 + [ANY] * len(after)
     shape = jax.ShapeDtypeStruct(end.shape, end.dtype)
-    return call(pick_kernel, "pick", shape, [VMEM] * 2, VMEM, [], middle, end)
+    return call(pick_kernel, "pick", shape, specs, VMEM, [], middle, end, *after)
 
 
 def update_kernel(groups, tensors, n_came, *refs):
@@ -276,8 +284,26 @@
     )
 
 
-def place_kernel(slot, masks, *refs):
-    pieces, (down, up, token, sems) = refs[: len(masks)], refs[-4:]
+def stack_kernel(count, *refs):
+    for i in range(count):
+        refs[-1][i] = refs[i][...]
+
+
+def bundle(pieces, *after):
+    return call(
+        functools.partial(stack_kernel, len(pieces)),
+        "bundle",
+        jax.ShapeDtypeStruct((len(pieces),) + pieces[0].shape, BF16),
+        [VMEM] * len(pieces) + [ANY] * len(after),
+        VMEM,
+        [],
+        *pieces,
+        *after,
+    )
+
+
+def place_kernel(keys, *refs):
+    bundles, (down, up, token, sems) = refs[: len(keys)], refs[-4:]
     token[...] = jnp.zeros_like(token)
     shard = lax.axis_index("shard")
     rows, width = down.shape[2:]
@@ -288,15 +314,15 @@
         copies.append(pltpu.make_async_copy(source, dest, sems.at[len(copies)]))
         copies[-1].start()
 
-    owner = owners()[slot]
-    for piece, mask in zip(pieces, masks):
-        place = jnp.bitwise_xor(shard, mask)
-        send(piece.at[pl.ds(0, rows)], down.at[owner, place])
-        for chunk in range(cols // width):
-            send(
-                piece.at[pl.ds(rows + chunk * tall, tall)],
-                up.at[owner, place, :, pl.ds(chunk * width, width)],
-            )
+    for pieces, (low, slots) in zip(bundles, keys):
+        for i, (slot, mask) in enumerate(slots):
+            owner, place = owners()[slot], jnp.bitwise_xor(shard, mask ^ low)
+            send(pieces.at[i, pl.ds(0, rows)], down.at[owner, place])
+            for chunk in range(cols // width):
+                send(
+                    pieces.at[i, pl.ds(rows + chunk * tall, tall)],
+                    up.at[owner, place, :, pl.ds(chunk * width, width)],
+                )
     for copy in copies:
         copy.wait()
 
@@ -313,15 +339,11 @@
         copy.wait()
 
 
-def spread(piece):
-    top = lax.axis_size("shard") // 2
-    return spread_low({0: piece, top: swap(piece, "shard", top)})
-
-
-def spread_low(pieces):
+def spread_low(x):
+    found = {0: x}
     for bit in bits_down(lax.axis_size("shard") // 2):
-        pieces.update({mask ^ bit: swap(x, "shard", bit) for mask, x in list(pieces.items())})
-    return pieces
+        found.update({mask ^ bit: swap(y, "shard", bit) for mask, y in list(found.items())})
+    return found
 
 
 def body(
@@ -354,34 +376,33 @@
     rank_rows = jax.ShapeDtypeStruct((rank, rows_embed), F32)
     packet = jax.ShapeDtypeStruct((rank + 16, rows_embed), BF16)
     token_shape = jax.ShapeDtypeStruct((8, 128), F32)
-    own_rows, *packets, projected = call(
+    own_rows, *packets = call(
         project_kernel,
         "project_rows",
-        [rank_rows] + [packet] * (replicas - 1) + [token_shape],
+        [rank_rows] + [packet] * (replicas - 1),
         [VMEM] * 3,
-        [VMEM] * (replicas + 1),
+        [VMEM] * replicas,
         [pltpu.VMEM((rank, replicas * rows_embed), F32)],
         pltpu.with_memory_space_constraint(trained_embed[0], pltpu.HBM),
         pltpu.with_memory_space_constraint(basis_t, pltpu.HBM),
         pltpu.with_memory_space_constraint(trained_norm[0], pltpu.HBM),
     )
-    packets_came = [swap(x, "replica", mask) for mask, x in enumerate(packets, 1)]
-
     down = trained_down[0].reshape(replicas, shards, rows_down, width)
     up = trained_up[0].reshape(replicas, shards, tall, half_cols)
     own, near, middle, end = call(
         pack_kernel,
         "pack_blocks",
         [packed] * replicas,
-        [HBM] * 2 + [VMEM],
+        [HBM] * 2,
         [VMEM] * replicas,
         [dma((replicas * (1 + chunks),))],
         pltpu.with_memory_space_constraint(down, pltpu.HBM),
         pltpu.with_memory_space_constraint(up, pltpu.HBM),
-        projected,
-    )
-    end = gate(end, packets_came[0])
+    )
     from_end = [along(x, INWARD) for x in (end, middle, near)]
+    end_sum = add(end, from_end[0])
+    packets[1] = gate(packets[1], end_sum)
+    packets_came = [swap(x, "replica", mask) for mask, x in enumerate(packets, 1)]
 
     state = jax.ShapeDtypeStruct((2, rows_up, half_cols), F32)
     states = call(
@@ -399,9 +420,6 @@
         for shift, x in enumerate(states, 1)
     ]
 
-    base = lax.dot_general(
-        basis_t, master_embed[0], (((1,), (1,)), ((), ())), precision=HIGHEST
-    )
     norm_state = jax.ShapeDtypeStruct(master_norm.shape, F32)
     embed_rows = jax.ShapeDtypeStruct((rows_embed, width), BF16)
     stored_rows, recast_rows, velocity_rows, norm_cast, stored_norm, velocity_norm = call(
@@ -415,11 +433,10 @@
             norm_state,
             norm_state,
         ],
-        [VMEM] * (7 + replicas) + [ANY],
+        [VMEM] * (6 + replicas),
         [VMEM] * 6,
         [],
         own_rows,
-        base,
         master_embed[0],
         moment_embed[0].T,
         basis_t,
@@ -427,15 +444,12 @@
         master_norm,
         moment_norm,
         *packets_came,
-        end,
     )
 
     embed_out = along(recast_rows, OUTWARD)
-    embed_middle = along(recast_rows, ACROSS)
-    end_partial = along(add(end, from_end[0], embed_out, embed_middle), ACROSS)
+    end_partial = along(end_sum, ACROSS)
     middle_partial = along(add(middle, from_end[1]), ACROSS)
-    embed_middle_out = along(embed_middle, OUTWARD)
-    to_end = along(add(near, end_partial, embed_middle_out), OUTWARD)
+    to_end = along(add(near, end_partial, embed_out), OUTWARD)
     came0 = [own, from_end[2], middle_partial, to_end]
     half_sum = jax.ShapeDtypeStruct((rows_up, half_cols), F32)
     down_state = jax.ShapeDtypeStruct((rows_down, width), F32)
@@ -455,23 +469,39 @@
     )
 
     top = shards // 2
-    near_piece = swap(piece, "replica", 1)
+    far_piece = swap(piece, "shard", top)
     middle_piece = along(piece, ACROSS)
+    near_piece = gate(swap(piece, "replica", 1), far_piece, middle_piece)
+    far_near = swap(near_piece, "shard", top)
     end_piece = along(near_piece, ACROSS)
-    second = pick(middle_piece, along(middle_piece, OUTWARD))
-    third = pick(end_piece, along(end_piece, OUTWARD))
-    groups = [spread(x) for x in (piece, near_piece, second)]
-
-    embed_in = along(gate(recast_rows, near_piece), INWARD)
-    embed_end = along(embed_in, ACROSS)
-    embed_last = along(embed_end, OUTWARD)
-
+    embed_late = gate(recast_rows, near_piece)
+    embed_in = along(embed_late, INWARD)
+    embed_middle = along(embed_late, ACROSS)
     sums = [sums[0]] + [
         lax.ppermute(
-            gate(x, second), "tensor", [(i, (i + shift) % tensors) for i in range(tensors)]
+            gate(x, near_piece), "tensor", [(i, (i + shift) % tensors) for i in range(tensors)]
         )
         for shift, x in enumerate(sums[1:], 1)
     ]
+    second = pick(middle_piece, along(middle_piece, OUTWARD), embed_in, far_near)
+    far_second = swap(second, "shard", top)
+    third = pick(end_piece, along(end_piece, OUTWARD), embed_middle, far_second, *sums[1:])
+    far_third = swap(third, "shard", top)
+    bundles = [
+        (
+            [(0, 0), (0, top), (1, 0), (1, top)],
+            spread_low(bundle([piece, far_piece, near_piece, far_near], third)),
+        ),
+        (
+            [(2, 0), (2, top), (3, 0)],
+            spread_low(bundle([second, far_second, third])),
+        ),
+    ]
+
+    embed_middle_out = along(embed_middle, OUTWARD)
+    embed_end = along(gate(embed_in, third), ACROSS)
+    embed_last = along(embed_end, OUTWARD)
+
     stored_up, velocity_up, token = call(
         functools.partial(up_kernel, replicas, tensors),
         "update_up",
@@ -500,27 +530,27 @@
 
     shapes = [jax.ShapeDtypeStruct(down.shape, BF16), jax.ShapeDtypeStruct(up.shape, BF16)]
 
-    def place(slot, group, placed, *after):
-        count = len(group) + len(after)
+    def place(slots, arrays, placed, *after):
+        keys = [(low, slots) for low in arrays]
+        count = len(keys) + len(after)
         return call(
-            functools.partial(place_kernel, slot, list(group)),
+            functools.partial(place_kernel, keys),
             "place_rows",
             shapes + [token_shape],
             [VMEM] * count + [HBM] * len(placed),
             [HBM] * 2 + [VMEM],
-            [dma((len(group) * (1 + chunks),))],
-            *group.values(),
+            [dma((len(keys) * len(slots) * (1 + chunks),))],
+            *arrays.values(),
             *after,
             *placed,
             aliases={count: 0, count + 1: 1} if placed else {},
         )
 
     placed = []
-    for slot, group in enumerate(groups):
-        *placed, token = place(slot, group, placed, token)
-    far = gate(swap(third, "shard", top), token)
-    *placed, token = place(3, spread_low({0: third}), placed)
-    recast_down, recast_up, token = place(3, spread_low({top: far}), placed)
+    for slots, arrays in bundles:
+        *placed, token = place(slots, arrays, placed, token)
+    last = spread_low(bundle([far_third], token))
+    recast_down, recast_up, token = place([(3, top)], last, placed)
     recast_embed = call(
         functools.partial(place_embed_kernel, [3]),
         "place_embed",

time: 129 us -> 135 us (1.047)
  waiting for transfers between devices: 60.4 us -> 69.8 us
  matrix products: 2.4 us -> 0 us
  starting transfers between devices: 45.5 us -> 44 us
    ppermute x16, waiting for transfers between devices: 34.1 us -> 44.1 us  [along(): return lax.ppermute(x, 'replica', pairs)]
    ppermute x16 -> x11, waiting for transfers between devices: 26.3 us -> 20.8 us  [swap(): lax.ppermute(x, axis, [(i, i ^ bit) for i in range(lax.axis_size(axis))])]
    ppermute x1, waiting for transfers between devices: 0.01 us -> 4.88 us  [body(): lax.ppermute(gate(x, near_piece), 'tensor', [(i, (i + shift) % tensors) f...]
    dot_general x1 -> x0, matrix products: 2.4 us -> none  [body(): lax.dot_general(basis_t, master_embed[0], (((1,), (1,)), ((), ())), preci...]
    ppermute x16 -> x11, starting transfers between devices: 14.2 us -> 13.3 us  [swap(): lax.ppermute(x, axis, [(i, i ^ bit) for i in range(lax.axis_size(axis))])]
    pallas_call x25 -> x27, Pallas kernels: 18.8 us -> 19.7 us  [call(): pl.pallas_call(kernel, name=name, out_shape=out_shape, in_specs=in_specs,...]
  transfers between devices with their start and end apart: 34 -> 29, of which waited for: 14 -> 15; matrix products, arithmetic and copies ran while one was open for 2% -> 0% of each run, Pallas kernels for 8% -> 11%
where the time goes in v2:
time: 135 us
  waiting for transfers between devices  69.8 us (52%)
  starting transfers between devices  44 us (33%)
  Pallas kernels  19.7 us (15%)
    ppermute x16, waiting for transfers between devices, along(): return lax.ppermute(x, 'replica', pairs)  44.1 us
    ppermute x16, starting transfers between devices, along(): return lax.ppermute(x, 'replica', pairs)  27.6 us
    ppermute x11, waiting for transfers between devices, swap(): lax.ppermute(x, axis, [(i, i ^ bit) for i in range(lax.axis_size(axis))])  20.8 us
    pallas_call x27, Pallas kernels, call(): pl.pallas_call(kernel, name=name, out_shape=out_shape, in_specs=in_specs,...  19.7 us
    ppermute x11, starting transfers between devices, swap(): lax.ppermute(x, axis, [(i, i ^ bit) for i in range(lax.axis_size(axis))])  13.3 us
    ppermute x1, waiting for transfers between devices, body(): lax.ppermute(gate(x, near_piece), 'tensor', [(i, (i + shift) % tensors) f...  4.88 us
  transfers between devices with their start and end apart: 29, of which 15 were waited for; matrix products, arithmetic and copies ran while one was open for 0% of the time, Pallas kernels for 11%

profile of v2, /device:TPU:0, one launch (start us, length us, event | category | flops | bytes accessed | tf_op | source)
XLA Modules:
  0.0 134.7 jit_solution(5943115066777093431)
XLA Ops:
  0.6 1.7 %pack_blocks.1 = (bf16[256,1024]{1,0:T(8,128)(2,1)S(1)}, bf16[256,1024]{1,0:T(8,128)(2,1)S(1)}, bf16[256,1024]{1,0:T(8,128)(2,1)S(1)}, bf16[256,1024]{1,0:T(8,128)(2,1)S(1)}) custom-call(bf16[4,4,128,1024]{3,2,1,0:T(8,128)(2,1)} %bitcast.31, bf16[4,4,64,2048]{3,2,1,0:T(8,128)(2,1)} %bitcast.32), custom_call_target="tpu_custom_call" | custom-call | bytes 6291456 | tf_op jit(solution)/shard_map/pack_blocks/pallas_call | solution.py:26
  2.4 5.1 %collective-permute-start.3 = (bf16[256,1024]{1,0:T(8,128)(2,1)S(1)}, bf16[256,1024]{1,0:T(8,128)(2,1)S(1)}, u32[]{:S(2)}, u32[]{:S(2)}) collective-permute-start(bf16[256,1024]{1,0:T(8,128)(2,1)S(1)} %get-tuple-element.46.block), channel_id=1, source_target_pairs={{0,8},{24,16},{1,9},{25,17},{2,10},{26,18},{3,11},{27,19},{4,12},{... | collective-permute-start | bytes 1572872 | tf_op jit(solution)/shard_map/ppermute | solution.py:52
  7.5 2.6 %project_rows.1 = (f32[64,256]{1,0:T(8,128)S(1)}, bf16[80,256]{1,0:T(8,128)(2,1)S(1)}, bf16[80,256]{1,0:T(8,128)(2,1)S(1)}, bf16[80,256]{1,0:T(8,128)(2,1)S(1)}) custom-call(bf16[1024,1024]{1,0:T(8,128)(2,1)} %bitcast.33, f32[64,1024]{1,0:T(8,128)} %bitcast.21, bf16[2,1024]{1,0:T(2,128)(2,1)} %bitcast.26), custom_call_target="tpu_custom_call" | custom-call | bytes 565248 | tf_op jit(solution)/shard_map/project_rows/pallas_call | solution.py:26
  10.2 2.6 %collective-permute-start.7 = (bf16[80,256]{1,0:T(8,128)(2,1)S(1)}, bf16[80,256]{1,0:T(8,128)(2,1)S(1)}, u32[]{:S(2)}, u32[]{:S(2)}) collective-permute-start(bf16[80,256]{1,0:T(8,128)(2,1)S(1)} %get-tuple-element.50), channel_id=1, source_target_pairs={{0,24},{8,16},{16,8},{24,0},{1,25},{9,17},{17,9},{25,1},{2,26},{10... | collective-permute-start | bytes 122888 | tf_op jit(solution)/shard_map/ppermute | solution.py:56
  12.7 6.8 %collective-permute-done.3.came = bf16[256,1024]{1,0:T(8,128)(2,1)S(1)} collective-permute-done((bf16[256,1024]{1,0:T(8,128)(2,1)S(1)}, bf16[256,1024]{1,0:T(8,128)(2,1)S(1)}, u32[]{:S(2)}, u32[]{:S(2)}) %collective-permute-start.3) | collective-permute-done | bytes 524320 | tf_op jit(solution)/shard_map/ppermute | solution.py:52
  19.7 3.6 %collective-permute-start.6 = (bf16[80,256]{1,0:T(8,128)(2,1)S(1)}, bf16[80,256]{1,0:T(8,128)(2,1)S(1)}, u32[]{:S(2)}, u32[]{:S(2)}) collective-permute-start(bf16[80,256]{1,0:T(8,128)(2,1)S(1)} %gate.5), channel_id=1, source_target_pairs={{0,16},{8,24},{16,0},{24,8},{1,17},{9,25},{17,1},{25,9},{2,18},{10... | collective-permute-start | bytes 122888 | tf_op jit(solution)/shard_map/ppermute | solution.py:56
  25.5 4.6 %embed_update.1 = (f32[256,1024]{1,0:T(8,128)}, bf16[256,1024]{1,0:T(8,128)(2,1)S(1)}, f32[64,256]{1,0:T(8,128)}, bf16[2,1024]{1,0:T(2,128)(2,1)}, f32[2,1024]{1,0:T(2,128)}, /*index=5*/f32[2,1024]{1,0:T(2,128)}) custom-call(f32[64,256]{1,0:T(8,128)S(1)} %get-tuple-element.47.refs_0_, f32[256,1024]{1,0:T(8,128)S(1)} %bitcast.20, f32[64,256]{1,0:T(8,128)S(1)} %bitcast.25, ...), custom_call_target="tpu_custom_call" | custom-call | bytes 4976640 | tf_op jit(solution)/shard_map/embed_update/pallas_call | solution.py:26
  33.0 4.6 %collective-permute-start = (bf16[256,1024]{1,0:T(8,128)(2,1)S(1)}, bf16[256,1024]{1,0:T(8,128)(2,1)S(1)}, u32[]{:S(2)}, u32[]{:S(2)}) collective-permute-start(bf16[256,1024]{1,0:T(8,128)(2,1)S(1)} %get-tuple-element.44.block), channel_id=1, source_target_pairs={{0,8},{24,16},{1,9},{25,17},{2,10},{26,18},{3,11},{27,19},{4,12},{... | collective-permute-start | bytes 1572872 | tf_op jit(solution)/shard_map/ppermute | solution.py:52
  38.4 5.0 %collective-permute-done.8.refs_0_.end = bf16[256,1024]{1,0:T(8,128)(2,1)S(1)} collective-permute-done((bf16[256,1024]{1,0:T(8,128)(2,1)S(1)}, bf16[256,1024]{1,0:T(8,128)(2,1)S(1)}, u32[]{:S(2)}, u32[]{:S(2)}) %collective-permute-start.8) | collective-permute-done | bytes 524320 | tf_op jit(solution)/shard_map/ppermute | solution.py:52
  46.0 10.0 %collective-permute-done.9.refs_7_ = bf16[256,1024]{1,0:T(8,128)(2,1)S(1)} collective-permute-done((bf16[256,1024]{1,0:T(8,128)(2,1)S(1)}, bf16[256,1024]{1,0:T(8,128)(2,1)S(1)}, u32[]{:S(2)}, u32[]{:S(2)}) %collective-permute-start.9) | collective-permute-done | bytes 524320 | tf_op jit(solution)/shard_map/ppermute | solution.py:52
  56.0 1.7 %update_rows.1 = (bf16[256,1024]{1,0:T(8,128)(2,1)S(1)}, f32[128,1024]{1,0:T(8,128)}, f32[128,1024]{1,0:T(8,128)}, f32[32,2048]{1,0:T(8,128)S(1)}, f32[32,2048]{1,0:T(8,128)S(1)}) custom-call(f32[128,1024]{1,0:T(8,128)S(1)} %bitcast.23, f32[128,1024]{1,0:T(8,128)S(1)} %bitcast.24, f32[32,4096]{1,0:T(8,128)S(1)} %copy-done, f32[32,4096]{1,0:T(8,128)S(1)} %copy-done.1, ...), custom_call_target="tpu_custom_call" | custom-call | bytes 6291456 | tf_op jit(solution)/shard_map/update_rows/pallas_call | solution.py:26
  60.0 2.1 %collective-permute-start.11 = (bf16[256,1024]{1,0:T(8,128)(2,1)S(1)}, bf16[256,1024]{1,0:T(8,128)(2,1)S(1)}, u32[]{:S(2)}, u32[]{:S(2)}) collective-permute-start(bf16[256,1024]{1,0:T(8,128)(2,1)S(1)} %get-tuple-element.52.refs_0_), channel_id=1, source_target_pairs={{0,8},{8,0},{16,24},{24,16},{1,9},{9,1},{17,25},{25,17},{2,10},{10... | collective-permute-start | bytes 1572872 | tf_op jit(solution)/shard_map/ppermute | solution.py:56
  62.0 6.0 %collective-permute-done.12.refs_0_.refs_1_ = bf16[256,1024]{1,0:T(8,128)(2,1)S(1)} collective-permute-done((bf16[256,1024]{1,0:T(8,128)(2,1)S(1)}, bf16[256,1024]{1,0:T(8,128)(2,1)S(1)}, u32[]{:S(2)}, u32[]{:S(2)}) %collective-permute-start.12) | collective-permute-done | bytes 524320 | tf_op jit(solution)/shard_map/ppermute | solution.py:56
  68.1 2.0 %collective-permute-done.11.x = bf16[256,1024]{1,0:T(8,128)(2,1)S(1)} collective-permute-done((bf16[256,1024]{1,0:T(8,128)(2,1)S(1)}, bf16[256,1024]{1,0:T(8,128)(2,1)S(1)}, u32[]{:S(2)}, u32[]{:S(2)}) %collective-permute-start.11) | collective-permute-done | bytes 524320 | tf_op jit(solution)/shard_map/ppermute | solution.py:56
  71.5 4.6 %collective-permute-start.18 = (bf16[256,1024]{1,0:T(8,128)(2,1)S(1)}, bf16[256,1024]{1,0:T(8,128)(2,1)S(1)}, u32[]{:S(2)}, u32[]{:S(2)}) collective-permute-start(bf16[256,1024]{1,0:T(8,128)(2,1)S(1)} %gate.7), channel_id=1, source_target_pairs={{0,8},{24,16},{1,9},{25,17},{2,10},{26,18},{3,11},{27,19},{4,12},{... | collective-permute-start | bytes 1572872 | tf_op jit(solution)/shard_map/ppermute | solution.py:52
  78.1 3.2 %collective-permute-done.17.end = bf16[256,1024]{1,0:T(8,128)(2,1)S(1)} collective-permute-done((bf16[256,1024]{1,0:T(8,128)(2,1)S(1)}, bf16[256,1024]{1,0:T(8,128)(2,1)S(1)}, u32[]{:S(2)}, u32[]{:S(2)}) %collective-permute-start.17) | collective-permute-done | bytes 524320 | tf_op jit(solution)/shard_map/ppermute | solution.py:52
  82.8 7.3 %collective-permute-done.19.refs_1_.refs_3_ = bf16[256,1024]{1,0:T(8,128)(2,1)S(1)} collective-permute-done((bf16[256,1024]{1,0:T(8,128)(2,1)S(1)}, bf16[256,1024]{1,0:T(8,128)(2,1)S(1)}, u32[]{:S(2)}, u32[]{:S(2)}) %collective-permute-start.19) | collective-permute-done | bytes 524320 | tf_op jit(solution)/shard_map/ppermute | solution.py:56
  93.5 4.9 %collective-permute-done.21.refs_2_.refs_1_ = f32[32,2048]{1,0:T(8,128)S(1)} collective-permute-done((f32[32,2048]{1,0:T(8,128)S(1)}, f32[32,2048]{1,0:T(8,128)S(1)}, u32[]{:S(2)}, u32[]{:S(2)}) %collective-permute-start.21) | collective-permute-done | bytes 262176 | tf_op jit(solution)/shard_map/ppermute | solution.py:481
  99.3 2.4 %collective-permute-done.15.end = bf16[256,1024]{1,0:T(8,128)(2,1)S(1)} collective-permute-done((bf16[256,1024]{1,0:T(8,128)(2,1)S(1)}, bf16[256,1024]{1,0:T(8,128)(2,1)S(1)}, u32[]{:S(2)}, u32[]{:S(2)}) %collective-permute-start.15) | collective-permute-done | bytes 524320 | tf_op jit(solution)/shard_map/ppermute | solution.py:52
  108.7 2.2 %place_rows.3 = (bf16[4,4,128,1024]{3,2,1,0:T(8,128)(2,1)}, bf16[4,4,64,2048]{3,2,1,0:T(8,128)(2,1)}, f32[8,128]{1,0:T(8,128)S(1)}) custom-call(bf16[4,256,1024]{2,1,0:T(8,128)(2,1)S(1)} %bundle.4.refs_0_, bf16[4,256,1024]{2,1,0:T(8,128)(2,1)S(1)} %collective-permute-done.24.refs_1_, f32[8,128]{1,0:T(8,128)S(1)} %get-tuple-element.55.refs_2_.refs_3_), custom_call_target="tpu_custom_call" | custom-call | bytes 25178112 | tf_op jit(solution)/shard_map/place_rows/pallas_call | solution.py:26
  110.9 1.8 %place_rows.4 = (bf16[4,4,128,1024]{3,2,1,0:T(8,128)(2,1)}, bf16[4,4,64,2048]{3,2,1,0:T(8,128)(2,1)}, f32[8,128]{1,0:T(8,128)S(1)}) custom-call(bf16[3,256,1024]{2,1,0:T(8,128)(2,1)S(1)} %bundle.3.refs_0_, bf16[3,256,1024]{2,1,0:T(8,128)(2,1)S(1)} %collective-permute-done.23.refs_1_, ...), custom_call_target="tpu_custom_call", output_to_operand_aliasing={{0}: (3, {}), {1}: (4, {})} | custom-call | bytes 25178112 | tf_op jit(solution)/shard_map/place_rows/pallas_call | solution.py:26
  112.7 4.5 %collective-permute-done.22.refs_0_ = bf16[256,1024]{1,0:T(8,128)(2,1)S(1)} collective-permute-done((bf16[256,1024]{1,0:T(8,128)(2,1)S(1)}, bf16[256,1024]{1,0:T(8,128)(2,1)S(1)}, u32[]{:S(2)}, u32[]{:S(2)}) %collective-permute-start.22) | collective-permute-done | bytes 524320 | tf_op jit(solution)/shard_map/ppermute | solution.py:56
  117.5 5.3 %collective-permute-done.28.end = bf16[256,1024]{1,0:T(8,128)(2,1)S(1)} collective-permute-done((bf16[256,1024]{1,0:T(8,128)(2,1)S(1)}, bf16[256,1024]{1,0:T(8,128)(2,1)S(1)}, u32[]{:S(2)}, u32[]{:S(2)}) %collective-permute-start.28) | collective-permute-done | bytes 524320 | tf_op jit(solution)/shard_map/ppermute | solution.py:52
  124.0 8.8 %collective-permute-done.27.end = bf16[256,1024]{1,0:T(8,128)(2,1)S(1)} collective-permute-done((bf16[256,1024]{1,0:T(8,128)(2,1)S(1)}, bf16[256,1024]{1,0:T(8,128)(2,1)S(1)}, u32[]{:S(2)}, u32[]{:S(2)}) %collective-permute-start.27) | collective-permute-done | bytes 524320 | tf_op jit(solution)/shard_map/ppermute | solution.py:52
  (81 shorter events, 30.3 us)
Async XLA Ops:
  2.4 17.1 %collective-permute-start.3 = (bf16[256,1024]{1,0:T(8,128)(2,1)S(1)}, bf16[256,1024]{1,0:T(8,128)(2,1)S(1)}, u32[]{:S(2)}, u32[]{:S(2)}) collective-permute-start(bf16[256,1024]{1,0:T(8,128)(2,1)S(1)} %get-tuple-element.46.block), channel_id=1, source_target_pairs={{0,8},{24,16},{1,9},{25,17},{2,10},{26,18},{3,11},{27,19},{4,12},{... | collective-permute-start | bytes 1572872 | tf_op jit(solution)/shard_map/ppermute | solution.py:52
  10.1 15.3 %collective-permute-start.5 = (bf16[80,256]{1,0:T(8,128)(2,1)S(1)}, bf16[80,256]{1,0:T(8,128)(2,1)S(1)}, u32[]{:S(2)}, u32[]{:S(2)}) collective-permute-start(bf16[80,256]{1,0:T(8,128)(2,1)S(1)} %get-tuple-element.48), channel_id=1, source_target_pairs={{0,8},{8,0},{16,24},{24,16},{1,9},{9,1},{17,25},{25,17},{2,10},{10... | collective-permute-start | bytes 122888 | tf_op jit(solution)/shard_map/ppermute | solution.py:56
  10.2 15.2 %collective-permute-start.7 = (bf16[80,256]{1,0:T(8,128)(2,1)S(1)}, bf16[80,256]{1,0:T(8,128)(2,1)S(1)}, u32[]{:S(2)}, u32[]{:S(2)}) collective-permute-start(bf16[80,256]{1,0:T(8,128)(2,1)S(1)} %get-tuple-element.50), channel_id=1, source_target_pairs={{0,24},{8,16},{16,8},{24,0},{1,25},{9,17},{17,9},{25,1},{2,26},{10... | collective-permute-start | bytes 122888 | tf_op jit(solution)/shard_map/ppermute | solution.py:56
  23.2 14.4 %collective-permute-start.1 = (bf16[256,1024]{1,0:T(8,128)(2,1)S(1)}, bf16[256,1024]{1,0:T(8,128)(2,1)S(1)}, u32[]{:S(2)}, u32[]{:S(2)}) collective-permute-start(bf16[256,1024]{1,0:T(8,128)(2,1)S(1)} %get-tuple-element.45.block), channel_id=1, source_target_pairs={{0,8},{24,16},{1,9},{25,17},{2,10},{26,18},{3,11},{27,19},{4,12},{... | collective-permute-start | bytes 1572872 | tf_op jit(solution)/shard_map/ppermute | solution.py:52
  24.7 13.7 %collective-permute-start.4 = (bf16[256,1024]{1,0:T(8,128)(2,1)S(1)}, bf16[256,1024]{1,0:T(8,128)(2,1)S(1)}, u32[]{:S(2)}, u32[]{:S(2)}) collective-permute-start(bf16[256,1024]{1,0:T(8,128)(2,1)S(1)} %add_block.4.refs_0_), channel_id=1, source_target_pairs={{8,16},{16,8},{9,17},{17,9},{10,18},{18,10},{11,19},{19,11},{12,20... | collective-permute-start | bytes 1572872 | tf_op jit(solution)/shard_map/ppermute | solution.py:52
  30.1 13.4 %collective-permute-start.8 = (bf16[256,1024]{1,0:T(8,128)(2,1)S(1)}, bf16[256,1024]{1,0:T(8,128)(2,1)S(1)}, u32[]{:S(2)}, u32[]{:S(2)}) collective-permute-start(bf16[256,1024]{1,0:T(8,128)(2,1)S(1)} %get-tuple-element.51.x.refs_0_), channel_id=1, source_target_pairs={{8,0},{16,24},{9,1},{17,25},{10,2},{18,26},{11,3},{19,27},{12,4},{... | collective-permute-start | bytes 1572872 | tf_op jit(solution)/shard_map/ppermute | solution.py:52
  31.4 13.4 %collective-permute-start.10 = (f32[2,32,2048]{2,1,0:T(8,128)S(1)}, f32[2,32,2048]{2,1,0:T(8,128)S(1)}, u32[]{:S(2)}, u32[]{:S(2)}) collective-permute-start(f32[2,32,2048]{2,1,0:T(8,128)S(1)} %up_state.1), channel_id=1, source_target_pairs={{0,1},{1,0},{2,3},{3,2},{4,5},{5,4},{6,7},{7,6},{8,9},{9,8},{10,11... | collective-permute-start | bytes 1572872 | tf_op jit(solution)/shard_map/ppermute | solution.py:419
  33.0 13.0 %collective-permute-start = (bf16[256,1024]{1,0:T(8,128)(2,1)S(1)}, bf16[256,1024]{1,0:T(8,128)(2,1)S(1)}, u32[]{:S(2)}, u32[]{:S(2)}) collective-permute-start(bf16[256,1024]{1,0:T(8,128)(2,1)S(1)} %get-tuple-element.44.block), channel_id=1, source_target_pairs={{0,8},{24,16},{1,9},{25,17},{2,10},{26,18},{3,11},{27,19},{4,12},{... | collective-permute-start | bytes 1572872 | tf_op jit(solution)/shard_map/ppermute | solution.py:52
  37.7 8.2 %collective-permute-start.2 = (bf16[256,1024]{1,0:T(8,128)(2,1)S(1)}, bf16[256,1024]{1,0:T(8,128)(2,1)S(1)}, u32[]{:S(2)}, u32[]{:S(2)}) collective-permute-start(bf16[256,1024]{1,0:T(8,128)(2,1)S(1)} %add_block.3), channel_id=1, source_target_pairs={{8,16},{16,8},{9,17},{17,9},{10,18},{18,10},{11,19},{19,11},{12,20... | collective-permute-start | bytes 1572872 | tf_op jit(solution)/shard_map/ppermute | solution.py:52
  43.5 12.4 %collective-permute-start.9 = (bf16[256,1024]{1,0:T(8,128)(2,1)S(1)}, bf16[256,1024]{1,0:T(8,128)(2,1)S(1)}, u32[]{:S(2)}, u32[]{:S(2)}) collective-permute-start(bf16[256,1024]{1,0:T(8,128)(2,1)S(1)} %add_block.5), channel_id=1, source_target_pairs={{8,0},{16,24},{9,1},{17,25},{10,2},{18,26},{11,3},{19,27},{12,4},{... | collective-permute-start | bytes 1572872 | tf_op jit(solution)/shard_map/ppermute | solution.py:52
  58.4 9.7 %collective-permute-start.12 = (bf16[256,1024]{1,0:T(8,128)(2,1)S(1)}, bf16[256,1024]{1,0:T(8,128)(2,1)S(1)}, u32[]{:S(2)}, u32[]{:S(2)}) collective-permute-start(bf16[256,1024]{1,0:T(8,128)(2,1)S(1)} %get-tuple-element.52.refs_0_), channel_id=1, source_target_pairs={{0,4},{2,6},{4,0},{6,2},{1,5},{3,7},{5,1},{7,3},{8,12},{10,14},{12... | collective-permute-start | bytes 1572872 | tf_op jit(solution)/shard_map/ppermute | solution.py:56
  60.0 10.1 %collective-permute-start.11 = (bf16[256,1024]{1,0:T(8,128)(2,1)S(1)}, bf16[256,1024]{1,0:T(8,128)(2,1)S(1)}, u32[]{:S(2)}, u32[]{:S(2)}) collective-permute-start(bf16[256,1024]{1,0:T(8,128)(2,1)S(1)} %get-tuple-element.52.refs_0_), channel_id=1, source_target_pairs={{0,8},{8,0},{16,24},{24,16},{1,9},{9,1},{17,25},{25,17},{2,10},{10... | collective-permute-start | bytes 1572872 | tf_op jit(solution)/shard_map/ppermute | solution.py:56
  70.2 11.1 %collective-permute-start.17 = (bf16[256,1024]{1,0:T(8,128)(2,1)S(1)}, bf16[256,1024]{1,0:T(8,128)(2,1)S(1)}, u32[]{:S(2)}, u32[]{:S(2)}) collective-permute-start(bf16[256,1024]{1,0:T(8,128)(2,1)S(1)} %collective-permute-done.13.refs_1_.middle), channel_id=1, source_target_pairs={{8,0},{16,24},{9,1},{17,25},{10,2},{18,26},{11,3},{19,27},{12,4},{... | collective-permute-start | bytes 1572872 | tf_op jit(solution)/shard_map/ppermute | solution.py:52
  71.5 11.3 %collective-permute-start.18 = (bf16[256,1024]{1,0:T(8,128)(2,1)S(1)}, bf16[256,1024]{1,0:T(8,128)(2,1)S(1)}, u32[]{:S(2)}, u32[]{:S(2)}) collective-permute-start(bf16[256,1024]{1,0:T(8,128)(2,1)S(1)} %gate.7), channel_id=1, source_target_pairs={{0,8},{24,16},{1,9},{25,17},{2,10},{26,18},{3,11},{27,19},{4,12},{... | collective-permute-start | bytes 1572872 | tf_op jit(solution)/shard_map/ppermute | solution.py:52
  76.1 13.9 %collective-permute-start.19 = (bf16[256,1024]{1,0:T(8,128)(2,1)S(1)}, bf16[256,1024]{1,0:T(8,128)(2,1)S(1)}, u32[]{:S(2)}, u32[]{:S(2)}) collective-permute-start(bf16[256,1024]{1,0:T(8,128)(2,1)S(1)} %gate.6.refs_0_.refs_2_), channel_id=1, source_target_pairs={{0,4},{2,6},{4,0},{6,2},{1,5},{3,7},{5,1},{7,3},{8,12},{10,14},{12... | collective-permute-start | bytes 1572872 | tf_op jit(solution)/shard_map/ppermute | solution.py:56
  76.7 14.0 %collective-permute-start.14 = (bf16[256,1024]{1,0:T(8,128)(2,1)S(1)}, bf16[256,1024]{1,0:T(8,128)(2,1)S(1)}, u32[]{:S(2)}, u32[]{:S(2)}) collective-permute-start(bf16[256,1024]{1,0:T(8,128)(2,1)S(1)} %gate.6.refs_0_.refs_2_), channel_id=1, source_target_pairs={{8,16},{16,8},{9,17},{17,9},{10,18},{18,10},{11,19},{19,11},{12,20... | collective-permute-start | bytes 1572872 | tf_op jit(solution)/shard_map/ppermute | solution.py:52
  77.4 21.0 %collective-permute-start.16 = (bf16[256,1024]{1,0:T(8,128)(2,1)S(1)}, bf16[256,1024]{1,0:T(8,128)(2,1)S(1)}, u32[]{:S(2)}, u32[]{:S(2)}) collective-permute-start(bf16[256,1024]{1,0:T(8,128)(2,1)S(1)} %gate.7), channel_id=1, source_target_pairs={{8,16},{16,8},{9,17},{17,9},{10,18},{18,10},{11,19},{19,11},{12,20... | collective-permute-start | bytes 1572872 | tf_op jit(solution)/shard_map/ppermute | solution.py:52
  90.1 9.2 %collective-permute-start.20 = (bf16[256,1024]{1,0:T(8,128)(2,1)S(1)}, bf16[256,1024]{1,0:T(8,128)(2,1)S(1)}, u32[]{:S(2)}, u32[]{:S(2)}) collective-permute-start(bf16[256,1024]{1,0:T(8,128)(2,1)S(1)} %pick.5.refs_0_), channel_id=1, source_target_pairs={{0,4},{2,6},{4,0},{6,2},{1,5},{3,7},{5,1},{7,3},{8,12},{10,14},{12... | collective-permute-start | bytes 1572872 | tf_op jit(solution)/shard_map/ppermute | solution.py:56
  90.6 11.1 %collective-permute-start.15 = (bf16[256,1024]{1,0:T(8,128)(2,1)S(1)}, bf16[256,1024]{1,0:T(8,128)(2,1)S(1)}, u32[]{:S(2)}, u32[]{:S(2)}) collective-permute-start(bf16[256,1024]{1,0:T(8,128)(2,1)S(1)} %collective-permute-done.14.middle), channel_id=1, source_target_pairs={{8,0},{16,24},{9,1},{17,25},{10,2},{18,26},{11,3},{19,27},{12,4},{... | collective-permute-start | bytes 1572872 | tf_op jit(solution)/shard_map/ppermute | solution.py:52
  102.1 8.8 %collective-permute-start.23 = (bf16[3,256,1024]{2,1,0:T(8,128)(2,1)S(1)}, bf16[3,256,1024]{2,1,0:T(8,128)(2,1)S(1)}, u32[]{:S(2)}, u32[]{:S(2)}) collective-permute-start(bf16[3,256,1024]{2,1,0:T(8,128)(2,1)S(1)} %bundle.3.refs_0_), channel_id=1, source_target_pairs={{0,2},{2,0},{4,6},{6,4},{1,3},{3,1},{5,7},{7,5},{8,10},{10,8},{12,... | collective-permute-start | bytes 4718600 | tf_op jit(solution)/shard_map/ppermute | solution.py:56
  103.4 13.9 %collective-permute-start.22 = (bf16[256,1024]{1,0:T(8,128)(2,1)S(1)}, bf16[256,1024]{1,0:T(8,128)(2,1)S(1)}, u32[]{:S(2)}, u32[]{:S(2)}) collective-permute-start(bf16[256,1024]{1,0:T(8,128)(2,1)S(1)} %pick.6.refs_2_.refs_4_.refs_0_), channel_id=1, source_target_pairs={{0,4},{2,6},{4,0},{6,2},{1,5},{3,7},{5,1},{7,3},{8,12},{10,14},{12... | collective-permute-start | bytes 1572872 | tf_op jit(solution)/shard_map/ppermute | solution.py:56
  106.1 16.7 %collective-permute-start.28 = (bf16[256,1024]{1,0:T(8,128)(2,1)S(1)}, bf16[256,1024]{1,0:T(8,128)(2,1)S(1)}, u32[]{:S(2)}, u32[]{:S(2)}) collective-permute-start(bf16[256,1024]{1,0:T(8,128)(2,1)S(1)} %collective-permute-done.16.refs_0_.middle), channel_id=1, source_target_pairs={{8,0},{16,24},{9,1},{17,25},{10,2},{18,26},{11,3},{19,27},{12,4},{... | collective-permute-start | bytes 1572872 | tf_op jit(solution)/shard_map/ppermute | solution.py:52
  107.4 25.4 %collective-permute-start.27 = (bf16[256,1024]{1,0:T(8,128)(2,1)S(1)}, bf16[256,1024]{1,0:T(8,128)(2,1)S(1)}, u32[]{:S(2)}, u32[]{:S(2)}) collective-permute-start(bf16[256,1024]{1,0:T(8,128)(2,1)S(1)} %collective-permute-done.26.middle), channel_id=1, source_target_pairs={{8,0},{16,24},{9,1},{17,25},{10,2},{18,26},{11,3},{19,27},{12,4},{... | collective-permute-start | bytes 1572872 | tf_op jit(solution)/shard_map/ppermute | solution.py:52
  117.3 15.5 %collective-permute-start.25 = (bf16[1,256,1024]{2,1,0:T(8,128)(2,1)S(1)}, bf16[1,256,1024]{2,1,0:T(8,128)(2,1)S(1)}, u32[]{:S(2)}, u32[]{:S(2)}) collective-permute-start(bf16[1,256,1024]{2,1,0:T(8,128)(2,1)S(1)} %bundle.5.refs_0_), channel_id=1, source_target_pairs={{0,2},{2,0},{4,6},{6,4},{1,3},{3,1},{5,7},{7,5},{8,10},{10,8},{12,... | collective-permute-start | bytes 1572872 | tf_op jit(solution)/shard_map/ppermute | solution.py:56
  (15 other events, 316.3 us)

commit v3 on v2

--- a/solution.py
+++ b/solution.py
@@ -94,21 +94,14 @@
 
 def embed_kernel(groups, n_came, *refs):
     refs = list(refs)
-    own, master, moment, basis, norm, master_norm, moment_norm = refs[:7]
-    came = refs[7 : 7 + n_came]
+    own, base, master, moment, basis, norm, master_norm, moment_norm = refs[:8]
+    came = refs[8 : 8 + n_came]
     stored, recast, velocity, norm_cast, norm_stored, norm_velocity = refs[-6:]
     rank, rows = own.shape
     total = own[...]
     for ref in came:
         total = total + ref[:rank, :].astype(F32)
-    base = lax.dot_general(
-        basis[...],
-        master[...],
-        (((1,), (1,)), ((), ())),
-        precision=HIGHEST,
-        preferred_element_type=F32,
-    )
-    coefficient = base - total / groups
+    coefficient = base[...] - total / groups
     moved = 0.5 * moment[...] + coefficient
     velocity[...] = moved
     change = lax.dot_general(
@@ -401,7 +394,6 @@
     )
     from_end = [along(x, INWARD) for x in (end, middle, near)]
     end_sum = add(end, from_end[0])
-    packets[1] = gate(packets[1], end_sum)
     packets_came = [swap(x, "replica", mask) for mask, x in enumerate(packets, 1)]
 
     state = jax.ShapeDtypeStruct((2, rows_up, half_cols), F32)
@@ -420,6 +412,9 @@
         for shift, x in enumerate(states, 1)
     ]
 
+    base = lax.dot_general(
+        basis_t, master_embed[0], (((1,), (1,)), ((), ())), precision=HIGHEST
+    )
     norm_state = jax.ShapeDtypeStruct(master_norm.shape, F32)
     embed_rows = jax.ShapeDtypeStruct((rows_embed, width), BF16)
     stored_rows, recast_rows, velocity_rows, norm_cast, stored_norm, velocity_norm = call(
@@ -433,10 +428,11 @@
             norm_state,
             norm_state,
         ],
-        [VMEM] * (6 + replicas),
+        [VMEM] * (7 + replicas),
         [VMEM] * 6,
         [],
         own_rows,
+        base,
         master_embed[0],
         moment_embed[0].T,
         basis_t,
@@ -483,9 +479,9 @@
         )
         for shift, x in enumerate(sums[1:], 1)
     ]
-    second = pick(middle_piece, along(middle_piece, OUTWARD), embed_in, far_near)
+    second = pick(middle_piece, along(middle_piece, OUTWARD), far_near)
     far_second = swap(second, "shard", top)
-    third = pick(end_piece, along(end_piece, OUTWARD), embed_middle, far_second, *sums[1:])
+    third = pick(end_piece, along(end_piece, OUTWARD), embed_in, embed_middle, far_second, *sums[1:])
     far_third = swap(third, "shard", top)
     bundles = [
         (

time: 135 us -> 130 us (0.963)
  waiting for transfers between devices: 69.8 us -> 66.8 us
  Pallas kernels: 19.7 us -> 17.2 us
    ppermute x16, waiting for transfers between devices: 44.1 us -> 33.5 us  [along(): return lax.ppermute(x, 'replica', pairs)]
    ppermute x11, waiting for transfers between devices: 20.8 us -> 28.4 us  [swap(): lax.ppermute(x, axis, [(i, i ^ bit) for i in range(lax.axis_size(axis))])]
    ppermute x11, starting transfers between devices: 13.3 us -> 9.94 us  [swap(): lax.ppermute(x, axis, [(i, i ^ bit) for i in range(lax.axis_size(axis))])]
    ppermute x16, starting transfers between devices: 27.6 us -> 30.6 us  [along(): return lax.ppermute(x, 'replica', pairs)]
    pallas_call x27 -> x26, Pallas kernels: 19.7 us -> 17.2 us  [call(): pl.pallas_call(kernel, name=name, out_shape=out_shape, in_specs=in_specs,...]
  transfers between devices with their start and end apart: 29 -> 29, of which waited for: 15 -> 15; matrix products, arithmetic and copies ran while one was open for 0% -> 1% of each run, Pallas kernels for 11% -> 9%
where the time goes in v3:
time: 130 us
  waiting for transfers between devices  66.8 us (51%)
  starting transfers between devices  43.7 us (34%)
  Pallas kernels  17.2 us (13%)
    ppermute x16, waiting for transfers between devices, along(): return lax.ppermute(x, 'replica', pairs)  33.5 us
    ppermute x16, starting transfers between devices, along(): return lax.ppermute(x, 'replica', pairs)  30.6 us
    ppermute x11, waiting for transfers between devices, swap(): lax.ppermute(x, axis, [(i, i ^ bit) for i in range(lax.axis_size(axis))])  28.4 us
    pallas_call x26, Pallas kernels, call(): pl.pallas_call(kernel, name=name, out_shape=out_shape, in_specs=in_specs,...  17.2 us
    ppermute x11, starting transfers between devices, swap(): lax.ppermute(x, axis, [(i, i ^ bit) for i in range(lax.axis_size(axis))])  9.94 us
    ppermute x1, waiting for transfers between devices, body(): lax.ppermute(gate(x, near_piece), 'tensor', [(i, (i + shift) % tensors) f...  4.86 us
  transfers between devices with their start and end apart: 29, of which 15 were waited for; matrix products, arithmetic and copies ran while one was open for 1% of the time, Pallas kernels for 9%

profile of v3, /device:TPU:0, one launch (start us, length us, event | category | flops | bytes accessed | tf_op | source)
XLA Modules:
  0.0 130.0 jit_solution(7001498286573326702)
XLA Ops:
  0.7 1.8 %pack_blocks.1 = (bf16[256,1024]{1,0:T(8,128)(2,1)S(1)}, bf16[256,1024]{1,0:T(8,128)(2,1)S(1)}, bf16[256,1024]{1,0:T(8,128)(2,1)S(1)}, bf16[256,1024]{1,0:T(8,128)(2,1)S(1)}) custom-call(bf16[4,4,128,1024]{3,2,1,0:T(8,128)(2,1)} %bitcast.34, bf16[4,4,64,2048]{3,2,1,0:T(8,128)(2,1)} %bitcast.35), custom_call_target="tpu_custom_call" | custom-call | bytes 6291456 | tf_op jit(solution)/shard_map/pack_blocks/pallas_call | solution.py:26
  2.5 5.1 %collective-permute-start.3 = (bf16[256,1024]{1,0:T(8,128)(2,1)S(1)}, bf16[256,1024]{1,0:T(8,128)(2,1)S(1)}, u32[]{:S(2)}, u32[]{:S(2)}) collective-permute-start(bf16[256,1024]{1,0:T(8,128)(2,1)S(1)} %get-tuple-element.46.block), channel_id=1, source_target_pairs={{0,8},{24,16},{1,9},{25,17},{2,10},{26,18},{3,11},{27,19},{4,12},{... | collective-permute-start | bytes 1572872 | tf_op jit(solution)/shard_map/ppermute | solution.py:52
  7.6 2.6 %project_rows.1 = (f32[64,256]{1,0:T(8,128)S(1)}, bf16[80,256]{1,0:T(8,128)(2,1)S(1)}, bf16[80,256]{1,0:T(8,128)(2,1)S(1)}, bf16[80,256]{1,0:T(8,128)(2,1)S(1)}) custom-call(bf16[1024,1024]{1,0:T(8,128)(2,1)} %bitcast.36, f32[64,1024]{1,0:T(8,128)} %bitcast.24, bf16[2,1024]{1,0:T(2,128)(2,1)} %bitcast.29), custom_call_target="tpu_custom_call" | custom-call | bytes 565248 | tf_op jit(solution)/shard_map/project_rows/pallas_call | solution.py:26
  10.2 3.0 %collective-permute-start.6 = (bf16[80,256]{1,0:T(8,128)(2,1)S(1)}, bf16[80,256]{1,0:T(8,128)(2,1)S(1)}, u32[]{:S(2)}, u32[]{:S(2)}) collective-permute-start(bf16[80,256]{1,0:T(8,128)(2,1)S(1)} %get-tuple-element.49), channel_id=1, source_target_pairs={{0,16},{8,24},{16,0},{24,8},{1,17},{9,25},{17,1},{25,9},{2,18},{10... | collective-permute-start | bytes 122888 | tf_op jit(solution)/shard_map/ppermute | solution.py:56
  17.0 3.7 %collective-permute-done.5.refs_8_ = bf16[80,256]{1,0:T(8,128)(2,1)S(1)} collective-permute-done((bf16[80,256]{1,0:T(8,128)(2,1)S(1)}, bf16[80,256]{1,0:T(8,128)(2,1)S(1)}, u32[]{:S(2)}, u32[]{:S(2)}) %collective-permute-start.5) | collective-permute-done | bytes 40992 | tf_op jit(solution)/shard_map/ppermute | solution.py:56
  21.6 3.8 %collective-permute-done.7.refs_10_ = bf16[80,256]{1,0:T(8,128)(2,1)S(1)} collective-permute-done((bf16[80,256]{1,0:T(8,128)(2,1)S(1)}, bf16[80,256]{1,0:T(8,128)(2,1)S(1)}, u32[]{:S(2)}, u32[]{:S(2)}) %collective-permute-start.7) | collective-permute-done | bytes 40992 | tf_op jit(solution)/shard_map/ppermute | solution.py:56
  25.5 2.0 %embed_update.1 = (f32[256,1024]{1,0:T(8,128)}, bf16[256,1024]{1,0:T(8,128)(2,1)S(1)}, f32[64,256]{1,0:T(8,128)}, bf16[2,1024]{1,0:T(2,128)(2,1)}, f32[2,1024]{1,0:T(2,128)}, /*index=5*/f32[2,1024]{1,0:T(2,128)}) custom-call(f32[64,256]{1,0:T(8,128)S(1)} %get-tuple-element.47.refs_0_, f32[64,256]{1,0:T(8,128)S(1)} %fusion.refs_1_, f32[256,1024]{1,0:T(8,128)S(1)} %bitcast.23, ...), custom_call_target="tpu_custom_call" | custom-call | bytes 4976640 | tf_op jit(solution)/shard_map/embed_update/pallas_call | solution.py:26
  31.3 6.3 %collective-permute-start = (bf16[256,1024]{1,0:T(8,128)(2,1)S(1)}, bf16[256,1024]{1,0:T(8,128)(2,1)S(1)}, u32[]{:S(2)}, u32[]{:S(2)}) collective-permute-start(bf16[256,1024]{1,0:T(8,128)(2,1)S(1)} %get-tuple-element.44.block), channel_id=1, source_target_pairs={{0,8},{24,16},{1,9},{25,17},{2,10},{26,18},{3,11},{27,19},{4,12},{... | collective-permute-start | bytes 1572872 | tf_op jit(solution)/shard_map/ppermute | solution.py:52
  38.4 2.4 %collective-permute-done.8.refs_0_.end = bf16[256,1024]{1,0:T(8,128)(2,1)S(1)} collective-permute-done((bf16[256,1024]{1,0:T(8,128)(2,1)S(1)}, bf16[256,1024]{1,0:T(8,128)(2,1)S(1)}, u32[]{:S(2)}, u32[]{:S(2)}) %collective-permute-start.8) | collective-permute-done | bytes 524320 | tf_op jit(solution)/shard_map/ppermute | solution.py:52
  42.2 3.3 %collective-permute-done.refs_5_ = bf16[256,1024]{1,0:T(8,128)(2,1)S(1)} collective-permute-done((bf16[256,1024]{1,0:T(8,128)(2,1)S(1)}, bf16[256,1024]{1,0:T(8,128)(2,1)S(1)}, u32[]{:S(2)}, u32[]{:S(2)}) %collective-permute-start) | collective-permute-done | bytes 524320 | tf_op jit(solution)/shard_map/ppermute | solution.py:52
  45.5 11.4 %collective-permute-done.9.refs_7_ = bf16[256,1024]{1,0:T(8,128)(2,1)S(1)} collective-permute-done((bf16[256,1024]{1,0:T(8,128)(2,1)S(1)}, bf16[256,1024]{1,0:T(8,128)(2,1)S(1)}, u32[]{:S(2)}, u32[]{:S(2)}) %collective-permute-start.9) | collective-permute-done | bytes 524320 | tf_op jit(solution)/shard_map/ppermute | solution.py:52
  56.9 1.7 %update_rows.1 = (bf16[256,1024]{1,0:T(8,128)(2,1)S(1)}, f32[128,1024]{1,0:T(8,128)}, f32[128,1024]{1,0:T(8,128)}, f32[32,2048]{1,0:T(8,128)S(1)}, f32[32,2048]{1,0:T(8,128)S(1)}) custom-call(f32[128,1024]{1,0:T(8,128)S(1)} %bitcast.26, f32[128,1024]{1,0:T(8,128)S(1)} %bitcast.27, f32[32,4096]{1,0:T(8,128)S(1)} %copy-done, f32[32,4096]{1,0:T(8,128)S(1)} %copy-done.1, ...), custom_call_target="tpu_custom_call" | custom-call | bytes 6291456 | tf_op jit(solution)/shard_map/update_rows/pallas_call | solution.py:26
  63.4 7.4 %collective-permute-done.12.refs_0_.refs_1_ = bf16[256,1024]{1,0:T(8,128)(2,1)S(1)} collective-permute-done((bf16[256,1024]{1,0:T(8,128)(2,1)S(1)}, bf16[256,1024]{1,0:T(8,128)(2,1)S(1)}, u32[]{:S(2)}, u32[]{:S(2)}) %collective-permute-start.12) | collective-permute-done | bytes 524320 | tf_op jit(solution)/shard_map/ppermute | solution.py:56
  70.8 2.8 %collective-permute-done.11.x = bf16[256,1024]{1,0:T(8,128)(2,1)S(1)} collective-permute-done((bf16[256,1024]{1,0:T(8,128)(2,1)S(1)}, bf16[256,1024]{1,0:T(8,128)(2,1)S(1)}, u32[]{:S(2)}, u32[]{:S(2)}) %collective-permute-start.11) | collective-permute-done | bytes 524320 | tf_op jit(solution)/shard_map/ppermute | solution.py:56
  75.2 6.1 %collective-permute-start.16 = (bf16[256,1024]{1,0:T(8,128)(2,1)S(1)}, bf16[256,1024]{1,0:T(8,128)(2,1)S(1)}, u32[]{:S(2)}, u32[]{:S(2)}) collective-permute-start(bf16[256,1024]{1,0:T(8,128)(2,1)S(1)} %gate.5), channel_id=1, source_target_pairs={{0,8},{24,16},{1,9},{25,17},{2,10},{26,18},{3,11},{27,19},{4,12},{... | collective-permute-start | bytes 1572872 | tf_op jit(solution)/shard_map/ppermute | solution.py:52
  81.3 4.0 %collective-permute-done.19.refs_0_.refs_3_ = bf16[256,1024]{1,0:T(8,128)(2,1)S(1)} collective-permute-done((bf16[256,1024]{1,0:T(8,128)(2,1)S(1)}, bf16[256,1024]{1,0:T(8,128)(2,1)S(1)}, u32[]{:S(2)}, u32[]{:S(2)}) %collective-permute-start.19) | collective-permute-done | bytes 524320 | tf_op jit(solution)/shard_map/ppermute | solution.py:56
  88.4 4.9 %collective-permute-done.21.refs_3_.refs_1_ = f32[32,2048]{1,0:T(8,128)S(1)} collective-permute-done((f32[32,2048]{1,0:T(8,128)S(1)}, f32[32,2048]{1,0:T(8,128)S(1)}, u32[]{:S(2)}, u32[]{:S(2)}) %collective-permute-start.21) | collective-permute-done | bytes 262176 | tf_op jit(solution)/shard_map/ppermute | solution.py:477
  94.6 2.1 %collective-permute-done.15.end = bf16[256,1024]{1,0:T(8,128)(2,1)S(1)} collective-permute-done((bf16[256,1024]{1,0:T(8,128)(2,1)S(1)}, bf16[256,1024]{1,0:T(8,128)(2,1)S(1)}, u32[]{:S(2)}, u32[]{:S(2)}) %collective-permute-start.15) | collective-permute-done | bytes 524320 | tf_op jit(solution)/shard_map/ppermute | solution.py:52
  98.4 1.9 %collective-permute-start.22 = (bf16[256,1024]{1,0:T(8,128)(2,1)S(1)}, bf16[256,1024]{1,0:T(8,128)(2,1)S(1)}, u32[]{:S(2)}, u32[]{:S(2)}) collective-permute-start(bf16[256,1024]{1,0:T(8,128)(2,1)S(1)} %pick.6.refs_2_.refs_4_.refs_0_), channel_id=1, source_target_pairs={{0,4},{2,6},{4,0},{6,2},{1,5},{3,7},{5,1},{7,3},{8,12},{10,14},{12... | collective-permute-start | bytes 1572872 | tf_op jit(solution)/shard_map/ppermute | solution.py:56
  104.0 2.2 %place_rows.3 = (bf16[4,4,128,1024]{3,2,1,0:T(8,128)(2,1)}, bf16[4,4,64,2048]{3,2,1,0:T(8,128)(2,1)}, f32[8,128]{1,0:T(8,128)S(1)}) custom-call(bf16[4,256,1024]{2,1,0:T(8,128)(2,1)S(1)} %bundle.4.refs_0_, bf16[4,256,1024]{2,1,0:T(8,128)(2,1)S(1)} %collective-permute-done.24.refs_1_, f32[8,128]{1,0:T(8,128)S(1)} %get-tuple-element.55.refs_2_.refs_3_), custom_call_target="tpu_custom_call" | custom-call | bytes 25178112 | tf_op jit(solution)/shard_map/place_rows/pallas_call | solution.py:26
  106.2 1.8 %place_rows.4 = (bf16[4,4,128,1024]{3,2,1,0:T(8,128)(2,1)}, bf16[4,4,64,2048]{3,2,1,0:T(8,128)(2,1)}, f32[8,128]{1,0:T(8,128)S(1)}) custom-call(bf16[3,256,1024]{2,1,0:T(8,128)(2,1)S(1)} %bundle.3.refs_0_, bf16[3,256,1024]{2,1,0:T(8,128)(2,1)S(1)} %collective-permute-done.23.refs_1_, ...), custom_call_target="tpu_custom_call", output_to_operand_aliasing={{0}: (3, {}), {1}: (4, {})} | custom-call | bytes 25178112 | tf_op jit(solution)/shard_map/place_rows/pallas_call | solution.py:26
  108.0 4.3 %collective-permute-done.22.refs_0_ = bf16[256,1024]{1,0:T(8,128)(2,1)S(1)} collective-permute-done((bf16[256,1024]{1,0:T(8,128)(2,1)S(1)}, bf16[256,1024]{1,0:T(8,128)(2,1)S(1)}, u32[]{:S(2)}, u32[]{:S(2)}) %collective-permute-start.22) | collective-permute-done | bytes 524320 | tf_op jit(solution)/shard_map/ppermute | solution.py:56
  112.5 5.5 %collective-permute-done.28.end = bf16[256,1024]{1,0:T(8,128)(2,1)S(1)} collective-permute-done((bf16[256,1024]{1,0:T(8,128)(2,1)S(1)}, bf16[256,1024]{1,0:T(8,128)(2,1)S(1)}, u32[]{:S(2)}, u32[]{:S(2)}) %collective-permute-start.28) | collective-permute-done | bytes 524320 | tf_op jit(solution)/shard_map/ppermute | solution.py:52
  119.3 8.8 %collective-permute-done.27.end = bf16[256,1024]{1,0:T(8,128)(2,1)S(1)} collective-permute-done((bf16[256,1024]{1,0:T(8,128)(2,1)S(1)}, bf16[256,1024]{1,0:T(8,128)(2,1)S(1)}, u32[]{:S(2)}, u32[]{:S(2)}) %collective-permute-start.27) | collective-permute-done | bytes 524320 | tf_op jit(solution)/shard_map/ppermute | solution.py:52
  (81 shorter events, 30.0 us)
Async XLA Ops:
  2.5 26.3 %collective-permute-start.3 = (bf16[256,1024]{1,0:T(8,128)(2,1)S(1)}, bf16[256,1024]{1,0:T(8,128)(2,1)S(1)}, u32[]{:S(2)}, u32[]{:S(2)}) collective-permute-start(bf16[256,1024]{1,0:T(8,128)(2,1)S(1)} %get-tuple-element.46.block), channel_id=1, source_target_pairs={{0,8},{24,16},{1,9},{25,17},{2,10},{26,18},{3,11},{27,19},{4,12},{... | collective-permute-start | bytes 1572872 | tf_op jit(solution)/shard_map/ppermute | solution.py:52
  10.2 10.6 %collective-permute-start.5 = (bf16[80,256]{1,0:T(8,128)(2,1)S(1)}, bf16[80,256]{1,0:T(8,128)(2,1)S(1)}, u32[]{:S(2)}, u32[]{:S(2)}) collective-permute-start(bf16[80,256]{1,0:T(8,128)(2,1)S(1)} %get-tuple-element.48), channel_id=1, source_target_pairs={{0,8},{8,0},{16,24},{24,16},{1,9},{9,1},{17,25},{25,17},{2,10},{10... | collective-permute-start | bytes 122888 | tf_op jit(solution)/shard_map/ppermute | solution.py:56
  10.2 11.4 %collective-permute-start.6 = (bf16[80,256]{1,0:T(8,128)(2,1)S(1)}, bf16[80,256]{1,0:T(8,128)(2,1)S(1)}, u32[]{:S(2)}, u32[]{:S(2)}) collective-permute-start(bf16[80,256]{1,0:T(8,128)(2,1)S(1)} %get-tuple-element.49), channel_id=1, source_target_pairs={{0,16},{8,24},{16,0},{24,8},{1,17},{9,25},{17,1},{25,9},{2,18},{10... | collective-permute-start | bytes 122888 | tf_op jit(solution)/shard_map/ppermute | solution.py:56
  13.3 12.2 %collective-permute-start.7 = (bf16[80,256]{1,0:T(8,128)(2,1)S(1)}, bf16[80,256]{1,0:T(8,128)(2,1)S(1)}, u32[]{:S(2)}, u32[]{:S(2)}) collective-permute-start(bf16[80,256]{1,0:T(8,128)(2,1)S(1)} %get-tuple-element.50), channel_id=1, source_target_pairs={{0,24},{8,16},{16,8},{24,0},{1,25},{9,17},{17,9},{25,1},{2,26},{10... | collective-permute-start | bytes 122888 | tf_op jit(solution)/shard_map/ppermute | solution.py:56
  14.6 22.9 %collective-permute-start.1 = (bf16[256,1024]{1,0:T(8,128)(2,1)S(1)}, bf16[256,1024]{1,0:T(8,128)(2,1)S(1)}, u32[]{:S(2)}, u32[]{:S(2)}) collective-permute-start(bf16[256,1024]{1,0:T(8,128)(2,1)S(1)} %get-tuple-element.45.block), channel_id=1, source_target_pairs={{0,8},{24,16},{1,9},{25,17},{2,10},{26,18},{3,11},{27,19},{4,12},{... | collective-permute-start | bytes 1572872 | tf_op jit(solution)/shard_map/ppermute | solution.py:52
  27.5 13.2 %collective-permute-start.8 = (bf16[256,1024]{1,0:T(8,128)(2,1)S(1)}, bf16[256,1024]{1,0:T(8,128)(2,1)S(1)}, u32[]{:S(2)}, u32[]{:S(2)}) collective-permute-start(bf16[256,1024]{1,0:T(8,128)(2,1)S(1)} %get-tuple-element.51.x.refs_0_), channel_id=1, source_target_pairs={{8,0},{16,24},{9,1},{17,25},{10,2},{18,26},{11,3},{19,27},{12,4},{... | collective-permute-start | bytes 1572872 | tf_op jit(solution)/shard_map/ppermute | solution.py:52
  28.9 11.8 %collective-permute-start.4 = (bf16[256,1024]{1,0:T(8,128)(2,1)S(1)}, bf16[256,1024]{1,0:T(8,128)(2,1)S(1)}, u32[]{:S(2)}, u32[]{:S(2)}) collective-permute-start(bf16[256,1024]{1,0:T(8,128)(2,1)S(1)} %add_block.4), channel_id=1, source_target_pairs={{8,16},{16,8},{9,17},{17,9},{10,18},{18,10},{11,19},{19,11},{12,20... | collective-permute-start | bytes 1572872 | tf_op jit(solution)/shard_map/ppermute | solution.py:52
  29.7 12.5 %collective-permute-start.10 = (f32[2,32,2048]{2,1,0:T(8,128)S(1)}, f32[2,32,2048]{2,1,0:T(8,128)S(1)}, u32[]{:S(2)}, u32[]{:S(2)}) collective-permute-start(f32[2,32,2048]{2,1,0:T(8,128)S(1)} %up_state.1), channel_id=1, source_target_pairs={{0,1},{1,0},{2,3},{3,2},{4,5},{5,4},{6,7},{7,6},{8,9},{9,8},{10,11... | collective-permute-start | bytes 1572872 | tf_op jit(solution)/shard_map/ppermute | solution.py:411
  31.3 14.2 %collective-permute-start = (bf16[256,1024]{1,0:T(8,128)(2,1)S(1)}, bf16[256,1024]{1,0:T(8,128)(2,1)S(1)}, u32[]{:S(2)}, u32[]{:S(2)}) collective-permute-start(bf16[256,1024]{1,0:T(8,128)(2,1)S(1)} %get-tuple-element.44.block), channel_id=1, source_target_pairs={{0,8},{24,16},{1,9},{25,17},{2,10},{26,18},{3,11},{27,19},{4,12},{... | collective-permute-start | bytes 1572872 | tf_op jit(solution)/shard_map/ppermute | solution.py:52
  40.9 16.1 %collective-permute-start.9 = (bf16[256,1024]{1,0:T(8,128)(2,1)S(1)}, bf16[256,1024]{1,0:T(8,128)(2,1)S(1)}, u32[]{:S(2)}, u32[]{:S(2)}) collective-permute-start(bf16[256,1024]{1,0:T(8,128)(2,1)S(1)} %add_block.5), channel_id=1, source_target_pairs={{8,0},{16,24},{9,1},{17,25},{10,2},{18,26},{11,3},{19,27},{12,4},{... | collective-permute-start | bytes 1572872 | tf_op jit(solution)/shard_map/ppermute | solution.py:52
  59.3 11.5 %collective-permute-start.12 = (bf16[256,1024]{1,0:T(8,128)(2,1)S(1)}, bf16[256,1024]{1,0:T(8,128)(2,1)S(1)}, u32[]{:S(2)}, u32[]{:S(2)}) collective-permute-start(bf16[256,1024]{1,0:T(8,128)(2,1)S(1)} %get-tuple-element.52.refs_0_), channel_id=1, source_target_pairs={{0,4},{2,6},{4,0},{6,2},{1,5},{3,7},{5,1},{7,3},{8,12},{10,14},{12... | collective-permute-start | bytes 1572872 | tf_op jit(solution)/shard_map/ppermute | solution.py:56
  60.9 12.8 %collective-permute-start.11 = (bf16[256,1024]{1,0:T(8,128)(2,1)S(1)}, bf16[256,1024]{1,0:T(8,128)(2,1)S(1)}, u32[]{:S(2)}, u32[]{:S(2)}) collective-permute-start(bf16[256,1024]{1,0:T(8,128)(2,1)S(1)} %get-tuple-element.52.refs_0_), channel_id=1, source_target_pairs={{0,8},{8,0},{16,24},{24,16},{1,9},{9,1},{17,25},{25,17},{2,10},{10... | collective-permute-start | bytes 1572872 | tf_op jit(solution)/shard_map/ppermute | solution.py:56
  62.1 19.2 %collective-permute-start.18 = (bf16[256,1024]{1,0:T(8,128)(2,1)S(1)}, bf16[256,1024]{1,0:T(8,128)(2,1)S(1)}, u32[]{:S(2)}, u32[]{:S(2)}) collective-permute-start(bf16[256,1024]{1,0:T(8,128)(2,1)S(1)} %collective-permute-done.13.refs_1_.middle), channel_id=1, source_target_pairs={{8,0},{16,24},{9,1},{17,25},{10,2},{18,26},{11,3},{19,27},{12,4},{... | collective-permute-start | bytes 1572872 | tf_op jit(solution)/shard_map/ppermute | solution.py:52
  73.7 11.6 %collective-permute-start.19 = (bf16[256,1024]{1,0:T(8,128)(2,1)S(1)}, bf16[256,1024]{1,0:T(8,128)(2,1)S(1)}, u32[]{:S(2)}, u32[]{:S(2)}) collective-permute-start(bf16[256,1024]{1,0:T(8,128)(2,1)S(1)} %gate.4.refs_0_.refs_2_), channel_id=1, source_target_pairs={{0,4},{2,6},{4,0},{6,2},{1,5},{3,7},{5,1},{7,3},{8,12},{10,14},{12... | collective-permute-start | bytes 1572872 | tf_op jit(solution)/shard_map/ppermute | solution.py:56
  73.8 11.6 %collective-permute-start.14 = (bf16[256,1024]{1,0:T(8,128)(2,1)S(1)}, bf16[256,1024]{1,0:T(8,128)(2,1)S(1)}, u32[]{:S(2)}, u32[]{:S(2)}) collective-permute-start(bf16[256,1024]{1,0:T(8,128)(2,1)S(1)} %gate.4.refs_0_.refs_2_), channel_id=1, source_target_pairs={{8,16},{16,8},{9,17},{17,9},{10,18},{18,10},{11,19},{19,11},{12,20... | collective-permute-start | bytes 1572872 | tf_op jit(solution)/shard_map/ppermute | solution.py:52
  74.5 18.7 %collective-permute-start.17 = (bf16[256,1024]{1,0:T(8,128)(2,1)S(1)}, bf16[256,1024]{1,0:T(8,128)(2,1)S(1)}, u32[]{:S(2)}, u32[]{:S(2)}) collective-permute-start(bf16[256,1024]{1,0:T(8,128)(2,1)S(1)} %gate.5), channel_id=1, source_target_pairs={{8,16},{16,8},{9,17},{17,9},{10,18},{18,10},{11,19},{19,11},{12,20... | collective-permute-start | bytes 1572872 | tf_op jit(solution)/shard_map/ppermute | solution.py:52
  75.2 18.0 %collective-permute-start.16 = (bf16[256,1024]{1,0:T(8,128)(2,1)S(1)}, bf16[256,1024]{1,0:T(8,128)(2,1)S(1)}, u32[]{:S(2)}, u32[]{:S(2)}) collective-permute-start(bf16[256,1024]{1,0:T(8,128)(2,1)S(1)} %gate.5), channel_id=1, source_target_pairs={{0,8},{24,16},{1,9},{25,17},{2,10},{26,18},{3,11},{27,19},{4,12},{... | collective-permute-start | bytes 1572872 | tf_op jit(solution)/shard_map/ppermute | solution.py:52
  85.4 9.2 %collective-permute-start.20 = (bf16[256,1024]{1,0:T(8,128)(2,1)S(1)}, bf16[256,1024]{1,0:T(8,128)(2,1)S(1)}, u32[]{:S(2)}, u32[]{:S(2)}) collective-permute-start(bf16[256,1024]{1,0:T(8,128)(2,1)S(1)} %pick.5.refs_0_), channel_id=1, source_target_pairs={{0,4},{2,6},{4,0},{6,2},{1,5},{3,7},{5,1},{7,3},{8,12},{10,14},{12... | collective-permute-start | bytes 1572872 | tf_op jit(solution)/shard_map/ppermute | solution.py:56
  85.4 11.3 %collective-permute-start.15 = (bf16[256,1024]{1,0:T(8,128)(2,1)S(1)}, bf16[256,1024]{1,0:T(8,128)(2,1)S(1)}, u32[]{:S(2)}, u32[]{:S(2)}) collective-permute-start(bf16[256,1024]{1,0:T(8,128)(2,1)S(1)} %collective-permute-done.14.middle), channel_id=1, source_target_pairs={{8,0},{16,24},{9,1},{17,25},{10,2},{18,26},{11,3},{19,27},{12,4},{... | collective-permute-start | bytes 1572872 | tf_op jit(solution)/shard_map/ppermute | solution.py:52
  97.1 9.1 %collective-permute-start.23 = (bf16[3,256,1024]{2,1,0:T(8,128)(2,1)S(1)}, bf16[3,256,1024]{2,1,0:T(8,128)(2,1)S(1)}, u32[]{:S(2)}, u32[]{:S(2)}) collective-permute-start(bf16[3,256,1024]{2,1,0:T(8,128)(2,1)S(1)} %bundle.3.refs_0_), channel_id=1, source_target_pairs={{0,2},{2,0},{4,6},{6,4},{1,3},{3,1},{5,7},{7,5},{8,10},{10,8},{12,... | collective-permute-start | bytes 4718600 | tf_op jit(solution)/shard_map/ppermute | solution.py:56
  98.4 14.0 %collective-permute-start.22 = (bf16[256,1024]{1,0:T(8,128)(2,1)S(1)}, bf16[256,1024]{1,0:T(8,128)(2,1)S(1)}, u32[]{:S(2)}, u32[]{:S(2)}) collective-permute-start(bf16[256,1024]{1,0:T(8,128)(2,1)S(1)} %pick.6.refs_2_.refs_4_.refs_0_), channel_id=1, source_target_pairs={{0,4},{2,6},{4,0},{6,2},{1,5},{3,7},{5,1},{7,3},{8,12},{10,14},{12... | collective-permute-start | bytes 1572872 | tf_op jit(solution)/shard_map/ppermute | solution.py:56
  101.4 16.7 %collective-permute-start.28 = (bf16[256,1024]{1,0:T(8,128)(2,1)S(1)}, bf16[256,1024]{1,0:T(8,128)(2,1)S(1)}, u32[]{:S(2)}, u32[]{:S(2)}) collective-permute-start(bf16[256,1024]{1,0:T(8,128)(2,1)S(1)} %collective-permute-done.17.refs_1_.middle), channel_id=1, source_target_pairs={{8,0},{16,24},{9,1},{17,25},{10,2},{18,26},{11,3},{19,27},{12,4},{... | collective-permute-start | bytes 1572872 | tf_op jit(solution)/shard_map/ppermute | solution.py:52
  102.7 25.4 %collective-permute-start.27 = (bf16[256,1024]{1,0:T(8,128)(2,1)S(1)}, bf16[256,1024]{1,0:T(8,128)(2,1)S(1)}, u32[]{:S(2)}, u32[]{:S(2)}) collective-permute-start(bf16[256,1024]{1,0:T(8,128)(2,1)S(1)} %collective-permute-done.26.middle), channel_id=1, source_target_pairs={{8,0},{16,24},{9,1},{17,25},{10,2},{18,26},{11,3},{19,27},{12,4},{... | collective-permute-start | bytes 1572872 | tf_op jit(solution)/shard_map/ppermute | solution.py:52
  112.4 15.7 %collective-permute-start.25 = (bf16[1,256,1024]{2,1,0:T(8,128)(2,1)S(1)}, bf16[1,256,1024]{2,1,0:T(8,128)(2,1)S(1)}, u32[]{:S(2)}, u32[]{:S(2)}) collective-permute-start(bf16[1,256,1024]{2,1,0:T(8,128)(2,1)S(1)} %bundle.5.refs_0_), channel_id=1, source_target_pairs={{0,2},{2,0},{4,6},{6,4},{1,3},{3,1},{5,7},{7,5},{8,10},{10,8},{12,... | collective-permute-start | bytes 1572872 | tf_op jit(solution)/shard_map/ppermute | solution.py:56
  (15 other events, 276.7 us)

commit v4 on v3

--- a/solution.py
+++ b/solution.py
@@ -392,9 +392,10 @@
         pltpu.with_memory_space_constraint(down, pltpu.HBM),
         pltpu.with_memory_space_constraint(up, pltpu.HBM),
     )
+    packets_came = [swap(packets[0], "replica", 1), swap(packets[1], "replica", 2)]
+    end = gate(end, packets_came[0])
+    packets_came.append(swap(gate(packets[2], end), "replica", 3))
     from_end = [along(x, INWARD) for x in (end, middle, near)]
-    end_sum = add(end, from_end[0])
-    packets_came = [swap(x, "replica", mask) for mask, x in enumerate(packets, 1)]
 
     state = jax.ShapeDtypeStruct((2, rows_up, half_cols), F32)
     states = call(
@@ -443,9 +444,11 @@
     )
 
     embed_out = along(recast_rows, OUTWARD)
-    end_partial = along(end_sum, ACROSS)
+    embed_middle = along(recast_rows, ACROSS)
+    end_partial = along(add(end, from_end[0], embed_middle), ACROSS)
     middle_partial = along(add(middle, from_end[1]), ACROSS)
-    to_end = along(add(near, end_partial, embed_out), OUTWARD)
+    embed_middle_out = along(embed_middle, OUTWARD)
+    to_end = along(add(near, end_partial, embed_out, embed_middle_out), OUTWARD)
     came0 = [own, from_end[2], middle_partial, to_end]
     half_sum = jax.ShapeDtypeStruct((rows_up, half_cols), F32)
     down_state = jax.ShapeDtypeStruct((rows_down, width), F32)
@@ -470,18 +473,17 @@
     near_piece = gate(swap(piece, "replica", 1), far_piece, middle_piece)
     far_near = swap(near_piece, "shard", top)
     end_piece = along(near_piece, ACROSS)
-    embed_late = gate(recast_rows, near_piece)
-    embed_in = along(embed_late, INWARD)
-    embed_middle = along(embed_late, ACROSS)
+    embed_in = along(gate(recast_rows, piece), INWARD)
     sums = [sums[0]] + [
         lax.ppermute(
             gate(x, near_piece), "tensor", [(i, (i + shift) % tensors) for i in range(tensors)]
         )
         for shift, x in enumerate(sums[1:], 1)
     ]
-    second = pick(middle_piece, along(middle_piece, OUTWARD), far_near)
+    second = pick(middle_piece, along(middle_piece, OUTWARD), far_near, embed_in)
     far_second = swap(second, "shard", top)
-    third = pick(end_piece, along(end_piece, OUTWARD), embed_in, embed_middle, far_second, *sums[1:])
+    embed_end = along(embed_in, ACROSS)
+    third = pick(end_piece, along(end_piece, OUTWARD), embed_end, far_second, *sums[1:])
     far_third = swap(third, "shard", top)
     bundles = [
         (
@@ -494,8 +496,6 @@
         ),
     ]
 
-    embed_middle_out = along(embed_middle, OUTWARD)
-    embed_end = along(gate(embed_in, third), ACROSS)
     embed_last = along(embed_end, OUTWARD)
 
     stored_up, velocity_up, token = call(

time: 130 us -> 128 us (0.985)
  starting transfers between devices: 43.7 us -> 41.1 us
    ppermute x16, waiting for transfers between devices: 33.5 us -> 43.3 us  [along(): return lax.ppermute(x, 'replica', pairs)]
    ppermute x11, waiting for transfers between devices: 28.4 us -> 18.6 us  [swap(): lax.ppermute(x, axis, [(i, i ^ bit) for i in range(lax.axis_size(axis))])]
    ppermute x16, starting transfers between devices: 30.6 us -> 23.2 us  [along(): return lax.ppermute(x, 'replica', pairs)]
    ppermute x11, starting transfers between devices: 9.94 us -> 14.8 us  [swap(): lax.ppermute(x, axis, [(i, i ^ bit) for i in range(lax.axis_size(axis))])]
    pallas_call x26 -> x27, Pallas kernels: 17.2 us -> 17.2 us  [call(): pl.pallas_call(kernel, name=name, out_shape=out_shape, in_specs=in_specs,...]
  transfers between devices with their start and end apart: 29 -> 29, of which waited for: 15 -> 16; matrix products, arithmetic and copies ran while one was open for 1% -> 1% of each run, Pallas kernels for 9% -> 9%
where the time goes in v4:
time: 128 us; the launch traced here: 127 us
  waiting for transfers between devices  66.8 us (52%)
  starting transfers between devices  41.1 us (32%)
  Pallas kernels  17.2 us (13%)
    ppermute x16, waiting for transfers between devices, along(): return lax.ppermute(x, 'replica', pairs)  43.3 us
    ppermute x16, starting transfers between devices, along(): return lax.ppermute(x, 'replica', pairs)  23.2 us
    ppermute x11, waiting for transfers between devices, swap(): lax.ppermute(x, axis, [(i, i ^ bit) for i in range(lax.axis_size(axis))])  18.6 us
    pallas_call x27, Pallas kernels, call(): pl.pallas_call(kernel, name=name, out_shape=out_shape, in_specs=in_specs,...  17.2 us
    ppermute x11, starting transfers between devices, swap(): lax.ppermute(x, axis, [(i, i ^ bit) for i in range(lax.axis_size(axis))])  14.8 us
    ppermute x1, waiting for transfers between devices, body(): lax.ppermute(gate(x, near_piece), 'tensor', [(i, (i + shift) % tensors) f...  4.88 us
  transfers between devices with their start and end apart: 29, of which 16 were waited for; matrix products, arithmetic and copies ran while one was open for 1% of the time, Pallas kernels for 9%

profile of v4, /device:TPU:0, one launch (start us, length us, event | category | flops | bytes accessed | tf_op | source)
XLA Modules:
  0.0 127.4 jit_solution(15135008903067115503)
XLA Ops:
  0.6 2.6 %project_rows.1 = (f32[64,256]{1,0:T(8,128)S(1)}, bf16[80,256]{1,0:T(8,128)(2,1)S(1)}, bf16[80,256]{1,0:T(8,128)(2,1)S(1)}, bf16[80,256]{1,0:T(8,128)(2,1)S(1)}) custom-call(bf16[1024,1024]{1,0:T(8,128)(2,1)} %bitcast.36, f32[64,1024]{1,0:T(8,128)} %bitcast.24, bf16[2,1024]{1,0:T(2,128)(2,1)} %bitcast.29), custom_call_target="tpu_custom_call" | custom-call | bytes 565248 | tf_op jit(solution)/shard_map/project_rows/pallas_call | solution.py:26
  3.2 3.1 %collective-permute-start.3 = (bf16[80,256]{1,0:T(8,128)(2,1)S(1)}, bf16[80,256]{1,0:T(8,128)(2,1)S(1)}, u32[]{:S(2)}, u32[]{:S(2)}) collective-permute-start(bf16[80,256]{1,0:T(8,128)(2,1)S(1)} %get-tuple-element.47), channel_id=1, source_target_pairs={{0,8},{8,0},{16,24},{24,16},{1,9},{9,1},{17,25},{25,17},{2,10},{10... | collective-permute-start | bytes 122888 | tf_op jit(solution)/shard_map/ppermute | solution.py:56
  6.3 2.6 %collective-permute-start.5 = (bf16[80,256]{1,0:T(8,128)(2,1)S(1)}, bf16[80,256]{1,0:T(8,128)(2,1)S(1)}, u32[]{:S(2)}, u32[]{:S(2)}) collective-permute-start(bf16[80,256]{1,0:T(8,128)(2,1)S(1)} %get-tuple-element.49), channel_id=1, source_target_pairs={{0,16},{8,24},{16,0},{24,8},{1,17},{9,25},{17,1},{25,9},{2,18},{10... | collective-permute-start | bytes 122888 | tf_op jit(solution)/shard_map/ppermute | solution.py:56
  10.8 2.0 %collective-permute-start.6 = (bf16[80,256]{1,0:T(8,128)(2,1)S(1)}, bf16[80,256]{1,0:T(8,128)(2,1)S(1)}, u32[]{:S(2)}, u32[]{:S(2)}) collective-permute-start(bf16[80,256]{1,0:T(8,128)(2,1)S(1)} %gate.6), channel_id=1, source_target_pairs={{0,24},{8,16},{16,8},{24,0},{1,25},{9,17},{17,9},{25,1},{2,26},{10... | collective-permute-start | bytes 122888 | tf_op jit(solution)/shard_map/ppermute | solution.py:56
  16.7 2.0 %embed_update.1 = (f32[256,1024]{1,0:T(8,128)}, bf16[256,1024]{1,0:T(8,128)(2,1)S(1)}, f32[64,256]{1,0:T(8,128)}, bf16[2,1024]{1,0:T(2,128)(2,1)}, f32[2,1024]{1,0:T(2,128)}, /*index=5*/f32[2,1024]{1,0:T(2,128)}) custom-call(f32[64,256]{1,0:T(8,128)S(1)} %get-tuple-element.48.refs_0_, f32[64,256]{1,0:T(8,128)S(1)} %fusion.refs_1_, f32[256,1024]{1,0:T(8,128)S(1)} %bitcast.23, ...), custom_call_target="tpu_custom_call" | custom-call | bytes 4976640 | tf_op jit(solution)/shard_map/embed_update/pallas_call | solution.py:26
  19.5 2.6 %collective-permute-start.1 = (bf16[256,1024]{1,0:T(8,128)(2,1)S(1)}, bf16[256,1024]{1,0:T(8,128)(2,1)S(1)}, u32[]{:S(2)}, u32[]{:S(2)}) collective-permute-start(bf16[256,1024]{1,0:T(8,128)(2,1)S(1)} %get-tuple-element.45.block), channel_id=1, source_target_pairs={{0,8},{24,16},{1,9},{25,17},{2,10},{26,18},{3,11},{27,19},{4,12},{... | collective-permute-start | bytes 1572872 | tf_op jit(solution)/shard_map/ppermute | solution.py:52
  23.4 4.2 %collective-permute-done.4.came = bf16[256,1024]{1,0:T(8,128)(2,1)S(1)} collective-permute-done((bf16[256,1024]{1,0:T(8,128)(2,1)S(1)}, bf16[256,1024]{1,0:T(8,128)(2,1)S(1)}, u32[]{:S(2)}, u32[]{:S(2)}) %collective-permute-start.4) | collective-permute-done | bytes 524320 | tf_op jit(solution)/shard_map/ppermute | solution.py:52
  31.3 5.4 %collective-permute-done.1.came = bf16[256,1024]{1,0:T(8,128)(2,1)S(1)} collective-permute-done((bf16[256,1024]{1,0:T(8,128)(2,1)S(1)}, bf16[256,1024]{1,0:T(8,128)(2,1)S(1)}, u32[]{:S(2)}, u32[]{:S(2)}) %collective-permute-start.1) | collective-permute-done | bytes 524320 | tf_op jit(solution)/shard_map/ppermute | solution.py:52
  36.7 4.4 %collective-permute-start = (bf16[256,1024]{1,0:T(8,128)(2,1)S(1)}, bf16[256,1024]{1,0:T(8,128)(2,1)S(1)}, u32[]{:S(2)}, u32[]{:S(2)}) collective-permute-start(bf16[256,1024]{1,0:T(8,128)(2,1)S(1)} %get-tuple-element.44.block), channel_id=1, source_target_pairs={{0,8},{24,16},{1,9},{25,17},{2,10},{26,18},{3,11},{27,19},{4,12},{... | collective-permute-start | bytes 1572872 | tf_op jit(solution)/shard_map/ppermute | solution.py:52
  42.0 5.2 %collective-permute-done.10.refs_1_.end = bf16[256,1024]{1,0:T(8,128)(2,1)S(1)} collective-permute-done((bf16[256,1024]{1,0:T(8,128)(2,1)S(1)}, bf16[256,1024]{1,0:T(8,128)(2,1)S(1)}, u32[]{:S(2)}, u32[]{:S(2)}) %collective-permute-start.10) | collective-permute-done | bytes 524320 | tf_op jit(solution)/shard_map/ppermute | solution.py:52
  48.6 1.9 %collective-permute-done.refs_5_ = bf16[256,1024]{1,0:T(8,128)(2,1)S(1)} collective-permute-done((bf16[256,1024]{1,0:T(8,128)(2,1)S(1)}, bf16[256,1024]{1,0:T(8,128)(2,1)S(1)}, u32[]{:S(2)}, u32[]{:S(2)}) %collective-permute-start) | collective-permute-done | bytes 524320 | tf_op jit(solution)/shard_map/ppermute | solution.py:52
  50.5 11.1 %collective-permute-done.11.refs_7_ = bf16[256,1024]{1,0:T(8,128)(2,1)S(1)} collective-permute-done((bf16[256,1024]{1,0:T(8,128)(2,1)S(1)}, bf16[256,1024]{1,0:T(8,128)(2,1)S(1)}, u32[]{:S(2)}, u32[]{:S(2)}) %collective-permute-start.11) | collective-permute-done | bytes 524320 | tf_op jit(solution)/shard_map/ppermute | solution.py:52
  66.6 2.9 %collective-permute-start.18 = (bf16[256,1024]{1,0:T(8,128)(2,1)S(1)}, bf16[256,1024]{1,0:T(8,128)(2,1)S(1)}, u32[]{:S(2)}, u32[]{:S(2)}) collective-permute-start(bf16[256,1024]{1,0:T(8,128)(2,1)S(1)} %gate.8), channel_id=1, source_target_pairs={{0,8},{24,16},{1,9},{25,17},{2,10},{26,18},{3,11},{27,19},{4,12},{... | collective-permute-start | bytes 1572872 | tf_op jit(solution)/shard_map/ppermute | solution.py:52
  70.8 4.6 %collective-permute-done.14.refs_0_.refs_1_ = bf16[256,1024]{1,0:T(8,128)(2,1)S(1)} collective-permute-done((bf16[256,1024]{1,0:T(8,128)(2,1)S(1)}, bf16[256,1024]{1,0:T(8,128)(2,1)S(1)}, u32[]{:S(2)}, u32[]{:S(2)}) %collective-permute-start.14) | collective-permute-done | bytes 524320 | tf_op jit(solution)/shard_map/ppermute | solution.py:56
  75.4 3.5 %collective-permute-done.13.x = bf16[256,1024]{1,0:T(8,128)(2,1)S(1)} collective-permute-done((bf16[256,1024]{1,0:T(8,128)(2,1)S(1)}, bf16[256,1024]{1,0:T(8,128)(2,1)S(1)}, u32[]{:S(2)}, u32[]{:S(2)}) %collective-permute-start.13) | collective-permute-done | bytes 524320 | tf_op jit(solution)/shard_map/ppermute | solution.py:56
  80.3 5.9 %collective-permute-done.18.refs_1_.middle = bf16[256,1024]{1,0:T(8,128)(2,1)S(1)} collective-permute-done((bf16[256,1024]{1,0:T(8,128)(2,1)S(1)}, bf16[256,1024]{1,0:T(8,128)(2,1)S(1)}, u32[]{:S(2)}, u32[]{:S(2)}) %collective-permute-start.18) | collective-permute-done | bytes 524320 | tf_op jit(solution)/shard_map/ppermute | solution.py:52
  91.7 4.9 %collective-permute-done.23.refs_2_.refs_1_ = f32[32,2048]{1,0:T(8,128)S(1)} collective-permute-done((f32[32,2048]{1,0:T(8,128)S(1)}, f32[32,2048]{1,0:T(8,128)S(1)}, u32[]{:S(2)}, u32[]{:S(2)}) %collective-permute-start.23) | collective-permute-done | bytes 262176 | tf_op jit(solution)/shard_map/ppermute | solution.py:478
  96.6 3.0 %collective-permute-done.22.refs_1_ = bf16[256,1024]{1,0:T(8,128)(2,1)S(1)} collective-permute-done((bf16[256,1024]{1,0:T(8,128)(2,1)S(1)}, bf16[256,1024]{1,0:T(8,128)(2,1)S(1)}, u32[]{:S(2)}, u32[]{:S(2)}) %collective-permute-start.22) | collective-permute-done | bytes 524320 | tf_op jit(solution)/shard_map/ppermute | solution.py:56
  99.7 5.6 %collective-permute-done.17.end = bf16[256,1024]{1,0:T(8,128)(2,1)S(1)} collective-permute-done((bf16[256,1024]{1,0:T(8,128)(2,1)S(1)}, bf16[256,1024]{1,0:T(8,128)(2,1)S(1)}, u32[]{:S(2)}, u32[]{:S(2)}) %collective-permute-start.17) | collective-permute-done | bytes 524320 | tf_op jit(solution)/shard_map/ppermute | solution.py:52
  106.2 2.6 %collective-permute-start.24 = (bf16[256,1024]{1,0:T(8,128)(2,1)S(1)}, bf16[256,1024]{1,0:T(8,128)(2,1)S(1)}, u32[]{:S(2)}, u32[]{:S(2)}) collective-permute-start(bf16[256,1024]{1,0:T(8,128)(2,1)S(1)} %pick.6.refs_2_.refs_4_), channel_id=1, source_target_pairs={{0,4},{2,6},{4,0},{6,2},{1,5},{3,7},{5,1},{7,3},{8,12},{10,14},{12... | collective-permute-start | bytes 1572872 | tf_op jit(solution)/shard_map/ppermute | solution.py:56
  111.3 2.2 %place_rows.3 = (bf16[4,4,128,1024]{3,2,1,0:T(8,128)(2,1)}, bf16[4,4,64,2048]{3,2,1,0:T(8,128)(2,1)}, f32[8,128]{1,0:T(8,128)S(1)}) custom-call(bf16[4,256,1024]{2,1,0:T(8,128)(2,1)S(1)} %bundle.4.refs_0_, bf16[4,256,1024]{2,1,0:T(8,128)(2,1)S(1)} %collective-permute-done.26.refs_1_, f32[8,128]{1,0:T(8,128)S(1)} %get-tuple-element.55.refs_2_.refs_3_), custom_call_target="tpu_custom_call" | custom-call | bytes 25178112 | tf_op jit(solution)/shard_map/place_rows/pallas_call | solution.py:26
  113.5 1.8 %place_rows.4 = (bf16[4,4,128,1024]{3,2,1,0:T(8,128)(2,1)}, bf16[4,4,64,2048]{3,2,1,0:T(8,128)(2,1)}, f32[8,128]{1,0:T(8,128)S(1)}) custom-call(bf16[3,256,1024]{2,1,0:T(8,128)(2,1)S(1)} %bundle.3.refs_0_, bf16[3,256,1024]{2,1,0:T(8,128)(2,1)S(1)} %collective-permute-done.25.refs_1_, ...), custom_call_target="tpu_custom_call", output_to_operand_aliasing={{0}: (3, {}), {1}: (4, {})} | custom-call | bytes 25178112 | tf_op jit(solution)/shard_map/place_rows/pallas_call | solution.py:26
  115.3 5.7 %collective-permute-done.24.refs_0_ = bf16[256,1024]{1,0:T(8,128)(2,1)S(1)} collective-permute-done((bf16[256,1024]{1,0:T(8,128)(2,1)S(1)}, bf16[256,1024]{1,0:T(8,128)(2,1)S(1)}, u32[]{:S(2)}, u32[]{:S(2)}) %collective-permute-start.24) | collective-permute-done | bytes 524320 | tf_op jit(solution)/shard_map/ppermute | solution.py:56
  122.4 3.0 %collective-permute-done.28.end = bf16[256,1024]{1,0:T(8,128)(2,1)S(1)} collective-permute-done((bf16[256,1024]{1,0:T(8,128)(2,1)S(1)}, bf16[256,1024]{1,0:T(8,128)(2,1)S(1)}, u32[]{:S(2)}, u32[]{:S(2)}) %collective-permute-start.28) | collective-permute-done | bytes 524320 | tf_op jit(solution)/shard_map/ppermute | solution.py:52
  (82 shorter events, 33.4 us)
Async XLA Ops:
  3.2 7.5 %collective-permute-start.3 = (bf16[80,256]{1,0:T(8,128)(2,1)S(1)}, bf16[80,256]{1,0:T(8,128)(2,1)S(1)}, u32[]{:S(2)}, u32[]{:S(2)}) collective-permute-start(bf16[80,256]{1,0:T(8,128)(2,1)S(1)} %get-tuple-element.47), channel_id=1, source_target_pairs={{0,8},{8,0},{16,24},{24,16},{1,9},{9,1},{17,25},{25,17},{2,10},{10... | collective-permute-start | bytes 122888 | tf_op jit(solution)/shard_map/ppermute | solution.py:56
  6.3 8.9 %collective-permute-start.5 = (bf16[80,256]{1,0:T(8,128)(2,1)S(1)}, bf16[80,256]{1,0:T(8,128)(2,1)S(1)}, u32[]{:S(2)}, u32[]{:S(2)}) collective-permute-start(bf16[80,256]{1,0:T(8,128)(2,1)S(1)} %get-tuple-element.49), channel_id=1, source_target_pairs={{0,16},{8,24},{16,0},{24,8},{1,17},{9,25},{17,1},{25,9},{2,18},{10... | collective-permute-start | bytes 122888 | tf_op jit(solution)/shard_map/ppermute | solution.py:56
  13.9 13.7 %collective-permute-start.4 = (bf16[256,1024]{1,0:T(8,128)(2,1)S(1)}, bf16[256,1024]{1,0:T(8,128)(2,1)S(1)}, u32[]{:S(2)}, u32[]{:S(2)}) collective-permute-start(bf16[256,1024]{1,0:T(8,128)(2,1)S(1)} %gate.5.refs_0_.block), channel_id=1, source_target_pairs={{0,8},{24,16},{1,9},{25,17},{2,10},{26,18},{3,11},{27,19},{4,12},{... | collective-permute-start | bytes 1572872 | tf_op jit(solution)/shard_map/ppermute | solution.py:52
  18.7 8.9 %collective-permute-start.7 = (bf16[256,1024]{1,0:T(8,128)(2,1)S(1)}, bf16[256,1024]{1,0:T(8,128)(2,1)S(1)}, u32[]{:S(2)}, u32[]{:S(2)}) collective-permute-start(bf16[256,1024]{1,0:T(8,128)(2,1)S(1)} %get-tuple-element.51.x.refs_0_), channel_id=1, source_target_pairs={{8,16},{16,8},{9,17},{17,9},{10,18},{18,10},{11,19},{19,11},{12,20... | collective-permute-start | bytes 1572872 | tf_op jit(solution)/shard_map/ppermute | solution.py:52
  19.5 17.2 %collective-permute-start.1 = (bf16[256,1024]{1,0:T(8,128)(2,1)S(1)}, bf16[256,1024]{1,0:T(8,128)(2,1)S(1)}, u32[]{:S(2)}, u32[]{:S(2)}) collective-permute-start(bf16[256,1024]{1,0:T(8,128)(2,1)S(1)} %get-tuple-element.45.block), channel_id=1, source_target_pairs={{0,8},{24,16},{1,9},{25,17},{2,10},{26,18},{3,11},{27,19},{4,12},{... | collective-permute-start | bytes 1572872 | tf_op jit(solution)/shard_map/ppermute | solution.py:52
  22.1 19.2 %collective-permute-start.9 = (bf16[256,1024]{1,0:T(8,128)(2,1)S(1)}, bf16[256,1024]{1,0:T(8,128)(2,1)S(1)}, u32[]{:S(2)}, u32[]{:S(2)}) collective-permute-start(bf16[256,1024]{1,0:T(8,128)(2,1)S(1)} %get-tuple-element.51.x.refs_0_), channel_id=1, source_target_pairs={{8,0},{16,24},{9,1},{17,25},{10,2},{18,26},{11,3},{19,27},{12,4},{... | collective-permute-start | bytes 1572872 | tf_op jit(solution)/shard_map/ppermute | solution.py:52
  27.7 14.3 %collective-permute-start.8 = (bf16[256,1024]{1,0:T(8,128)(2,1)S(1)}, bf16[256,1024]{1,0:T(8,128)(2,1)S(1)}, u32[]{:S(2)}, u32[]{:S(2)}) collective-permute-start(bf16[256,1024]{1,0:T(8,128)(2,1)S(1)} %add_block.4), channel_id=1, source_target_pairs={{8,16},{16,8},{9,17},{17,9},{10,18},{18,10},{11,19},{19,11},{12,20... | collective-permute-start | bytes 1572872 | tf_op jit(solution)/shard_map/ppermute | solution.py:52
  28.4 18.8 %collective-permute-start.10 = (bf16[256,1024]{1,0:T(8,128)(2,1)S(1)}, bf16[256,1024]{1,0:T(8,128)(2,1)S(1)}, u32[]{:S(2)}, u32[]{:S(2)}) collective-permute-start(bf16[256,1024]{1,0:T(8,128)(2,1)S(1)} %collective-permute-done.7.refs_0_.middle), channel_id=1, source_target_pairs={{8,0},{16,24},{9,1},{17,25},{10,2},{18,26},{11,3},{19,27},{12,4},{... | collective-permute-start | bytes 1572872 | tf_op jit(solution)/shard_map/ppermute | solution.py:52
  29.8 18.8 %collective-permute-start.12 = (f32[2,32,2048]{2,1,0:T(8,128)S(1)}, f32[2,32,2048]{2,1,0:T(8,128)S(1)}, u32[]{:S(2)}, u32[]{:S(2)}) collective-permute-start(f32[2,32,2048]{2,1,0:T(8,128)S(1)} %up_state.1), channel_id=1, source_target_pairs={{0,1},{1,0},{2,3},{3,2},{4,5},{5,4},{6,7},{7,6},{8,9},{9,8},{10,11... | collective-permute-start | bytes 1572872 | tf_op jit(solution)/shard_map/ppermute | solution.py:412
  36.7 13.8 %collective-permute-start = (bf16[256,1024]{1,0:T(8,128)(2,1)S(1)}, bf16[256,1024]{1,0:T(8,128)(2,1)S(1)}, u32[]{:S(2)}, u32[]{:S(2)}) collective-permute-start(bf16[256,1024]{1,0:T(8,128)(2,1)S(1)} %get-tuple-element.44.block), channel_id=1, source_target_pairs={{0,8},{24,16},{1,9},{25,17},{2,10},{26,18},{3,11},{27,19},{4,12},{... | collective-permute-start | bytes 1572872 | tf_op jit(solution)/shard_map/ppermute | solution.py:52
  41.3 9.2 %collective-permute-start.2 = (bf16[256,1024]{1,0:T(8,128)(2,1)S(1)}, bf16[256,1024]{1,0:T(8,128)(2,1)S(1)}, u32[]{:S(2)}, u32[]{:S(2)}) collective-permute-start(bf16[256,1024]{1,0:T(8,128)(2,1)S(1)} %add_block.3), channel_id=1, source_target_pairs={{8,16},{16,8},{9,17},{17,9},{10,18},{18,10},{11,19},{19,11},{12,20... | collective-permute-start | bytes 1572872 | tf_op jit(solution)/shard_map/ppermute | solution.py:52
  47.3 14.3 %collective-permute-start.11 = (bf16[256,1024]{1,0:T(8,128)(2,1)S(1)}, bf16[256,1024]{1,0:T(8,128)(2,1)S(1)}, u32[]{:S(2)}, u32[]{:S(2)}) collective-permute-start(bf16[256,1024]{1,0:T(8,128)(2,1)S(1)} %add_block.5), channel_id=1, source_target_pairs={{8,0},{16,24},{9,1},{17,25},{10,2},{18,26},{11,3},{19,27},{12,4},{... | collective-permute-start | bytes 1572872 | tf_op jit(solution)/shard_map/ppermute | solution.py:52
  63.9 11.5 %collective-permute-start.14 = (bf16[256,1024]{1,0:T(8,128)(2,1)S(1)}, bf16[256,1024]{1,0:T(8,128)(2,1)S(1)}, u32[]{:S(2)}, u32[]{:S(2)}) collective-permute-start(bf16[256,1024]{1,0:T(8,128)(2,1)S(1)} %get-tuple-element.52.refs_0_), channel_id=1, source_target_pairs={{0,4},{2,6},{4,0},{6,2},{1,5},{3,7},{5,1},{7,3},{8,12},{10,14},{12... | collective-permute-start | bytes 1572872 | tf_op jit(solution)/shard_map/ppermute | solution.py:56
  65.5 13.4 %collective-permute-start.13 = (bf16[256,1024]{1,0:T(8,128)(2,1)S(1)}, bf16[256,1024]{1,0:T(8,128)(2,1)S(1)}, u32[]{:S(2)}, u32[]{:S(2)}) collective-permute-start(bf16[256,1024]{1,0:T(8,128)(2,1)S(1)} %get-tuple-element.52.refs_0_), channel_id=1, source_target_pairs={{0,8},{8,0},{16,24},{24,16},{1,9},{9,1},{17,25},{25,17},{2,10},{10... | collective-permute-start | bytes 1572872 | tf_op jit(solution)/shard_map/ppermute | solution.py:56
  66.6 19.6 %collective-permute-start.18 = (bf16[256,1024]{1,0:T(8,128)(2,1)S(1)}, bf16[256,1024]{1,0:T(8,128)(2,1)S(1)}, u32[]{:S(2)}, u32[]{:S(2)}) collective-permute-start(bf16[256,1024]{1,0:T(8,128)(2,1)S(1)} %gate.8), channel_id=1, source_target_pairs={{0,8},{24,16},{1,9},{25,17},{2,10},{26,18},{3,11},{27,19},{4,12},{... | collective-permute-start | bytes 1572872 | tf_op jit(solution)/shard_map/ppermute | solution.py:52
  69.5 18.4 %collective-permute-start.20 = (bf16[256,1024]{1,0:T(8,128)(2,1)S(1)}, bf16[256,1024]{1,0:T(8,128)(2,1)S(1)}, u32[]{:S(2)}, u32[]{:S(2)}) collective-permute-start(bf16[256,1024]{1,0:T(8,128)(2,1)S(1)} %collective-permute-done.15.refs_1_.middle), channel_id=1, source_target_pairs={{8,0},{16,24},{9,1},{17,25},{10,2},{18,26},{11,3},{19,27},{12,4},{... | collective-permute-start | bytes 1572872 | tf_op jit(solution)/shard_map/ppermute | solution.py:52
  79.0 9.2 %collective-permute-start.21 = (bf16[256,1024]{1,0:T(8,128)(2,1)S(1)}, bf16[256,1024]{1,0:T(8,128)(2,1)S(1)}, u32[]{:S(2)}, u32[]{:S(2)}) collective-permute-start(bf16[256,1024]{1,0:T(8,128)(2,1)S(1)} %gate.7.refs_0_.refs_2_), channel_id=1, source_target_pairs={{0,4},{2,6},{4,0},{6,2},{1,5},{3,7},{5,1},{7,3},{8,12},{10,14},{12... | collective-permute-start | bytes 1572872 | tf_op jit(solution)/shard_map/ppermute | solution.py:56
  79.6 9.3 %collective-permute-start.16 = (bf16[256,1024]{1,0:T(8,128)(2,1)S(1)}, bf16[256,1024]{1,0:T(8,128)(2,1)S(1)}, u32[]{:S(2)}, u32[]{:S(2)}) collective-permute-start(bf16[256,1024]{1,0:T(8,128)(2,1)S(1)} %gate.7.refs_0_.refs_2_), channel_id=1, source_target_pairs={{8,16},{16,8},{9,17},{17,9},{10,18},{18,10},{11,19},{19,11},{12,20... | collective-permute-start | bytes 1572872 | tf_op jit(solution)/shard_map/ppermute | solution.py:52
  86.2 10.4 %collective-permute-start.19 = (bf16[256,1024]{1,0:T(8,128)(2,1)S(1)}, bf16[256,1024]{1,0:T(8,128)(2,1)S(1)}, u32[]{:S(2)}, u32[]{:S(2)}) collective-permute-start(bf16[256,1024]{1,0:T(8,128)(2,1)S(1)} %collective-permute-done.18.refs_1_.middle), channel_id=1, source_target_pairs={{8,16},{16,8},{9,17},{17,9},{10,18},{18,10},{11,19},{19,11},{12,20... | collective-permute-start | bytes 1572872 | tf_op jit(solution)/shard_map/ppermute | solution.py:52
  88.3 11.4 %collective-permute-start.22 = (bf16[256,1024]{1,0:T(8,128)(2,1)S(1)}, bf16[256,1024]{1,0:T(8,128)(2,1)S(1)}, u32[]{:S(2)}, u32[]{:S(2)}) collective-permute-start(bf16[256,1024]{1,0:T(8,128)(2,1)S(1)} %pick.5.refs_0_), channel_id=1, source_target_pairs={{0,4},{2,6},{4,0},{6,2},{1,5},{3,7},{5,1},{7,3},{8,12},{10,14},{12... | collective-permute-start | bytes 1572872 | tf_op jit(solution)/shard_map/ppermute | solution.py:56
  88.9 16.4 %collective-permute-start.17 = (bf16[256,1024]{1,0:T(8,128)(2,1)S(1)}, bf16[256,1024]{1,0:T(8,128)(2,1)S(1)}, u32[]{:S(2)}, u32[]{:S(2)}) collective-permute-start(bf16[256,1024]{1,0:T(8,128)(2,1)S(1)} %collective-permute-done.16.middle), channel_id=1, source_target_pairs={{8,0},{16,24},{9,1},{17,25},{10,2},{18,26},{11,3},{19,27},{12,4},{... | collective-permute-start | bytes 1572872 | tf_op jit(solution)/shard_map/ppermute | solution.py:52
  105.7 7.8 %collective-permute-start.25 = (bf16[3,256,1024]{2,1,0:T(8,128)(2,1)S(1)}, bf16[3,256,1024]{2,1,0:T(8,128)(2,1)S(1)}, u32[]{:S(2)}, u32[]{:S(2)}) collective-permute-start(bf16[3,256,1024]{2,1,0:T(8,128)(2,1)S(1)} %bundle.3.refs_0_), channel_id=1, source_target_pairs={{0,2},{2,0},{4,6},{6,4},{1,3},{3,1},{5,7},{7,5},{8,10},{10,8},{12,... | collective-permute-start | bytes 4718600 | tf_op jit(solution)/shard_map/ppermute | solution.py:56
  106.2 14.8 %collective-permute-start.24 = (bf16[256,1024]{1,0:T(8,128)(2,1)S(1)}, bf16[256,1024]{1,0:T(8,128)(2,1)S(1)}, u32[]{:S(2)}, u32[]{:S(2)}) collective-permute-start(bf16[256,1024]{1,0:T(8,128)(2,1)S(1)} %pick.6.refs_2_.refs_4_), channel_id=1, source_target_pairs={{0,4},{2,6},{4,0},{6,2},{1,5},{3,7},{5,1},{7,3},{8,12},{10,14},{12... | collective-permute-start | bytes 1572872 | tf_op jit(solution)/shard_map/ppermute | solution.py:56
  110.0 15.5 %collective-permute-start.28 = (bf16[256,1024]{1,0:T(8,128)(2,1)S(1)}, bf16[256,1024]{1,0:T(8,128)(2,1)S(1)}, u32[]{:S(2)}, u32[]{:S(2)}) collective-permute-start(bf16[256,1024]{1,0:T(8,128)(2,1)S(1)} %collective-permute-done.19.refs_0_.middle), channel_id=1, source_target_pairs={{8,0},{16,24},{9,1},{17,25},{10,2},{18,26},{11,3},{19,27},{12,4},{... | collective-permute-start | bytes 1572872 | tf_op jit(solution)/shard_map/ppermute | solution.py:52
  (15 other events, 191.5 us)

commit v5 on v4

--- a/solution.py
+++ b/solution.py
@@ -63,8 +63,25 @@
         bit //= 2
 
 
-def project_kernel(trained, basis, norm, own, *refs):
-    *outs, projected = refs
+def prepare_kernel(n_slots, trained, basis, norm, down, up, *refs):
+    blocks, (own, *outs, projected, sems) = refs[:n_slots], refs[n_slots:]
+    shard = lax.axis_index("shard")
+    height, width = down.shape[2:]
+    tall, cols = up.shape[2:]
+    copies = []
+
+    def bring(source, dest):
+        copies.append(pltpu.make_async_copy(source, dest, sems.at[len(copies)]))
+        copies[-1].start()
+
+    for owner, block in reversed(list(zip(owners(), blocks))):
+        bring(down.at[owner, shard], block.at[pl.ds(0, height)])
+        for chunk in range(cols // width):
+            bring(
+                up.at[owner, shard, :, pl.ds(chunk * width, width)],
+                block.at[pl.ds(height + chunk * tall, tall)],
+            )
+
     rank, rows = basis.shape[0], own.shape[1]
     high = basis[...].astype(BF16)
     rest = basis[...] - high.astype(F32)
@@ -90,6 +107,8 @@
         block = projected[:, pl.ds(pl.multiple_of(owner * rows, rows), rows)]
         out[:rank, :] = block.astype(BF16)
         out[rank:, :] = parts
+    for copy in copies:
+        copy.wait()
 
 
 def embed_kernel(groups, n_came, *refs):
@@ -130,28 +149,6 @@
     norm_cast[...] = norm_stored[...].astype(BF16)
 
 
-def pack_kernel(down, up, *refs):
-    *outs, sems = refs
-    shard = lax.axis_index("shard")
-    rows, width = down.shape[2:]
-    tall, cols = up.shape[2:]
-    copies = []
-
-    def bring(source, dest):
-        copies.append(pltpu.make_async_copy(source, dest, sems.at[len(copies)]))
-        copies[-1].start()
-
-    for owner, out in reversed(list(zip(owners(), outs))):
-        bring(down.at[owner, shard], out.at[pl.ds(0, rows)])
-        for chunk in range(cols // width):
-            bring(
-                up.at[owner, shard, :, pl.ds(chunk * width, width)],
-                out.at[pl.ds(rows + chunk * tall, tall)],
-            )
-    for copy in copies:
-        copy.wait()
-
-
 def add_kernel(block, came, *refs):
     refs[-1][...] = (block[...].astype(F32) + came[...].astype(F32)).astype(BF16)
 
@@ -236,7 +233,7 @@
 
 
 def up_kernel(groups, tensors, master_up, moment_up, *refs):
-    sums, (stored_up, velocity_up, token) = refs[:tensors], refs[tensors:]
+    sums, (stored_up, velocity_up, token) = refs[:tensors], refs[-3:]
     cols = sums[0].shape[1]
     me = lax.axis_index("tensor")
     for shift in range(tensors):
@@ -321,7 +318,8 @@
 
 
 def place_embed_kernel(slots, *refs):
-    pieces, (out, sems) = refs[: len(slots)], refs[-2:]
+    pieces, (out, token, sems) = refs[: len(slots)], refs[-3:]
+    token[...] = jnp.zeros_like(token)
     copies = [
         pltpu.make_async_copy(piece, out.at[owners()[slot]], sems.at[i])
         for i, (piece, slot) in enumerate(zip(pieces, slots))
@@ -369,33 +367,29 @@
     rank_rows = jax.ShapeDtypeStruct((rank, rows_embed), F32)
     packet = jax.ShapeDtypeStruct((rank + 16, rows_embed), BF16)
     token_shape = jax.ShapeDtypeStruct((8, 128), F32)
-    own_rows, *packets = call(
-        project_kernel,
-        "project_rows",
-        [rank_rows] + [packet] * (replicas - 1),
-        [VMEM] * 3,
-        [VMEM] * replicas,
-        [pltpu.VMEM((rank, replicas * rows_embed), F32)],
-        pltpu.with_memory_space_constraint(trained_embed[0], pltpu.HBM),
-        pltpu.with_memory_space_constraint(basis_t, pltpu.HBM),
-        pltpu.with_memory_space_constraint(trained_norm[0], pltpu.HBM),
-    )
     down = trained_down[0].reshape(replicas, shards, rows_down, width)
     up = trained_up[0].reshape(replicas, shards, tall, half_cols)
-    own, near, middle, end = call(
-        pack_kernel,
-        "pack_blocks",
-        [packed] * replicas,
-        [HBM] * 2,
-        [VMEM] * replicas,
-        [dma((replicas * (1 + chunks),))],
-        pltpu.with_memory_space_constraint(down, pltpu.HBM),
-        pltpu.with_memory_space_constraint(up, pltpu.HBM),
-    )
+    own, near, middle, end, own_rows, *packets = call(
+        functools.partial(prepare_kernel, replicas),
+        "prepare",
+        [packed] * replicas + [rank_rows] + [packet] * (replicas - 1),
+        [VMEM] * 3 + [HBM] * 2,
+        [VMEM] * (2 * replicas),
+        [
+            pltpu.VMEM((rank, replicas * rows_embed), F32),
+            dma((replicas * (1 + chunks),)),
+        ],
+        *[
+            pltpu.with_memory_space_constraint(x, pltpu.HBM)
+            for x in (trained_embed[0], basis_t, trained_norm[0], down, up)
+        ],
+    )
+
     packets_came = [swap(packets[0], "replica", 1), swap(packets[1], "replica", 2)]
     end = gate(end, packets_came[0])
     packets_came.append(swap(gate(packets[2], end), "replica", 3))
-    from_end = [along(x, INWARD) for x in (end, middle, near)]
+    from_end = along(end, INWARD)
+    from_middle = along(middle, INWARD)
 
     state = jax.ShapeDtypeStruct((2, rows_up, half_cols), F32)
     states = call(
@@ -445,11 +439,13 @@
 
     embed_out = along(recast_rows, OUTWARD)
     embed_middle = along(recast_rows, ACROSS)
-    end_partial = along(add(end, from_end[0], embed_middle), ACROSS)
-    middle_partial = along(add(middle, from_end[1]), ACROSS)
+    end_partial = along(add(end, from_end, embed_middle, embed_out), ACROSS)
+    middle_sum = add(middle, from_middle)
+    middle_partial = along(middle_sum, ACROSS)
     embed_middle_out = along(embed_middle, OUTWARD)
-    to_end = along(add(near, end_partial, embed_out, embed_middle_out), OUTWARD)
-    came0 = [own, from_end[2], middle_partial, to_end]
+    to_end = along(add(near, end_partial, embed_middle_out), OUTWARD)
+    from_near = along(gate(near, middle_sum), INWARD)
+    came0 = [own, middle_partial, from_near, to_end]
     half_sum = jax.ShapeDtypeStruct((rows_up, half_cols), F32)
     down_state = jax.ShapeDtypeStruct((rows_down, width), F32)
     piece, stored_down, velocity_down, *sums = call(
@@ -468,23 +464,26 @@
     )
 
     top = shards // 2
+    came_near = swap(piece, "replica", 1)
+    middle_piece = along(piece, ACROSS)
     far_piece = swap(piece, "shard", top)
-    middle_piece = along(piece, ACROSS)
-    near_piece = gate(swap(piece, "replica", 1), far_piece, middle_piece)
+    embed_in = along(gate(recast_rows, piece), INWARD)
+    end_piece = along(came_near, ACROSS)
+    second_out = along(gate(middle_piece, came_near), OUTWARD)
+    near_piece = gate(came_near, far_piece)
     far_near = swap(near_piece, "shard", top)
-    end_piece = along(near_piece, ACROSS)
-    embed_in = along(gate(recast_rows, piece), INWARD)
     sums = [sums[0]] + [
         lax.ppermute(
             gate(x, near_piece), "tensor", [(i, (i + shift) % tensors) for i in range(tensors)]
         )
         for shift, x in enumerate(sums[1:], 1)
     ]
-    second = pick(middle_piece, along(middle_piece, OUTWARD), far_near, embed_in)
+    second = pick(middle_piece, second_out, far_near, embed_in)
     far_second = swap(second, "shard", top)
     embed_end = along(embed_in, ACROSS)
     third = pick(end_piece, along(end_piece, OUTWARD), embed_end, far_second, *sums[1:])
     far_third = swap(third, "shard", top)
+    embed_last = along(embed_end, OUTWARD)
     bundles = [
         (
             [(0, 0), (0, top), (1, 0), (1, top)],
@@ -496,27 +495,26 @@
         ),
     ]
 
-    embed_last = along(embed_end, OUTWARD)
-
     stored_up, velocity_up, token = call(
         functools.partial(up_kernel, replicas, tensors),
         "update_up",
         [jax.ShapeDtypeStruct(master_up.shape, F32)] * 2 + [token_shape],
-        [VMEM] * (2 + tensors),
+        [VMEM] * (2 + tensors) + [ANY],
         [VMEM] * 3,
         [],
         master_up,
         moment_up,
         *sums,
+        list(bundles[0][1].values())[-1],
     )
 
     embed_shape = jax.ShapeDtypeStruct((replicas, rows_embed, width), BF16)
-    recast_embed = call(
+    recast_embed, token = call(
         functools.partial(place_embed_kernel, [0, 1, 2]),
         "place_embed",
-        embed_shape,
+        [embed_shape, token_shape],
         [VMEM] * 4,
-        HBM,
+        [HBM, VMEM],
         [dma((3,))],
         recast_rows,
         pick(embed_in, embed_out),
@@ -546,19 +544,19 @@
     for slots, arrays in bundles:
         *placed, token = place(slots, arrays, placed, token)
     last = spread_low(bundle([far_third], token))
-    recast_down, recast_up, token = place([(3, top)], last, placed)
-    recast_embed = call(
+    recast_embed, token = call(
         functools.partial(place_embed_kernel, [3]),
         "place_embed",
-        embed_shape,
+        [embed_shape, token_shape],
         [VMEM] * 2 + [HBM],
-        HBM,
+        [HBM, VMEM],
         [dma((1,))],
         pick(embed_end, embed_last),
-        token,
+        last[0],
         recast_embed,
         aliases={2: 0},
     )
+    recast_down, recast_up, _ = place([(3, top)], last, placed, token)
 
     return (
         recast_up.reshape(-1, half_cols),

time: 128 us -> 129 us (level)
  starting transfers between devices: 41.1 us -> 54.3 us
  waiting for transfers between devices: 66.8 us -> 55.1 us
    ppermute x16, starting transfers between devices: 23.2 us -> 32.5 us  [along(): return lax.ppermute(x, 'replica', pairs)]
    ppermute x16, waiting for transfers between devices: 43.3 us -> 35.6 us  [along(): return lax.ppermute(x, 'replica', pairs)]
    ppermute x11, waiting for transfers between devices: 18.6 us -> 14.6 us  [swap(): lax.ppermute(x, axis, [(i, i ^ bit) for i in range(lax.axis_size(axis))])]
    ppermute x11, starting transfers between devices: 14.8 us -> 18.8 us  [swap(): lax.ppermute(x, axis, [(i, i ^ bit) for i in range(lax.axis_size(axis))])]
    pallas_call x27 -> x28, Pallas kernels: 17.2 us -> 16.9 us  [call(): pl.pallas_call(kernel, name=name, out_shape=out_shape, in_specs=in_specs,...]
  transfers between devices with their start and end apart: 29 -> 29, of which waited for: 16 -> 13; matrix products, arithmetic and copies ran while one was open for 1% -> 1% of each run, Pallas kernels for 9% -> 8%
where the time goes in v5:
time: 129 us
  waiting for transfers between devices  55.1 us (43%)
  starting transfers between devices  54.3 us (42%)
  Pallas kernels  16.9 us (13%)
    ppermute x16, waiting for transfers between devices, along(): return lax.ppermute(x, 'replica', pairs)  35.6 us
    ppermute x16, starting transfers between devices, along(): return lax.ppermute(x, 'replica', pairs)  32.5 us
    ppermute x11, starting transfers between devices, swap(): lax.ppermute(x, axis, [(i, i ^ bit) for i in range(lax.axis_size(axis))])  18.8 us
    pallas_call x28, Pallas kernels, call(): pl.pallas_call(kernel, name=name, out_shape=out_shape, in_specs=in_specs,...  16.9 us
    ppermute x11, waiting for transfers between devices, swap(): lax.ppermute(x, axis, [(i, i ^ bit) for i in range(lax.axis_size(axis))])  14.6 us
    ppermute x1, waiting for transfers between devices, body(): lax.ppermute(gate(x, near_piece), 'tensor', [(i, (i + shift) % tensors) f...  4.92 us
  transfers between devices with their start and end apart: 29, of which 13 were waited for; matrix products, arithmetic and copies ran while one was open for 1% of the time, Pallas kernels for 8%

profile of v5, /device:TPU:0, one launch (start us, length us, event | category | flops | bytes accessed | tf_op | source)
XLA Modules:
  0.0 128.6 jit_solution(4089338032491182855)
XLA Ops:
  0.7 3.4 %prepare.1 = (bf16[256,1024]{1,0:T(8,128)(2,1)S(1)}, bf16[256,1024]{1,0:T(8,128)(2,1)S(1)}, bf16[256,1024]{1,0:T(8,128)(2,1)S(1)}, bf16[256,1024]{1,0:T(8,128)(2...) custom-call(bf16[1024,1024]{1,0:T(8,128)(2,1)} %bitcast.35, ...), custom_call_target="tpu_custom_call" | custom-call | bytes 6856704 | tf_op jit(solution)/shard_map/prepare/pallas_call | solution.py:26
  4.2 3.1 %collective-permute-start.3 = (bf16[80,256]{1,0:T(8,128)(2,1)S(1)}, bf16[80,256]{1,0:T(8,128)(2,1)S(1)}, u32[]{:S(2)}, u32[]{:S(2)}) collective-permute-start(bf16[80,256]{1,0:T(8,128)(2,1)S(1)} %get-tuple-element.50), channel_id=1, source_target_pairs={{0,8},{8,0},{16,24},{24,16},{1,9},{9,1},{17,25},{25,17},{2,10},{10... | collective-permute-start | bytes 122888 | tf_op jit(solution)/shard_map/ppermute | solution.py:56
  7.3 2.6 %collective-permute-start.5 = (bf16[80,256]{1,0:T(8,128)(2,1)S(1)}, bf16[80,256]{1,0:T(8,128)(2,1)S(1)}, u32[]{:S(2)}, u32[]{:S(2)}) collective-permute-start(bf16[80,256]{1,0:T(8,128)(2,1)S(1)} %get-tuple-element.52), channel_id=1, source_target_pairs={{0,16},{8,24},{16,0},{24,8},{1,17},{9,25},{17,1},{25,9},{2,18},{10... | collective-permute-start | bytes 122888 | tf_op jit(solution)/shard_map/ppermute | solution.py:56
  9.9 3.9 %collective-permute-start.6 = (bf16[80,256]{1,0:T(8,128)(2,1)S(1)}, bf16[80,256]{1,0:T(8,128)(2,1)S(1)}, u32[]{:S(2)}, u32[]{:S(2)}) collective-permute-start(bf16[80,256]{1,0:T(8,128)(2,1)S(1)} %gate.9), channel_id=1, source_target_pairs={{0,24},{8,16},{16,8},{24,0},{1,25},{9,17},{17,9},{25,1},{2,26},{10... | collective-permute-start | bytes 122888 | tf_op jit(solution)/shard_map/ppermute | solution.py:56
  16.3 2.0 %embed_update.1 = (f32[256,1024]{1,0:T(8,128)}, bf16[256,1024]{1,0:T(8,128)(2,1)S(1)}, f32[64,256]{1,0:T(8,128)}, bf16[2,1024]{1,0:T(2,128)(2,1)}, f32[2,1024]{1,0:T(2,128)}, /*index=5*/f32[2,1024]{1,0:T(2,128)}) custom-call(f32[64,256]{1,0:T(8,128)S(1)} %get-tuple-element.51.refs_0_, f32[64,256]{1,0:T(8,128)S(1)} %fusion.refs_1_, f32[256,1024]{1,0:T(8,128)S(1)} %bitcast.23, ...), custom_call_target="tpu_custom_call" | custom-call | bytes 4976640 | tf_op jit(solution)/shard_map/embed_update/pallas_call | solution.py:26
  20.3 8.8 %collective-permute-start = (bf16[256,1024]{1,0:T(8,128)(2,1)S(1)}, bf16[256,1024]{1,0:T(8,128)(2,1)S(1)}, u32[]{:S(2)}, u32[]{:S(2)}) collective-permute-start(bf16[256,1024]{1,0:T(8,128)(2,1)S(1)} %get-tuple-element.47.block), channel_id=1, source_target_pairs={{0,8},{24,16},{1,9},{25,17},{2,10},{26,18},{3,11},{27,19},{4,12},{... | collective-permute-start | bytes 1572872 | tf_op jit(solution)/shard_map/ppermute | solution.py:52
  29.1 2.9 %collective-permute-done.8.refs_1_.end = bf16[256,1024]{1,0:T(8,128)(2,1)S(1)} collective-permute-done((bf16[256,1024]{1,0:T(8,128)(2,1)S(1)}, bf16[256,1024]{1,0:T(8,128)(2,1)S(1)}, u32[]{:S(2)}, u32[]{:S(2)}) %collective-permute-start.8) | collective-permute-done | bytes 524320 | tf_op jit(solution)/shard_map/ppermute | solution.py:52
  35.8 1.7 %collective-permute-done.came = bf16[256,1024]{1,0:T(8,128)(2,1)S(1)} collective-permute-done((bf16[256,1024]{1,0:T(8,128)(2,1)S(1)}, bf16[256,1024]{1,0:T(8,128)(2,1)S(1)}, u32[]{:S(2)}, u32[]{:S(2)}) %collective-permute-start) | collective-permute-done | bytes 524320 | tf_op jit(solution)/shard_map/ppermute | solution.py:52
  38.4 8.4 %collective-permute-start.2 = (bf16[256,1024]{1,0:T(8,128)(2,1)S(1)}, bf16[256,1024]{1,0:T(8,128)(2,1)S(1)}, u32[]{:S(2)}, u32[]{:S(2)}) collective-permute-start(bf16[256,1024]{1,0:T(8,128)(2,1)S(1)} %gate.7), channel_id=1, source_target_pairs={{0,8},{24,16},{1,9},{25,17},{2,10},{26,18},{3,11},{27,19},{4,12},{... | collective-permute-start | bytes 1572872 | tf_op jit(solution)/shard_map/ppermute | solution.py:52
  46.8 1.9 %collective-permute-done.10.refs_0_.end = bf16[256,1024]{1,0:T(8,128)(2,1)S(1)} collective-permute-done((bf16[256,1024]{1,0:T(8,128)(2,1)S(1)}, bf16[256,1024]{1,0:T(8,128)(2,1)S(1)}, u32[]{:S(2)}, u32[]{:S(2)}) %collective-permute-start.10) | collective-permute-done | bytes 524320 | tf_op jit(solution)/shard_map/ppermute | solution.py:52
  50.1 3.3 %collective-permute-done.2.refs_6_ = bf16[256,1024]{1,0:T(8,128)(2,1)S(1)} collective-permute-done((bf16[256,1024]{1,0:T(8,128)(2,1)S(1)}, bf16[256,1024]{1,0:T(8,128)(2,1)S(1)}, u32[]{:S(2)}, u32[]{:S(2)}) %collective-permute-start.2) | collective-permute-done | bytes 524320 | tf_op jit(solution)/shard_map/ppermute | solution.py:52
  53.4 10.1 %collective-permute-done.11.refs_7_ = bf16[256,1024]{1,0:T(8,128)(2,1)S(1)} collective-permute-done((bf16[256,1024]{1,0:T(8,128)(2,1)S(1)}, bf16[256,1024]{1,0:T(8,128)(2,1)S(1)}, u32[]{:S(2)}, u32[]{:S(2)}) %collective-permute-start.11) | collective-permute-done | bytes 524320 | tf_op jit(solution)/shard_map/ppermute | solution.py:52
  65.9 2.7 %collective-permute-start.13 = (bf16[256,1024]{1,0:T(8,128)(2,1)S(1)}, bf16[256,1024]{1,0:T(8,128)(2,1)S(1)}, u32[]{:S(2)}, u32[]{:S(2)}) collective-permute-start(bf16[256,1024]{1,0:T(8,128)(2,1)S(1)} %get-tuple-element.55.refs_0_), channel_id=1, source_target_pairs={{0,8},{8,0},{16,24},{24,16},{1,9},{9,1},{17,25},{25,17},{2,10},{10... | collective-permute-start | bytes 1572872 | tf_op jit(solution)/shard_map/ppermute | solution.py:56
  70.1 2.0 %collective-permute-start.16 = (bf16[256,1024]{1,0:T(8,128)(2,1)S(1)}, bf16[256,1024]{1,0:T(8,128)(2,1)S(1)}, u32[]{:S(2)}, u32[]{:S(2)}) collective-permute-start(bf16[256,1024]{1,0:T(8,128)(2,1)S(1)} %gate.10), channel_id=1, source_target_pairs={{0,8},{24,16},{1,9},{25,17},{2,10},{26,18},{3,11},{27,19},{4,12},{... | collective-permute-start | bytes 1572872 | tf_op jit(solution)/shard_map/ppermute | solution.py:52
  72.1 8.1 %collective-permute-done.13.refs_0_.x = bf16[256,1024]{1,0:T(8,128)(2,1)S(1)} collective-permute-done((bf16[256,1024]{1,0:T(8,128)(2,1)S(1)}, bf16[256,1024]{1,0:T(8,128)(2,1)S(1)}, u32[]{:S(2)}, u32[]{:S(2)}) %collective-permute-start.13) | collective-permute-done | bytes 524320 | tf_op jit(solution)/shard_map/ppermute | solution.py:56
  84.9 10.5 %collective-permute-done.19.end = bf16[256,1024]{1,0:T(8,128)(2,1)S(1)} collective-permute-done((bf16[256,1024]{1,0:T(8,128)(2,1)S(1)}, bf16[256,1024]{1,0:T(8,128)(2,1)S(1)}, u32[]{:S(2)}, u32[]{:S(2)}) %collective-permute-start.19) | collective-permute-done | bytes 524320 | tf_op jit(solution)/shard_map/ppermute | solution.py:52
  95.5 2.7 %collective-permute-start.22 = (bf16[256,1024]{1,0:T(8,128)(2,1)S(1)}, bf16[256,1024]{1,0:T(8,128)(2,1)S(1)}, u32[]{:S(2)}, u32[]{:S(2)}) collective-permute-start(bf16[256,1024]{1,0:T(8,128)(2,1)S(1)} %pick.5.refs_0_), channel_id=1, source_target_pairs={{0,4},{2,6},{4,0},{6,2},{1,5},{3,7},{5,1},{7,3},{8,12},{10,14},{12... | collective-permute-start | bytes 1572872 | tf_op jit(solution)/shard_map/ppermute | solution.py:56
  101.0 4.9 %collective-permute-done.23.refs_2_.refs_1_ = f32[32,2048]{1,0:T(8,128)S(1)} collective-permute-done((f32[32,2048]{1,0:T(8,128)S(1)}, f32[32,2048]{1,0:T(8,128)S(1)}, u32[]{:S(2)}, u32[]{:S(2)}) %collective-permute-start.23) | collective-permute-done | bytes 262176 | tf_op jit(solution)/shard_map/ppermute | solution.py:476
  106.0 3.3 %collective-permute-done.15.end = bf16[256,1024]{1,0:T(8,128)(2,1)S(1)} collective-permute-done((bf16[256,1024]{1,0:T(8,128)(2,1)S(1)}, bf16[256,1024]{1,0:T(8,128)(2,1)S(1)}, u32[]{:S(2)}, u32[]{:S(2)}) %collective-permute-start.15) | collective-permute-done | bytes 524320 | tf_op jit(solution)/shard_map/ppermute | solution.py:52
  111.6 2.0 %collective-permute-done.26.refs_2_.refs_1_ = bf16[4,256,1024]{2,1,0:T(8,128)(2,1)S(1)} collective-permute-done((bf16[4,256,1024]{2,1,0:T(8,128)(2,1)S(1)}, bf16[4,256,1024]{2,1,0:T(8,128)(2,1)S(1)}, u32[]{:S(2)}, u32[]{:S(2)}) %collective-permute-start.26) | collective-permute-done | bytes 2097184 | tf_op jit(solution)/shard_map/ppermute | solution.py:56
  116.0 2.2 %place_rows.3 = (bf16[4,4,128,1024]{3,2,1,0:T(8,128)(2,1)}, bf16[4,4,64,2048]{3,2,1,0:T(8,128)(2,1)}, f32[8,128]{1,0:T(8,128)S(1)}) custom-call(bf16[4,256,1024]{2,1,0:T(8,128)(2,1)S(1)} %bundle.4.refs_0_, bf16[4,256,1024]{2,1,0:T(8,128)(2,1)S(1)} %collective-permute-done.26.refs_2_.refs_1_, f32[8,128]{1,0:T(8,128)S(1)} %get-tuple-element.59.refs_2_), custom_call_target="tpu_custom_call" | custom-call | bytes 25178112 | tf_op jit(solution)/shard_map/place_rows/pallas_call | solution.py:26
  118.2 1.8 %place_rows.4 = (bf16[4,4,128,1024]{3,2,1,0:T(8,128)(2,1)}, bf16[4,4,64,2048]{3,2,1,0:T(8,128)(2,1)}, f32[8,128]{1,0:T(8,128)S(1)}) custom-call(bf16[3,256,1024]{2,1,0:T(8,128)(2,1)S(1)} %bundle.3.refs_0_, bf16[3,256,1024]{2,1,0:T(8,128)(2,1)S(1)} %collective-permute-done.25.refs_1_, ...), custom_call_target="tpu_custom_call", output_to_operand_aliasing={{0}: (3, {}), {1}: (4, {})} | custom-call | bytes 25178112 | tf_op jit(solution)/shard_map/place_rows/pallas_call | solution.py:26
  120.0 4.1 %collective-permute-done.24.refs_0_ = bf16[256,1024]{1,0:T(8,128)(2,1)S(1)} collective-permute-done((bf16[256,1024]{1,0:T(8,128)(2,1)S(1)}, bf16[256,1024]{1,0:T(8,128)(2,1)S(1)}, u32[]{:S(2)}, u32[]{:S(2)}) %collective-permute-start.24) | collective-permute-done | bytes 524320 | tf_op jit(solution)/shard_map/ppermute | solution.py:56
  124.2 1.9 %collective-permute-done.28.end = bf16[256,1024]{1,0:T(8,128)(2,1)S(1)} collective-permute-done((bf16[256,1024]{1,0:T(8,128)(2,1)S(1)}, bf16[256,1024]{1,0:T(8,128)(2,1)S(1)}, u32[]{:S(2)}, u32[]{:S(2)}) %collective-permute-start.28) | collective-permute-done | bytes 524320 | tf_op jit(solution)/shard_map/ppermute | solution.py:52
  (83 shorter events, 29.0 us)
Async XLA Ops:
  7.3 8.9 %collective-permute-start.5 = (bf16[80,256]{1,0:T(8,128)(2,1)S(1)}, bf16[80,256]{1,0:T(8,128)(2,1)S(1)}, u32[]{:S(2)}, u32[]{:S(2)}) collective-permute-start(bf16[80,256]{1,0:T(8,128)(2,1)S(1)} %get-tuple-element.52), channel_id=1, source_target_pairs={{0,16},{8,24},{16,0},{24,8},{1,17},{9,25},{17,1},{25,9},{2,18},{10... | collective-permute-start | bytes 122888 | tf_op jit(solution)/shard_map/ppermute | solution.py:56
  14.9 14.3 %collective-permute-start.4 = (bf16[256,1024]{1,0:T(8,128)(2,1)S(1)}, bf16[256,1024]{1,0:T(8,128)(2,1)S(1)}, u32[]{:S(2)}, u32[]{:S(2)}) collective-permute-start(bf16[256,1024]{1,0:T(8,128)(2,1)S(1)} %gate.8.refs_0_.block), channel_id=1, source_target_pairs={{0,8},{24,16},{1,9},{25,17},{2,10},{26,18},{3,11},{27,19},{4,12},{... | collective-permute-start | bytes 1572872 | tf_op jit(solution)/shard_map/ppermute | solution.py:52
  18.3 13.7 %collective-permute-start.8 = (bf16[256,1024]{1,0:T(8,128)(2,1)S(1)}, bf16[256,1024]{1,0:T(8,128)(2,1)S(1)}, u32[]{:S(2)}, u32[]{:S(2)}) collective-permute-start(bf16[256,1024]{1,0:T(8,128)(2,1)S(1)} %get-tuple-element.54.x.refs_0_), channel_id=1, source_target_pairs={{8,0},{16,24},{9,1},{17,25},{10,2},{18,26},{11,3},{19,27},{12,4},{... | collective-permute-start | bytes 1572872 | tf_op jit(solution)/shard_map/ppermute | solution.py:52
  19.6 12.5 %collective-permute-start.7 = (bf16[256,1024]{1,0:T(8,128)(2,1)S(1)}, bf16[256,1024]{1,0:T(8,128)(2,1)S(1)}, u32[]{:S(2)}, u32[]{:S(2)}) collective-permute-start(bf16[256,1024]{1,0:T(8,128)(2,1)S(1)} %get-tuple-element.54.x.refs_0_), channel_id=1, source_target_pairs={{8,16},{16,8},{9,17},{17,9},{10,18},{18,10},{11,19},{19,11},{12,20... | collective-permute-start | bytes 1572872 | tf_op jit(solution)/shard_map/ppermute | solution.py:52
  20.3 17.2 %collective-permute-start = (bf16[256,1024]{1,0:T(8,128)(2,1)S(1)}, bf16[256,1024]{1,0:T(8,128)(2,1)S(1)}, u32[]{:S(2)}, u32[]{:S(2)}) collective-permute-start(bf16[256,1024]{1,0:T(8,128)(2,1)S(1)} %get-tuple-element.47.block), channel_id=1, source_target_pairs={{0,8},{24,16},{1,9},{25,17},{2,10},{26,18},{3,11},{27,19},{4,12},{... | collective-permute-start | bytes 1572872 | tf_op jit(solution)/shard_map/ppermute | solution.py:52
  32.2 14.6 %collective-permute-start.9 = (bf16[256,1024]{1,0:T(8,128)(2,1)S(1)}, bf16[256,1024]{1,0:T(8,128)(2,1)S(1)}, u32[]{:S(2)}, u32[]{:S(2)}) collective-permute-start(bf16[256,1024]{1,0:T(8,128)(2,1)S(1)} %add_block.4), channel_id=1, source_target_pairs={{8,16},{16,8},{9,17},{17,9},{10,18},{18,10},{11,19},{19,11},{12,20... | collective-permute-start | bytes 1572872 | tf_op jit(solution)/shard_map/ppermute | solution.py:52
  32.9 15.8 %collective-permute-start.10 = (bf16[256,1024]{1,0:T(8,128)(2,1)S(1)}, bf16[256,1024]{1,0:T(8,128)(2,1)S(1)}, u32[]{:S(2)}, u32[]{:S(2)}) collective-permute-start(bf16[256,1024]{1,0:T(8,128)(2,1)S(1)} %collective-permute-done.7.refs_0_.middle), channel_id=1, source_target_pairs={{8,0},{16,24},{9,1},{17,25},{10,2},{18,26},{11,3},{19,27},{12,4},{... | collective-permute-start | bytes 1572872 | tf_op jit(solution)/shard_map/ppermute | solution.py:52
  34.2 15.9 %collective-permute-start.12 = (f32[2,32,2048]{2,1,0:T(8,128)S(1)}, f32[2,32,2048]{2,1,0:T(8,128)S(1)}, u32[]{:S(2)}, u32[]{:S(2)}) collective-permute-start(f32[2,32,2048]{2,1,0:T(8,128)S(1)} %up_state.1), channel_id=1, source_target_pairs={{0,1},{1,0},{2,3},{3,2},{4,5},{5,4},{6,7},{7,6},{8,9},{9,8},{10,11... | collective-permute-start | bytes 1572872 | tf_op jit(solution)/shard_map/ppermute | solution.py:406
  37.6 15.8 %collective-permute-start.1 = (bf16[256,1024]{1,0:T(8,128)(2,1)S(1)}, bf16[256,1024]{1,0:T(8,128)(2,1)S(1)}, u32[]{:S(2)}, u32[]{:S(2)}) collective-permute-start(bf16[256,1024]{1,0:T(8,128)(2,1)S(1)} %add_block.3.refs_0_), channel_id=1, source_target_pairs={{8,16},{16,8},{9,17},{17,9},{10,18},{18,10},{11,19},{19,11},{12,20... | collective-permute-start | bytes 1572872 | tf_op jit(solution)/shard_map/ppermute | solution.py:52
  38.4 15.1 %collective-permute-start.2 = (bf16[256,1024]{1,0:T(8,128)(2,1)S(1)}, bf16[256,1024]{1,0:T(8,128)(2,1)S(1)}, u32[]{:S(2)}, u32[]{:S(2)}) collective-permute-start(bf16[256,1024]{1,0:T(8,128)(2,1)S(1)} %gate.7), channel_id=1, source_target_pairs={{0,8},{24,16},{1,9},{25,17},{2,10},{26,18},{3,11},{27,19},{4,12},{... | collective-permute-start | bytes 1572872 | tf_op jit(solution)/shard_map/ppermute | solution.py:52
  48.8 14.7 %collective-permute-start.11 = (bf16[256,1024]{1,0:T(8,128)(2,1)S(1)}, bf16[256,1024]{1,0:T(8,128)(2,1)S(1)}, u32[]{:S(2)}, u32[]{:S(2)}) collective-permute-start(bf16[256,1024]{1,0:T(8,128)(2,1)S(1)} %add_block.5), channel_id=1, source_target_pairs={{8,0},{16,24},{9,1},{17,25},{10,2},{18,26},{11,3},{19,27},{12,4},{... | collective-permute-start | bytes 1572872 | tf_op jit(solution)/shard_map/ppermute | solution.py:52
  65.2 6.9 %collective-permute-start.18 = (bf16[256,1024]{1,0:T(8,128)(2,1)S(1)}, bf16[256,1024]{1,0:T(8,128)(2,1)S(1)}, u32[]{:S(2)}, u32[]{:S(2)}) collective-permute-start(bf16[256,1024]{1,0:T(8,128)(2,1)S(1)} %get-tuple-element.55.refs_0_), channel_id=1, source_target_pairs={{8,16},{16,8},{9,17},{17,9},{10,18},{18,10},{11,19},{19,11},{12,20... | collective-permute-start | bytes 1572872 | tf_op jit(solution)/shard_map/ppermute | solution.py:52
  65.9 14.4 %collective-permute-start.13 = (bf16[256,1024]{1,0:T(8,128)(2,1)S(1)}, bf16[256,1024]{1,0:T(8,128)(2,1)S(1)}, u32[]{:S(2)}, u32[]{:S(2)}) collective-permute-start(bf16[256,1024]{1,0:T(8,128)(2,1)S(1)} %get-tuple-element.55.refs_0_), channel_id=1, source_target_pairs={{0,8},{8,0},{16,24},{24,16},{1,9},{9,1},{17,25},{25,17},{2,10},{10... | collective-permute-start | bytes 1572872 | tf_op jit(solution)/shard_map/ppermute | solution.py:56
  68.5 13.3 %collective-permute-start.20 = (bf16[256,1024]{1,0:T(8,128)(2,1)S(1)}, bf16[256,1024]{1,0:T(8,128)(2,1)S(1)}, u32[]{:S(2)}, u32[]{:S(2)}) collective-permute-start(bf16[256,1024]{1,0:T(8,128)(2,1)S(1)} %get-tuple-element.55.refs_0_), channel_id=1, source_target_pairs={{0,4},{2,6},{4,0},{6,2},{1,5},{3,7},{5,1},{7,3},{8,12},{10,14},{12... | collective-permute-start | bytes 1572872 | tf_op jit(solution)/shard_map/ppermute | solution.py:56
  70.1 14.1 %collective-permute-start.16 = (bf16[256,1024]{1,0:T(8,128)(2,1)S(1)}, bf16[256,1024]{1,0:T(8,128)(2,1)S(1)}, u32[]{:S(2)}, u32[]{:S(2)}) collective-permute-start(bf16[256,1024]{1,0:T(8,128)(2,1)S(1)} %gate.10), channel_id=1, source_target_pairs={{0,8},{24,16},{1,9},{25,17},{2,10},{26,18},{3,11},{27,19},{4,12},{... | collective-permute-start | bytes 1572872 | tf_op jit(solution)/shard_map/ppermute | solution.py:52
  80.3 15.1 %collective-permute-start.19 = (bf16[256,1024]{1,0:T(8,128)(2,1)S(1)}, bf16[256,1024]{1,0:T(8,128)(2,1)S(1)}, u32[]{:S(2)}, u32[]{:S(2)}) collective-permute-start(bf16[256,1024]{1,0:T(8,128)(2,1)S(1)} %gate.11), channel_id=1, source_target_pairs={{8,0},{16,24},{9,1},{17,25},{10,2},{18,26},{11,3},{19,27},{12,4},{... | collective-permute-start | bytes 1572872 | tf_op jit(solution)/shard_map/ppermute | solution.py:52
  81.9 13.5 %collective-permute-start.21 = (bf16[256,1024]{1,0:T(8,128)(2,1)S(1)}, bf16[256,1024]{1,0:T(8,128)(2,1)S(1)}, u32[]{:S(2)}, u32[]{:S(2)}) collective-permute-start(bf16[256,1024]{1,0:T(8,128)(2,1)S(1)} %gate.12.refs_0_.refs_2_), channel_id=1, source_target_pairs={{0,4},{2,6},{4,0},{6,2},{1,5},{3,7},{5,1},{7,3},{8,12},{10,14},{12... | collective-permute-start | bytes 1572872 | tf_op jit(solution)/shard_map/ppermute | solution.py:56
  83.5 14.7 %collective-permute-start.14 = (bf16[256,1024]{1,0:T(8,128)(2,1)S(1)}, bf16[256,1024]{1,0:T(8,128)(2,1)S(1)}, u32[]{:S(2)}, u32[]{:S(2)}) collective-permute-start(bf16[256,1024]{1,0:T(8,128)(2,1)S(1)} %collective-permute-done.13.refs_0_.x), channel_id=1, source_target_pairs={{8,16},{16,8},{9,17},{17,9},{10,18},{18,10},{11,19},{19,11},{12,20... | collective-permute-start | bytes 1572872 | tf_op jit(solution)/shard_map/ppermute | solution.py:52
  84.2 21.7 %collective-permute-start.17 = (bf16[256,1024]{1,0:T(8,128)(2,1)S(1)}, bf16[256,1024]{1,0:T(8,128)(2,1)S(1)}, u32[]{:S(2)}, u32[]{:S(2)}) collective-permute-start(bf16[256,1024]{1,0:T(8,128)(2,1)S(1)} %collective-permute-done.16.refs_1_.middle), channel_id=1, source_target_pairs={{8,16},{16,8},{9,17},{17,9},{10,18},{18,10},{11,19},{19,11},{12,20... | collective-permute-start | bytes 1572872 | tf_op jit(solution)/shard_map/ppermute | solution.py:52
  95.5 10.5 %collective-permute-start.22 = (bf16[256,1024]{1,0:T(8,128)(2,1)S(1)}, bf16[256,1024]{1,0:T(8,128)(2,1)S(1)}, u32[]{:S(2)}, u32[]{:S(2)}) collective-permute-start(bf16[256,1024]{1,0:T(8,128)(2,1)S(1)} %pick.5.refs_0_), channel_id=1, source_target_pairs={{0,4},{2,6},{4,0},{6,2},{1,5},{3,7},{5,1},{7,3},{8,12},{10,14},{12... | collective-permute-start | bytes 1572872 | tf_op jit(solution)/shard_map/ppermute | solution.py:56
  98.2 11.1 %collective-permute-start.15 = (bf16[256,1024]{1,0:T(8,128)(2,1)S(1)}, bf16[256,1024]{1,0:T(8,128)(2,1)S(1)}, u32[]{:S(2)}, u32[]{:S(2)}) collective-permute-start(bf16[256,1024]{1,0:T(8,128)(2,1)S(1)} %collective-permute-done.14.middle), channel_id=1, source_target_pairs={{8,0},{16,24},{9,1},{17,25},{10,2},{18,26},{11,3},{19,27},{12,4},{... | collective-permute-start | bytes 1572872 | tf_op jit(solution)/shard_map/ppermute | solution.py:52
  109.6 8.5 %collective-permute-start.25 = (bf16[3,256,1024]{2,1,0:T(8,128)(2,1)S(1)}, bf16[3,256,1024]{2,1,0:T(8,128)(2,1)S(1)}, u32[]{:S(2)}, u32[]{:S(2)}) collective-permute-start(bf16[3,256,1024]{2,1,0:T(8,128)(2,1)S(1)} %bundle.3.refs_0_), channel_id=1, source_target_pairs={{0,2},{2,0},{4,6},{6,4},{1,3},{3,1},{5,7},{7,5},{8,10},{10,8},{12,... | collective-permute-start | bytes 4718600 | tf_op jit(solution)/shard_map/ppermute | solution.py:56
  110.2 13.9 %collective-permute-start.24 = (bf16[256,1024]{1,0:T(8,128)(2,1)S(1)}, bf16[256,1024]{1,0:T(8,128)(2,1)S(1)}, u32[]{:S(2)}, u32[]{:S(2)}) collective-permute-start(bf16[256,1024]{1,0:T(8,128)(2,1)S(1)} %pick.6.refs_2_.refs_4_), channel_id=1, source_target_pairs={{0,4},{2,6},{4,0},{6,2},{1,5},{3,7},{5,1},{7,3},{8,12},{10,14},{12... | collective-permute-start | bytes 1572872 | tf_op jit(solution)/shard_map/ppermute | solution.py:56
  110.3 15.8 %collective-permute-start.28 = (bf16[256,1024]{1,0:T(8,128)(2,1)S(1)}, bf16[256,1024]{1,0:T(8,128)(2,1)S(1)}, u32[]{:S(2)}, u32[]{:S(2)}) collective-permute-start(bf16[256,1024]{1,0:T(8,128)(2,1)S(1)} %collective-permute-done.17.refs_0_.middle), channel_id=1, source_target_pairs={{8,0},{16,24},{9,1},{17,25},{10,2},{18,26},{11,3},{19,27},{12,4},{... | collective-permute-start | bytes 1572872 | tf_op jit(solution)/shard_map/ppermute | solution.py:52
  (15 other events, 260.5 us)

commit v6 on v5

--- a/solution.py
+++ b/solution.py
@@ -40,12 +40,14 @@
 INWARD = ((0, 1), (3, 2))
 ACROSS = ((1, 2), (2, 1))
 OUTWARD = ((1, 0), (2, 3))
+ENDS = ((0, 3), (3, 0))
 
 
 def owners():
     pos = lax.axis_index("replica")
     low = pos < 2
-    return pos, jnp.bitwise_xor(pos, 1), jnp.where(low, 2, 1), jnp.where(low, 3, 0)
+    middle, end = jnp.where(low, 2, 1), jnp.where(low, 3, 0)
+    return pos, jnp.bitwise_xor(pos, 1), middle, end, 3 - pos, jnp.bitwise_xor(3 - pos, 1)
 
 
 def along(x, pairs):
@@ -388,8 +390,10 @@
     packets_came = [swap(packets[0], "replica", 1), swap(packets[1], "replica", 2)]
     end = gate(end, packets_came[0])
     packets_came.append(swap(gate(packets[2], end), "replica", 3))
-    from_end = along(end, INWARD)
-    from_middle = along(middle, INWARD)
+    end_across = along(end, ACROSS)
+    middle_in = along(middle, INWARD)
+    end_direct = along(end, ENDS)
+    near_in = along(near, INWARD)
 
     state = jax.ShapeDtypeStruct((2, rows_up, half_cols), F32)
     states = call(
@@ -438,14 +442,11 @@
     )
 
     embed_out = along(recast_rows, OUTWARD)
-    embed_middle = along(recast_rows, ACROSS)
-    end_partial = along(add(end, from_end, embed_middle, embed_out), ACROSS)
-    middle_sum = add(middle, from_middle)
-    middle_partial = along(middle_sum, ACROSS)
-    embed_middle_out = along(embed_middle, OUTWARD)
-    to_end = along(add(near, end_partial, embed_middle_out), OUTWARD)
-    from_near = along(gate(near, middle_sum), INWARD)
-    came0 = [own, middle_partial, from_near, to_end]
+    middle_across = along(add(middle, middle_in), ACROSS)
+    near_sum = add(near, end_across, embed_out, end_direct)
+    near_out = along(near_sum, OUTWARD)
+    embed_middle = along(gate(recast_rows, near_sum), ACROSS)
+    came0 = [own, near_in, end_direct, middle_across, near_out]
     half_sum = jax.ShapeDtypeStruct((rows_up, half_cols), F32)
     down_state = jax.ShapeDtypeStruct((rows_down, width), F32)
     piece, stored_down, velocity_down, *sums = call(
@@ -464,24 +465,25 @@
     )
 
     top = shards // 2
-    came_near = swap(piece, "replica", 1)
+    near_piece = swap(piece, "replica", 1)
     middle_piece = along(piece, ACROSS)
+    end_piece = along(piece, ENDS)
     far_piece = swap(piece, "shard", top)
     embed_in = along(gate(recast_rows, piece), INWARD)
-    end_piece = along(came_near, ACROSS)
-    second_out = along(gate(middle_piece, came_near), OUTWARD)
-    near_piece = gate(came_near, far_piece)
-    far_near = swap(near_piece, "shard", top)
+    middle_out = along(middle_piece, OUTWARD)
+    near_across = along(near_piece, ACROSS)
+    far_near = swap(gate(near_piece, far_piece), "shard", top)
+    second = pick(middle_piece, end_piece, far_near, embed_middle)
+    far_second = swap(second, "shard", top)
+    embed_end = along(embed_in, ACROSS)
+    embed_middle_out = along(embed_middle, OUTWARD)
     sums = [sums[0]] + [
         lax.ppermute(
             gate(x, near_piece), "tensor", [(i, (i + shift) % tensors) for i in range(tensors)]
         )
         for shift, x in enumerate(sums[1:], 1)
     ]
-    second = pick(middle_piece, second_out, far_near, embed_in)
-    far_second = swap(second, "shard", top)
-    embed_end = along(embed_in, ACROSS)
-    third = pick(end_piece, along(end_piece, OUTWARD), embed_end, far_second, *sums[1:])
+    third = pick(near_across, middle_out, far_second, embed_in, *sums[1:])
     far_third = swap(third, "shard", top)
     embed_last = along(embed_end, OUTWARD)
     bundles = [
@@ -490,7 +492,7 @@
             spread_low(bundle([piece, far_piece, near_piece, far_near], third)),
         ),
         (
-            [(2, 0), (2, top), (3, 0)],
+            [(4, 0), (4, top), (5, 0)],
             spread_low(bundle([second, far_second, third])),
         ),
     ]
@@ -556,7 +558,7 @@
         recast_embed,
         aliases={2: 0},
     )
-    recast_down, recast_up, _ = place([(3, top)], last, placed, token)
+    recast_down, recast_up, _ = place([(5, top)], last, placed, token)
 
     return (
         recast_up.reshape(-1, half_cols),

time: 129 us -> 153 us (1.19)
  waiting for transfers between devices: 55.1 us -> 89.6 us
  starting transfers between devices: 54.3 us -> 43.4 us
    ppermute x16, waiting for transfers between devices: 35.6 us -> 73.5 us  [along(): return lax.ppermute(x, 'replica', pairs)]
    ppermute x11, starting transfers between devices: 18.8 us -> 11.1 us  [swap(): lax.ppermute(x, axis, [(i, i ^ bit) for i in range(lax.axis_size(axis))])]
    ppermute x1, waiting for transfers between devices: 4.92 us -> 0.63 us  [body(): lax.ppermute(gate(x, near_piece), 'tensor', [(i, (i + shift) % tensors) f...]
    ppermute x16, starting transfers between devices: 32.5 us -> 29.2 us  [along(): return lax.ppermute(x, 'replica', pairs)]
    pallas_call x28 -> x26, Pallas kernels: 16.9 us -> 16.9 us  [call(): pl.pallas_call(kernel, name=name, out_shape=out_shape, in_specs=in_specs,...]
  transfers between devices with their start and end apart: 29 -> 29, of which waited for: 13 -> 12; matrix products, arithmetic and copies ran while one was open for 1% -> 1% of each run, Pallas kernels for 8% -> 6%
where the time goes in v6:
time: 153 us; the launch traced here: 152 us
  waiting for transfers between devices  89.6 us (59%)
  starting transfers between devices  43.4 us (28%)
  Pallas kernels  16.9 us (11%)
    ppermute x16, waiting for transfers between devices, along(): return lax.ppermute(x, 'replica', pairs)  73.5 us
    ppermute x16, starting transfers between devices, along(): return lax.ppermute(x, 'replica', pairs)  29.2 us
    pallas_call x26, Pallas kernels, call(): pl.pallas_call(kernel, name=name, out_shape=out_shape, in_specs=in_specs,...  16.9 us
    ppermute x11, waiting for transfers between devices, swap(): lax.ppermute(x, axis, [(i, i ^ bit) for i in range(lax.axis_size(axis))])  15.5 us
    ppermute x11, starting transfers between devices, swap(): lax.ppermute(x, axis, [(i, i ^ bit) for i in range(lax.axis_size(axis))])  11.1 us
  transfers between devices with their start and end apart: 29, of which 12 were waited for; matrix products, arithmetic and copies ran while one was open for 1% of the time, Pallas kernels for 6%

profile of v6, /device:TPU:0, one launch (start us, length us, event | category | flops | bytes accessed | tf_op | source)
XLA Modules:
  0.0 152.2 jit_solution(2905174779923828646)
XLA Ops:
  0.7 3.4 %prepare.1 = (bf16[256,1024]{1,0:T(8,128)(2,1)S(1)}, bf16[256,1024]{1,0:T(8,128)(2,1)S(1)}, bf16[256,1024]{1,0:T(8,128)(2,1)S(1)}, bf16[256,1024]{1,0:T(8,128)(2...) custom-call(bf16[1024,1024]{1,0:T(8,128)(2,1)} %bitcast.35, ...), custom_call_target="tpu_custom_call" | custom-call | bytes 6856704 | tf_op jit(solution)/shard_map/prepare/pallas_call | solution.py:26
  4.2 3.1 %collective-permute-start.1 = (bf16[80,256]{1,0:T(8,128)(2,1)S(1)}, bf16[80,256]{1,0:T(8,128)(2,1)S(1)}, u32[]{:S(2)}, u32[]{:S(2)}) collective-permute-start(bf16[80,256]{1,0:T(8,128)(2,1)S(1)} %get-tuple-element.49), channel_id=1, source_target_pairs={{0,8},{8,0},{16,24},{24,16},{1,9},{9,1},{17,25},{25,17},{2,10},{10... | collective-permute-start | bytes 122888 | tf_op jit(solution)/shard_map/ppermute | solution.py:58
  7.3 2.6 %collective-permute-start.6 = (bf16[80,256]{1,0:T(8,128)(2,1)S(1)}, bf16[80,256]{1,0:T(8,128)(2,1)S(1)}, u32[]{:S(2)}, u32[]{:S(2)}) collective-permute-start(bf16[80,256]{1,0:T(8,128)(2,1)S(1)} %get-tuple-element.52), channel_id=1, source_target_pairs={{0,16},{8,24},{16,0},{24,8},{1,17},{9,25},{17,1},{25,9},{2,18},{10... | collective-permute-start | bytes 122888 | tf_op jit(solution)/shard_map/ppermute | solution.py:58
  9.8 2.4 %collective-permute-start.3 = (bf16[256,1024]{1,0:T(8,128)(2,1)S(1)}, bf16[256,1024]{1,0:T(8,128)(2,1)S(1)}, u32[]{:S(2)}, u32[]{:S(2)}) collective-permute-start(bf16[256,1024]{1,0:T(8,128)(2,1)S(1)} %get-tuple-element.50.block), channel_id=1, source_target_pairs={{0,8},{24,16},{1,9},{25,17},{2,10},{26,18},{3,11},{27,19},{4,12},{... | collective-permute-start | bytes 1572872 | tf_op jit(solution)/shard_map/ppermute | solution.py:54
  15.6 4.3 %collective-permute-start.2 = (bf16[256,1024]{1,0:T(8,128)(2,1)S(1)}, bf16[256,1024]{1,0:T(8,128)(2,1)S(1)}, u32[]{:S(2)}, u32[]{:S(2)}) collective-permute-start(bf16[256,1024]{1,0:T(8,128)(2,1)S(1)} %gate.6.refs_0_), channel_id=1, source_target_pairs={{0,24},{24,0},{1,25},{25,1},{2,26},{26,2},{3,27},{27,3},{4,28},{28... | collective-permute-start | bytes 1572872 | tf_op jit(solution)/shard_map/ppermute | solution.py:54
  19.9 7.4 %collective-permute-done.7.refs_10_ = bf16[80,256]{1,0:T(8,128)(2,1)S(1)} collective-permute-done((bf16[80,256]{1,0:T(8,128)(2,1)S(1)}, bf16[80,256]{1,0:T(8,128)(2,1)S(1)}, u32[]{:S(2)}, u32[]{:S(2)}) %collective-permute-start.7) | collective-permute-done | bytes 40992 | tf_op jit(solution)/shard_map/ppermute | solution.py:58
  27.4 2.0 %embed_update.1 = (f32[256,1024]{1,0:T(8,128)}, bf16[256,1024]{1,0:T(8,128)(2,1)S(1)}, f32[64,256]{1,0:T(8,128)}, bf16[2,1024]{1,0:T(2,128)(2,1)}, f32[2,1024]{1,0:T(2,128)}, /*index=5*/f32[2,1024]{1,0:T(2,128)}) custom-call(f32[64,256]{1,0:T(8,128)S(1)} %get-tuple-element.51.refs_0_, f32[64,256]{1,0:T(8,128)S(1)} %fusion.refs_1_, f32[256,1024]{1,0:T(8,128)S(1)} %bitcast.23, ...), custom_call_target="tpu_custom_call" | custom-call | bytes 4976640 | tf_op jit(solution)/shard_map/embed_update/pallas_call | solution.py:26
  30.8 1.6 %collective-permute-start.10 = (f32[2,32,2048]{2,1,0:T(8,128)S(1)}, f32[2,32,2048]{2,1,0:T(8,128)S(1)}, u32[]{:S(2)}, u32[]{:S(2)}) collective-permute-start(f32[2,32,2048]{2,1,0:T(8,128)S(1)} %up_state.1), channel_id=1, source_target_pairs={{0,1},{1,0},{2,3},{3,2},{4,5},{5,4},{6,7},{7,6},{8,9},{9,8},{10,11... | collective-permute-start | bytes 1572872 | tf_op jit(solution)/shard_map/ppermute | solution.py:410
  32.3 4.6 %collective-permute-start = (bf16[256,1024]{1,0:T(8,128)(2,1)S(1)}, bf16[256,1024]{1,0:T(8,128)(2,1)S(1)}, u32[]{:S(2)}, u32[]{:S(2)}) collective-permute-start(bf16[256,1024]{1,0:T(8,128)(2,1)S(1)} %get-tuple-element.47.block), channel_id=1, source_target_pairs={{0,8},{24,16},{1,9},{25,17},{2,10},{26,18},{3,11},{27,19},{4,12},{... | collective-permute-start | bytes 1572872 | tf_op jit(solution)/shard_map/ppermute | solution.py:54
  38.0 10.1 %collective-permute-done.8.refs_0_.end = bf16[256,1024]{1,0:T(8,128)(2,1)S(1)} collective-permute-done((bf16[256,1024]{1,0:T(8,128)(2,1)S(1)}, bf16[256,1024]{1,0:T(8,128)(2,1)S(1)}, u32[]{:S(2)}, u32[]{:S(2)}) %collective-permute-start.8) | collective-permute-done | bytes 524320 | tf_op jit(solution)/shard_map/ppermute | solution.py:54
  49.5 14.4 %collective-permute-done.9.refs_8_ = bf16[256,1024]{1,0:T(8,128)(2,1)S(1)} collective-permute-done((bf16[256,1024]{1,0:T(8,128)(2,1)S(1)}, bf16[256,1024]{1,0:T(8,128)(2,1)S(1)}, u32[]{:S(2)}, u32[]{:S(2)}) %collective-permute-start.9) | collective-permute-done | bytes 524320 | tf_op jit(solution)/shard_map/ppermute | solution.py:54
  63.9 1.8 %update_rows.1 = (bf16[256,1024]{1,0:T(8,128)(2,1)S(1)}, f32[128,1024]{1,0:T(8,128)}, f32[128,1024]{1,0:T(8,128)}, f32[32,2048]{1,0:T(8,128)S(1)}, f32[32,2048]{1,0:T(8,128)S(1)}) custom-call(f32[128,1024]{1,0:T(8,128)S(1)} %bitcast.26, f32[128,1024]{1,0:T(8,128)S(1)} %bitcast.27, f32[32,4096]{1,0:T(8,128)S(1)} %copy-done, f32[32,4096]{1,0:T(8,128)S(1)} %copy-done.1, ...), custom_call_target="tpu_custom_call" | custom-call | bytes 6291456 | tf_op jit(solution)/shard_map/update_rows/pallas_call | solution.py:26
  68.0 4.4 %collective-permute-start.15 = (bf16[256,1024]{1,0:T(8,128)(2,1)S(1)}, bf16[256,1024]{1,0:T(8,128)(2,1)S(1)}, u32[]{:S(2)}, u32[]{:S(2)}) collective-permute-start(bf16[256,1024]{1,0:T(8,128)(2,1)S(1)} %get-tuple-element.55.refs_0_), channel_id=1, source_target_pairs={{0,24},{24,0},{1,25},{25,1},{2,26},{26,2},{3,27},{27,3},{4,28},{28... | collective-permute-start | bytes 1572872 | tf_op jit(solution)/shard_map/ppermute | solution.py:54
  73.1 5.6 %collective-permute-done.16.refs_0_.refs_1_ = bf16[256,1024]{1,0:T(8,128)(2,1)S(1)} collective-permute-done((bf16[256,1024]{1,0:T(8,128)(2,1)S(1)}, bf16[256,1024]{1,0:T(8,128)(2,1)S(1)}, u32[]{:S(2)}, u32[]{:S(2)}) %collective-permute-start.16) | collective-permute-done | bytes 524320 | tf_op jit(solution)/shard_map/ppermute | solution.py:58
  78.7 2.4 %collective-permute-done.11.x.refs_0_.refs_2_ = bf16[256,1024]{1,0:T(8,128)(2,1)S(1)} collective-permute-done((bf16[256,1024]{1,0:T(8,128)(2,1)S(1)}, bf16[256,1024]{1,0:T(8,128)(2,1)S(1)}, u32[]{:S(2)}, u32[]{:S(2)}) %collective-permute-start.11) | collective-permute-done | bytes 524320 | tf_op jit(solution)/shard_map/ppermute | solution.py:58
  81.7 3.0 %collective-permute-start.20 = (bf16[256,1024]{1,0:T(8,128)(2,1)S(1)}, bf16[256,1024]{1,0:T(8,128)(2,1)S(1)}, u32[]{:S(2)}, u32[]{:S(2)}) collective-permute-start(bf16[256,1024]{1,0:T(8,128)(2,1)S(1)} %gate.10), channel_id=1, source_target_pairs={{0,8},{24,16},{1,9},{25,17},{2,10},{26,18},{3,11},{27,19},{4,12},{... | collective-permute-start | bytes 1572872 | tf_op jit(solution)/shard_map/ppermute | solution.py:54
  86.7 7.1 %collective-permute-done.15.end = bf16[256,1024]{1,0:T(8,128)(2,1)S(1)} collective-permute-done((bf16[256,1024]{1,0:T(8,128)(2,1)S(1)}, bf16[256,1024]{1,0:T(8,128)(2,1)S(1)}, u32[]{:S(2)}, u32[]{:S(2)}) %collective-permute-start.15) | collective-permute-done | bytes 524320 | tf_op jit(solution)/shard_map/ppermute | solution.py:54
  96.0 4.3 %collective-permute-done.20.refs_1_.middle = bf16[256,1024]{1,0:T(8,128)(2,1)S(1)} collective-permute-done((bf16[256,1024]{1,0:T(8,128)(2,1)S(1)}, bf16[256,1024]{1,0:T(8,128)(2,1)S(1)}, u32[]{:S(2)}, u32[]{:S(2)}) %collective-permute-start.20) | collective-permute-done | bytes 524320 | tf_op jit(solution)/shard_map/ppermute | solution.py:54
  100.9 16.2 %collective-permute-done.14.end = bf16[256,1024]{1,0:T(8,128)(2,1)S(1)} collective-permute-done((bf16[256,1024]{1,0:T(8,128)(2,1)S(1)}, bf16[256,1024]{1,0:T(8,128)(2,1)S(1)}, u32[]{:S(2)}, u32[]{:S(2)}) %collective-permute-start.14) | collective-permute-done | bytes 524320 | tf_op jit(solution)/shard_map/ppermute | solution.py:54
  120.7 13.1 %collective-permute-done.25.end = bf16[256,1024]{1,0:T(8,128)(2,1)S(1)} collective-permute-done((bf16[256,1024]{1,0:T(8,128)(2,1)S(1)}, bf16[256,1024]{1,0:T(8,128)(2,1)S(1)}, u32[]{:S(2)}, u32[]{:S(2)}) %collective-permute-start.25) | collective-permute-done | bytes 524320 | tf_op jit(solution)/shard_map/ppermute | solution.py:54
  137.5 2.2 %place_rows.3 = (bf16[4,4,128,1024]{3,2,1,0:T(8,128)(2,1)}, bf16[4,4,64,2048]{3,2,1,0:T(8,128)(2,1)}, f32[8,128]{1,0:T(8,128)S(1)}) custom-call(bf16[4,256,1024]{2,1,0:T(8,128)(2,1)S(1)} %bundle.4.refs_0_, bf16[4,256,1024]{2,1,0:T(8,128)(2,1)S(1)} %collective-permute-done.24.refs_2_.refs_1_, f32[8,128]{1,0:T(8,128)S(1)} %get-tuple-element.59.refs_2_), custom_call_target="tpu_custom_call" | custom-call | bytes 25178112 | tf_op jit(solution)/shard_map/place_rows/pallas_call | solution.py:26
  139.7 1.8 %place_rows.4 = (bf16[4,4,128,1024]{3,2,1,0:T(8,128)(2,1)}, bf16[4,4,64,2048]{3,2,1,0:T(8,128)(2,1)}, f32[8,128]{1,0:T(8,128)S(1)}) custom-call(bf16[3,256,1024]{2,1,0:T(8,128)(2,1)S(1)} %bundle.3.refs_0_, bf16[3,256,1024]{2,1,0:T(8,128)(2,1)S(1)} %collective-permute-done.23.refs_1_, ...), custom_call_target="tpu_custom_call", output_to_operand_aliasing={{0}: (3, {}), {1}: (4, {})} | custom-call | bytes 25178112 | tf_op jit(solution)/shard_map/place_rows/pallas_call | solution.py:26
  141.7 8.1 %collective-permute-done.28.end = bf16[256,1024]{1,0:T(8,128)(2,1)S(1)} collective-permute-done((bf16[256,1024]{1,0:T(8,128)(2,1)S(1)}, bf16[256,1024]{1,0:T(8,128)(2,1)S(1)}, u32[]{:S(2)}, u32[]{:S(2)}) %collective-permute-start.28) | collective-permute-done | bytes 524320 | tf_op jit(solution)/shard_map/ppermute | solution.py:54
  150.6 1.6 %place_rows.5 = (bf16[4,4,128,1024]{3,2,1,0:T(8,128)(2,1)}, bf16[4,4,64,2048]{3,2,1,0:T(8,128)(2,1)}, f32[8,128]{1,0:T(8,128)}) custom-call(bf16[1,256,1024]{2,1,0:T(8,128)(2,1)S(1)} %bundle.5.refs_1_.refs_0_, bf16[1,256,1024]{2,1,0:T(8,128)(2,1)S(1)} %collective-permute-done.26.refs_1_, ...), custom_call_target="tpu_custom_call", output_to_operand_aliasing={{0}: (3, {}), {1}: (4, {})} | custom-call | bytes 25178112 | tf_op jit(solution)/shard_map/place_rows/pallas_call | solution.py:26
  (81 shorter events, 23.6 us)
Async XLA Ops:
  9.8 22.5 %collective-permute-start.3 = (bf16[256,1024]{1,0:T(8,128)(2,1)S(1)}, bf16[256,1024]{1,0:T(8,128)(2,1)S(1)}, u32[]{:S(2)}, u32[]{:S(2)}) collective-permute-start(bf16[256,1024]{1,0:T(8,128)(2,1)S(1)} %get-tuple-element.50.block), channel_id=1, source_target_pairs={{0,8},{24,16},{1,9},{25,17},{2,10},{26,18},{3,11},{27,19},{4,12},{... | collective-permute-start | bytes 1572872 | tf_op jit(solution)/shard_map/ppermute | solution.py:54
  12.3 15.0 %collective-permute-start.7 = (bf16[80,256]{1,0:T(8,128)(2,1)S(1)}, bf16[80,256]{1,0:T(8,128)(2,1)S(1)}, u32[]{:S(2)}, u32[]{:S(2)}) collective-permute-start(bf16[80,256]{1,0:T(8,128)(2,1)S(1)} %gate.7), channel_id=1, source_target_pairs={{0,24},{8,16},{16,8},{24,0},{1,25},{9,17},{17,9},{25,1},{2,26},{10... | collective-permute-start | bytes 122888 | tf_op jit(solution)/shard_map/ppermute | solution.py:58
  14.9 22.2 %collective-permute-start.5 = (bf16[256,1024]{1,0:T(8,128)(2,1)S(1)}, bf16[256,1024]{1,0:T(8,128)(2,1)S(1)}, u32[]{:S(2)}, u32[]{:S(2)}) collective-permute-start(bf16[256,1024]{1,0:T(8,128)(2,1)S(1)} %gate.6.refs_0_), channel_id=1, source_target_pairs={{8,16},{16,8},{9,17},{17,9},{10,18},{18,10},{11,19},{19,11},{12,20... | collective-permute-start | bytes 1572872 | tf_op jit(solution)/shard_map/ppermute | solution.py:54
  15.6 22.4 %collective-permute-start.2 = (bf16[256,1024]{1,0:T(8,128)(2,1)S(1)}, bf16[256,1024]{1,0:T(8,128)(2,1)S(1)}, u32[]{:S(2)}, u32[]{:S(2)}) collective-permute-start(bf16[256,1024]{1,0:T(8,128)(2,1)S(1)} %gate.6.refs_0_), channel_id=1, source_target_pairs={{0,24},{24,0},{1,25},{25,1},{2,26},{26,2},{3,27},{27,3},{4,28},{28... | collective-permute-start | bytes 1572872 | tf_op jit(solution)/shard_map/ppermute | solution.py:54
  29.4 18.7 %collective-permute-start.8 = (bf16[256,1024]{1,0:T(8,128)(2,1)S(1)}, bf16[256,1024]{1,0:T(8,128)(2,1)S(1)}, u32[]{:S(2)}, u32[]{:S(2)}) collective-permute-start(bf16[256,1024]{1,0:T(8,128)(2,1)S(1)} %get-tuple-element.54.x.refs_0_), channel_id=1, source_target_pairs={{8,0},{16,24},{9,1},{17,25},{10,2},{18,26},{11,3},{19,27},{12,4},{... | collective-permute-start | bytes 1572872 | tf_op jit(solution)/shard_map/ppermute | solution.py:54
  30.8 18.7 %collective-permute-start.10 = (f32[2,32,2048]{2,1,0:T(8,128)S(1)}, f32[2,32,2048]{2,1,0:T(8,128)S(1)}, u32[]{:S(2)}, u32[]{:S(2)}) collective-permute-start(f32[2,32,2048]{2,1,0:T(8,128)S(1)} %up_state.1), channel_id=1, source_target_pairs={{0,1},{1,0},{2,3},{3,2},{4,5},{5,4},{6,7},{7,6},{8,9},{9,8},{10,11... | collective-permute-start | bytes 1572872 | tf_op jit(solution)/shard_map/ppermute | solution.py:410
  32.3 17.2 %collective-permute-start = (bf16[256,1024]{1,0:T(8,128)(2,1)S(1)}, bf16[256,1024]{1,0:T(8,128)(2,1)S(1)}, u32[]{:S(2)}, u32[]{:S(2)}) collective-permute-start(bf16[256,1024]{1,0:T(8,128)(2,1)S(1)} %get-tuple-element.47.block), channel_id=1, source_target_pairs={{0,8},{24,16},{1,9},{25,17},{2,10},{26,18},{3,11},{27,19},{4,12},{... | collective-permute-start | bytes 1572872 | tf_op jit(solution)/shard_map/ppermute | solution.py:54
  48.2 15.7 %collective-permute-start.9 = (bf16[256,1024]{1,0:T(8,128)(2,1)S(1)}, bf16[256,1024]{1,0:T(8,128)(2,1)S(1)}, u32[]{:S(2)}, u32[]{:S(2)}) collective-permute-start(bf16[256,1024]{1,0:T(8,128)(2,1)S(1)} %add_block.3.refs_0_), channel_id=1, source_target_pairs={{8,0},{16,24},{9,1},{17,25},{10,2},{18,26},{11,3},{19,27},{12,4},{... | collective-permute-start | bytes 1572872 | tf_op jit(solution)/shard_map/ppermute | solution.py:54
  65.7 13.0 %collective-permute-start.16 = (bf16[256,1024]{1,0:T(8,128)(2,1)S(1)}, bf16[256,1024]{1,0:T(8,128)(2,1)S(1)}, u32[]{:S(2)}, u32[]{:S(2)}) collective-permute-start(bf16[256,1024]{1,0:T(8,128)(2,1)S(1)} %get-tuple-element.55.refs_0_), channel_id=1, source_target_pairs={{0,4},{2,6},{4,0},{6,2},{1,5},{3,7},{5,1},{7,3},{8,12},{10,14},{12... | collective-permute-start | bytes 1572872 | tf_op jit(solution)/shard_map/ppermute | solution.py:58
  67.2 13.8 %collective-permute-start.11 = (bf16[256,1024]{1,0:T(8,128)(2,1)S(1)}, bf16[256,1024]{1,0:T(8,128)(2,1)S(1)}, u32[]{:S(2)}, u32[]{:S(2)}) collective-permute-start(bf16[256,1024]{1,0:T(8,128)(2,1)S(1)} %get-tuple-element.55.refs_0_), channel_id=1, source_target_pairs={{0,8},{8,0},{16,24},{24,16},{1,9},{9,1},{17,25},{25,17},{2,10},{10... | collective-permute-start | bytes 1572872 | tf_op jit(solution)/shard_map/ppermute | solution.py:58
  67.3 17.4 %collective-permute-start.18 = (bf16[256,1024]{1,0:T(8,128)(2,1)S(1)}, bf16[256,1024]{1,0:T(8,128)(2,1)S(1)}, u32[]{:S(2)}, u32[]{:S(2)}) collective-permute-start(bf16[256,1024]{1,0:T(8,128)(2,1)S(1)} %gate.9), channel_id=1, source_target_pairs={{8,16},{16,8},{9,17},{17,9},{10,18},{18,10},{11,19},{19,11},{12,20... | collective-permute-start | bytes 1572872 | tf_op jit(solution)/shard_map/ppermute | solution.py:54
  68.0 25.8 %collective-permute-start.15 = (bf16[256,1024]{1,0:T(8,128)(2,1)S(1)}, bf16[256,1024]{1,0:T(8,128)(2,1)S(1)}, u32[]{:S(2)}, u32[]{:S(2)}) collective-permute-start(bf16[256,1024]{1,0:T(8,128)(2,1)S(1)} %get-tuple-element.55.refs_0_), channel_id=1, source_target_pairs={{0,24},{24,0},{1,25},{25,1},{2,26},{26,2},{3,27},{27,3},{4,28},{28... | collective-permute-start | bytes 1572872 | tf_op jit(solution)/shard_map/ppermute | solution.py:54
  72.4 13.0 %collective-permute-start.13 = (bf16[256,1024]{1,0:T(8,128)(2,1)S(1)}, bf16[256,1024]{1,0:T(8,128)(2,1)S(1)}, u32[]{:S(2)}, u32[]{:S(2)}) collective-permute-start(bf16[256,1024]{1,0:T(8,128)(2,1)S(1)} %get-tuple-element.55.refs_0_), channel_id=1, source_target_pairs={{8,16},{16,8},{9,17},{17,9},{10,18},{18,10},{11,19},{19,11},{12,20... | collective-permute-start | bytes 1572872 | tf_op jit(solution)/shard_map/ppermute | solution.py:54
  81.1 12.7 %collective-permute-start.17 = (bf16[256,1024]{1,0:T(8,128)(2,1)S(1)}, bf16[256,1024]{1,0:T(8,128)(2,1)S(1)}, u32[]{:S(2)}, u32[]{:S(2)}) collective-permute-start(bf16[256,1024]{1,0:T(8,128)(2,1)S(1)} %gate.8), channel_id=1, source_target_pairs={{0,4},{2,6},{4,0},{6,2},{1,5},{3,7},{5,1},{7,3},{8,12},{10,14},{12... | collective-permute-start | bytes 1572872 | tf_op jit(solution)/shard_map/ppermute | solution.py:58
  81.7 18.5 %collective-permute-start.20 = (bf16[256,1024]{1,0:T(8,128)(2,1)S(1)}, bf16[256,1024]{1,0:T(8,128)(2,1)S(1)}, u32[]{:S(2)}, u32[]{:S(2)}) collective-permute-start(bf16[256,1024]{1,0:T(8,128)(2,1)S(1)} %gate.10), channel_id=1, source_target_pairs={{0,8},{24,16},{1,9},{25,17},{2,10},{26,18},{3,11},{27,19},{4,12},{... | collective-permute-start | bytes 1572872 | tf_op jit(solution)/shard_map/ppermute | solution.py:54
  84.7 32.4 %collective-permute-start.12 = (bf16[256,1024]{1,0:T(8,128)(2,1)S(1)}, bf16[256,1024]{1,0:T(8,128)(2,1)S(1)}, u32[]{:S(2)}, u32[]{:S(2)}) collective-permute-start(bf16[256,1024]{1,0:T(8,128)(2,1)S(1)} %collective-permute-done.11.x.refs_0_.refs_2_), channel_id=1, source_target_pairs={{8,16},{16,8},{9,17},{17,9},{10,18},{18,10},{11,19},{19,11},{12,20... | collective-permute-start | bytes 1572872 | tf_op jit(solution)/shard_map/ppermute | solution.py:54
  85.4 31.7 %collective-permute-start.14 = (bf16[256,1024]{1,0:T(8,128)(2,1)S(1)}, bf16[256,1024]{1,0:T(8,128)(2,1)S(1)}, u32[]{:S(2)}, u32[]{:S(2)}) collective-permute-start(bf16[256,1024]{1,0:T(8,128)(2,1)S(1)} %collective-permute-done.13.middle), channel_id=1, source_target_pairs={{8,0},{16,24},{9,1},{17,25},{10,2},{18,26},{11,3},{19,27},{12,4},{... | collective-permute-start | bytes 1572872 | tf_op jit(solution)/shard_map/ppermute | solution.py:54
  93.9 23.3 %collective-permute-start.19 = (bf16[256,1024]{1,0:T(8,128)(2,1)S(1)}, bf16[256,1024]{1,0:T(8,128)(2,1)S(1)}, u32[]{:S(2)}, u32[]{:S(2)}) collective-permute-start(bf16[256,1024]{1,0:T(8,128)(2,1)S(1)} %pick.5.refs_0_), channel_id=1, source_target_pairs={{0,4},{2,6},{4,0},{6,2},{1,5},{3,7},{5,1},{7,3},{8,12},{10,14},{12... | collective-permute-start | bytes 1572872 | tf_op jit(solution)/shard_map/ppermute | solution.py:58
  117.3 17.8 %collective-permute-start.24 = (bf16[4,256,1024]{2,1,0:T(8,128)(2,1)S(1)}, bf16[4,256,1024]{2,1,0:T(8,128)(2,1)S(1)}, u32[]{:S(2)}, u32[]{:S(2)}) collective-permute-start(bf16[4,256,1024]{2,1,0:T(8,128)(2,1)S(1)} %bundle.4.refs_0_), channel_id=1, source_target_pairs={{0,2},{2,0},{4,6},{6,4},{1,3},{3,1},{5,7},{7,5},{8,10},{10,8},{12,... | collective-permute-start | bytes 6291464 | tf_op jit(solution)/shard_map/ppermute | solution.py:58
  117.5 22.2 %collective-permute-start.23 = (bf16[3,256,1024]{2,1,0:T(8,128)(2,1)S(1)}, bf16[3,256,1024]{2,1,0:T(8,128)(2,1)S(1)}, u32[]{:S(2)}, u32[]{:S(2)}) collective-permute-start(bf16[3,256,1024]{2,1,0:T(8,128)(2,1)S(1)} %bundle.3.refs_0_), channel_id=1, source_target_pairs={{0,2},{2,0},{4,6},{6,4},{1,3},{3,1},{5,7},{7,5},{8,10},{10,8},{12,... | collective-permute-start | bytes 4718600 | tf_op jit(solution)/shard_map/ppermute | solution.py:58
  118.1 15.7 %collective-permute-start.25 = (bf16[256,1024]{1,0:T(8,128)(2,1)S(1)}, bf16[256,1024]{1,0:T(8,128)(2,1)S(1)}, u32[]{:S(2)}, u32[]{:S(2)}) collective-permute-start(bf16[256,1024]{1,0:T(8,128)(2,1)S(1)} %collective-permute-done.18.refs_1_.middle), channel_id=1, source_target_pairs={{8,0},{16,24},{9,1},{17,25},{10,2},{18,26},{11,3},{19,27},{12,4},{... | collective-permute-start | bytes 1572872 | tf_op jit(solution)/shard_map/ppermute | solution.py:54
  119.4 14.5 %collective-permute-start.27 = (bf16[256,1024]{1,0:T(8,128)(2,1)S(1)}, bf16[256,1024]{1,0:T(8,128)(2,1)S(1)}, u32[]{:S(2)}, u32[]{:S(2)}) collective-permute-start(bf16[256,1024]{1,0:T(8,128)(2,1)S(1)} %collective-permute-done.20.refs_1_.middle), channel_id=1, source_target_pairs={{8,16},{16,8},{9,17},{17,9},{10,18},{18,10},{11,19},{19,11},{12,20... | collective-permute-start | bytes 1572872 | tf_op jit(solution)/shard_map/ppermute | solution.py:54
  120.1 21.5 %collective-permute-start.22 = (bf16[256,1024]{1,0:T(8,128)(2,1)S(1)}, bf16[256,1024]{1,0:T(8,128)(2,1)S(1)}, u32[]{:S(2)}, u32[]{:S(2)}) collective-permute-start(bf16[256,1024]{1,0:T(8,128)(2,1)S(1)} %pick.6.refs_2_.refs_4_), channel_id=1, source_target_pairs={{0,4},{2,6},{4,0},{6,2},{1,5},{3,7},{5,1},{7,3},{8,12},{10,14},{12... | collective-permute-start | bytes 1572872 | tf_op jit(solution)/shard_map/ppermute | solution.py:58
  133.9 15.8 %collective-permute-start.28 = (bf16[256,1024]{1,0:T(8,128)(2,1)S(1)}, bf16[256,1024]{1,0:T(8,128)(2,1)S(1)}, u32[]{:S(2)}, u32[]{:S(2)}) collective-permute-start(bf16[256,1024]{1,0:T(8,128)(2,1)S(1)} %collective-permute-done.27.middle), channel_id=1, source_target_pairs={{8,0},{16,24},{9,1},{17,25},{10,2},{18,26},{11,3},{19,27},{12,4},{... | collective-permute-start | bytes 1572872 | tf_op jit(solution)/shard_map/ppermute | solution.py:54
  (15 other events, 337.9 us)

commit v7 on v4

--- a/solution.py
+++ b/solution.py
@@ -236,7 +236,7 @@
 
 
 def up_kernel(groups, tensors, master_up, moment_up, *refs):
-    sums, (stored_up, velocity_up, token) = refs[:tensors], refs[tensors:]
+    sums, (stored_up, velocity_up, token) = refs[:tensors], refs[-3:]
     cols = sums[0].shape[1]
     me = lax.axis_index("tensor")
     for shift in range(tensors):
@@ -277,6 +277,28 @@
     )
 
 
+def join_kernel(top, bottom, out):
+    rows = top.shape[0]
+    out[:rows, :] = top[...]
+    out[rows:, :] = bottom[...]
+
+
+def join(top, bottom):
+    shape = jax.ShapeDtypeStruct((top.shape[0] + bottom.shape[0], top.shape[1]), BF16)
+    return call(join_kernel, "join", shape, [VMEM] * 2, VMEM, [], top, bottom)
+
+
+def tail_kernel(x, *refs):
+    out = refs[-1]
+    out[...] = x[x.shape[0] - out.shape[0] :, :]
+
+
+def tail(x, rows, *after):
+    shape = jax.ShapeDtypeStruct((rows, x.shape[1]), x.dtype)
+    specs = [VMEM] + [ANY] * len(after)
+    return call(tail_kernel, "tail", shape, specs, VMEM, [], x, *after)
+
+
 def stack_kernel(count, *refs):
     for i in range(count):
         refs[-1][i] = refs[i][...]
@@ -321,7 +343,8 @@
 
 
 def place_embed_kernel(slots, *refs):
-    pieces, (out, sems) = refs[: len(slots)], refs[-2:]
+    pieces, (out, token, sems) = refs[: len(slots)], refs[-3:]
+    token[...] = jnp.zeros_like(token)
     copies = [
         pltpu.make_async_copy(piece, out.at[owners()[slot]], sems.at[i])
         for i, (piece, slot) in enumerate(zip(pieces, slots))
@@ -395,7 +418,7 @@
     packets_came = [swap(packets[0], "replica", 1), swap(packets[1], "replica", 2)]
     end = gate(end, packets_came[0])
     packets_came.append(swap(gate(packets[2], end), "replica", 3))
-    from_end = [along(x, INWARD) for x in (end, middle, near)]
+    from_end = [along(end, INWARD)]
 
     state = jax.ShapeDtypeStruct((2, rows_up, half_cols), F32)
     states = call(
@@ -445,11 +468,14 @@
 
     embed_out = along(recast_rows, OUTWARD)
     embed_middle = along(recast_rows, ACROSS)
-    end_partial = along(add(end, from_end[0], embed_middle), ACROSS)
+    end_sum = gate(add(end, from_end[0]), embed_out, embed_middle)
+    end_partial = along(end_sum, ACROSS)
+    from_end.append(along(middle, INWARD))
     middle_partial = along(add(middle, from_end[1]), ACROSS)
+    from_near = along(join(near, recast_rows), INWARD)
     embed_middle_out = along(embed_middle, OUTWARD)
-    to_end = along(add(near, end_partial, embed_out, embed_middle_out), OUTWARD)
-    came0 = [own, from_end[2], middle_partial, to_end]
+    to_end = along(add(near, end_partial, embed_middle_out), OUTWARD)
+    came0 = [own, from_near, middle_partial, to_end]
     half_sum = jax.ShapeDtypeStruct((rows_up, half_cols), F32)
     down_state = jax.ShapeDtypeStruct((rows_down, width), F32)
     piece, stored_down, velocity_down, *sums = call(
@@ -468,23 +494,26 @@
     )
 
     top = shards // 2
+    came_near = swap(piece, "replica", 1)
+    middle_piece = along(piece, ACROSS)
     far_piece = swap(piece, "shard", top)
-    middle_piece = along(piece, ACROSS)
-    near_piece = gate(swap(piece, "replica", 1), far_piece, middle_piece)
+    end_piece = along(came_near, ACROSS)
+    second_out = along(middle_piece, OUTWARD)
+    near_piece = gate(came_near, far_piece)
     far_near = swap(near_piece, "shard", top)
-    end_piece = along(near_piece, ACROSS)
-    embed_in = along(gate(recast_rows, piece), INWARD)
     sums = [sums[0]] + [
         lax.ppermute(
             gate(x, near_piece), "tensor", [(i, (i + shift) % tensors) for i in range(tensors)]
         )
         for shift, x in enumerate(sums[1:], 1)
     ]
-    second = pick(middle_piece, along(middle_piece, OUTWARD), far_near, embed_in)
+    second = pick(middle_piece, second_out, far_near)
     far_second = swap(second, "shard", top)
+    embed_in = tail(from_near, rows_embed, near_piece)
     embed_end = along(embed_in, ACROSS)
-    third = pick(end_piece, along(end_piece, OUTWARD), embed_end, far_second, *sums[1:])
+    third = pick(end_piece, along(end_piece, OUTWARD), far_second, embed_end, *sums[1:])
     far_third = swap(third, "shard", top)
+    embed_last = along(embed_end, OUTWARD)
     bundles = [
         (
             [(0, 0), (0, top), (1, 0), (1, top)],
@@ -496,27 +525,26 @@
         ),
     ]
 
-    embed_last = along(embed_end, OUTWARD)
-
     stored_up, velocity_up, token = call(
         functools.partial(up_kernel, replicas, tensors),
         "update_up",
         [jax.ShapeDtypeStruct(master_up.shape, F32)] * 2 + [token_shape],
-        [VMEM] * (2 + tensors),
+        [VMEM] * (2 + tensors) + [ANY],
         [VMEM] * 3,
         [],
         master_up,
         moment_up,
         *sums,
+        list(bundles[0][1].values())[-1],
     )
 
     embed_shape = jax.ShapeDtypeStruct((replicas, rows_embed, width), BF16)
-    recast_embed = call(
+    recast_embed, token = call(
         functools.partial(place_embed_kernel, [0, 1, 2]),
         "place_embed",
-        embed_shape,
+        [embed_shape, token_shape],
         [VMEM] * 4,
-        HBM,
+        [HBM, VMEM],
         [dma((3,))],
         recast_rows,
         pick(embed_in, embed_out),
@@ -546,19 +574,19 @@
     for slots, arrays in bundles:
         *placed, token = place(slots, arrays, placed, token)
     last = spread_low(bundle([far_third], token))
-    recast_down, recast_up, token = place([(3, top)], last, placed)
-    recast_embed = call(
+    recast_embed, token = call(
         functools.partial(place_embed_kernel, [3]),
         "place_embed",
-        embed_shape,
+        [embed_shape, token_shape],
         [VMEM] * 2 + [HBM],
-        HBM,
+        [HBM, VMEM],
         [dma((1,))],
         pick(embed_end, embed_last),
-        token,
+        last[0],
         recast_embed,
         aliases={2: 0},
     )
+    recast_down, recast_up, _ = place([(3, top)], last, placed, token)
 
     return (
         recast_up.reshape(-1, half_cols),

time: 128 us -> 123 us (0.961)
  starting transfers between devices: 41.1 us -> 38.2 us
  waiting for transfers between devices: 66.8 us -> 64.2 us
    ppermute x16 -> x15, waiting for transfers between devices: 43.3 us -> 36.8 us  [along(): return lax.ppermute(x, 'replica', pairs)]
    ppermute x1, waiting for transfers between devices: 0.01 us -> 2.92 us  [body(): lax.ppermute(x, 'tensor', [(i, (i + shift) % tensors) for i in range(tens...]
    ppermute x16 -> x15, starting transfers between devices: 23.2 us -> 20.6 us  [along(): return lax.ppermute(x, 'replica', pairs)]
    pallas_call x27 -> x29, Pallas kernels: 17.2 us -> 17.9 us  [call(): pl.pallas_call(kernel, name=name, out_shape=out_shape, in_specs=in_specs,...]
  transfers between devices with their start and end apart: 29 -> 28, of which waited for: 16 -> 17; matrix products, arithmetic and copies ran while one was open for 1% -> 1% of each run, Pallas kernels for 9% -> 10%
where the time goes in v7:
time: 123 us; the launch traced here: 122 us
  waiting for transfers between devices  64.2 us (52%)
  starting transfers between devices  38.2 us (31%)
  Pallas kernels  17.9 us (15%)
    ppermute x15, waiting for transfers between devices, along(): return lax.ppermute(x, 'replica', pairs)  36.8 us
    ppermute x15, starting transfers between devices, along(): return lax.ppermute(x, 'replica', pairs)  20.6 us
    ppermute x11, waiting for transfers between devices, swap(): lax.ppermute(x, axis, [(i, i ^ bit) for i in range(lax.axis_size(axis))])  19.6 us
    pallas_call x29, Pallas kernels, call(): pl.pallas_call(kernel, name=name, out_shape=out_shape, in_specs=in_specs,...  17.9 us
    ppermute x11, starting transfers between devices, swap(): lax.ppermute(x, axis, [(i, i ^ bit) for i in range(lax.axis_size(axis))])  14.5 us
    ppermute x1, waiting for transfers between devices, body(): lax.ppermute(gate(x, near_piece), 'tensor', [(i, (i + shift) % tensors) f...  4.87 us
    ppermute x1, waiting for transfers between devices, body(): lax.ppermute(x, 'tensor', [(i, (i + shift) % tensors) for i in range(tens...  2.92 us
  transfers between devices with their start and end apart: 28, of which 17 were waited for; matrix products, arithmetic and copies ran while one was open for 1% of the time, Pallas kernels for 10%

profile of v7, /device:TPU:0, one launch (start us, length us, event | category | flops | bytes accessed | tf_op | source)
XLA Modules:
  0.0 122.5 jit_solution(16590552933370648209)
XLA Ops:
  0.6 2.6 %project_rows.1 = (f32[64,256]{1,0:T(8,128)S(1)}, bf16[80,256]{1,0:T(8,128)(2,1)S(1)}, bf16[80,256]{1,0:T(8,128)(2,1)S(1)}, bf16[80,256]{1,0:T(8,128)(2,1)S(1)}) custom-call(bf16[1024,1024]{1,0:T(8,128)(2,1)} %bitcast.35, f32[64,1024]{1,0:T(8,128)} %bitcast.24, bf16[2,1024]{1,0:T(2,128)(2,1)} %bitcast.29), custom_call_target="tpu_custom_call" | custom-call | bytes 565248 | tf_op jit(solution)/shard_map/project_rows/pallas_call | solution.py:26
  3.2 3.1 %collective-permute-start = (bf16[80,256]{1,0:T(8,128)(2,1)S(1)}, bf16[80,256]{1,0:T(8,128)(2,1)S(1)}, u32[]{:S(2)}, u32[]{:S(2)}) collective-permute-start(bf16[80,256]{1,0:T(8,128)(2,1)S(1)} %get-tuple-element.49), channel_id=1, source_target_pairs={{0,8},{8,0},{16,24},{24,16},{1,9},{9,1},{17,25},{25,17},{2,10},{10... | collective-permute-start | bytes 122888 | tf_op jit(solution)/shard_map/ppermute | solution.py:56
  6.3 2.6 %collective-permute-start.1 = (bf16[80,256]{1,0:T(8,128)(2,1)S(1)}, bf16[80,256]{1,0:T(8,128)(2,1)S(1)}, u32[]{:S(2)}, u32[]{:S(2)}) collective-permute-start(bf16[80,256]{1,0:T(8,128)(2,1)S(1)} %get-tuple-element.50), channel_id=1, source_target_pairs={{0,16},{8,24},{16,0},{24,8},{1,17},{9,25},{17,1},{25,9},{2,18},{10... | collective-permute-start | bytes 122888 | tf_op jit(solution)/shard_map/ppermute | solution.py:56
  8.9 1.8 %pack_blocks.1 = (bf16[256,1024]{1,0:T(8,128)(2,1)S(1)}, bf16[256,1024]{1,0:T(8,128)(2,1)S(1)}, bf16[256,1024]{1,0:T(8,128)(2,1)S(1)}, bf16[256,1024]{1,0:T(8,128)(2,1)S(1)}) custom-call(bf16[4,4,128,1024]{3,2,1,0:T(8,128)(2,1)} %bitcast.33, bf16[4,4,64,2048]{3,2,1,0:T(8,128)(2,1)} %bitcast.34), custom_call_target="tpu_custom_call" | custom-call | bytes 6291456 | tf_op jit(solution)/shard_map/pack_blocks/pallas_call | solution.py:26
  10.8 2.1 %collective-permute-start.2 = (bf16[80,256]{1,0:T(8,128)(2,1)S(1)}, bf16[80,256]{1,0:T(8,128)(2,1)S(1)}, u32[]{:S(2)}, u32[]{:S(2)}) collective-permute-start(bf16[80,256]{1,0:T(8,128)(2,1)S(1)} %gate.6), channel_id=1, source_target_pairs={{0,24},{8,16},{16,8},{24,0},{1,25},{9,17},{17,9},{25,1},{2,26},{10... | collective-permute-start | bytes 122888 | tf_op jit(solution)/shard_map/ppermute | solution.py:56
  16.7 2.0 %embed_update.1 = (f32[256,1024]{1,0:T(8,128)}, bf16[256,1024]{1,0:T(8,128)(2,1)S(1)}, f32[64,256]{1,0:T(8,128)}, bf16[2,1024]{1,0:T(2,128)(2,1)}, f32[2,1024]{1,0:T(2,128)}, /*index=5*/f32[2,1024]{1,0:T(2,128)}) custom-call(f32[64,256]{1,0:T(8,128)S(1)} %get-tuple-element.48.refs_0_, f32[64,256]{1,0:T(8,128)S(1)} %fusion.refs_1_, f32[256,1024]{1,0:T(8,128)S(1)} %bitcast.23, ...), custom_call_target="tpu_custom_call" | custom-call | bytes 4976640 | tf_op jit(solution)/shard_map/embed_update/pallas_call | solution.py:26
  20.7 4.6 %collective-permute-start.4 = (bf16[256,1024]{1,0:T(8,128)(2,1)S(1)}, bf16[256,1024]{1,0:T(8,128)(2,1)S(1)}, u32[]{:S(2)}, u32[]{:S(2)}) collective-permute-start(bf16[256,1024]{1,0:T(8,128)(2,1)S(1)} %get-tuple-element.54.block), channel_id=1, source_target_pairs={{0,8},{24,16},{1,9},{25,17},{2,10},{26,18},{3,11},{27,19},{4,12},{... | collective-permute-start | bytes 1572872 | tf_op jit(solution)/shard_map/ppermute | solution.py:52
  25.4 2.2 %collective-permute-done.6.came = bf16[256,1024]{1,0:T(8,128)(2,1)S(1)} collective-permute-done((bf16[256,1024]{1,0:T(8,128)(2,1)S(1)}, bf16[256,1024]{1,0:T(8,128)(2,1)S(1)}, u32[]{:S(2)}, u32[]{:S(2)}) %collective-permute-start.6) | collective-permute-done | bytes 524320 | tf_op jit(solution)/shard_map/ppermute | solution.py:52
  29.0 7.1 %collective-permute-done.7.refs_0_.end = bf16[256,1024]{1,0:T(8,128)(2,1)S(1)} collective-permute-done((bf16[256,1024]{1,0:T(8,128)(2,1)S(1)}, bf16[256,1024]{1,0:T(8,128)(2,1)S(1)}, u32[]{:S(2)}, u32[]{:S(2)}) %collective-permute-start.7) | collective-permute-done | bytes 524320 | tf_op jit(solution)/shard_map/ppermute | solution.py:52
  36.9 2.7 %collective-permute-start.3 = (bf16[512,1024]{1,0:T(8,128)(2,1)S(1)}, bf16[512,1024]{1,0:T(8,128)(2,1)S(1)}, u32[]{:S(2)}, u32[]{:S(2)}) collective-permute-start(bf16[512,1024]{1,0:T(8,128)(2,1)S(1)} %join.1), channel_id=1, source_target_pairs={{0,8},{24,16},{1,9},{25,17},{2,10},{26,18},{3,11},{27,19},{4,12},{... | collective-permute-start | bytes 3145736 | tf_op jit(solution)/shard_map/ppermute | solution.py:52
  42.1 2.5 %collective-permute-done.10.refs_0_.end = bf16[256,1024]{1,0:T(8,128)(2,1)S(1)} collective-permute-done((bf16[256,1024]{1,0:T(8,128)(2,1)S(1)}, bf16[256,1024]{1,0:T(8,128)(2,1)S(1)}, u32[]{:S(2)}, u32[]{:S(2)}) %collective-permute-start.10) | collective-permute-done | bytes 524320 | tf_op jit(solution)/shard_map/ppermute | solution.py:52
  46.0 2.9 %collective-permute-done.12.refs_8_ = f32[2,32,2048]{2,1,0:T(8,128)S(1)} collective-permute-done((f32[2,32,2048]{2,1,0:T(8,128)S(1)}, f32[2,32,2048]{2,1,0:T(8,128)S(1)}, u32[]{:S(2)}, u32[]{:S(2)}) %collective-permute-start.12) | collective-permute-done | bytes 524320 | tf_op jit(solution)/shard_map/ppermute | solution.py:435
  49.0 10.2 %collective-permute-done.3.refs_5_.x = bf16[512,1024]{1,0:T(8,128)(2,1)S(1)} collective-permute-done((bf16[512,1024]{1,0:T(8,128)(2,1)S(1)}, bf16[512,1024]{1,0:T(8,128)(2,1)S(1)}, u32[]{:S(2)}, u32[]{:S(2)}) %collective-permute-start.3) | collective-permute-done | bytes 1048608 | tf_op jit(solution)/shard_map/ppermute | solution.py:52
  64.4 3.8 %collective-permute-start.13 = (bf16[256,1024]{1,0:T(8,128)(2,1)S(1)}, bf16[256,1024]{1,0:T(8,128)(2,1)S(1)}, u32[]{:S(2)}, u32[]{:S(2)}) collective-permute-start(bf16[256,1024]{1,0:T(8,128)(2,1)S(1)} %get-tuple-element.55.refs_0_), channel_id=1, source_target_pairs={{0,8},{8,0},{16,24},{24,16},{1,9},{9,1},{17,25},{25,17},{2,10},{10... | collective-permute-start | bytes 1572872 | tf_op jit(solution)/shard_map/ppermute | solution.py:56
  69.5 2.6 %collective-permute-done.18.refs_0_.refs_1_ = bf16[256,1024]{1,0:T(8,128)(2,1)S(1)} collective-permute-done((bf16[256,1024]{1,0:T(8,128)(2,1)S(1)}, bf16[256,1024]{1,0:T(8,128)(2,1)S(1)}, u32[]{:S(2)}, u32[]{:S(2)}) %collective-permute-start.18) | collective-permute-done | bytes 524320 | tf_op jit(solution)/shard_map/ppermute | solution.py:56
  72.0 5.9 %collective-permute-done.13.x = bf16[256,1024]{1,0:T(8,128)(2,1)S(1)} collective-permute-done((bf16[256,1024]{1,0:T(8,128)(2,1)S(1)}, bf16[256,1024]{1,0:T(8,128)(2,1)S(1)}, u32[]{:S(2)}, u32[]{:S(2)}) %collective-permute-start.13) | collective-permute-done | bytes 524320 | tf_op jit(solution)/shard_map/ppermute | solution.py:56
  79.5 7.0 %collective-permute-done.17.end = bf16[256,1024]{1,0:T(8,128)(2,1)S(1)} collective-permute-done((bf16[256,1024]{1,0:T(8,128)(2,1)S(1)}, bf16[256,1024]{1,0:T(8,128)(2,1)S(1)}, u32[]{:S(2)}, u32[]{:S(2)}) %collective-permute-start.17) | collective-permute-done | bytes 524320 | tf_op jit(solution)/shard_map/ppermute | solution.py:52
  90.9 4.9 %collective-permute-done.22.refs_2_.refs_1_ = f32[32,2048]{1,0:T(8,128)S(1)} collective-permute-done((f32[32,2048]{1,0:T(8,128)S(1)}, f32[32,2048]{1,0:T(8,128)S(1)}, u32[]{:S(2)}, u32[]{:S(2)}) %collective-permute-start.22) | collective-permute-done | bytes 262176 | tf_op jit(solution)/shard_map/ppermute | solution.py:505
  95.8 2.7 %collective-permute-done.20.refs_0_.refs_1_ = bf16[256,1024]{1,0:T(8,128)(2,1)S(1)} collective-permute-done((bf16[256,1024]{1,0:T(8,128)(2,1)S(1)}, bf16[256,1024]{1,0:T(8,128)(2,1)S(1)}, u32[]{:S(2)}, u32[]{:S(2)}) %collective-permute-start.20) | collective-permute-done | bytes 524320 | tf_op jit(solution)/shard_map/ppermute | solution.py:56
  98.5 4.5 %collective-permute-done.15.end = bf16[256,1024]{1,0:T(8,128)(2,1)S(1)} collective-permute-done((bf16[256,1024]{1,0:T(8,128)(2,1)S(1)}, bf16[256,1024]{1,0:T(8,128)(2,1)S(1)}, u32[]{:S(2)}, u32[]{:S(2)}) %collective-permute-start.15) | collective-permute-done | bytes 524320 | tf_op jit(solution)/shard_map/ppermute | solution.py:52
  109.6 2.2 %place_rows.3 = (bf16[4,4,128,1024]{3,2,1,0:T(8,128)(2,1)}, bf16[4,4,64,2048]{3,2,1,0:T(8,128)(2,1)}, f32[8,128]{1,0:T(8,128)S(1)}) custom-call(bf16[4,256,1024]{2,1,0:T(8,128)(2,1)S(1)} %bundle.4.refs_0_, bf16[4,256,1024]{2,1,0:T(8,128)(2,1)S(1)} %collective-permute-done.25.refs_2_.refs_1_, f32[8,128]{1,0:T(8,128)S(1)} %get-tuple-element.59.refs_2_), custom_call_target="tpu_custom_call" | custom-call | bytes 25178112 | tf_op jit(solution)/shard_map/place_rows/pallas_call | solution.py:26
  111.9 1.8 %place_rows.4 = (bf16[4,4,128,1024]{3,2,1,0:T(8,128)(2,1)}, bf16[4,4,64,2048]{3,2,1,0:T(8,128)(2,1)}, f32[8,128]{1,0:T(8,128)S(1)}) custom-call(bf16[3,256,1024]{2,1,0:T(8,128)(2,1)S(1)} %bundle.3.refs_0_, bf16[3,256,1024]{2,1,0:T(8,128)(2,1)S(1)} %collective-permute-done.24.refs_1_, ...), custom_call_target="tpu_custom_call", output_to_operand_aliasing={{0}: (3, {}), {1}: (4, {})} | custom-call | bytes 25178112 | tf_op jit(solution)/shard_map/place_rows/pallas_call | solution.py:26
  113.7 4.1 %collective-permute-done.23.refs_0_ = bf16[256,1024]{1,0:T(8,128)(2,1)S(1)} collective-permute-done((bf16[256,1024]{1,0:T(8,128)(2,1)S(1)}, bf16[256,1024]{1,0:T(8,128)(2,1)S(1)}, u32[]{:S(2)}, u32[]{:S(2)}) %collective-permute-start.23) | collective-permute-done | bytes 524320 | tf_op jit(solution)/shard_map/ppermute | solution.py:56
  117.9 2.1 %collective-permute-done.27.end = bf16[256,1024]{1,0:T(8,128)(2,1)S(1)} collective-permute-done((bf16[256,1024]{1,0:T(8,128)(2,1)S(1)}, bf16[256,1024]{1,0:T(8,128)(2,1)S(1)}, u32[]{:S(2)}, u32[]{:S(2)}) %collective-permute-start.27) | collective-permute-done | bytes 524320 | tf_op jit(solution)/shard_map/ppermute | solution.py:52
  (82 shorter events, 33.4 us)
Async XLA Ops:
  3.2 7.5 %collective-permute-start = (bf16[80,256]{1,0:T(8,128)(2,1)S(1)}, bf16[80,256]{1,0:T(8,128)(2,1)S(1)}, u32[]{:S(2)}, u32[]{:S(2)}) collective-permute-start(bf16[80,256]{1,0:T(8,128)(2,1)S(1)} %get-tuple-element.49), channel_id=1, source_target_pairs={{0,8},{8,0},{16,24},{24,16},{1,9},{9,1},{17,25},{25,17},{2,10},{10... | collective-permute-start | bytes 122888 | tf_op jit(solution)/shard_map/ppermute | solution.py:56
  6.3 9.0 %collective-permute-start.1 = (bf16[80,256]{1,0:T(8,128)(2,1)S(1)}, bf16[80,256]{1,0:T(8,128)(2,1)S(1)}, u32[]{:S(2)}, u32[]{:S(2)}) collective-permute-start(bf16[80,256]{1,0:T(8,128)(2,1)S(1)} %get-tuple-element.50), channel_id=1, source_target_pairs={{0,16},{8,24},{16,0},{24,8},{1,17},{9,25},{17,1},{25,9},{2,18},{10... | collective-permute-start | bytes 122888 | tf_op jit(solution)/shard_map/ppermute | solution.py:56
  13.9 13.7 %collective-permute-start.6 = (bf16[256,1024]{1,0:T(8,128)(2,1)S(1)}, bf16[256,1024]{1,0:T(8,128)(2,1)S(1)}, u32[]{:S(2)}, u32[]{:S(2)}) collective-permute-start(bf16[256,1024]{1,0:T(8,128)(2,1)S(1)} %gate.5.refs_0_.block), channel_id=1, source_target_pairs={{0,8},{24,16},{1,9},{25,17},{2,10},{26,18},{3,11},{27,19},{4,12},{... | collective-permute-start | bytes 1572872 | tf_op jit(solution)/shard_map/ppermute | solution.py:52
  18.7 9.0 %collective-permute-start.8 = (bf16[256,1024]{1,0:T(8,128)(2,1)S(1)}, bf16[256,1024]{1,0:T(8,128)(2,1)S(1)}, u32[]{:S(2)}, u32[]{:S(2)}) collective-permute-start(bf16[256,1024]{1,0:T(8,128)(2,1)S(1)} %get-tuple-element.53.bottom.refs_0_), channel_id=1, source_target_pairs={{8,16},{16,8},{9,17},{17,9},{10,18},{18,10},{11,19},{19,11},{12,20... | collective-permute-start | bytes 1572872 | tf_op jit(solution)/shard_map/ppermute | solution.py:52
  19.4 16.8 %collective-permute-start.7 = (bf16[256,1024]{1,0:T(8,128)(2,1)S(1)}, bf16[256,1024]{1,0:T(8,128)(2,1)S(1)}, u32[]{:S(2)}, u32[]{:S(2)}) collective-permute-start(bf16[256,1024]{1,0:T(8,128)(2,1)S(1)} %get-tuple-element.53.bottom.refs_0_), channel_id=1, source_target_pairs={{8,0},{16,24},{9,1},{17,25},{10,2},{18,26},{11,3},{19,27},{12,4},{... | collective-permute-start | bytes 1572872 | tf_op jit(solution)/shard_map/ppermute | solution.py:52
  20.7 20.6 %collective-permute-start.4 = (bf16[256,1024]{1,0:T(8,128)(2,1)S(1)}, bf16[256,1024]{1,0:T(8,128)(2,1)S(1)}, u32[]{:S(2)}, u32[]{:S(2)}) collective-permute-start(bf16[256,1024]{1,0:T(8,128)(2,1)S(1)} %get-tuple-element.54.block), channel_id=1, source_target_pairs={{0,8},{24,16},{1,9},{25,17},{2,10},{26,18},{3,11},{27,19},{4,12},{... | collective-permute-start | bytes 1572872 | tf_op jit(solution)/shard_map/ppermute | solution.py:52
  27.7 16.9 %collective-permute-start.10 = (bf16[256,1024]{1,0:T(8,128)(2,1)S(1)}, bf16[256,1024]{1,0:T(8,128)(2,1)S(1)}, u32[]{:S(2)}, u32[]{:S(2)}) collective-permute-start(bf16[256,1024]{1,0:T(8,128)(2,1)S(1)} %collective-permute-done.8.refs_1_.middle), channel_id=1, source_target_pairs={{8,0},{16,24},{9,1},{17,25},{10,2},{18,26},{11,3},{19,27},{12,4},{... | collective-permute-start | bytes 1572872 | tf_op jit(solution)/shard_map/ppermute | solution.py:52
  36.2 8.4 %collective-permute-start.9 = (bf16[256,1024]{1,0:T(8,128)(2,1)S(1)}, bf16[256,1024]{1,0:T(8,128)(2,1)S(1)}, u32[]{:S(2)}, u32[]{:S(2)}) collective-permute-start(bf16[256,1024]{1,0:T(8,128)(2,1)S(1)} %gate.7), channel_id=1, source_target_pairs={{8,16},{16,8},{9,17},{17,9},{10,18},{18,10},{11,19},{19,11},{12,20... | collective-permute-start | bytes 1572872 | tf_op jit(solution)/shard_map/ppermute | solution.py:52
  36.9 22.3 %collective-permute-start.3 = (bf16[512,1024]{1,0:T(8,128)(2,1)S(1)}, bf16[512,1024]{1,0:T(8,128)(2,1)S(1)}, u32[]{:S(2)}, u32[]{:S(2)}) collective-permute-start(bf16[512,1024]{1,0:T(8,128)(2,1)S(1)} %join.1), channel_id=1, source_target_pairs={{0,8},{24,16},{1,9},{25,17},{2,10},{26,18},{3,11},{27,19},{4,12},{... | collective-permute-start | bytes 3145736 | tf_op jit(solution)/shard_map/ppermute | solution.py:52
  39.7 9.2 %collective-permute-start.12 = (f32[2,32,2048]{2,1,0:T(8,128)S(1)}, f32[2,32,2048]{2,1,0:T(8,128)S(1)}, u32[]{:S(2)}, u32[]{:S(2)}) collective-permute-start(f32[2,32,2048]{2,1,0:T(8,128)S(1)} %up_state.1), channel_id=1, source_target_pairs={{0,1},{1,0},{2,3},{3,2},{4,5},{5,4},{6,7},{7,6},{8,9},{9,8},{10,11... | collective-permute-start | bytes 1572872 | tf_op jit(solution)/shard_map/ppermute | solution.py:435
  41.4 7.6 %collective-permute-start.5 = (bf16[256,1024]{1,0:T(8,128)(2,1)S(1)}, bf16[256,1024]{1,0:T(8,128)(2,1)S(1)}, u32[]{:S(2)}, u32[]{:S(2)}) collective-permute-start(bf16[256,1024]{1,0:T(8,128)(2,1)S(1)} %add_block.3), channel_id=1, source_target_pairs={{8,16},{16,8},{9,17},{17,9},{10,18},{18,10},{11,19},{19,11},{12,20... | collective-permute-start | bytes 1572872 | tf_op jit(solution)/shard_map/ppermute | solution.py:52
  44.7 15.6 %collective-permute-start.11 = (bf16[256,1024]{1,0:T(8,128)(2,1)S(1)}, bf16[256,1024]{1,0:T(8,128)(2,1)S(1)}, u32[]{:S(2)}, u32[]{:S(2)}) collective-permute-start(bf16[256,1024]{1,0:T(8,128)(2,1)S(1)} %add_block.5), channel_id=1, source_target_pairs={{8,0},{16,24},{9,1},{17,25},{10,2},{18,26},{11,3},{19,27},{12,4},{... | collective-permute-start | bytes 1572872 | tf_op jit(solution)/shard_map/ppermute | solution.py:52
  62.8 9.2 %collective-permute-start.18 = (bf16[256,1024]{1,0:T(8,128)(2,1)S(1)}, bf16[256,1024]{1,0:T(8,128)(2,1)S(1)}, u32[]{:S(2)}, u32[]{:S(2)}) collective-permute-start(bf16[256,1024]{1,0:T(8,128)(2,1)S(1)} %get-tuple-element.55.refs_0_), channel_id=1, source_target_pairs={{0,4},{2,6},{4,0},{6,2},{1,5},{3,7},{5,1},{7,3},{8,12},{10,14},{12... | collective-permute-start | bytes 1572872 | tf_op jit(solution)/shard_map/ppermute | solution.py:56
  64.4 13.6 %collective-permute-start.13 = (bf16[256,1024]{1,0:T(8,128)(2,1)S(1)}, bf16[256,1024]{1,0:T(8,128)(2,1)S(1)}, u32[]{:S(2)}, u32[]{:S(2)}) collective-permute-start(bf16[256,1024]{1,0:T(8,128)(2,1)S(1)} %get-tuple-element.55.refs_0_), channel_id=1, source_target_pairs={{0,8},{8,0},{16,24},{24,16},{1,9},{9,1},{17,25},{25,17},{2,10},{10... | collective-permute-start | bytes 1572872 | tf_op jit(solution)/shard_map/ppermute | solution.py:56
  68.2 18.4 %collective-permute-start.17 = (bf16[256,1024]{1,0:T(8,128)(2,1)S(1)}, bf16[256,1024]{1,0:T(8,128)(2,1)S(1)}, u32[]{:S(2)}, u32[]{:S(2)}) collective-permute-start(bf16[256,1024]{1,0:T(8,128)(2,1)S(1)} %collective-permute-done.16.middle), channel_id=1, source_target_pairs={{8,0},{16,24},{9,1},{17,25},{10,2},{18,26},{11,3},{19,27},{12,4},{... | collective-permute-start | bytes 1572872 | tf_op jit(solution)/shard_map/ppermute | solution.py:52
  78.0 9.9 %collective-permute-start.19 = (bf16[256,1024]{1,0:T(8,128)(2,1)S(1)}, bf16[256,1024]{1,0:T(8,128)(2,1)S(1)}, u32[]{:S(2)}, u32[]{:S(2)}) collective-permute-start(bf16[256,1024]{1,0:T(8,128)(2,1)S(1)} %gate.8.refs_0_.refs_2_), channel_id=1, source_target_pairs={{0,4},{2,6},{4,0},{6,2},{1,5},{3,7},{5,1},{7,3},{8,12},{10,14},{12... | collective-permute-start | bytes 1572872 | tf_op jit(solution)/shard_map/ppermute | solution.py:56
  78.1 9.9 %collective-permute-start.14 = (bf16[256,1024]{1,0:T(8,128)(2,1)S(1)}, bf16[256,1024]{1,0:T(8,128)(2,1)S(1)}, u32[]{:S(2)}, u32[]{:S(2)}) collective-permute-start(bf16[256,1024]{1,0:T(8,128)(2,1)S(1)} %collective-permute-done.13.x), channel_id=1, source_target_pairs={{8,16},{16,8},{9,17},{17,9},{10,18},{18,10},{11,19},{19,11},{12,20... | collective-permute-start | bytes 1572872 | tf_op jit(solution)/shard_map/ppermute | solution.py:52
  78.8 16.9 %collective-permute-start.21 = (bf16[256,1024]{1,0:T(8,128)(2,1)S(1)}, bf16[256,1024]{1,0:T(8,128)(2,1)S(1)}, u32[]{:S(2)}, u32[]{:S(2)}) collective-permute-start(bf16[256,1024]{1,0:T(8,128)(2,1)S(1)} %tail.1.middle), channel_id=1, source_target_pairs={{8,16},{16,8},{9,17},{17,9},{10,18},{18,10},{11,19},{19,11},{12,20... | collective-permute-start | bytes 1572872 | tf_op jit(solution)/shard_map/ppermute | solution.py:52
  87.9 10.6 %collective-permute-start.20 = (bf16[256,1024]{1,0:T(8,128)(2,1)S(1)}, bf16[256,1024]{1,0:T(8,128)(2,1)S(1)}, u32[]{:S(2)}, u32[]{:S(2)}) collective-permute-start(bf16[256,1024]{1,0:T(8,128)(2,1)S(1)} %pick.5.refs_0_), channel_id=1, source_target_pairs={{0,4},{2,6},{4,0},{6,2},{1,5},{3,7},{5,1},{7,3},{8,12},{10,14},{12... | collective-permute-start | bytes 1572872 | tf_op jit(solution)/shard_map/ppermute | solution.py:56
  88.0 14.9 %collective-permute-start.15 = (bf16[256,1024]{1,0:T(8,128)(2,1)S(1)}, bf16[256,1024]{1,0:T(8,128)(2,1)S(1)}, u32[]{:S(2)}, u32[]{:S(2)}) collective-permute-start(bf16[256,1024]{1,0:T(8,128)(2,1)S(1)} %collective-permute-done.14.middle), channel_id=1, source_target_pairs={{8,0},{16,24},{9,1},{17,25},{10,2},{18,26},{11,3},{19,27},{12,4},{... | collective-permute-start | bytes 1572872 | tf_op jit(solution)/shard_map/ppermute | solution.py:52
  89.3 6.4 %collective-permute-start.22 = (f32[32,2048]{1,0:T(8,128)S(1)}, f32[32,2048]{1,0:T(8,128)S(1)}, u32[]{:S(2)}, u32[]{:S(2)}) collective-permute-start(f32[32,2048]{1,0:T(8,128)S(1)} %gate.9), channel_id=1, source_target_pairs={{0,1},{1,0},{2,3},{3,2},{4,5},{5,4},{6,7},{7,6},{8,9},{9,8},{10,11... | collective-permute-start | bytes 786440 | tf_op jit(solution)/shard_map/ppermute | solution.py:505
  103.3 8.5 %collective-permute-start.24 = (bf16[3,256,1024]{2,1,0:T(8,128)(2,1)S(1)}, bf16[3,256,1024]{2,1,0:T(8,128)(2,1)S(1)}, u32[]{:S(2)}, u32[]{:S(2)}) collective-permute-start(bf16[3,256,1024]{2,1,0:T(8,128)(2,1)S(1)} %bundle.3.refs_0_), channel_id=1, source_target_pairs={{0,2},{2,0},{4,6},{6,4},{1,3},{3,1},{5,7},{7,5},{8,10},{10,8},{12,... | collective-permute-start | bytes 4718600 | tf_op jit(solution)/shard_map/ppermute | solution.py:56
  103.9 13.9 %collective-permute-start.23 = (bf16[256,1024]{1,0:T(8,128)(2,1)S(1)}, bf16[256,1024]{1,0:T(8,128)(2,1)S(1)}, u32[]{:S(2)}, u32[]{:S(2)}) collective-permute-start(bf16[256,1024]{1,0:T(8,128)(2,1)S(1)} %pick.6.refs_2_.refs_4_), channel_id=1, source_target_pairs={{0,4},{2,6},{4,0},{6,2},{1,5},{3,7},{5,1},{7,3},{8,12},{10,14},{12... | collective-permute-start | bytes 1572872 | tf_op jit(solution)/shard_map/ppermute | solution.py:56
  104.5 15.5 %collective-permute-start.27 = (bf16[256,1024]{1,0:T(8,128)(2,1)S(1)}, bf16[256,1024]{1,0:T(8,128)(2,1)S(1)}, u32[]{:S(2)}, u32[]{:S(2)}) collective-permute-start(bf16[256,1024]{1,0:T(8,128)(2,1)S(1)} %collective-permute-done.21.refs_1_.middle), channel_id=1, source_target_pairs={{8,0},{16,24},{9,1},{17,25},{10,2},{18,26},{11,3},{19,27},{12,4},{... | collective-permute-start | bytes 1572872 | tf_op jit(solution)/shard_map/ppermute | solution.py:52
  (14 other events, 185.9 us)

commit v8 on v7

--- a/solution.py
+++ b/solution.py
@@ -275,28 +275,6 @@
         x,
         *after,
     )
-
-
-def join_kernel(top, bottom, out):
-    rows = top.shape[0]
-    out[:rows, :] = top[...]
-    out[rows:, :] = bottom[...]
-
-
-def join(top, bottom):
-    shape = jax.ShapeDtypeStruct((top.shape[0] + bottom.shape[0], top.shape[1]), BF16)
-    return call(join_kernel, "join", shape, [VMEM] * 2, VMEM, [], top, bottom)
-
-
-def tail_kernel(x, *refs):
-    out = refs[-1]
-    out[...] = x[x.shape[0] - out.shape[0] :, :]
-
-
-def tail(x, rows, *after):
-    shape = jax.ShapeDtypeStruct((rows, x.shape[1]), x.dtype)
-    specs = [VMEM] + [ANY] * len(after)
-    return call(tail_kernel, "tail", shape, specs, VMEM, [], x, *after)
 
 
 def stack_kernel(count, *refs):
@@ -418,7 +396,7 @@
     packets_came = [swap(packets[0], "replica", 1), swap(packets[1], "replica", 2)]
     end = gate(end, packets_came[0])
     packets_came.append(swap(gate(packets[2], end), "replica", 3))
-    from_end = [along(end, INWARD)]
+    from_end = along(end, INWARD)
 
     state = jax.ShapeDtypeStruct((2, rows_up, half_cols), F32)
     states = call(
@@ -468,11 +446,11 @@
 
     embed_out = along(recast_rows, OUTWARD)
     embed_middle = along(recast_rows, ACROSS)
-    end_sum = gate(add(end, from_end[0]), embed_out, embed_middle)
+    end_sum = gate(add(end, from_end), embed_middle)
     end_partial = along(end_sum, ACROSS)
-    from_end.append(along(middle, INWARD))
-    middle_partial = along(add(middle, from_end[1]), ACROSS)
-    from_near = along(join(near, recast_rows), INWARD)
+    middle_sum = add(middle, along(gate(middle, from_end), INWARD), embed_out)
+    middle_partial = along(middle_sum, ACROSS)
+    from_near = along(gate(near, middle_sum), INWARD)
     embed_middle_out = along(embed_middle, OUTWARD)
     to_end = along(add(near, end_partial, embed_middle_out), OUTWARD)
     came0 = [own, from_near, middle_partial, to_end]
@@ -509,7 +487,7 @@
     ]
     second = pick(middle_piece, second_out, far_near)
     far_second = swap(second, "shard", top)
-    embed_in = tail(from_near, rows_embed, near_piece)
+    embed_in = along(gate(recast_rows, near_piece), INWARD)
     embed_end = along(embed_in, ACROSS)
     third = pick(end_piece, along(end_piece, OUTWARD), far_second, embed_end, *sums[1:])
     far_third = swap(third, "shard", top)

time: 123 us -> 122 us (level)
  waiting for transfers between devices: 64.2 us -> 59.3 us
  starting transfers between devices: 38.2 us -> 42.5 us
    ppermute x15 -> x16, starting transfers between devices: 20.6 us -> 26.3 us  [along(): return lax.ppermute(x, 'replica', pairs)]
    ppermute x1, waiting for transfers between devices: 2.92 us -> 0.01 us  [body(): lax.ppermute(x, 'tensor', [(i, (i + shift) % tensors) for i in range(tens...]
    ppermute x15 -> x16, waiting for transfers between devices: 36.8 us -> 33.9 us  [along(): return lax.ppermute(x, 'replica', pairs)]
    ppermute x11, starting transfers between devices: 14.5 us -> 13 us  [swap(): lax.ppermute(x, axis, [(i, i ^ bit) for i in range(lax.axis_size(axis))])]
    pallas_call x29 -> x30, Pallas kernels: 17.9 us -> 17.9 us  [call(): pl.pallas_call(kernel, name=name, out_shape=out_shape, in_specs=in_specs,...]
  transfers between devices with their start and end apart: 28 -> 29, of which waited for: 17 -> 15; matrix products, arithmetic and copies ran while one was open for 1% -> 1% of each run, Pallas kernels for 10% -> 10%
where the time goes in v8:
time: 122 us
  waiting for transfers between devices  59.3 us (49%)
  starting transfers between devices  42.5 us (35%)
  Pallas kernels  17.9 us (15%)
    ppermute x16, waiting for transfers between devices, along(): return lax.ppermute(x, 'replica', pairs)  33.9 us
    ppermute x16, starting transfers between devices, along(): return lax.ppermute(x, 'replica', pairs)  26.3 us
    ppermute x11, waiting for transfers between devices, swap(): lax.ppermute(x, axis, [(i, i ^ bit) for i in range(lax.axis_size(axis))])  20.6 us
    pallas_call x30, Pallas kernels, call(): pl.pallas_call(kernel, name=name, out_shape=out_shape, in_specs=in_specs,...  17.9 us
    ppermute x11, starting transfers between devices, swap(): lax.ppermute(x, axis, [(i, i ^ bit) for i in range(lax.axis_size(axis))])  13 us
    ppermute x1, waiting for transfers between devices, body(): lax.ppermute(gate(x, near_piece), 'tensor', [(i, (i + shift) % tensors) f...  4.82 us
  transfers between devices with their start and end apart: 29, of which 15 were waited for; matrix products, arithmetic and copies ran while one was open for 1% of the time, Pallas kernels for 10%

profile of v8, /device:TPU:0, one launch (start us, length us, event | category | flops | bytes accessed | tf_op | source)
XLA Modules:
  0.0 122.0 jit_solution(11959715204434457697)
XLA Ops:
  0.6 2.6 %project_rows.1 = (f32[64,256]{1,0:T(8,128)S(1)}, bf16[80,256]{1,0:T(8,128)(2,1)S(1)}, bf16[80,256]{1,0:T(8,128)(2,1)S(1)}, bf16[80,256]{1,0:T(8,128)(2,1)S(1)}) custom-call(bf16[1024,1024]{1,0:T(8,128)(2,1)} %bitcast.35, f32[64,1024]{1,0:T(8,128)} %bitcast.24, bf16[2,1024]{1,0:T(2,128)(2,1)} %bitcast.29), custom_call_target="tpu_custom_call" | custom-call | bytes 565248 | tf_op jit(solution)/shard_map/project_rows/pallas_call | solution.py:26
  3.2 3.1 %collective-permute-start = (bf16[80,256]{1,0:T(8,128)(2,1)S(1)}, bf16[80,256]{1,0:T(8,128)(2,1)S(1)}, u32[]{:S(2)}, u32[]{:S(2)}) collective-permute-start(bf16[80,256]{1,0:T(8,128)(2,1)S(1)} %get-tuple-element.50), channel_id=1, source_target_pairs={{0,8},{8,0},{16,24},{24,16},{1,9},{9,1},{17,25},{25,17},{2,10},{10... | collective-permute-start | bytes 122888 | tf_op jit(solution)/shard_map/ppermute | solution.py:56
  6.3 2.6 %collective-permute-start.3 = (bf16[80,256]{1,0:T(8,128)(2,1)S(1)}, bf16[80,256]{1,0:T(8,128)(2,1)S(1)}, u32[]{:S(2)}, u32[]{:S(2)}) collective-permute-start(bf16[80,256]{1,0:T(8,128)(2,1)S(1)} %get-tuple-element.52), channel_id=1, source_target_pairs={{0,16},{8,24},{16,0},{24,8},{1,17},{9,25},{17,1},{25,9},{2,18},{10... | collective-permute-start | bytes 122888 | tf_op jit(solution)/shard_map/ppermute | solution.py:56
  8.9 1.8 %pack_blocks.1 = (bf16[256,1024]{1,0:T(8,128)(2,1)S(1)}, bf16[256,1024]{1,0:T(8,128)(2,1)S(1)}, bf16[256,1024]{1,0:T(8,128)(2,1)S(1)}, bf16[256,1024]{1,0:T(8,128)(2,1)S(1)}) custom-call(bf16[4,4,128,1024]{3,2,1,0:T(8,128)(2,1)} %bitcast.33, bf16[4,4,64,2048]{3,2,1,0:T(8,128)(2,1)} %bitcast.34), custom_call_target="tpu_custom_call" | custom-call | bytes 6291456 | tf_op jit(solution)/shard_map/pack_blocks/pallas_call | solution.py:26
  10.8 2.1 %collective-permute-start.4 = (bf16[80,256]{1,0:T(8,128)(2,1)S(1)}, bf16[80,256]{1,0:T(8,128)(2,1)S(1)}, u32[]{:S(2)}, u32[]{:S(2)}) collective-permute-start(bf16[80,256]{1,0:T(8,128)(2,1)S(1)} %gate.10), channel_id=1, source_target_pairs={{0,24},{8,16},{16,8},{24,0},{1,25},{9,17},{17,9},{25,1},{2,26},{10... | collective-permute-start | bytes 122888 | tf_op jit(solution)/shard_map/ppermute | solution.py:56
  16.7 2.0 %embed_update.1 = (f32[256,1024]{1,0:T(8,128)}, bf16[256,1024]{1,0:T(8,128)(2,1)S(1)}, f32[64,256]{1,0:T(8,128)}, bf16[2,1024]{1,0:T(2,128)(2,1)}, f32[2,1024]{1,0:T(2,128)}, /*index=5*/f32[2,1024]{1,0:T(2,128)}) custom-call(f32[64,256]{1,0:T(8,128)S(1)} %get-tuple-element.51.refs_0_, f32[64,256]{1,0:T(8,128)S(1)} %fusion.refs_1_, f32[256,1024]{1,0:T(8,128)S(1)} %bitcast.23, ...), custom_call_target="tpu_custom_call" | custom-call | bytes 4976640 | tf_op jit(solution)/shard_map/embed_update/pallas_call | solution.py:26
  20.7 4.8 %collective-permute-done.1.refs_0_.came = bf16[256,1024]{1,0:T(8,128)(2,1)S(1)} collective-permute-done((bf16[256,1024]{1,0:T(8,128)(2,1)S(1)}, bf16[256,1024]{1,0:T(8,128)(2,1)S(1)}, u32[]{:S(2)}, u32[]{:S(2)}) %collective-permute-start.1) | collective-permute-done | bytes 524320 | tf_op jit(solution)/shard_map/ppermute | solution.py:52
  25.5 4.4 %collective-permute-start.2 = (bf16[256,1024]{1,0:T(8,128)(2,1)S(1)}, bf16[256,1024]{1,0:T(8,128)(2,1)S(1)}, u32[]{:S(2)}, u32[]{:S(2)}) collective-permute-start(bf16[256,1024]{1,0:T(8,128)(2,1)S(1)} %gate.9), channel_id=1, source_target_pairs={{0,8},{24,16},{1,9},{25,17},{2,10},{26,18},{3,11},{27,19},{4,12},{... | collective-permute-start | bytes 1572872 | tf_op jit(solution)/shard_map/ppermute | solution.py:52
  34.0 5.3 %collective-permute-done.2.came = bf16[256,1024]{1,0:T(8,128)(2,1)S(1)} collective-permute-done((bf16[256,1024]{1,0:T(8,128)(2,1)S(1)}, bf16[256,1024]{1,0:T(8,128)(2,1)S(1)}, u32[]{:S(2)}, u32[]{:S(2)}) %collective-permute-start.2) | collective-permute-done | bytes 524320 | tf_op jit(solution)/shard_map/ppermute | solution.py:52
  40.2 7.1 %collective-permute-start.6 = (bf16[256,1024]{1,0:T(8,128)(2,1)S(1)}, bf16[256,1024]{1,0:T(8,128)(2,1)S(1)}, u32[]{:S(2)}, u32[]{:S(2)}) collective-permute-start(bf16[256,1024]{1,0:T(8,128)(2,1)S(1)} %gate.11), channel_id=1, source_target_pairs={{0,8},{24,16},{1,9},{25,17},{2,10},{26,18},{3,11},{27,19},{4,12},{... | collective-permute-start | bytes 1572872 | tf_op jit(solution)/shard_map/ppermute | solution.py:52
  48.7 6.8 %collective-permute-done.6.refs_5_ = bf16[256,1024]{1,0:T(8,128)(2,1)S(1)} collective-permute-done((bf16[256,1024]{1,0:T(8,128)(2,1)S(1)}, bf16[256,1024]{1,0:T(8,128)(2,1)S(1)}, u32[]{:S(2)}, u32[]{:S(2)}) %collective-permute-start.6) | collective-permute-done | bytes 524320 | tf_op jit(solution)/shard_map/ppermute | solution.py:52
  55.6 4.3 %collective-permute-done.11.refs_7_ = bf16[256,1024]{1,0:T(8,128)(2,1)S(1)} collective-permute-done((bf16[256,1024]{1,0:T(8,128)(2,1)S(1)}, bf16[256,1024]{1,0:T(8,128)(2,1)S(1)}, u32[]{:S(2)}, u32[]{:S(2)}) %collective-permute-start.11) | collective-permute-done | bytes 524320 | tf_op jit(solution)/shard_map/ppermute | solution.py:52
  59.9 1.7 %update_rows.1 = (bf16[256,1024]{1,0:T(8,128)(2,1)S(1)}, f32[128,1024]{1,0:T(8,128)}, f32[128,1024]{1,0:T(8,128)}, f32[32,2048]{1,0:T(8,128)S(1)}, f32[32,2048]{1,0:T(8,128)S(1)}) custom-call(f32[128,1024]{1,0:T(8,128)S(1)} %bitcast.26, f32[128,1024]{1,0:T(8,128)S(1)} %bitcast.27, f32[32,4096]{1,0:T(8,128)S(1)} %copy-done, f32[32,4096]{1,0:T(8,128)S(1)} %copy-done.1, ...), custom_call_target="tpu_custom_call" | custom-call | bytes 6291456 | tf_op jit(solution)/shard_map/update_rows/pallas_call | solution.py:26
  66.3 7.1 %collective-permute-done.18.refs_0_.refs_1_ = bf16[256,1024]{1,0:T(8,128)(2,1)S(1)} collective-permute-done((bf16[256,1024]{1,0:T(8,128)(2,1)S(1)}, bf16[256,1024]{1,0:T(8,128)(2,1)S(1)}, u32[]{:S(2)}, u32[]{:S(2)}) %collective-permute-start.18) | collective-permute-done | bytes 524320 | tf_op jit(solution)/shard_map/ppermute | solution.py:56
  73.3 3.3 %collective-permute-done.13.x = bf16[256,1024]{1,0:T(8,128)(2,1)S(1)} collective-permute-done((bf16[256,1024]{1,0:T(8,128)(2,1)S(1)}, bf16[256,1024]{1,0:T(8,128)(2,1)S(1)}, u32[]{:S(2)}, u32[]{:S(2)}) %collective-permute-start.13) | collective-permute-done | bytes 524320 | tf_op jit(solution)/shard_map/ppermute | solution.py:56
  79.0 5.4 %collective-permute-done.17.end = bf16[256,1024]{1,0:T(8,128)(2,1)S(1)} collective-permute-done((bf16[256,1024]{1,0:T(8,128)(2,1)S(1)}, bf16[256,1024]{1,0:T(8,128)(2,1)S(1)}, u32[]{:S(2)}, u32[]{:S(2)}) %collective-permute-start.17) | collective-permute-done | bytes 524320 | tf_op jit(solution)/shard_map/ppermute | solution.py:52
  84.4 3.7 %collective-permute-done.19.refs_0_.refs_3_ = bf16[256,1024]{1,0:T(8,128)(2,1)S(1)} collective-permute-done((bf16[256,1024]{1,0:T(8,128)(2,1)S(1)}, bf16[256,1024]{1,0:T(8,128)(2,1)S(1)}, u32[]{:S(2)}, u32[]{:S(2)}) %collective-permute-start.19) | collective-permute-done | bytes 524320 | tf_op jit(solution)/shard_map/ppermute | solution.py:56
  91.9 4.8 %collective-permute-done.23.refs_2_.refs_1_ = f32[32,2048]{1,0:T(8,128)S(1)} collective-permute-done((f32[32,2048]{1,0:T(8,128)S(1)}, f32[32,2048]{1,0:T(8,128)S(1)}, u32[]{:S(2)}, u32[]{:S(2)}) %collective-permute-start.23) | collective-permute-done | bytes 262176 | tf_op jit(solution)/shard_map/ppermute | solution.py:483
  97.4 3.9 %collective-permute-done.15.end = bf16[256,1024]{1,0:T(8,128)(2,1)S(1)} collective-permute-done((bf16[256,1024]{1,0:T(8,128)(2,1)S(1)}, bf16[256,1024]{1,0:T(8,128)(2,1)S(1)}, u32[]{:S(2)}, u32[]{:S(2)}) %collective-permute-start.15) | collective-permute-done | bytes 524320 | tf_op jit(solution)/shard_map/ppermute | solution.py:52
  102.2 1.7 %collective-permute-start.24 = (bf16[256,1024]{1,0:T(8,128)(2,1)S(1)}, bf16[256,1024]{1,0:T(8,128)(2,1)S(1)}, u32[]{:S(2)}, u32[]{:S(2)}) collective-permute-start(bf16[256,1024]{1,0:T(8,128)(2,1)S(1)} %pick.6.refs_2_.refs_4_), channel_id=1, source_target_pairs={{0,4},{2,6},{4,0},{6,2},{1,5},{3,7},{5,1},{7,3},{8,12},{10,14},{12... | collective-permute-start | bytes 1572872 | tf_op jit(solution)/shard_map/ppermute | solution.py:56
  108.0 2.2 %place_rows.3 = (bf16[4,4,128,1024]{3,2,1,0:T(8,128)(2,1)}, bf16[4,4,64,2048]{3,2,1,0:T(8,128)(2,1)}, f32[8,128]{1,0:T(8,128)S(1)}) custom-call(bf16[4,256,1024]{2,1,0:T(8,128)(2,1)S(1)} %bundle.4.refs_0_, bf16[4,256,1024]{2,1,0:T(8,128)(2,1)S(1)} %collective-permute-done.26.refs_2_.refs_1_, f32[8,128]{1,0:T(8,128)S(1)} %get-tuple-element.59.refs_2_), custom_call_target="tpu_custom_call" | custom-call | bytes 25178112 | tf_op jit(solution)/shard_map/place_rows/pallas_call | solution.py:26
  110.2 1.8 %place_rows.4 = (bf16[4,4,128,1024]{3,2,1,0:T(8,128)(2,1)}, bf16[4,4,64,2048]{3,2,1,0:T(8,128)(2,1)}, f32[8,128]{1,0:T(8,128)S(1)}) custom-call(bf16[3,256,1024]{2,1,0:T(8,128)(2,1)S(1)} %bundle.3.refs_0_, bf16[3,256,1024]{2,1,0:T(8,128)(2,1)S(1)} %collective-permute-done.25.refs_1_, ...), custom_call_target="tpu_custom_call", output_to_operand_aliasing={{0}: (3, {}), {1}: (4, {})} | custom-call | bytes 25178112 | tf_op jit(solution)/shard_map/place_rows/pallas_call | solution.py:26
  112.0 4.1 %collective-permute-done.24.refs_0_ = bf16[256,1024]{1,0:T(8,128)(2,1)S(1)} collective-permute-done((bf16[256,1024]{1,0:T(8,128)(2,1)S(1)}, bf16[256,1024]{1,0:T(8,128)(2,1)S(1)}, u32[]{:S(2)}, u32[]{:S(2)}) %collective-permute-start.24) | collective-permute-done | bytes 524320 | tf_op jit(solution)/shard_map/ppermute | solution.py:56
  116.2 3.3 %collective-permute-done.28.end = bf16[256,1024]{1,0:T(8,128)(2,1)S(1)} collective-permute-done((bf16[256,1024]{1,0:T(8,128)(2,1)S(1)}, bf16[256,1024]{1,0:T(8,128)(2,1)S(1)}, u32[]{:S(2)}, u32[]{:S(2)}) %collective-permute-start.28) | collective-permute-done | bytes 524320 | tf_op jit(solution)/shard_map/ppermute | solution.py:52
  (85 shorter events, 31.1 us)
Async XLA Ops:
  3.2 7.5 %collective-permute-start = (bf16[80,256]{1,0:T(8,128)(2,1)S(1)}, bf16[80,256]{1,0:T(8,128)(2,1)S(1)}, u32[]{:S(2)}, u32[]{:S(2)}) collective-permute-start(bf16[80,256]{1,0:T(8,128)(2,1)S(1)} %get-tuple-element.50), channel_id=1, source_target_pairs={{0,8},{8,0},{16,24},{24,16},{1,9},{9,1},{17,25},{25,17},{2,10},{10... | collective-permute-start | bytes 122888 | tf_op jit(solution)/shard_map/ppermute | solution.py:56
  6.3 9.0 %collective-permute-start.3 = (bf16[80,256]{1,0:T(8,128)(2,1)S(1)}, bf16[80,256]{1,0:T(8,128)(2,1)S(1)}, u32[]{:S(2)}, u32[]{:S(2)}) collective-permute-start(bf16[80,256]{1,0:T(8,128)(2,1)S(1)} %get-tuple-element.52), channel_id=1, source_target_pairs={{0,16},{8,24},{16,0},{24,8},{1,17},{9,25},{17,1},{25,9},{2,18},{10... | collective-permute-start | bytes 122888 | tf_op jit(solution)/shard_map/ppermute | solution.py:56
  13.9 11.6 %collective-permute-start.1 = (bf16[256,1024]{1,0:T(8,128)(2,1)S(1)}, bf16[256,1024]{1,0:T(8,128)(2,1)S(1)}, u32[]{:S(2)}, u32[]{:S(2)}) collective-permute-start(bf16[256,1024]{1,0:T(8,128)(2,1)S(1)} %gate.8.refs_0_.block), channel_id=1, source_target_pairs={{0,8},{24,16},{1,9},{25,17},{2,10},{26,18},{3,11},{27,19},{4,12},{... | collective-permute-start | bytes 1572872 | tf_op jit(solution)/shard_map/ppermute | solution.py:52
  18.7 11.4 %collective-permute-start.8 = (bf16[256,1024]{1,0:T(8,128)(2,1)S(1)}, bf16[256,1024]{1,0:T(8,128)(2,1)S(1)}, u32[]{:S(2)}, u32[]{:S(2)}) collective-permute-start(bf16[256,1024]{1,0:T(8,128)(2,1)S(1)} %get-tuple-element.54.x.refs_0_), channel_id=1, source_target_pairs={{8,16},{16,8},{9,17},{17,9},{10,18},{18,10},{11,19},{19,11},{12,20... | collective-permute-start | bytes 1572872 | tf_op jit(solution)/shard_map/ppermute | solution.py:52
  19.4 14.6 %collective-permute-start.5 = (bf16[256,1024]{1,0:T(8,128)(2,1)S(1)}, bf16[256,1024]{1,0:T(8,128)(2,1)S(1)}, u32[]{:S(2)}, u32[]{:S(2)}) collective-permute-start(bf16[256,1024]{1,0:T(8,128)(2,1)S(1)} %get-tuple-element.54.x.refs_0_), channel_id=1, source_target_pairs={{8,0},{16,24},{9,1},{17,25},{10,2},{18,26},{11,3},{19,27},{12,4},{... | collective-permute-start | bytes 1572872 | tf_op jit(solution)/shard_map/ppermute | solution.py:52
  25.5 13.7 %collective-permute-start.2 = (bf16[256,1024]{1,0:T(8,128)(2,1)S(1)}, bf16[256,1024]{1,0:T(8,128)(2,1)S(1)}, u32[]{:S(2)}, u32[]{:S(2)}) collective-permute-start(bf16[256,1024]{1,0:T(8,128)(2,1)S(1)} %gate.9), channel_id=1, source_target_pairs={{0,8},{24,16},{1,9},{25,17},{2,10},{26,18},{3,11},{27,19},{4,12},{... | collective-permute-start | bytes 1572872 | tf_op jit(solution)/shard_map/ppermute | solution.py:52
  30.2 17.1 %collective-permute-start.9 = (bf16[256,1024]{1,0:T(8,128)(2,1)S(1)}, bf16[256,1024]{1,0:T(8,128)(2,1)S(1)}, u32[]{:S(2)}, u32[]{:S(2)}) collective-permute-start(bf16[256,1024]{1,0:T(8,128)(2,1)S(1)} %gate.12), channel_id=1, source_target_pairs={{8,16},{16,8},{9,17},{17,9},{10,18},{18,10},{11,19},{19,11},{12,20... | collective-permute-start | bytes 1572872 | tf_op jit(solution)/shard_map/ppermute | solution.py:52
  31.0 16.3 %collective-permute-start.10 = (bf16[256,1024]{1,0:T(8,128)(2,1)S(1)}, bf16[256,1024]{1,0:T(8,128)(2,1)S(1)}, u32[]{:S(2)}, u32[]{:S(2)}) collective-permute-start(bf16[256,1024]{1,0:T(8,128)(2,1)S(1)} %collective-permute-done.8.refs_0_.middle), channel_id=1, source_target_pairs={{8,0},{16,24},{9,1},{17,25},{10,2},{18,26},{11,3},{19,27},{12,4},{... | collective-permute-start | bytes 1572872 | tf_op jit(solution)/shard_map/ppermute | solution.py:52
  32.4 16.3 %collective-permute-start.12 = (f32[2,32,2048]{2,1,0:T(8,128)S(1)}, f32[2,32,2048]{2,1,0:T(8,128)S(1)}, u32[]{:S(2)}, u32[]{:S(2)}) collective-permute-start(f32[2,32,2048]{2,1,0:T(8,128)S(1)} %up_state.1), channel_id=1, source_target_pairs={{0,1},{1,0},{2,3},{3,2},{4,5},{5,4},{6,7},{7,6},{8,9},{9,8},{10,11... | collective-permute-start | bytes 1572872 | tf_op jit(solution)/shard_map/ppermute | solution.py:413
  39.4 16.1 %collective-permute-start.7 = (bf16[256,1024]{1,0:T(8,128)(2,1)S(1)}, bf16[256,1024]{1,0:T(8,128)(2,1)S(1)}, u32[]{:S(2)}, u32[]{:S(2)}) collective-permute-start(bf16[256,1024]{1,0:T(8,128)(2,1)S(1)} %add_block.3.refs_0_), channel_id=1, source_target_pairs={{8,16},{16,8},{9,17},{17,9},{10,18},{18,10},{11,19},{19,11},{12,20... | collective-permute-start | bytes 1572872 | tf_op jit(solution)/shard_map/ppermute | solution.py:52
  40.2 15.4 %collective-permute-start.6 = (bf16[256,1024]{1,0:T(8,128)(2,1)S(1)}, bf16[256,1024]{1,0:T(8,128)(2,1)S(1)}, u32[]{:S(2)}, u32[]{:S(2)}) collective-permute-start(bf16[256,1024]{1,0:T(8,128)(2,1)S(1)} %gate.11), channel_id=1, source_target_pairs={{0,8},{24,16},{1,9},{25,17},{2,10},{26,18},{3,11},{27,19},{4,12},{... | collective-permute-start | bytes 1572872 | tf_op jit(solution)/shard_map/ppermute | solution.py:52
  47.4 12.4 %collective-permute-start.11 = (bf16[256,1024]{1,0:T(8,128)(2,1)S(1)}, bf16[256,1024]{1,0:T(8,128)(2,1)S(1)}, u32[]{:S(2)}, u32[]{:S(2)}) collective-permute-start(bf16[256,1024]{1,0:T(8,128)(2,1)S(1)} %add_block.5), channel_id=1, source_target_pairs={{8,0},{16,24},{9,1},{17,25},{10,2},{18,26},{11,3},{19,27},{12,4},{... | collective-permute-start | bytes 1572872 | tf_op jit(solution)/shard_map/ppermute | solution.py:52
  62.2 11.1 %collective-permute-start.18 = (bf16[256,1024]{1,0:T(8,128)(2,1)S(1)}, bf16[256,1024]{1,0:T(8,128)(2,1)S(1)}, u32[]{:S(2)}, u32[]{:S(2)}) collective-permute-start(bf16[256,1024]{1,0:T(8,128)(2,1)S(1)} %get-tuple-element.55.refs_0_), channel_id=1, source_target_pairs={{0,4},{2,6},{4,0},{6,2},{1,5},{3,7},{5,1},{7,3},{8,12},{10,14},{12... | collective-permute-start | bytes 1572872 | tf_op jit(solution)/shard_map/ppermute | solution.py:56
  63.8 12.8 %collective-permute-start.13 = (bf16[256,1024]{1,0:T(8,128)(2,1)S(1)}, bf16[256,1024]{1,0:T(8,128)(2,1)S(1)}, u32[]{:S(2)}, u32[]{:S(2)}) collective-permute-start(bf16[256,1024]{1,0:T(8,128)(2,1)S(1)} %get-tuple-element.55.refs_0_), channel_id=1, source_target_pairs={{0,8},{8,0},{16,24},{24,16},{1,9},{9,1},{17,25},{25,17},{2,10},{10... | collective-permute-start | bytes 1572872 | tf_op jit(solution)/shard_map/ppermute | solution.py:56
  65.0 19.4 %collective-permute-start.17 = (bf16[256,1024]{1,0:T(8,128)(2,1)S(1)}, bf16[256,1024]{1,0:T(8,128)(2,1)S(1)}, u32[]{:S(2)}, u32[]{:S(2)}) collective-permute-start(bf16[256,1024]{1,0:T(8,128)(2,1)S(1)} %collective-permute-done.16.middle), channel_id=1, source_target_pairs={{8,0},{16,24},{9,1},{17,25},{10,2},{18,26},{11,3},{19,27},{12,4},{... | collective-permute-start | bytes 1572872 | tf_op jit(solution)/shard_map/ppermute | solution.py:52
  76.7 11.4 %collective-permute-start.19 = (bf16[256,1024]{1,0:T(8,128)(2,1)S(1)}, bf16[256,1024]{1,0:T(8,128)(2,1)S(1)}, u32[]{:S(2)}, u32[]{:S(2)}) collective-permute-start(bf16[256,1024]{1,0:T(8,128)(2,1)S(1)} %gate.13.refs_0_.refs_2_), channel_id=1, source_target_pairs={{0,4},{2,6},{4,0},{6,2},{1,5},{3,7},{5,1},{7,3},{8,12},{10,14},{12... | collective-permute-start | bytes 1572872 | tf_op jit(solution)/shard_map/ppermute | solution.py:56
  76.8 11.4 %collective-permute-start.21 = (bf16[256,1024]{1,0:T(8,128)(2,1)S(1)}, bf16[256,1024]{1,0:T(8,128)(2,1)S(1)}, u32[]{:S(2)}, u32[]{:S(2)}) collective-permute-start(bf16[256,1024]{1,0:T(8,128)(2,1)S(1)} %gate.14), channel_id=1, source_target_pairs={{0,8},{24,16},{1,9},{25,17},{2,10},{26,18},{3,11},{27,19},{4,12},{... | collective-permute-start | bytes 1572872 | tf_op jit(solution)/shard_map/ppermute | solution.py:52
  78.3 10.6 %collective-permute-start.14 = (bf16[256,1024]{1,0:T(8,128)(2,1)S(1)}, bf16[256,1024]{1,0:T(8,128)(2,1)S(1)}, u32[]{:S(2)}, u32[]{:S(2)}) collective-permute-start(bf16[256,1024]{1,0:T(8,128)(2,1)S(1)} %collective-permute-done.13.x), channel_id=1, source_target_pairs={{8,16},{16,8},{9,17},{17,9},{10,18},{18,10},{11,19},{19,11},{12,20... | collective-permute-start | bytes 1572872 | tf_op jit(solution)/shard_map/ppermute | solution.py:52
  88.1 9.2 %collective-permute-start.20 = (bf16[256,1024]{1,0:T(8,128)(2,1)S(1)}, bf16[256,1024]{1,0:T(8,128)(2,1)S(1)}, u32[]{:S(2)}, u32[]{:S(2)}) collective-permute-start(bf16[256,1024]{1,0:T(8,128)(2,1)S(1)} %pick.5.refs_0_), channel_id=1, source_target_pairs={{0,4},{2,6},{4,0},{6,2},{1,5},{3,7},{5,1},{7,3},{8,12},{10,14},{12... | collective-permute-start | bytes 1572872 | tf_op jit(solution)/shard_map/ppermute | solution.py:56
  88.2 8.5 %collective-permute-start.22 = (bf16[256,1024]{1,0:T(8,128)(2,1)S(1)}, bf16[256,1024]{1,0:T(8,128)(2,1)S(1)}, u32[]{:S(2)}, u32[]{:S(2)}) collective-permute-start(bf16[256,1024]{1,0:T(8,128)(2,1)S(1)} %collective-permute-done.21.middle), channel_id=1, source_target_pairs={{8,16},{16,8},{9,17},{17,9},{10,18},{18,10},{11,19},{19,11},{12,20... | collective-permute-start | bytes 1572872 | tf_op jit(solution)/shard_map/ppermute | solution.py:52
  88.9 12.4 %collective-permute-start.15 = (bf16[256,1024]{1,0:T(8,128)(2,1)S(1)}, bf16[256,1024]{1,0:T(8,128)(2,1)S(1)}, u32[]{:S(2)}, u32[]{:S(2)}) collective-permute-start(bf16[256,1024]{1,0:T(8,128)(2,1)S(1)} %collective-permute-done.14.middle), channel_id=1, source_target_pairs={{8,0},{16,24},{9,1},{17,25},{10,2},{18,26},{11,3},{19,27},{12,4},{... | collective-permute-start | bytes 1572872 | tf_op jit(solution)/shard_map/ppermute | solution.py:52
  101.7 8.5 %collective-permute-start.25 = (bf16[3,256,1024]{2,1,0:T(8,128)(2,1)S(1)}, bf16[3,256,1024]{2,1,0:T(8,128)(2,1)S(1)}, u32[]{:S(2)}, u32[]{:S(2)}) collective-permute-start(bf16[3,256,1024]{2,1,0:T(8,128)(2,1)S(1)} %bundle.3.refs_0_), channel_id=1, source_target_pairs={{0,2},{2,0},{4,6},{6,4},{1,3},{3,1},{5,7},{7,5},{8,10},{10,8},{12,... | collective-permute-start | bytes 4718600 | tf_op jit(solution)/shard_map/ppermute | solution.py:56
  102.2 13.9 %collective-permute-start.24 = (bf16[256,1024]{1,0:T(8,128)(2,1)S(1)}, bf16[256,1024]{1,0:T(8,128)(2,1)S(1)}, u32[]{:S(2)}, u32[]{:S(2)}) collective-permute-start(bf16[256,1024]{1,0:T(8,128)(2,1)S(1)} %pick.6.refs_2_.refs_4_), channel_id=1, source_target_pairs={{0,4},{2,6},{4,0},{6,2},{1,5},{3,7},{5,1},{7,3},{8,12},{10,14},{12... | collective-permute-start | bytes 1572872 | tf_op jit(solution)/shard_map/ppermute | solution.py:56
  104.0 15.5 %collective-permute-start.28 = (bf16[256,1024]{1,0:T(8,128)(2,1)S(1)}, bf16[256,1024]{1,0:T(8,128)(2,1)S(1)}, u32[]{:S(2)}, u32[]{:S(2)}) collective-permute-start(bf16[256,1024]{1,0:T(8,128)(2,1)S(1)} %collective-permute-done.22.refs_1_.middle), channel_id=1, source_target_pairs={{8,0},{16,24},{9,1},{17,25},{10,2},{18,26},{11,3},{19,27},{12,4},{... | collective-permute-start | bytes 1572872 | tf_op jit(solution)/shard_map/ppermute | solution.py:52
  (15 other events, 165.7 us)

commit v9 on v8

--- a/solution.py
+++ b/solution.py
@@ -21,7 +21,9 @@
     return (master - 0.7 * (difference + 0.5 * velocity), velocity)
 
 
-def call(kernel, name, out_shape, in_specs, out_specs, scratch, *operands, limit=24, aliases={}):
+def call(
+    kernel, name, out_shape, in_specs, out_specs, scratch, *operands, limit=24, aliases={}, weight=3
+):
     size = sum(x.size * x.dtype.itemsize for x in jax.tree.leaves(out_shape))
     return pl.pallas_call(
         kernel,
@@ -32,7 +34,7 @@
         scratch_shapes=scratch,
         input_output_aliases=aliases,
         compiler_params=pltpu.CompilerParams(vmem_limit_bytes=limit * 2**20),
-        cost_estimate=pl.CostEstimate(flops=0, bytes_accessed=3 * size, transcendentals=0),
+        cost_estimate=pl.CostEstimate(flops=0, bytes_accessed=weight * size, transcendentals=0),
     )(*operands)
 
 
@@ -194,7 +196,8 @@
     refs = list(refs)
     master_down, moment_down, master_up, moment_up = refs[:4]
     came, state_came = refs[4 : 4 + n_came], refs[4 + n_came : 3 + n_came + tensors]
-    piece, stored_down, velocity_down, *sums = refs[3 + n_came + tensors : -3]
+    piece, token, stored_down, velocity_down, *sums = refs[3 + n_came + tensors : -3]
+    token[...] = jnp.zeros_like(token)
     summed, master, moment = refs[-3:]
     me = lax.axis_index("tensor")
     rows_down, width = master_down.shape
@@ -446,7 +449,7 @@
 
     embed_out = along(recast_rows, OUTWARD)
     embed_middle = along(recast_rows, ACROSS)
-    end_sum = gate(add(end, from_end), embed_middle)
+    end_sum = add(end, from_end)
     end_partial = along(end_sum, ACROSS)
     middle_sum = add(middle, along(gate(middle, from_end), INWARD), embed_out)
     middle_partial = along(middle_sum, ACROSS)
@@ -456,12 +459,12 @@
     came0 = [own, from_near, middle_partial, to_end]
     half_sum = jax.ShapeDtypeStruct((rows_up, half_cols), F32)
     down_state = jax.ShapeDtypeStruct((rows_down, width), F32)
-    piece, stored_down, velocity_down, *sums = call(
+    piece, token, stored_down, velocity_down, *sums = call(
         functools.partial(update_kernel, replicas, tensors, len(came0)),
         "update_rows",
-        [packed, down_state, down_state] + [half_sum] * tensors,
+        [packed, token_shape, down_state, down_state] + [half_sum] * tensors,
         [VMEM] * (4 + len(came0) + len(states)),
-        [VMEM] * (3 + tensors),
+        [VMEM] * (4 + tensors),
         [pltpu.VMEM((tall, half_cols), F32)] * 3,
         master_down[0],
         moment_down[0],
@@ -474,10 +477,10 @@
     top = shards // 2
     came_near = swap(piece, "replica", 1)
     middle_piece = along(piece, ACROSS)
-    far_piece = swap(piece, "shard", top)
+    far_piece = swap(gate(piece, swap(token, "shard", 1)), "shard", top)
     end_piece = along(came_near, ACROSS)
     second_out = along(middle_piece, OUTWARD)
-    near_piece = gate(came_near, far_piece)
+    near_piece = came_near
     far_near = swap(near_piece, "shard", top)
     sums = [sums[0]] + [
         lax.ppermute(
@@ -485,7 +488,7 @@
         )
         for shift, x in enumerate(sums[1:], 1)
     ]
-    second = pick(middle_piece, second_out, far_near)
+    second = pick(middle_piece, second_out, far_near, far_piece)
     far_second = swap(second, "shard", top)
     embed_in = along(gate(recast_rows, near_piece), INWARD)
     embed_end = along(embed_in, ACROSS)
@@ -563,6 +566,7 @@
         last[0],
         recast_embed,
         aliases={2: 0},
+        weight=30,
     )
     recast_down, recast_up, _ = place([(3, top)], last, placed, token)
 

time: 122 us -> 128 us (1.049)
  starting transfers between devices: 42.5 us -> 45.7 us
  waiting for transfers between devices: 59.3 us -> 61.2 us
    ppermute x11 -> x12, waiting for transfers between devices: 20.6 us -> 24.2 us  [swap(): lax.ppermute(x, axis, [(i, i ^ bit) for i in range(lax.axis_size(axis))])]
    ppermute x11 -> x12, starting transfers between devices: 13 us -> 15.9 us  [swap(): lax.ppermute(x, axis, [(i, i ^ bit) for i in range(lax.axis_size(axis))])]
    ppermute x16, waiting for transfers between devices: 33.9 us -> 31.3 us  [along(): return lax.ppermute(x, 'replica', pairs)]
    pallas_call x30 -> x29, Pallas kernels: 17.9 us -> 17.9 us  [call(): pl.pallas_call(kernel, name=name, out_shape=out_shape, in_specs=in_specs,...]
  transfers between devices with their start and end apart: 29 -> 30, of which waited for: 15 -> 16; matrix products, arithmetic and copies ran while one was open for 1% -> 1% of each run, Pallas kernels for 10% -> 9%
where the time goes in v9:
time: 128 us; the launch traced here: 127 us
  waiting for transfers between devices  61.2 us (48%)
  starting transfers between devices  45.7 us (36%)
  Pallas kernels  17.9 us (14%)
    ppermute x16, waiting for transfers between devices, along(): return lax.ppermute(x, 'replica', pairs)  31.3 us
    ppermute x16, starting transfers between devices, along(): return lax.ppermute(x, 'replica', pairs)  26.6 us
    ppermute x12, waiting for transfers between devices, swap(): lax.ppermute(x, axis, [(i, i ^ bit) for i in range(lax.axis_size(axis))])  24.2 us
    pallas_call x29, Pallas kernels, call(): pl.pallas_call(kernel, name=name, out_shape=out_shape, in_specs=in_specs,...  17.9 us
    ppermute x12, starting transfers between devices, swap(): lax.ppermute(x, axis, [(i, i ^ bit) for i in range(lax.axis_size(axis))])  15.9 us
    ppermute x1, waiting for transfers between devices, body(): lax.ppermute(gate(x, near_piece), 'tensor', [(i, (i + shift) % tensors) f...  5.77 us
  transfers between devices with their start and end apart: 30, of which 16 were waited for; matrix products, arithmetic and copies ran while one was open for 1% of the time, Pallas kernels for 9%

profile of v9, /device:TPU:0, one launch (start us, length us, event | category | flops | bytes accessed | tf_op | source)
XLA Modules:
  0.0 127.1 jit_solution(4521873202946081395)
XLA Ops:
  0.6 2.6 %project_rows.1 = (f32[64,256]{1,0:T(8,128)S(1)}, bf16[80,256]{1,0:T(8,128)(2,1)S(1)}, bf16[80,256]{1,0:T(8,128)(2,1)S(1)}, bf16[80,256]{1,0:T(8,128)(2,1)S(1)}) custom-call(bf16[1024,1024]{1,0:T(8,128)(2,1)} %bitcast.35, f32[64,1024]{1,0:T(8,128)} %bitcast.24, bf16[2,1024]{1,0:T(2,128)(2,1)} %bitcast.29), custom_call_target="tpu_custom_call" | custom-call | bytes 565248 | tf_op jit(solution)/shard_map/project_rows/pallas_call | solution.py:28
  3.2 3.1 %collective-permute-start = (bf16[80,256]{1,0:T(8,128)(2,1)S(1)}, bf16[80,256]{1,0:T(8,128)(2,1)S(1)}, u32[]{:S(2)}, u32[]{:S(2)}) collective-permute-start(bf16[80,256]{1,0:T(8,128)(2,1)S(1)} %get-tuple-element.51), channel_id=1, source_target_pairs={{0,8},{8,0},{16,24},{24,16},{1,9},{9,1},{17,25},{25,17},{2,10},{10... | collective-permute-start | bytes 122888 | tf_op jit(solution)/shard_map/ppermute | solution.py:58
  6.3 2.6 %collective-permute-start.3 = (bf16[80,256]{1,0:T(8,128)(2,1)S(1)}, bf16[80,256]{1,0:T(8,128)(2,1)S(1)}, u32[]{:S(2)}, u32[]{:S(2)}) collective-permute-start(bf16[80,256]{1,0:T(8,128)(2,1)S(1)} %get-tuple-element.53), channel_id=1, source_target_pairs={{0,16},{8,24},{16,0},{24,8},{1,17},{9,25},{17,1},{25,9},{2,18},{10... | collective-permute-start | bytes 122888 | tf_op jit(solution)/shard_map/ppermute | solution.py:58
  8.9 1.8 %pack_blocks.1 = (bf16[256,1024]{1,0:T(8,128)(2,1)S(1)}, bf16[256,1024]{1,0:T(8,128)(2,1)S(1)}, bf16[256,1024]{1,0:T(8,128)(2,1)S(1)}, bf16[256,1024]{1,0:T(8,128)(2,1)S(1)}) custom-call(bf16[4,4,128,1024]{3,2,1,0:T(8,128)(2,1)} %bitcast.33, bf16[4,4,64,2048]{3,2,1,0:T(8,128)(2,1)} %bitcast.34), custom_call_target="tpu_custom_call" | custom-call | bytes 6291456 | tf_op jit(solution)/shard_map/pack_blocks/pallas_call | solution.py:28
  10.8 2.0 %collective-permute-start.4 = (bf16[80,256]{1,0:T(8,128)(2,1)S(1)}, bf16[80,256]{1,0:T(8,128)(2,1)S(1)}, u32[]{:S(2)}, u32[]{:S(2)}) collective-permute-start(bf16[80,256]{1,0:T(8,128)(2,1)S(1)} %gate.9), channel_id=1, source_target_pairs={{0,24},{8,16},{16,8},{24,0},{1,25},{9,17},{17,9},{25,1},{2,26},{10... | collective-permute-start | bytes 122888 | tf_op jit(solution)/shard_map/ppermute | solution.py:58
  16.7 2.0 %embed_update.1 = (f32[256,1024]{1,0:T(8,128)}, bf16[256,1024]{1,0:T(8,128)(2,1)S(1)}, f32[64,256]{1,0:T(8,128)}, bf16[2,1024]{1,0:T(2,128)(2,1)}, f32[2,1024]{1,0:T(2,128)}, /*index=5*/f32[2,1024]{1,0:T(2,128)}) custom-call(f32[64,256]{1,0:T(8,128)S(1)} %get-tuple-element.52.refs_0_, f32[64,256]{1,0:T(8,128)S(1)} %fusion.refs_1_, f32[256,1024]{1,0:T(8,128)S(1)} %bitcast.23, ...), custom_call_target="tpu_custom_call" | custom-call | bytes 4976640 | tf_op jit(solution)/shard_map/embed_update/pallas_call | solution.py:28
  20.7 4.8 %collective-permute-done.1.refs_0_.came = bf16[256,1024]{1,0:T(8,128)(2,1)S(1)} collective-permute-done((bf16[256,1024]{1,0:T(8,128)(2,1)S(1)}, bf16[256,1024]{1,0:T(8,128)(2,1)S(1)}, u32[]{:S(2)}, u32[]{:S(2)}) %collective-permute-start.1) | collective-permute-done | bytes 524320 | tf_op jit(solution)/shard_map/ppermute | solution.py:54
  25.6 4.5 %collective-permute-start.2 = (bf16[256,1024]{1,0:T(8,128)(2,1)S(1)}, bf16[256,1024]{1,0:T(8,128)(2,1)S(1)}, u32[]{:S(2)}, u32[]{:S(2)}) collective-permute-start(bf16[256,1024]{1,0:T(8,128)(2,1)S(1)} %gate.8), channel_id=1, source_target_pairs={{0,8},{24,16},{1,9},{25,17},{2,10},{26,18},{3,11},{27,19},{4,12},{... | collective-permute-start | bytes 1572872 | tf_op jit(solution)/shard_map/ppermute | solution.py:54
  33.9 5.6 %collective-permute-done.2.came = bf16[256,1024]{1,0:T(8,128)(2,1)S(1)} collective-permute-done((bf16[256,1024]{1,0:T(8,128)(2,1)S(1)}, bf16[256,1024]{1,0:T(8,128)(2,1)S(1)}, u32[]{:S(2)}, u32[]{:S(2)}) %collective-permute-start.2) | collective-permute-done | bytes 524320 | tf_op jit(solution)/shard_map/ppermute | solution.py:54
  40.4 7.0 %collective-permute-start.6 = (bf16[256,1024]{1,0:T(8,128)(2,1)S(1)}, bf16[256,1024]{1,0:T(8,128)(2,1)S(1)}, u32[]{:S(2)}, u32[]{:S(2)}) collective-permute-start(bf16[256,1024]{1,0:T(8,128)(2,1)S(1)} %gate.10), channel_id=1, source_target_pairs={{0,8},{24,16},{1,9},{25,17},{2,10},{26,18},{3,11},{27,19},{4,12},{... | collective-permute-start | bytes 1572872 | tf_op jit(solution)/shard_map/ppermute | solution.py:54
  48.9 6.8 %collective-permute-done.6.refs_5_ = bf16[256,1024]{1,0:T(8,128)(2,1)S(1)} collective-permute-done((bf16[256,1024]{1,0:T(8,128)(2,1)S(1)}, bf16[256,1024]{1,0:T(8,128)(2,1)S(1)}, u32[]{:S(2)}, u32[]{:S(2)}) %collective-permute-start.6) | collective-permute-done | bytes 524320 | tf_op jit(solution)/shard_map/ppermute | solution.py:54
  55.7 4.3 %collective-permute-done.11.refs_7_ = bf16[256,1024]{1,0:T(8,128)(2,1)S(1)} collective-permute-done((bf16[256,1024]{1,0:T(8,128)(2,1)S(1)}, bf16[256,1024]{1,0:T(8,128)(2,1)S(1)}, u32[]{:S(2)}, u32[]{:S(2)}) %collective-permute-start.11) | collective-permute-done | bytes 524320 | tf_op jit(solution)/shard_map/ppermute | solution.py:54
  67.8 5.5 %collective-permute-done.13.refs_0_.refs_2_ = bf16[256,1024]{1,0:T(8,128)(2,1)S(1)} collective-permute-done((bf16[256,1024]{1,0:T(8,128)(2,1)S(1)}, bf16[256,1024]{1,0:T(8,128)(2,1)S(1)}, u32[]{:S(2)}, u32[]{:S(2)}) %collective-permute-start.13) | collective-permute-done | bytes 524320 | tf_op jit(solution)/shard_map/ppermute | solution.py:58
  73.3 2.5 %collective-permute-start.18 = (bf16[256,1024]{1,0:T(8,128)(2,1)S(1)}, bf16[256,1024]{1,0:T(8,128)(2,1)S(1)}, u32[]{:S(2)}, u32[]{:S(2)}) collective-permute-start(bf16[256,1024]{1,0:T(8,128)(2,1)S(1)} %collective-permute-done.13.refs_0_.refs_2_), channel_id=1, source_target_pairs={{0,4},{2,6},{4,0},{6,2},{1,5},{3,7},{5,1},{7,3},{8,12},{10,14},{12... | collective-permute-start | bytes 1572872 | tf_op jit(solution)/shard_map/ppermute | solution.py:58
  75.8 1.8 %collective-permute-start.22 = (bf16[256,1024]{1,0:T(8,128)(2,1)S(1)}, bf16[256,1024]{1,0:T(8,128)(2,1)S(1)}, u32[]{:S(2)}, u32[]{:S(2)}) collective-permute-start(bf16[256,1024]{1,0:T(8,128)(2,1)S(1)} %gate.12), channel_id=1, source_target_pairs={{0,8},{24,16},{1,9},{25,17},{2,10},{26,18},{3,11},{27,19},{4,12},{... | collective-permute-start | bytes 1572872 | tf_op jit(solution)/shard_map/ppermute | solution.py:54
  79.7 3.6 %collective-permute-done.17.end = bf16[256,1024]{1,0:T(8,128)(2,1)S(1)} collective-permute-done((bf16[256,1024]{1,0:T(8,128)(2,1)S(1)}, bf16[256,1024]{1,0:T(8,128)(2,1)S(1)}, u32[]{:S(2)}, u32[]{:S(2)}) %collective-permute-start.17) | collective-permute-done | bytes 524320 | tf_op jit(solution)/shard_map/ppermute | solution.py:54
  83.3 6.9 %collective-permute-done.18.refs_0_.refs_3_ = bf16[256,1024]{1,0:T(8,128)(2,1)S(1)} collective-permute-done((bf16[256,1024]{1,0:T(8,128)(2,1)S(1)}, bf16[256,1024]{1,0:T(8,128)(2,1)S(1)}, u32[]{:S(2)}, u32[]{:S(2)}) %collective-permute-start.18) | collective-permute-done | bytes 524320 | tf_op jit(solution)/shard_map/ppermute | solution.py:58
  95.4 5.8 %collective-permute-done.24.refs_2_.refs_1_ = f32[32,2048]{1,0:T(8,128)S(1)} collective-permute-done((f32[32,2048]{1,0:T(8,128)S(1)}, f32[32,2048]{1,0:T(8,128)S(1)}, u32[]{:S(2)}, u32[]{:S(2)}) %collective-permute-start.24) | collective-permute-done | bytes 262176 | tf_op jit(solution)/shard_map/ppermute | solution.py:486
  101.2 2.3 %collective-permute-done.21.refs_0_.refs_1_ = bf16[256,1024]{1,0:T(8,128)(2,1)S(1)} collective-permute-done((bf16[256,1024]{1,0:T(8,128)(2,1)S(1)}, bf16[256,1024]{1,0:T(8,128)(2,1)S(1)}, u32[]{:S(2)}, u32[]{:S(2)}) %collective-permute-start.21) | collective-permute-done | bytes 524320 | tf_op jit(solution)/shard_map/ppermute | solution.py:58
  103.5 4.0 %collective-permute-done.15.end = bf16[256,1024]{1,0:T(8,128)(2,1)S(1)} collective-permute-done((bf16[256,1024]{1,0:T(8,128)(2,1)S(1)}, bf16[256,1024]{1,0:T(8,128)(2,1)S(1)}, u32[]{:S(2)}, u32[]{:S(2)}) %collective-permute-start.15) | collective-permute-done | bytes 524320 | tf_op jit(solution)/shard_map/ppermute | solution.py:54
  114.2 2.2 %place_rows.3 = (bf16[4,4,128,1024]{3,2,1,0:T(8,128)(2,1)}, bf16[4,4,64,2048]{3,2,1,0:T(8,128)(2,1)}, f32[8,128]{1,0:T(8,128)S(1)}) custom-call(bf16[4,256,1024]{2,1,0:T(8,128)(2,1)S(1)} %bundle.4.refs_0_, bf16[4,256,1024]{2,1,0:T(8,128)(2,1)S(1)} %collective-permute-done.27.refs_2_.refs_1_, f32[8,128]{1,0:T(8,128)S(1)} %get-tuple-element.61.refs_2_), custom_call_target="tpu_custom_call" | custom-call | bytes 25178112 | tf_op jit(solution)/shard_map/place_rows/pallas_call | solution.py:28
  116.5 1.8 %place_rows.4 = (bf16[4,4,128,1024]{3,2,1,0:T(8,128)(2,1)}, bf16[4,4,64,2048]{3,2,1,0:T(8,128)(2,1)}, f32[8,128]{1,0:T(8,128)S(1)}) custom-call(bf16[3,256,1024]{2,1,0:T(8,128)(2,1)S(1)} %bundle.3.refs_0_, bf16[3,256,1024]{2,1,0:T(8,128)(2,1)S(1)} %collective-permute-done.26.refs_1_, ...), custom_call_target="tpu_custom_call", output_to_operand_aliasing={{0}: (3, {}), {1}: (4, {})} | custom-call | bytes 25178112 | tf_op jit(solution)/shard_map/place_rows/pallas_call | solution.py:28
  118.3 4.1 %collective-permute-done.25.refs_0_ = bf16[256,1024]{1,0:T(8,128)(2,1)S(1)} collective-permute-done((bf16[256,1024]{1,0:T(8,128)(2,1)S(1)}, bf16[256,1024]{1,0:T(8,128)(2,1)S(1)}, u32[]{:S(2)}, u32[]{:S(2)}) %collective-permute-start.25) | collective-permute-done | bytes 524320 | tf_op jit(solution)/shard_map/ppermute | solution.py:58
  122.5 2.1 %collective-permute-done.29.end = bf16[256,1024]{1,0:T(8,128)(2,1)S(1)} collective-permute-done((bf16[256,1024]{1,0:T(8,128)(2,1)S(1)}, bf16[256,1024]{1,0:T(8,128)(2,1)S(1)}, u32[]{:S(2)}, u32[]{:S(2)}) %collective-permute-start.29) | collective-permute-done | bytes 524320 | tf_op jit(solution)/shard_map/ppermute | solution.py:54
  (86 shorter events, 36.2 us)
Async XLA Ops:
  3.2 7.5 %collective-permute-start = (bf16[80,256]{1,0:T(8,128)(2,1)S(1)}, bf16[80,256]{1,0:T(8,128)(2,1)S(1)}, u32[]{:S(2)}, u32[]{:S(2)}) collective-permute-start(bf16[80,256]{1,0:T(8,128)(2,1)S(1)} %get-tuple-element.51), channel_id=1, source_target_pairs={{0,8},{8,0},{16,24},{24,16},{1,9},{9,1},{17,25},{25,17},{2,10},{10... | collective-permute-start | bytes 122888 | tf_op jit(solution)/shard_map/ppermute | solution.py:58
  6.3 8.9 %collective-permute-start.3 = (bf16[80,256]{1,0:T(8,128)(2,1)S(1)}, bf16[80,256]{1,0:T(8,128)(2,1)S(1)}, u32[]{:S(2)}, u32[]{:S(2)}) collective-permute-start(bf16[80,256]{1,0:T(8,128)(2,1)S(1)} %get-tuple-element.53), channel_id=1, source_target_pairs={{0,16},{8,24},{16,0},{24,8},{1,17},{9,25},{17,1},{25,9},{2,18},{10... | collective-permute-start | bytes 122888 | tf_op jit(solution)/shard_map/ppermute | solution.py:58
  13.9 11.6 %collective-permute-start.1 = (bf16[256,1024]{1,0:T(8,128)(2,1)S(1)}, bf16[256,1024]{1,0:T(8,128)(2,1)S(1)}, u32[]{:S(2)}, u32[]{:S(2)}) collective-permute-start(bf16[256,1024]{1,0:T(8,128)(2,1)S(1)} %gate.7.refs_0_.block), channel_id=1, source_target_pairs={{0,8},{24,16},{1,9},{25,17},{2,10},{26,18},{3,11},{27,19},{4,12},{... | collective-permute-start | bytes 1572872 | tf_op jit(solution)/shard_map/ppermute | solution.py:54
  18.7 12.3 %collective-permute-start.9 = (bf16[256,1024]{1,0:T(8,128)(2,1)S(1)}, bf16[256,1024]{1,0:T(8,128)(2,1)S(1)}, u32[]{:S(2)}, u32[]{:S(2)}) collective-permute-start(bf16[256,1024]{1,0:T(8,128)(2,1)S(1)} %get-tuple-element.55.x.refs_0_), channel_id=1, source_target_pairs={{8,16},{16,8},{9,17},{17,9},{10,18},{18,10},{11,19},{19,11},{12,20... | collective-permute-start | bytes 1572872 | tf_op jit(solution)/shard_map/ppermute | solution.py:54
  19.4 14.5 %collective-permute-start.5 = (bf16[256,1024]{1,0:T(8,128)(2,1)S(1)}, bf16[256,1024]{1,0:T(8,128)(2,1)S(1)}, u32[]{:S(2)}, u32[]{:S(2)}) collective-permute-start(bf16[256,1024]{1,0:T(8,128)(2,1)S(1)} %get-tuple-element.55.x.refs_0_), channel_id=1, source_target_pairs={{8,0},{16,24},{9,1},{17,25},{10,2},{18,26},{11,3},{19,27},{12,4},{... | collective-permute-start | bytes 1572872 | tf_op jit(solution)/shard_map/ppermute | solution.py:54
  25.6 13.9 %collective-permute-start.2 = (bf16[256,1024]{1,0:T(8,128)(2,1)S(1)}, bf16[256,1024]{1,0:T(8,128)(2,1)S(1)}, u32[]{:S(2)}, u32[]{:S(2)}) collective-permute-start(bf16[256,1024]{1,0:T(8,128)(2,1)S(1)} %gate.8), channel_id=1, source_target_pairs={{0,8},{24,16},{1,9},{25,17},{2,10},{26,18},{3,11},{27,19},{4,12},{... | collective-permute-start | bytes 1572872 | tf_op jit(solution)/shard_map/ppermute | solution.py:54
  30.3 17.2 %collective-permute-start.8 = (bf16[256,1024]{1,0:T(8,128)(2,1)S(1)}, bf16[256,1024]{1,0:T(8,128)(2,1)S(1)}, u32[]{:S(2)}, u32[]{:S(2)}) collective-permute-start(bf16[256,1024]{1,0:T(8,128)(2,1)S(1)} %add_block.4), channel_id=1, source_target_pairs={{8,16},{16,8},{9,17},{17,9},{10,18},{18,10},{11,19},{19,11},{12,20... | collective-permute-start | bytes 1572872 | tf_op jit(solution)/shard_map/ppermute | solution.py:54
  31.0 16.5 %collective-permute-start.10 = (bf16[256,1024]{1,0:T(8,128)(2,1)S(1)}, bf16[256,1024]{1,0:T(8,128)(2,1)S(1)}, u32[]{:S(2)}, u32[]{:S(2)}) collective-permute-start(bf16[256,1024]{1,0:T(8,128)(2,1)S(1)} %collective-permute-done.9.middle), channel_id=1, source_target_pairs={{8,0},{16,24},{9,1},{17,25},{10,2},{18,26},{11,3},{19,27},{12,4},{... | collective-permute-start | bytes 1572872 | tf_op jit(solution)/shard_map/ppermute | solution.py:54
  32.3 16.5 %collective-permute-start.12 = (f32[2,32,2048]{2,1,0:T(8,128)S(1)}, f32[2,32,2048]{2,1,0:T(8,128)S(1)}, u32[]{:S(2)}, u32[]{:S(2)}) collective-permute-start(f32[2,32,2048]{2,1,0:T(8,128)S(1)} %up_state.1), channel_id=1, source_target_pairs={{0,1},{1,0},{2,3},{3,2},{4,5},{5,4},{6,7},{7,6},{8,9},{9,8},{10,11... | collective-permute-start | bytes 1572872 | tf_op jit(solution)/shard_map/ppermute | solution.py:416
  39.6 16.1 %collective-permute-start.7 = (bf16[256,1024]{1,0:T(8,128)(2,1)S(1)}, bf16[256,1024]{1,0:T(8,128)(2,1)S(1)}, u32[]{:S(2)}, u32[]{:S(2)}) collective-permute-start(bf16[256,1024]{1,0:T(8,128)(2,1)S(1)} %add_block.3.refs_0_), channel_id=1, source_target_pairs={{8,16},{16,8},{9,17},{17,9},{10,18},{18,10},{11,19},{19,11},{12,20... | collective-permute-start | bytes 1572872 | tf_op jit(solution)/shard_map/ppermute | solution.py:54
  40.4 15.3 %collective-permute-start.6 = (bf16[256,1024]{1,0:T(8,128)(2,1)S(1)}, bf16[256,1024]{1,0:T(8,128)(2,1)S(1)}, u32[]{:S(2)}, u32[]{:S(2)}) collective-permute-start(bf16[256,1024]{1,0:T(8,128)(2,1)S(1)} %gate.10), channel_id=1, source_target_pairs={{0,8},{24,16},{1,9},{25,17},{2,10},{26,18},{3,11},{27,19},{4,12},{... | collective-permute-start | bytes 1572872 | tf_op jit(solution)/shard_map/ppermute | solution.py:54
  47.6 12.4 %collective-permute-start.11 = (bf16[256,1024]{1,0:T(8,128)(2,1)S(1)}, bf16[256,1024]{1,0:T(8,128)(2,1)S(1)}, u32[]{:S(2)}, u32[]{:S(2)}) collective-permute-start(bf16[256,1024]{1,0:T(8,128)(2,1)S(1)} %add_block.5), channel_id=1, source_target_pairs={{8,0},{16,24},{9,1},{17,25},{10,2},{18,26},{11,3},{19,27},{12,4},{... | collective-permute-start | bytes 1572872 | tf_op jit(solution)/shard_map/ppermute | solution.py:54
  62.4 10.8 %collective-permute-start.13 = (bf16[256,1024]{1,0:T(8,128)(2,1)S(1)}, bf16[256,1024]{1,0:T(8,128)(2,1)S(1)}, u32[]{:S(2)}, u32[]{:S(2)}) collective-permute-start(bf16[256,1024]{1,0:T(8,128)(2,1)S(1)} %get-tuple-element.56.x.refs_0_), channel_id=1, source_target_pairs={{0,8},{8,0},{16,24},{24,16},{1,9},{9,1},{17,25},{25,17},{2,10},{10... | collective-permute-start | bytes 1572872 | tf_op jit(solution)/shard_map/ppermute | solution.py:58
  64.9 14.8 %collective-permute-start.20 = (bf16[256,1024]{1,0:T(8,128)(2,1)S(1)}, bf16[256,1024]{1,0:T(8,128)(2,1)S(1)}, u32[]{:S(2)}, u32[]{:S(2)}) collective-permute-start(bf16[256,1024]{1,0:T(8,128)(2,1)S(1)} %gate.11), channel_id=1, source_target_pairs={{0,4},{2,6},{4,0},{6,2},{1,5},{3,7},{5,1},{7,3},{8,12},{10,14},{12... | collective-permute-start | bytes 1572872 | tf_op jit(solution)/shard_map/ppermute | solution.py:58
  66.5 16.8 %collective-permute-start.17 = (bf16[256,1024]{1,0:T(8,128)(2,1)S(1)}, bf16[256,1024]{1,0:T(8,128)(2,1)S(1)}, u32[]{:S(2)}, u32[]{:S(2)}) collective-permute-start(bf16[256,1024]{1,0:T(8,128)(2,1)S(1)} %collective-permute-done.16.middle), channel_id=1, source_target_pairs={{8,0},{16,24},{9,1},{17,25},{10,2},{18,26},{11,3},{19,27},{12,4},{... | collective-permute-start | bytes 1572872 | tf_op jit(solution)/shard_map/ppermute | solution.py:54
  73.3 16.9 %collective-permute-start.18 = (bf16[256,1024]{1,0:T(8,128)(2,1)S(1)}, bf16[256,1024]{1,0:T(8,128)(2,1)S(1)}, u32[]{:S(2)}, u32[]{:S(2)}) collective-permute-start(bf16[256,1024]{1,0:T(8,128)(2,1)S(1)} %collective-permute-done.13.refs_0_.refs_2_), channel_id=1, source_target_pairs={{0,4},{2,6},{4,0},{6,2},{1,5},{3,7},{5,1},{7,3},{8,12},{10,14},{12... | collective-permute-start | bytes 1572872 | tf_op jit(solution)/shard_map/ppermute | solution.py:58
  75.8 16.0 %collective-permute-start.22 = (bf16[256,1024]{1,0:T(8,128)(2,1)S(1)}, bf16[256,1024]{1,0:T(8,128)(2,1)S(1)}, u32[]{:S(2)}, u32[]{:S(2)}) collective-permute-start(bf16[256,1024]{1,0:T(8,128)(2,1)S(1)} %gate.12), channel_id=1, source_target_pairs={{0,8},{24,16},{1,9},{25,17},{2,10},{26,18},{3,11},{27,19},{4,12},{... | collective-permute-start | bytes 1572872 | tf_op jit(solution)/shard_map/ppermute | solution.py:54
  77.7 14.9 %collective-permute-start.14 = (bf16[256,1024]{1,0:T(8,128)(2,1)S(1)}, bf16[256,1024]{1,0:T(8,128)(2,1)S(1)}, u32[]{:S(2)}, u32[]{:S(2)}) collective-permute-start(bf16[256,1024]{1,0:T(8,128)(2,1)S(1)} %collective-permute-done.13.refs_0_.refs_2_), channel_id=1, source_target_pairs={{8,16},{16,8},{9,17},{17,9},{10,18},{18,10},{11,19},{19,11},{12,20... | collective-permute-start | bytes 1572872 | tf_op jit(solution)/shard_map/ppermute | solution.py:54
  90.3 13.2 %collective-permute-start.21 = (bf16[256,1024]{1,0:T(8,128)(2,1)S(1)}, bf16[256,1024]{1,0:T(8,128)(2,1)S(1)}, u32[]{:S(2)}, u32[]{:S(2)}) collective-permute-start(bf16[256,1024]{1,0:T(8,128)(2,1)S(1)} %pick.5.refs_0_), channel_id=1, source_target_pairs={{0,4},{2,6},{4,0},{6,2},{1,5},{3,7},{5,1},{7,3},{8,12},{10,14},{12... | collective-permute-start | bytes 1572872 | tf_op jit(solution)/shard_map/ppermute | solution.py:58
  91.8 9.4 %collective-permute-start.23 = (bf16[256,1024]{1,0:T(8,128)(2,1)S(1)}, bf16[256,1024]{1,0:T(8,128)(2,1)S(1)}, u32[]{:S(2)}, u32[]{:S(2)}) collective-permute-start(bf16[256,1024]{1,0:T(8,128)(2,1)S(1)} %collective-permute-done.22.middle), channel_id=1, source_target_pairs={{8,16},{16,8},{9,17},{17,9},{10,18},{18,10},{11,19},{19,11},{12,20... | collective-permute-start | bytes 1572872 | tf_op jit(solution)/shard_map/ppermute | solution.py:54
  92.6 15.0 %collective-permute-start.15 = (bf16[256,1024]{1,0:T(8,128)(2,1)S(1)}, bf16[256,1024]{1,0:T(8,128)(2,1)S(1)}, u32[]{:S(2)}, u32[]{:S(2)}) collective-permute-start(bf16[256,1024]{1,0:T(8,128)(2,1)S(1)} %collective-permute-done.14.middle), channel_id=1, source_target_pairs={{8,0},{16,24},{9,1},{17,25},{10,2},{18,26},{11,3},{19,27},{12,4},{... | collective-permute-start | bytes 1572872 | tf_op jit(solution)/shard_map/ppermute | solution.py:54
  107.9 8.5 %collective-permute-start.26 = (bf16[3,256,1024]{2,1,0:T(8,128)(2,1)S(1)}, bf16[3,256,1024]{2,1,0:T(8,128)(2,1)S(1)}, u32[]{:S(2)}, u32[]{:S(2)}) collective-permute-start(bf16[3,256,1024]{2,1,0:T(8,128)(2,1)S(1)} %bundle.3.refs_0_), channel_id=1, source_target_pairs={{0,2},{2,0},{4,6},{6,4},{1,3},{3,1},{5,7},{7,5},{8,10},{10,8},{12,... | collective-permute-start | bytes 4718600 | tf_op jit(solution)/shard_map/ppermute | solution.py:58
  108.5 13.9 %collective-permute-start.25 = (bf16[256,1024]{1,0:T(8,128)(2,1)S(1)}, bf16[256,1024]{1,0:T(8,128)(2,1)S(1)}, u32[]{:S(2)}, u32[]{:S(2)}) collective-permute-start(bf16[256,1024]{1,0:T(8,128)(2,1)S(1)} %pick.6.refs_2_.refs_4_), channel_id=1, source_target_pairs={{0,4},{2,6},{4,0},{6,2},{1,5},{3,7},{5,1},{7,3},{8,12},{10,14},{12... | collective-permute-start | bytes 1572872 | tf_op jit(solution)/shard_map/ppermute | solution.py:58
  109.1 15.5 %collective-permute-start.29 = (bf16[256,1024]{1,0:T(8,128)(2,1)S(1)}, bf16[256,1024]{1,0:T(8,128)(2,1)S(1)}, u32[]{:S(2)}, u32[]{:S(2)}) collective-permute-start(bf16[256,1024]{1,0:T(8,128)(2,1)S(1)} %collective-permute-done.23.refs_1_.middle), channel_id=1, source_target_pairs={{8,0},{16,24},{9,1},{17,25},{10,2},{18,26},{11,3},{19,27},{12,4},{... | collective-permute-start | bytes 1572872 | tf_op jit(solution)/shard_map/ppermute | solution.py:54
  (16 other events, 177.4 us)

commit v10 on v8

--- a/solution.py
+++ b/solution.py
@@ -190,16 +190,22 @@
     return call(pick_kernel, "pick", shape, specs, VMEM, [], middle, end, *after)
 
 
-def update_kernel(groups, tensors, n_came, *refs):
+def total(came, lo, hi):
+    value = came[0][lo:hi, :].astype(F32)
+    for ref in came[1:]:
+        value = value + ref[lo:hi, :].astype(F32)
+    return value
+
+
+def rows_kernel(groups, tensors, n_came, *refs):
     refs = list(refs)
     master_down, moment_down, master_up, moment_up = refs[:4]
     came, state_came = refs[4 : 4 + n_came], refs[4 + n_came : 3 + n_came + tensors]
-    piece, stored_down, velocity_down, *sums = refs[3 + n_came + tensors : -3]
-    summed, master, moment = refs[-3:]
+    piece, master, moment = refs[-3:]
     me = lax.axis_index("tensor")
     rows_down, width = master_down.shape
     rows_up = master_up.shape[0]
-    tall, cols = summed.shape
+    tall, cols = master.shape
 
     def at(index):
         return pl.ds(pl.multiple_of(index * rows_up, rows_up), rows_up)
@@ -211,28 +217,38 @@
         source = lax.rem(me + tensors - shift, tensors)
         master[at(source), :] = state_came[shift - 1][0]
         moment[at(source), :] = state_came[shift - 1][1]
-
-    def total(lo, hi):
-        value = came[0][lo:hi, :].astype(F32)
-        for ref in came[1:]:
-            value = value + ref[lo:hi, :].astype(F32)
-        return value
-
-    stored, velocity = outer_step(
-        master_down[...], moment_down[...], total(0, rows_down), groups
-    )
-    stored_down[...] = stored
-    velocity_down[...] = velocity
+    stored, _ = outer_step(
+        master_down[...], moment_down[...], total(came, 0, rows_down), groups
+    )
     piece[:rows_down, :] = stored.astype(BF16)
     for chunk in range(cols // width):
         lo = rows_down + chunk * tall
-        part = total(lo, lo + tall)
         span = slice(chunk * width, (chunk + 1) * width)
-        summed[:, span] = part
-        stored, _ = outer_step(master[:, span], moment[:, span], part, groups)
+        stored, _ = outer_step(
+            master[:, span], moment[:, span], total(came, lo, lo + tall), groups
+        )
         piece[lo : lo + tall, :] = stored.astype(BF16)
+
+
+def states_kernel(groups, tensors, n_came, *refs):
+    master_down, moment_down = refs[:2]
+    came = refs[2 : 2 + n_came]
+    stored_down, velocity_down, *sums, summed = refs[-3 - tensors :]
+    rows_down, width = master_down.shape
+    rows_up = sums[0].shape[0]
+    tall, cols = summed.shape
+    me = lax.axis_index("tensor")
+    stored, velocity = outer_step(
+        master_down[...], moment_down[...], total(came, 0, rows_down), groups
+    )
+    stored_down[...] = stored
+    velocity_down[...] = velocity
+    for chunk in range(cols // width):
+        lo = rows_down + chunk * tall
+        summed[:, chunk * width : (chunk + 1) * width] = total(came, lo, lo + tall)
     for shift in range(tensors):
-        sums[shift][...] = summed[at(lax.rem(me + shift, tensors)), :]
+        owner = lax.rem(me + shift, tensors)
+        sums[shift][...] = summed[pl.ds(pl.multiple_of(owner * rows_up, rows_up), rows_up), :]
 
 
 def up_kernel(groups, tensors, master_up, moment_up, *refs):
@@ -415,7 +431,7 @@
     ]
 
     base = lax.dot_general(
-        basis_t, master_embed[0], (((1,), (1,)), ((), ())), precision=HIGHEST
+        gate(basis_t, packets_came[1]), master_embed[0], (((1,), (1,)), ((), ())), precision=HIGHEST
     )
     norm_state = jax.ShapeDtypeStruct(master_norm.shape, F32)
     embed_rows = jax.ShapeDtypeStruct((rows_embed, width), BF16)
@@ -456,13 +472,13 @@
     came0 = [own, from_near, middle_partial, to_end]
     half_sum = jax.ShapeDtypeStruct((rows_up, half_cols), F32)
     down_state = jax.ShapeDtypeStruct((rows_down, width), F32)
-    piece, stored_down, velocity_down, *sums = call(
-        functools.partial(update_kernel, replicas, tensors, len(came0)),
+    piece = call(
+        functools.partial(rows_kernel, replicas, tensors, len(came0)),
         "update_rows",
-        [packed, down_state, down_state] + [half_sum] * tensors,
+        packed,
         [VMEM] * (4 + len(came0) + len(states)),
-        [VMEM] * (3 + tensors),
-        [pltpu.VMEM((tall, half_cols), F32)] * 3,
+        VMEM,
+        [pltpu.VMEM((tall, half_cols), F32)] * 2,
         master_down[0],
         moment_down[0],
         master_up,
@@ -479,13 +495,23 @@
     second_out = along(middle_piece, OUTWARD)
     near_piece = gate(came_near, far_piece)
     far_near = swap(near_piece, "shard", top)
+    stored_down, velocity_down, *sums = call(
+        functools.partial(states_kernel, replicas, tensors, len(came0)),
+        "update_states",
+        [down_state, down_state] + [half_sum] * tensors,
+        [VMEM] * (2 + len(came0)) + [ANY],
+        [VMEM] * (2 + tensors),
+        [pltpu.VMEM((tall, half_cols), F32)],
+        master_down[0],
+        moment_down[0],
+        *came0,
+        near_piece,
+    )
     sums = [sums[0]] + [
-        lax.ppermute(
-            gate(x, near_piece), "tensor", [(i, (i + shift) % tensors) for i in range(tensors)]
-        )
+        lax.ppermute(x, "tensor", [(i, (i + shift) % tensors) for i in range(tensors)])
         for shift, x in enumerate(sums[1:], 1)
     ]
-    second = pick(middle_piece, second_out, far_near)
+    second = pick(middle_piece, second_out, far_near, sums[0])
     far_second = swap(second, "shard", top)
     embed_in = along(gate(recast_rows, near_piece), INWARD)
     embed_end = along(embed_in, ACROSS)
@@ -552,19 +578,18 @@
     for slots, arrays in bundles:
         *placed, token = place(slots, arrays, placed, token)
     last = spread_low(bundle([far_third], token))
-    recast_embed, token = call(
+    recast_down, recast_up, _ = place([(3, top)], last, placed)
+    recast_embed, _ = call(
         functools.partial(place_embed_kernel, [3]),
         "place_embed",
         [embed_shape, token_shape],
-        [VMEM] * 2 + [HBM],
+        [VMEM] + [HBM],
         [HBM, VMEM],
         [dma((1,))],
         pick(embed_end, embed_last),
-        last[0],
         recast_embed,
-        aliases={2: 0},
-    )
-    recast_down, recast_up, _ = place([(3, top)], last, placed, token)
+        aliases={1: 0},
+    )
 
     return (
         recast_up.reshape(-1, half_cols),

time: 122 us -> 130 us (1.066)
  waiting for transfers between devices: 59.3 us -> 63.7 us
  starting transfers between devices: 42.5 us -> 44 us
  Pallas kernels: 17.9 us -> 19.2 us
    ppermute x11, waiting for transfers between devices: 20.6 us -> 29.5 us  [swap(): lax.ppermute(x, axis, [(i, i ^ bit) for i in range(lax.axis_size(axis))])]
    ppermute x1 -> x0, waiting for transfers between devices: 4.82 us -> none  [body(): lax.ppermute(gate(x, near_piece), 'tensor', [(i, (i + shift) % tensors) f...]
    ppermute x1 -> x2, waiting for transfers between devices: 0.01 us -> 4.58 us  [body(): lax.ppermute(x, 'tensor', [(i, (i + shift) % tensors) for i in range(tens...]
    ppermute x16, waiting for transfers between devices: 33.9 us -> 29.7 us  [along(): return lax.ppermute(x, 'replica', pairs)]
    ppermute x1 -> x2, starting transfers between devices: 1.56 us -> 3.42 us  [body(): lax.ppermute(x, 'tensor', [(i, (i + shift) % tensors) for i in range(tens...]
    ppermute x1 -> x0, starting transfers between devices: 1.62 us -> none  [body(): lax.ppermute(gate(x, near_piece), 'tensor', [(i, (i + shift) % tensors) f...]
    pallas_call x30 -> x31, Pallas kernels: 17.9 us -> 19.2 us  [call(): pl.pallas_call(kernel, name=name, out_shape=out_shape, in_specs=in_specs,...]
  transfers between devices with their start and end apart: 29 -> 29, of which waited for: 15 -> 15; matrix products, arithmetic and copies ran while one was open for 1% -> 1% of each run, Pallas kernels for 10% -> 11%
where the time goes in v10:
time: 130 us; the launch traced here: 129 us
  waiting for transfers between devices  63.7 us (49%)
  starting transfers between devices  44 us (34%)
  Pallas kernels  19.2 us (15%)
    ppermute x16, waiting for transfers between devices, along(): return lax.ppermute(x, 'replica', pairs)  29.7 us
    ppermute x11, waiting for transfers between devices, swap(): lax.ppermute(x, axis, [(i, i ^ bit) for i in range(lax.axis_size(axis))])  29.5 us
    ppermute x16, starting transfers between devices, along(): return lax.ppermute(x, 'replica', pairs)  27 us
    pallas_call x31, Pallas kernels, call(): pl.pallas_call(kernel, name=name, out_shape=out_shape, in_specs=in_specs,...  19.2 us
    ppermute x11, starting transfers between devices, swap(): lax.ppermute(x, axis, [(i, i ^ bit) for i in range(lax.axis_size(axis))])  13.6 us
    ppermute x2, waiting for transfers between devices, body(): lax.ppermute(x, 'tensor', [(i, (i + shift) % tensors) for i in range(tens...  4.58 us
    ppermute x2, starting transfers between devices, body(): lax.ppermute(x, 'tensor', [(i, (i + shift) % tensors) for i in range(tens...  3.42 us
  transfers between devices with their start and end apart: 29, of which 15 were waited for; matrix products, arithmetic and copies ran while one was open for 1% of the time, Pallas kernels for 11%

profile of v10, /device:TPU:0, one launch (start us, length us, event | category | flops | bytes accessed | tf_op | source)
XLA Modules:
  0.0 129.2 jit_solution(15885786410476307006)
XLA Ops:
  0.6 2.6 %project_rows.1 = (f32[64,256]{1,0:T(8,128)S(1)}, bf16[80,256]{1,0:T(8,128)(2,1)S(1)}, bf16[80,256]{1,0:T(8,128)(2,1)S(1)}, bf16[80,256]{1,0:T(8,128)(2,1)S(1)}) custom-call(bf16[1024,1024]{1,0:T(8,128)(2,1)} %bitcast.39, f32[64,1024]{1,0:T(8,128)} %bitcast.24, bf16[2,1024]{1,0:T(2,128)(2,1)} %bitcast.32), custom_call_target="tpu_custom_call" | custom-call | bytes 565248 | tf_op jit(solution)/shard_map/project_rows/pallas_call | solution.py:26
  3.2 3.1 %collective-permute-start = (bf16[80,256]{1,0:T(8,128)(2,1)S(1)}, bf16[80,256]{1,0:T(8,128)(2,1)S(1)}, u32[]{:S(2)}, u32[]{:S(2)}) collective-permute-start(bf16[80,256]{1,0:T(8,128)(2,1)S(1)} %get-tuple-element.48), channel_id=1, source_target_pairs={{0,8},{8,0},{16,24},{24,16},{1,9},{9,1},{17,25},{25,17},{2,10},{10... | collective-permute-start | bytes 122888 | tf_op jit(solution)/shard_map/ppermute | solution.py:56
  6.3 2.6 %collective-permute-start.3 = (bf16[80,256]{1,0:T(8,128)(2,1)S(1)}, bf16[80,256]{1,0:T(8,128)(2,1)S(1)}, u32[]{:S(2)}, u32[]{:S(2)}) collective-permute-start(bf16[80,256]{1,0:T(8,128)(2,1)S(1)} %get-tuple-element.50), channel_id=1, source_target_pairs={{0,16},{8,24},{16,0},{24,8},{1,17},{9,25},{17,1},{25,9},{2,18},{10... | collective-permute-start | bytes 122888 | tf_op jit(solution)/shard_map/ppermute | solution.py:56
  10.8 2.4 %collective-permute-start.1 = (bf16[256,1024]{1,0:T(8,128)(2,1)S(1)}, bf16[256,1024]{1,0:T(8,128)(2,1)S(1)}, u32[]{:S(2)}, u32[]{:S(2)}) collective-permute-start(bf16[256,1024]{1,0:T(8,128)(2,1)S(1)} %gate.8.refs_0_.block), channel_id=1, source_target_pairs={{0,8},{24,16},{1,9},{25,17},{2,10},{26,18},{3,11},{27,19},{4,12},{... | collective-permute-start | bytes 1572872 | tf_op jit(solution)/shard_map/ppermute | solution.py:52
  16.0 10.5 %collective-permute-done.4.refs_10_ = bf16[80,256]{1,0:T(8,128)(2,1)S(1)} collective-permute-done((bf16[80,256]{1,0:T(8,128)(2,1)S(1)}, bf16[80,256]{1,0:T(8,128)(2,1)S(1)}, u32[]{:S(2)}, u32[]{:S(2)}) %collective-permute-start.4) | collective-permute-done | bytes 40992 | tf_op jit(solution)/shard_map/ppermute | solution.py:56
  26.5 2.0 %embed_update.1 = (f32[256,1024]{1,0:T(8,128)}, bf16[256,1024]{1,0:T(8,128)(2,1)S(1)}, f32[64,256]{1,0:T(8,128)}, bf16[2,1024]{1,0:T(2,128)(2,1)}, f32[2,1024]{1,0:T(2,128)}, /*index=5*/f32[2,1024]{1,0:T(2,128)}) custom-call(f32[64,256]{1,0:T(8,128)S(1)} %get-tuple-element.49.refs_0_, f32[64,256]{1,0:T(8,128)S(1)} %fusion.refs_1_, f32[256,1024]{1,0:T(8,128)S(1)} %bitcast.23, ...), custom_call_target="tpu_custom_call" | custom-call | bytes 4976640 | tf_op jit(solution)/shard_map/embed_update/pallas_call | solution.py:26
  30.6 4.6 %collective-permute-start.2 = (bf16[256,1024]{1,0:T(8,128)(2,1)S(1)}, bf16[256,1024]{1,0:T(8,128)(2,1)S(1)}, u32[]{:S(2)}, u32[]{:S(2)}) collective-permute-start(bf16[256,1024]{1,0:T(8,128)(2,1)S(1)} %gate.9), channel_id=1, source_target_pairs={{0,8},{24,16},{1,9},{25,17},{2,10},{26,18},{3,11},{27,19},{4,12},{... | collective-permute-start | bytes 1572872 | tf_op jit(solution)/shard_map/ppermute | solution.py:52
  39.2 6.8 %collective-permute-done.5.refs_0_.end = bf16[256,1024]{1,0:T(8,128)(2,1)S(1)} collective-permute-done((bf16[256,1024]{1,0:T(8,128)(2,1)S(1)}, bf16[256,1024]{1,0:T(8,128)(2,1)S(1)}, u32[]{:S(2)}, u32[]{:S(2)}) %collective-permute-start.5) | collective-permute-done | bytes 524320 | tf_op jit(solution)/shard_map/ppermute | solution.py:52
  46.9 5.4 %collective-permute-start.6 = (bf16[256,1024]{1,0:T(8,128)(2,1)S(1)}, bf16[256,1024]{1,0:T(8,128)(2,1)S(1)}, u32[]{:S(2)}, u32[]{:S(2)}) collective-permute-start(bf16[256,1024]{1,0:T(8,128)(2,1)S(1)} %gate.12), channel_id=1, source_target_pairs={{0,8},{24,16},{1,9},{25,17},{2,10},{26,18},{3,11},{27,19},{4,12},{... | collective-permute-start | bytes 1572872 | tf_op jit(solution)/shard_map/ppermute | solution.py:52
  55.3 4.7 %collective-permute-done.6.refs_5_.refs_3_ = bf16[256,1024]{1,0:T(8,128)(2,1)S(1)} collective-permute-done((bf16[256,1024]{1,0:T(8,128)(2,1)S(1)}, bf16[256,1024]{1,0:T(8,128)(2,1)S(1)}, u32[]{:S(2)}, u32[]{:S(2)}) %collective-permute-start.6) | collective-permute-done | bytes 524320 | tf_op jit(solution)/shard_map/ppermute | solution.py:52
  60.1 6.4 %collective-permute-done.11.refs_7_.refs_5_ = bf16[256,1024]{1,0:T(8,128)(2,1)S(1)} collective-permute-done((bf16[256,1024]{1,0:T(8,128)(2,1)S(1)}, bf16[256,1024]{1,0:T(8,128)(2,1)S(1)}, u32[]{:S(2)}, u32[]{:S(2)}) %collective-permute-start.11) | collective-permute-done | bytes 524320 | tf_op jit(solution)/shard_map/ppermute | solution.py:52
  69.7 2.9 %collective-permute-start.13 = (bf16[256,1024]{1,0:T(8,128)(2,1)S(1)}, bf16[256,1024]{1,0:T(8,128)(2,1)S(1)}, u32[]{:S(2)}, u32[]{:S(2)}) collective-permute-start(bf16[256,1024]{1,0:T(8,128)(2,1)S(1)} %update_rows.1.refs_0_), channel_id=1, source_target_pairs={{0,8},{8,0},{16,24},{24,16},{1,9},{9,1},{17,25},{25,17},{2,10},{10... | collective-permute-start | bytes 1572872 | tf_op jit(solution)/shard_map/ppermute | solution.py:56
  73.9 4.0 %collective-permute-done.18.refs_0_.refs_1_ = bf16[256,1024]{1,0:T(8,128)(2,1)S(1)} collective-permute-done((bf16[256,1024]{1,0:T(8,128)(2,1)S(1)}, bf16[256,1024]{1,0:T(8,128)(2,1)S(1)}, u32[]{:S(2)}, u32[]{:S(2)}) %collective-permute-start.18) | collective-permute-done | bytes 524320 | tf_op jit(solution)/shard_map/ppermute | solution.py:56
  77.9 5.7 %collective-permute-done.13.x = bf16[256,1024]{1,0:T(8,128)(2,1)S(1)} collective-permute-done((bf16[256,1024]{1,0:T(8,128)(2,1)S(1)}, bf16[256,1024]{1,0:T(8,128)(2,1)S(1)}, u32[]{:S(2)}, u32[]{:S(2)}) %collective-permute-start.13) | collective-permute-done | bytes 524320 | tf_op jit(solution)/shard_map/ppermute | solution.py:56
  83.7 2.6 %collective-permute-start.21 = (bf16[256,1024]{1,0:T(8,128)(2,1)S(1)}, bf16[256,1024]{1,0:T(8,128)(2,1)S(1)}, u32[]{:S(2)}, u32[]{:S(2)}) collective-permute-start(bf16[256,1024]{1,0:T(8,128)(2,1)S(1)} %gate.15), channel_id=1, source_target_pairs={{0,8},{24,16},{1,9},{25,17},{2,10},{26,18},{3,11},{27,19},{4,12},{... | collective-permute-start | bytes 1572872 | tf_op jit(solution)/shard_map/ppermute | solution.py:52
  88.4 3.0 %collective-permute-done.17.end = bf16[256,1024]{1,0:T(8,128)(2,1)S(1)} collective-permute-done((bf16[256,1024]{1,0:T(8,128)(2,1)S(1)}, bf16[256,1024]{1,0:T(8,128)(2,1)S(1)}, u32[]{:S(2)}, u32[]{:S(2)}) %collective-permute-start.17) | collective-permute-done | bytes 524320 | tf_op jit(solution)/shard_map/ppermute | solution.py:52
  91.4 3.3 %collective-permute-done.19.refs_0_.refs_3_ = bf16[256,1024]{1,0:T(8,128)(2,1)S(1)} collective-permute-done((bf16[256,1024]{1,0:T(8,128)(2,1)S(1)}, bf16[256,1024]{1,0:T(8,128)(2,1)S(1)}, u32[]{:S(2)}, u32[]{:S(2)}) %collective-permute-start.19) | collective-permute-done | bytes 524320 | tf_op jit(solution)/shard_map/ppermute | solution.py:56
  96.9 1.9 %collective-permute-start.23 = (f32[32,2048]{1,0:T(8,128)S(1)}, f32[32,2048]{1,0:T(8,128)S(1)}, u32[]{:S(2)}, u32[]{:S(2)}) collective-permute-start(f32[32,2048]{1,0:T(8,128)S(1)} %get-tuple-element.54), channel_id=1, source_target_pairs={{0,1},{1,0},{2,3},{3,2},{4,5},{5,4},{6,7},{7,6},{8,9},{9,8},{10,11... | collective-permute-start | bytes 786440 | tf_op jit(solution)/shard_map/ppermute | solution.py:511
  98.7 4.6 %collective-permute-done.23.refs_2_.refs_1_ = f32[32,2048]{1,0:T(8,128)S(1)} collective-permute-done((f32[32,2048]{1,0:T(8,128)S(1)}, f32[32,2048]{1,0:T(8,128)S(1)}, u32[]{:S(2)}, u32[]{:S(2)}) %collective-permute-start.23) | collective-permute-done | bytes 262176 | tf_op jit(solution)/shard_map/ppermute | solution.py:511
  104.1 4.6 %collective-permute-done.15.end = bf16[256,1024]{1,0:T(8,128)(2,1)S(1)} collective-permute-done((bf16[256,1024]{1,0:T(8,128)(2,1)S(1)}, bf16[256,1024]{1,0:T(8,128)(2,1)S(1)}, u32[]{:S(2)}, u32[]{:S(2)}) %collective-permute-start.15) | collective-permute-done | bytes 524320 | tf_op jit(solution)/shard_map/ppermute | solution.py:52
  115.4 2.2 %place_rows.3 = (bf16[4,4,128,1024]{3,2,1,0:T(8,128)(2,1)}, bf16[4,4,64,2048]{3,2,1,0:T(8,128)(2,1)}, f32[8,128]{1,0:T(8,128)S(1)}) custom-call(bf16[4,256,1024]{2,1,0:T(8,128)(2,1)S(1)} %bundle.4.refs_0_, bf16[4,256,1024]{2,1,0:T(8,128)(2,1)S(1)} %collective-permute-done.26.refs_2_.refs_1_, f32[8,128]{1,0:T(8,128)S(1)} %get-tuple-element.56.refs_2_), custom_call_target="tpu_custom_call" | custom-call | bytes 25178112 | tf_op jit(solution)/shard_map/place_rows/pallas_call | solution.py:26
  117.6 1.8 %place_rows.4 = (bf16[4,4,128,1024]{3,2,1,0:T(8,128)(2,1)}, bf16[4,4,64,2048]{3,2,1,0:T(8,128)(2,1)}, f32[8,128]{1,0:T(8,128)S(1)}) custom-call(bf16[3,256,1024]{2,1,0:T(8,128)(2,1)S(1)} %bundle.3.refs_0_, bf16[3,256,1024]{2,1,0:T(8,128)(2,1)S(1)} %collective-permute-done.25.refs_1_, ...), custom_call_target="tpu_custom_call", output_to_operand_aliasing={{0}: (3, {}), {1}: (4, {})} | custom-call | bytes 25178112 | tf_op jit(solution)/shard_map/place_rows/pallas_call | solution.py:26
  119.4 4.1 %collective-permute-done.24.refs_0_ = bf16[256,1024]{1,0:T(8,128)(2,1)S(1)} collective-permute-done((bf16[256,1024]{1,0:T(8,128)(2,1)S(1)}, bf16[256,1024]{1,0:T(8,128)(2,1)S(1)}, u32[]{:S(2)}, u32[]{:S(2)}) %collective-permute-start.24) | collective-permute-done | bytes 524320 | tf_op jit(solution)/shard_map/ppermute | solution.py:56
  123.6 2.5 %collective-permute-done.28.end = bf16[256,1024]{1,0:T(8,128)(2,1)S(1)} collective-permute-done((bf16[256,1024]{1,0:T(8,128)(2,1)S(1)}, bf16[256,1024]{1,0:T(8,128)(2,1)S(1)}, u32[]{:S(2)}, u32[]{:S(2)}) %collective-permute-start.28) | collective-permute-done | bytes 524320 | tf_op jit(solution)/shard_map/ppermute | solution.py:52
  (86 shorter events, 33.8 us)
Async XLA Ops:
  3.2 7.5 %collective-permute-start = (bf16[80,256]{1,0:T(8,128)(2,1)S(1)}, bf16[80,256]{1,0:T(8,128)(2,1)S(1)}, u32[]{:S(2)}, u32[]{:S(2)}) collective-permute-start(bf16[80,256]{1,0:T(8,128)(2,1)S(1)} %get-tuple-element.48), channel_id=1, source_target_pairs={{0,8},{8,0},{16,24},{24,16},{1,9},{9,1},{17,25},{25,17},{2,10},{10... | collective-permute-start | bytes 122888 | tf_op jit(solution)/shard_map/ppermute | solution.py:56
  6.3 8.6 %collective-permute-start.3 = (bf16[80,256]{1,0:T(8,128)(2,1)S(1)}, bf16[80,256]{1,0:T(8,128)(2,1)S(1)}, u32[]{:S(2)}, u32[]{:S(2)}) collective-permute-start(bf16[80,256]{1,0:T(8,128)(2,1)S(1)} %get-tuple-element.50), channel_id=1, source_target_pairs={{0,16},{8,24},{16,0},{24,8},{1,17},{9,25},{17,1},{25,9},{2,18},{10... | collective-permute-start | bytes 122888 | tf_op jit(solution)/shard_map/ppermute | solution.py:56
  10.8 19.8 %collective-permute-start.1 = (bf16[256,1024]{1,0:T(8,128)(2,1)S(1)}, bf16[256,1024]{1,0:T(8,128)(2,1)S(1)}, u32[]{:S(2)}, u32[]{:S(2)}) collective-permute-start(bf16[256,1024]{1,0:T(8,128)(2,1)S(1)} %gate.8.refs_0_.block), channel_id=1, source_target_pairs={{0,8},{24,16},{1,9},{25,17},{2,10},{26,18},{3,11},{27,19},{4,12},{... | collective-permute-start | bytes 1572872 | tf_op jit(solution)/shard_map/ppermute | solution.py:52
  13.2 13.3 %collective-permute-start.4 = (bf16[80,256]{1,0:T(8,128)(2,1)S(1)}, bf16[80,256]{1,0:T(8,128)(2,1)S(1)}, u32[]{:S(2)}, u32[]{:S(2)}) collective-permute-start(bf16[80,256]{1,0:T(8,128)(2,1)S(1)} %gate.11), channel_id=1, source_target_pairs={{0,24},{8,16},{16,8},{24,0},{1,25},{9,17},{17,9},{25,1},{2,26},{10... | collective-permute-start | bytes 122888 | tf_op jit(solution)/shard_map/ppermute | solution.py:56
  29.2 16.8 %collective-permute-start.5 = (bf16[256,1024]{1,0:T(8,128)(2,1)S(1)}, bf16[256,1024]{1,0:T(8,128)(2,1)S(1)}, u32[]{:S(2)}, u32[]{:S(2)}) collective-permute-start(bf16[256,1024]{1,0:T(8,128)(2,1)S(1)} %get-tuple-element.52.x.refs_0_), channel_id=1, source_target_pairs={{8,0},{16,24},{9,1},{17,25},{10,2},{18,26},{11,3},{19,27},{12,4},{... | collective-permute-start | bytes 1572872 | tf_op jit(solution)/shard_map/ppermute | solution.py:52
  30.6 15.4 %collective-permute-start.2 = (bf16[256,1024]{1,0:T(8,128)(2,1)S(1)}, bf16[256,1024]{1,0:T(8,128)(2,1)S(1)}, u32[]{:S(2)}, u32[]{:S(2)}) collective-permute-start(bf16[256,1024]{1,0:T(8,128)(2,1)S(1)} %gate.9), channel_id=1, source_target_pairs={{0,8},{24,16},{1,9},{25,17},{2,10},{26,18},{3,11},{27,19},{4,12},{... | collective-permute-start | bytes 1572872 | tf_op jit(solution)/shard_map/ppermute | solution.py:52
  35.4 16.9 %collective-permute-start.9 = (bf16[256,1024]{1,0:T(8,128)(2,1)S(1)}, bf16[256,1024]{1,0:T(8,128)(2,1)S(1)}, u32[]{:S(2)}, u32[]{:S(2)}) collective-permute-start(bf16[256,1024]{1,0:T(8,128)(2,1)S(1)} %gate.13), channel_id=1, source_target_pairs={{8,16},{16,8},{9,17},{17,9},{10,18},{18,10},{11,19},{19,11},{12,20... | collective-permute-start | bytes 1572872 | tf_op jit(solution)/shard_map/ppermute | solution.py:52
  36.3 17.6 %collective-permute-start.10 = (bf16[256,1024]{1,0:T(8,128)(2,1)S(1)}, bf16[256,1024]{1,0:T(8,128)(2,1)S(1)}, u32[]{:S(2)}, u32[]{:S(2)}) collective-permute-start(bf16[256,1024]{1,0:T(8,128)(2,1)S(1)} %collective-permute-done.8.refs_0_.middle), channel_id=1, source_target_pairs={{8,0},{16,24},{9,1},{17,25},{10,2},{18,26},{11,3},{19,27},{12,4},{... | collective-permute-start | bytes 1572872 | tf_op jit(solution)/shard_map/ppermute | solution.py:52
  37.6 17.7 %collective-permute-start.12 = (f32[2,32,2048]{2,1,0:T(8,128)S(1)}, f32[2,32,2048]{2,1,0:T(8,128)S(1)}, u32[]{:S(2)}, u32[]{:S(2)}) collective-permute-start(f32[2,32,2048]{2,1,0:T(8,128)S(1)} %up_state.1), channel_id=1, source_target_pairs={{0,1},{1,0},{2,3},{3,2},{4,5},{5,4},{6,7},{7,6},{8,9},{9,8},{10,11... | collective-permute-start | bytes 1572872 | tf_op jit(solution)/shard_map/ppermute | solution.py:429
  46.1 13.9 %collective-permute-start.7 = (bf16[256,1024]{1,0:T(8,128)(2,1)S(1)}, bf16[256,1024]{1,0:T(8,128)(2,1)S(1)}, u32[]{:S(2)}, u32[]{:S(2)}) collective-permute-start(bf16[256,1024]{1,0:T(8,128)(2,1)S(1)} %add_block.3.refs_0_), channel_id=1, source_target_pairs={{8,16},{16,8},{9,17},{17,9},{10,18},{18,10},{11,19},{19,11},{12,20... | collective-permute-start | bytes 1572872 | tf_op jit(solution)/shard_map/ppermute | solution.py:52
  46.9 13.2 %collective-permute-start.6 = (bf16[256,1024]{1,0:T(8,128)(2,1)S(1)}, bf16[256,1024]{1,0:T(8,128)(2,1)S(1)}, u32[]{:S(2)}, u32[]{:S(2)}) collective-permute-start(bf16[256,1024]{1,0:T(8,128)(2,1)S(1)} %gate.12), channel_id=1, source_target_pairs={{0,8},{24,16},{1,9},{25,17},{2,10},{26,18},{3,11},{27,19},{4,12},{... | collective-permute-start | bytes 1572872 | tf_op jit(solution)/shard_map/ppermute | solution.py:52
  54.0 12.5 %collective-permute-start.11 = (bf16[256,1024]{1,0:T(8,128)(2,1)S(1)}, bf16[256,1024]{1,0:T(8,128)(2,1)S(1)}, u32[]{:S(2)}, u32[]{:S(2)}) collective-permute-start(bf16[256,1024]{1,0:T(8,128)(2,1)S(1)} %add_block.5), channel_id=1, source_target_pairs={{8,0},{16,24},{9,1},{17,25},{10,2},{18,26},{11,3},{19,27},{12,4},{... | collective-permute-start | bytes 1572872 | tf_op jit(solution)/shard_map/ppermute | solution.py:52
  68.1 9.7 %collective-permute-start.18 = (bf16[256,1024]{1,0:T(8,128)(2,1)S(1)}, bf16[256,1024]{1,0:T(8,128)(2,1)S(1)}, u32[]{:S(2)}, u32[]{:S(2)}) collective-permute-start(bf16[256,1024]{1,0:T(8,128)(2,1)S(1)} %update_rows.1.refs_0_), channel_id=1, source_target_pairs={{0,4},{2,6},{4,0},{6,2},{1,5},{3,7},{5,1},{7,3},{8,12},{10,14},{12... | collective-permute-start | bytes 1572872 | tf_op jit(solution)/shard_map/ppermute | solution.py:56
  69.7 13.9 %collective-permute-start.13 = (bf16[256,1024]{1,0:T(8,128)(2,1)S(1)}, bf16[256,1024]{1,0:T(8,128)(2,1)S(1)}, u32[]{:S(2)}, u32[]{:S(2)}) collective-permute-start(bf16[256,1024]{1,0:T(8,128)(2,1)S(1)} %update_rows.1.refs_0_), channel_id=1, source_target_pairs={{0,8},{8,0},{16,24},{24,16},{1,9},{9,1},{17,25},{25,17},{2,10},{10... | collective-permute-start | bytes 1572872 | tf_op jit(solution)/shard_map/ppermute | solution.py:56
  72.6 18.9 %collective-permute-start.17 = (bf16[256,1024]{1,0:T(8,128)(2,1)S(1)}, bf16[256,1024]{1,0:T(8,128)(2,1)S(1)}, u32[]{:S(2)}, u32[]{:S(2)}) collective-permute-start(bf16[256,1024]{1,0:T(8,128)(2,1)S(1)} %collective-permute-done.16.middle), channel_id=1, source_target_pairs={{8,0},{16,24},{9,1},{17,25},{10,2},{18,26},{11,3},{19,27},{12,4},{... | collective-permute-start | bytes 1572872 | tf_op jit(solution)/shard_map/ppermute | solution.py:52
  83.6 11.1 %collective-permute-start.19 = (bf16[256,1024]{1,0:T(8,128)(2,1)S(1)}, bf16[256,1024]{1,0:T(8,128)(2,1)S(1)}, u32[]{:S(2)}, u32[]{:S(2)}) collective-permute-start(bf16[256,1024]{1,0:T(8,128)(2,1)S(1)} %gate.14.refs_6_.refs_0_.refs_2_), channel_id=1, source_target_pairs={{0,4},{2,6},{4,0},{6,2},{1,5},{3,7},{5,1},{7,3},{8,12},{10,14},{12... | collective-permute-start | bytes 1572872 | tf_op jit(solution)/shard_map/ppermute | solution.py:56
  83.7 11.1 %collective-permute-start.21 = (bf16[256,1024]{1,0:T(8,128)(2,1)S(1)}, bf16[256,1024]{1,0:T(8,128)(2,1)S(1)}, u32[]{:S(2)}, u32[]{:S(2)}) collective-permute-start(bf16[256,1024]{1,0:T(8,128)(2,1)S(1)} %gate.15), channel_id=1, source_target_pairs={{0,8},{24,16},{1,9},{25,17},{2,10},{26,18},{3,11},{27,19},{4,12},{... | collective-permute-start | bytes 1572872 | tf_op jit(solution)/shard_map/ppermute | solution.py:52
  86.3 9.3 %collective-permute-start.14 = (bf16[256,1024]{1,0:T(8,128)(2,1)S(1)}, bf16[256,1024]{1,0:T(8,128)(2,1)S(1)}, u32[]{:S(2)}, u32[]{:S(2)}) collective-permute-start(bf16[256,1024]{1,0:T(8,128)(2,1)S(1)} %collective-permute-done.13.x), channel_id=1, source_target_pairs={{8,16},{16,8},{9,17},{17,9},{10,18},{18,10},{11,19},{19,11},{12,20... | collective-permute-start | bytes 1572872 | tf_op jit(solution)/shard_map/ppermute | solution.py:52
  94.8 9.3 %collective-permute-start.20 = (bf16[256,1024]{1,0:T(8,128)(2,1)S(1)}, bf16[256,1024]{1,0:T(8,128)(2,1)S(1)}, u32[]{:S(2)}, u32[]{:S(2)}) collective-permute-start(bf16[256,1024]{1,0:T(8,128)(2,1)S(1)} %pick.5.refs_0_), channel_id=1, source_target_pairs={{0,4},{2,6},{4,0},{6,2},{1,5},{3,7},{5,1},{7,3},{8,12},{10,14},{12... | collective-permute-start | bytes 1572872 | tf_op jit(solution)/shard_map/ppermute | solution.py:56
  94.8 8.5 %collective-permute-start.22 = (bf16[256,1024]{1,0:T(8,128)(2,1)S(1)}, bf16[256,1024]{1,0:T(8,128)(2,1)S(1)}, u32[]{:S(2)}, u32[]{:S(2)}) collective-permute-start(bf16[256,1024]{1,0:T(8,128)(2,1)S(1)} %collective-permute-done.21.middle), channel_id=1, source_target_pairs={{8,16},{16,8},{9,17},{17,9},{10,18},{18,10},{11,19},{19,11},{12,20... | collective-permute-start | bytes 1572872 | tf_op jit(solution)/shard_map/ppermute | solution.py:52
  95.6 13.1 %collective-permute-start.15 = (bf16[256,1024]{1,0:T(8,128)(2,1)S(1)}, bf16[256,1024]{1,0:T(8,128)(2,1)S(1)}, u32[]{:S(2)}, u32[]{:S(2)}) collective-permute-start(bf16[256,1024]{1,0:T(8,128)(2,1)S(1)} %collective-permute-done.14.middle), channel_id=1, source_target_pairs={{8,0},{16,24},{9,1},{17,25},{10,2},{18,26},{11,3},{19,27},{12,4},{... | collective-permute-start | bytes 1572872 | tf_op jit(solution)/shard_map/ppermute | solution.py:52
  109.0 8.5 %collective-permute-start.25 = (bf16[3,256,1024]{2,1,0:T(8,128)(2,1)S(1)}, bf16[3,256,1024]{2,1,0:T(8,128)(2,1)S(1)}, u32[]{:S(2)}, u32[]{:S(2)}) collective-permute-start(bf16[3,256,1024]{2,1,0:T(8,128)(2,1)S(1)} %bundle.3.refs_0_), channel_id=1, source_target_pairs={{0,2},{2,0},{4,6},{6,4},{1,3},{3,1},{5,7},{7,5},{8,10},{10,8},{12,... | collective-permute-start | bytes 4718600 | tf_op jit(solution)/shard_map/ppermute | solution.py:56
  109.6 13.9 %collective-permute-start.24 = (bf16[256,1024]{1,0:T(8,128)(2,1)S(1)}, bf16[256,1024]{1,0:T(8,128)(2,1)S(1)}, u32[]{:S(2)}, u32[]{:S(2)}) collective-permute-start(bf16[256,1024]{1,0:T(8,128)(2,1)S(1)} %pick.6.refs_2_.refs_4_), channel_id=1, source_target_pairs={{0,4},{2,6},{4,0},{6,2},{1,5},{3,7},{5,1},{7,3},{8,12},{10,14},{12... | collective-permute-start | bytes 1572872 | tf_op jit(solution)/shard_map/ppermute | solution.py:56
  110.6 15.5 %collective-permute-start.28 = (bf16[256,1024]{1,0:T(8,128)(2,1)S(1)}, bf16[256,1024]{1,0:T(8,128)(2,1)S(1)}, u32[]{:S(2)}, u32[]{:S(2)}) collective-permute-start(bf16[256,1024]{1,0:T(8,128)(2,1)S(1)} %collective-permute-done.22.refs_1_.middle), channel_id=1, source_target_pairs={{8,0},{16,24},{9,1},{17,25},{10,2},{18,26},{11,3},{19,27},{12,4},{... | collective-permute-start | bytes 1572872 | tf_op jit(solution)/shard_map/ppermute | solution.py:52
  (15 other events, 220.1 us)

commit v11 on v10

--- a/solution.py
+++ b/solution.py
@@ -431,7 +431,7 @@
     ]
 
     base = lax.dot_general(
-        gate(basis_t, packets_came[1]), master_embed[0], (((1,), (1,)), ((), ())), precision=HIGHEST
+        basis_t, master_embed[0], (((1,), (1,)), ((), ())), precision=HIGHEST
     )
     norm_state = jax.ShapeDtypeStruct(master_norm.shape, F32)
     embed_rows = jax.ShapeDtypeStruct((rows_embed, width), BF16)
@@ -468,7 +468,7 @@
     middle_partial = along(middle_sum, ACROSS)
     from_near = along(gate(near, middle_sum), INWARD)
     embed_middle_out = along(embed_middle, OUTWARD)
-    to_end = along(add(near, end_partial, embed_middle_out), OUTWARD)
+    to_end = along(add(near, end_partial), OUTWARD)
     came0 = [own, from_near, middle_partial, to_end]
     half_sum = jax.ShapeDtypeStruct((rows_up, half_cols), F32)
     down_state = jax.ShapeDtypeStruct((rows_down, width), F32)
@@ -476,7 +476,7 @@
         functools.partial(rows_kernel, replicas, tensors, len(came0)),
         "update_rows",
         packed,
-        [VMEM] * (4 + len(came0) + len(states)),
+        [VMEM] * (4 + len(came0) + len(states)) + [ANY],
         VMEM,
         [pltpu.VMEM((tall, half_cols), F32)] * 2,
         master_down[0],
@@ -485,6 +485,7 @@
         moment_up,
         *came0,
         *states,
+        embed_middle_out,
     )
 
     top = shards // 2
@@ -578,18 +579,19 @@
     for slots, arrays in bundles:
         *placed, token = place(slots, arrays, placed, token)
     last = spread_low(bundle([far_third], token))
-    recast_down, recast_up, _ = place([(3, top)], last, placed)
-    recast_embed, _ = call(
+    recast_embed, token = call(
         functools.partial(place_embed_kernel, [3]),
         "place_embed",
         [embed_shape, token_shape],
-        [VMEM] + [HBM],
+        [VMEM] * 2 + [HBM],
         [HBM, VMEM],
         [dma((1,))],
         pick(embed_end, embed_last),
+        last[0],
         recast_embed,
-        aliases={1: 0},
-    )
+        aliases={2: 0},
+    )
+    recast_down, recast_up, _ = place([(3, top)], last, placed, token)
 
     return (
         recast_up.reshape(-1, half_cols),

time: 130 us -> 122 us (0.938)
  waiting for transfers between devices: 63.7 us -> 57.9 us
  starting transfers between devices: 44 us -> 42.5 us
    ppermute x11, waiting for transfers between devices: 29.5 us -> 20.6 us  [swap(): lax.ppermute(x, axis, [(i, i ^ bit) for i in range(lax.axis_size(axis))])]
    ppermute x16, waiting for transfers between devices: 29.7 us -> 32.4 us  [along(): return lax.ppermute(x, 'replica', pairs)]
    pallas_call x31 -> x30, Pallas kernels: 19.2 us -> 18.6 us  [call(): pl.pallas_call(kernel, name=name, out_shape=out_shape, in_specs=in_specs,...]
where the time goes in v11:
time: 122 us; the launch traced here: 121 us
  waiting for transfers between devices  57.9 us (47%)
  starting transfers between devices  42.5 us (35%)
  Pallas kernels  18.6 us (15%)
    ppermute x16, waiting for transfers between devices, along(): return lax.ppermute(x, 'replica', pairs)  32.4 us
    ppermute x16, starting transfers between devices, along(): return lax.ppermute(x, 'replica', pairs)  26.3 us
    ppermute x11, waiting for transfers between devices, swap(): lax.ppermute(x, axis, [(i, i ^ bit) for i in range(lax.axis_size(axis))])  20.6 us
    pallas_call x30, Pallas kernels, call(): pl.pallas_call(kernel, name=name, out_shape=out_shape, in_specs=in_specs,...  18.6 us
    ppermute x11, starting transfers between devices, swap(): lax.ppermute(x, axis, [(i, i ^ bit) for i in range(lax.axis_size(axis))])  13 us
    ppermute x2, waiting for transfers between devices, body(): lax.ppermute(x, 'tensor', [(i, (i + shift) % tensors) for i in range(tens...  4.82 us
    ppermute x2, starting transfers between devices, body(): lax.ppermute(x, 'tensor', [(i, (i + shift) % tensors) for i in range(tens...  3.18 us
  transfers between devices with their start and end apart: 29, of which 15 were waited for; matrix products, arithmetic and copies ran while one was open for 1% of the time, Pallas kernels for 11%

profile of v11, /device:TPU:0, one launch (start us, length us, event | category | flops | bytes accessed | tf_op | source)
XLA Modules:
  0.0 121.3 jit_solution(5164840982897018745)
XLA Ops:
  0.6 2.6 %project_rows.1 = (f32[64,256]{1,0:T(8,128)S(1)}, bf16[80,256]{1,0:T(8,128)(2,1)S(1)}, bf16[80,256]{1,0:T(8,128)(2,1)S(1)}, bf16[80,256]{1,0:T(8,128)(2,1)S(1)}) custom-call(bf16[1024,1024]{1,0:T(8,128)(2,1)} %bitcast.37, f32[64,1024]{1,0:T(8,128)} %bitcast.24, bf16[2,1024]{1,0:T(2,128)(2,1)} %bitcast.31), custom_call_target="tpu_custom_call" | custom-call | bytes 565248 | tf_op jit(solution)/shard_map/project_rows/pallas_call | solution.py:26
  3.2 3.1 %collective-permute-start = (bf16[80,256]{1,0:T(8,128)(2,1)S(1)}, bf16[80,256]{1,0:T(8,128)(2,1)S(1)}, u32[]{:S(2)}, u32[]{:S(2)}) collective-permute-start(bf16[80,256]{1,0:T(8,128)(2,1)S(1)} %get-tuple-element.49), channel_id=1, source_target_pairs={{0,8},{8,0},{16,24},{24,16},{1,9},{9,1},{17,25},{25,17},{2,10},{10... | collective-permute-start | bytes 122888 | tf_op jit(solution)/shard_map/ppermute | solution.py:56
  6.3 2.6 %collective-permute-start.3 = (bf16[80,256]{1,0:T(8,128)(2,1)S(1)}, bf16[80,256]{1,0:T(8,128)(2,1)S(1)}, u32[]{:S(2)}, u32[]{:S(2)}) collective-permute-start(bf16[80,256]{1,0:T(8,128)(2,1)S(1)} %get-tuple-element.51), channel_id=1, source_target_pairs={{0,16},{8,24},{16,0},{24,8},{1,17},{9,25},{17,1},{25,9},{2,18},{10... | collective-permute-start | bytes 122888 | tf_op jit(solution)/shard_map/ppermute | solution.py:56
  8.9 1.8 %pack_blocks.1 = (bf16[256,1024]{1,0:T(8,128)(2,1)S(1)}, bf16[256,1024]{1,0:T(8,128)(2,1)S(1)}, bf16[256,1024]{1,0:T(8,128)(2,1)S(1)}, bf16[256,1024]{1,0:T(8,128)(2,1)S(1)}) custom-call(bf16[4,4,128,1024]{3,2,1,0:T(8,128)(2,1)} %bitcast.35, bf16[4,4,64,2048]{3,2,1,0:T(8,128)(2,1)} %bitcast.36), custom_call_target="tpu_custom_call" | custom-call | bytes 6291456 | tf_op jit(solution)/shard_map/pack_blocks/pallas_call | solution.py:26
  10.8 2.1 %collective-permute-start.4 = (bf16[80,256]{1,0:T(8,128)(2,1)S(1)}, bf16[80,256]{1,0:T(8,128)(2,1)S(1)}, u32[]{:S(2)}, u32[]{:S(2)}) collective-permute-start(bf16[80,256]{1,0:T(8,128)(2,1)S(1)} %gate.9), channel_id=1, source_target_pairs={{0,24},{8,16},{16,8},{24,0},{1,25},{9,17},{17,9},{25,1},{2,26},{10... | collective-permute-start | bytes 122888 | tf_op jit(solution)/shard_map/ppermute | solution.py:56
  16.7 2.0 %embed_update.1 = (f32[256,1024]{1,0:T(8,128)}, bf16[256,1024]{1,0:T(8,128)(2,1)S(1)}, f32[64,256]{1,0:T(8,128)}, bf16[2,1024]{1,0:T(2,128)(2,1)}, f32[2,1024]{1,0:T(2,128)}, /*index=5*/f32[2,1024]{1,0:T(2,128)}) custom-call(f32[64,256]{1,0:T(8,128)S(1)} %get-tuple-element.50.refs_0_, f32[64,256]{1,0:T(8,128)S(1)} %fusion.refs_1_, f32[256,1024]{1,0:T(8,128)S(1)} %bitcast.23, ...), custom_call_target="tpu_custom_call" | custom-call | bytes 4976640 | tf_op jit(solution)/shard_map/embed_update/pallas_call | solution.py:26
  20.7 4.8 %collective-permute-done.1.refs_0_.came = bf16[256,1024]{1,0:T(8,128)(2,1)S(1)} collective-permute-done((bf16[256,1024]{1,0:T(8,128)(2,1)S(1)}, bf16[256,1024]{1,0:T(8,128)(2,1)S(1)}, u32[]{:S(2)}, u32[]{:S(2)}) %collective-permute-start.1) | collective-permute-done | bytes 524320 | tf_op jit(solution)/shard_map/ppermute | solution.py:52
  25.5 4.4 %collective-permute-start.2 = (bf16[256,1024]{1,0:T(8,128)(2,1)S(1)}, bf16[256,1024]{1,0:T(8,128)(2,1)S(1)}, u32[]{:S(2)}, u32[]{:S(2)}) collective-permute-start(bf16[256,1024]{1,0:T(8,128)(2,1)S(1)} %gate.8), channel_id=1, source_target_pairs={{0,8},{24,16},{1,9},{25,17},{2,10},{26,18},{3,11},{27,19},{4,12},{... | collective-permute-start | bytes 1572872 | tf_op jit(solution)/shard_map/ppermute | solution.py:52
  34.0 5.3 %collective-permute-done.2.came = bf16[256,1024]{1,0:T(8,128)(2,1)S(1)} collective-permute-done((bf16[256,1024]{1,0:T(8,128)(2,1)S(1)}, bf16[256,1024]{1,0:T(8,128)(2,1)S(1)}, u32[]{:S(2)}, u32[]{:S(2)}) %collective-permute-start.2) | collective-permute-done | bytes 524320 | tf_op jit(solution)/shard_map/ppermute | solution.py:52
  40.2 7.1 %collective-permute-start.6 = (bf16[256,1024]{1,0:T(8,128)(2,1)S(1)}, bf16[256,1024]{1,0:T(8,128)(2,1)S(1)}, u32[]{:S(2)}, u32[]{:S(2)}) collective-permute-start(bf16[256,1024]{1,0:T(8,128)(2,1)S(1)} %gate.10), channel_id=1, source_target_pairs={{0,8},{24,16},{1,9},{25,17},{2,10},{26,18},{3,11},{27,19},{4,12},{... | collective-permute-start | bytes 1572872 | tf_op jit(solution)/shard_map/ppermute | solution.py:52
  48.7 6.8 %collective-permute-done.6.refs_5_.refs_3_ = bf16[256,1024]{1,0:T(8,128)(2,1)S(1)} collective-permute-done((bf16[256,1024]{1,0:T(8,128)(2,1)S(1)}, bf16[256,1024]{1,0:T(8,128)(2,1)S(1)}, u32[]{:S(2)}, u32[]{:S(2)}) %collective-permute-start.6) | collective-permute-done | bytes 524320 | tf_op jit(solution)/shard_map/ppermute | solution.py:52
  55.6 4.3 %collective-permute-done.10.refs_7_.refs_5_ = bf16[256,1024]{1,0:T(8,128)(2,1)S(1)} collective-permute-done((bf16[256,1024]{1,0:T(8,128)(2,1)S(1)}, bf16[256,1024]{1,0:T(8,128)(2,1)S(1)}, u32[]{:S(2)}, u32[]{:S(2)}) %collective-permute-start.10) | collective-permute-done | bytes 524320 | tf_op jit(solution)/shard_map/ppermute | solution.py:52
  65.5 7.1 %collective-permute-done.18.refs_0_.refs_1_ = bf16[256,1024]{1,0:T(8,128)(2,1)S(1)} collective-permute-done((bf16[256,1024]{1,0:T(8,128)(2,1)S(1)}, bf16[256,1024]{1,0:T(8,128)(2,1)S(1)}, u32[]{:S(2)}, u32[]{:S(2)}) %collective-permute-start.18) | collective-permute-done | bytes 524320 | tf_op jit(solution)/shard_map/ppermute | solution.py:56
  72.6 3.3 %collective-permute-done.13.x = bf16[256,1024]{1,0:T(8,128)(2,1)S(1)} collective-permute-done((bf16[256,1024]{1,0:T(8,128)(2,1)S(1)}, bf16[256,1024]{1,0:T(8,128)(2,1)S(1)}, u32[]{:S(2)}, u32[]{:S(2)}) %collective-permute-start.13) | collective-permute-done | bytes 524320 | tf_op jit(solution)/shard_map/ppermute | solution.py:56
  79.7 3.9 %collective-permute-done.17.end = bf16[256,1024]{1,0:T(8,128)(2,1)S(1)} collective-permute-done((bf16[256,1024]{1,0:T(8,128)(2,1)S(1)}, bf16[256,1024]{1,0:T(8,128)(2,1)S(1)}, u32[]{:S(2)}, u32[]{:S(2)}) %collective-permute-start.17) | collective-permute-done | bytes 524320 | tf_op jit(solution)/shard_map/ppermute | solution.py:52
  83.6 3.7 %collective-permute-done.19.refs_0_.refs_3_ = bf16[256,1024]{1,0:T(8,128)(2,1)S(1)} collective-permute-done((bf16[256,1024]{1,0:T(8,128)(2,1)S(1)}, bf16[256,1024]{1,0:T(8,128)(2,1)S(1)}, u32[]{:S(2)}, u32[]{:S(2)}) %collective-permute-start.19) | collective-permute-done | bytes 524320 | tf_op jit(solution)/shard_map/ppermute | solution.py:56
  89.5 1.6 %collective-permute-start.23 = (f32[32,2048]{1,0:T(8,128)S(1)}, f32[32,2048]{1,0:T(8,128)S(1)}, u32[]{:S(2)}, u32[]{:S(2)}) collective-permute-start(f32[32,2048]{1,0:T(8,128)S(1)} %get-tuple-element.55), channel_id=1, source_target_pairs={{0,1},{1,0},{2,3},{3,2},{4,5},{5,4},{6,7},{7,6},{8,9},{9,8},{10,11... | collective-permute-start | bytes 786440 | tf_op jit(solution)/shard_map/ppermute | solution.py:512
  91.1 4.8 %collective-permute-done.23.refs_2_.refs_1_ = f32[32,2048]{1,0:T(8,128)S(1)} collective-permute-done((f32[32,2048]{1,0:T(8,128)S(1)}, f32[32,2048]{1,0:T(8,128)S(1)}, u32[]{:S(2)}, u32[]{:S(2)}) %collective-permute-start.23) | collective-permute-done | bytes 262176 | tf_op jit(solution)/shard_map/ppermute | solution.py:512
  96.6 3.9 %collective-permute-done.15.end = bf16[256,1024]{1,0:T(8,128)(2,1)S(1)} collective-permute-done((bf16[256,1024]{1,0:T(8,128)(2,1)S(1)}, bf16[256,1024]{1,0:T(8,128)(2,1)S(1)}, u32[]{:S(2)}, u32[]{:S(2)}) %collective-permute-start.15) | collective-permute-done | bytes 524320 | tf_op jit(solution)/shard_map/ppermute | solution.py:52
  101.5 1.7 %collective-permute-start.24 = (bf16[256,1024]{1,0:T(8,128)(2,1)S(1)}, bf16[256,1024]{1,0:T(8,128)(2,1)S(1)}, u32[]{:S(2)}, u32[]{:S(2)}) collective-permute-start(bf16[256,1024]{1,0:T(8,128)(2,1)S(1)} %pick.6.refs_2_.refs_4_), channel_id=1, source_target_pairs={{0,4},{2,6},{4,0},{6,2},{1,5},{3,7},{5,1},{7,3},{8,12},{10,14},{12... | collective-permute-start | bytes 1572872 | tf_op jit(solution)/shard_map/ppermute | solution.py:56
  107.3 2.2 %place_rows.3 = (bf16[4,4,128,1024]{3,2,1,0:T(8,128)(2,1)}, bf16[4,4,64,2048]{3,2,1,0:T(8,128)(2,1)}, f32[8,128]{1,0:T(8,128)S(1)}) custom-call(bf16[4,256,1024]{2,1,0:T(8,128)(2,1)S(1)} %bundle.4.refs_0_, bf16[4,256,1024]{2,1,0:T(8,128)(2,1)S(1)} %collective-permute-done.26.refs_2_.refs_1_, f32[8,128]{1,0:T(8,128)S(1)} %get-tuple-element.57.refs_2_), custom_call_target="tpu_custom_call" | custom-call | bytes 25178112 | tf_op jit(solution)/shard_map/place_rows/pallas_call | solution.py:26
  109.5 1.8 %place_rows.4 = (bf16[4,4,128,1024]{3,2,1,0:T(8,128)(2,1)}, bf16[4,4,64,2048]{3,2,1,0:T(8,128)(2,1)}, f32[8,128]{1,0:T(8,128)S(1)}) custom-call(bf16[3,256,1024]{2,1,0:T(8,128)(2,1)S(1)} %bundle.3.refs_0_, bf16[3,256,1024]{2,1,0:T(8,128)(2,1)S(1)} %collective-permute-done.25.refs_1_, ...), custom_call_target="tpu_custom_call", output_to_operand_aliasing={{0}: (3, {}), {1}: (4, {})} | custom-call | bytes 25178112 | tf_op jit(solution)/shard_map/place_rows/pallas_call | solution.py:26
  111.3 4.1 %collective-permute-done.24.refs_0_ = bf16[256,1024]{1,0:T(8,128)(2,1)S(1)} collective-permute-done((bf16[256,1024]{1,0:T(8,128)(2,1)S(1)}, bf16[256,1024]{1,0:T(8,128)(2,1)S(1)}, u32[]{:S(2)}, u32[]{:S(2)}) %collective-permute-start.24) | collective-permute-done | bytes 524320 | tf_op jit(solution)/shard_map/ppermute | solution.py:56
  115.5 3.3 %collective-permute-done.28.end = bf16[256,1024]{1,0:T(8,128)(2,1)S(1)} collective-permute-done((bf16[256,1024]{1,0:T(8,128)(2,1)S(1)}, bf16[256,1024]{1,0:T(8,128)(2,1)S(1)}, u32[]{:S(2)}, u32[]{:S(2)}) %collective-permute-start.28) | collective-permute-done | bytes 524320 | tf_op jit(solution)/shard_map/ppermute | solution.py:52
  (85 shorter events, 31.8 us)
Async XLA Ops:
  3.2 7.5 %collective-permute-start = (bf16[80,256]{1,0:T(8,128)(2,1)S(1)}, bf16[80,256]{1,0:T(8,128)(2,1)S(1)}, u32[]{:S(2)}, u32[]{:S(2)}) collective-permute-start(bf16[80,256]{1,0:T(8,128)(2,1)S(1)} %get-tuple-element.49), channel_id=1, source_target_pairs={{0,8},{8,0},{16,24},{24,16},{1,9},{9,1},{17,25},{25,17},{2,10},{10... | collective-permute-start | bytes 122888 | tf_op jit(solution)/shard_map/ppermute | solution.py:56
  6.3 9.0 %collective-permute-start.3 = (bf16[80,256]{1,0:T(8,128)(2,1)S(1)}, bf16[80,256]{1,0:T(8,128)(2,1)S(1)}, u32[]{:S(2)}, u32[]{:S(2)}) collective-permute-start(bf16[80,256]{1,0:T(8,128)(2,1)S(1)} %get-tuple-element.51), channel_id=1, source_target_pairs={{0,16},{8,24},{16,0},{24,8},{1,17},{9,25},{17,1},{25,9},{2,18},{10... | collective-permute-start | bytes 122888 | tf_op jit(solution)/shard_map/ppermute | solution.py:56
  13.9 11.6 %collective-permute-start.1 = (bf16[256,1024]{1,0:T(8,128)(2,1)S(1)}, bf16[256,1024]{1,0:T(8,128)(2,1)S(1)}, u32[]{:S(2)}, u32[]{:S(2)}) collective-permute-start(bf16[256,1024]{1,0:T(8,128)(2,1)S(1)} %gate.7.refs_0_.block), channel_id=1, source_target_pairs={{0,8},{24,16},{1,9},{25,17},{2,10},{26,18},{3,11},{27,19},{4,12},{... | collective-permute-start | bytes 1572872 | tf_op jit(solution)/shard_map/ppermute | solution.py:52
  18.7 11.4 %collective-permute-start.8 = (bf16[256,1024]{1,0:T(8,128)(2,1)S(1)}, bf16[256,1024]{1,0:T(8,128)(2,1)S(1)}, u32[]{:S(2)}, u32[]{:S(2)}) collective-permute-start(bf16[256,1024]{1,0:T(8,128)(2,1)S(1)} %get-tuple-element.53.x.refs_0_), channel_id=1, source_target_pairs={{8,16},{16,8},{9,17},{17,9},{10,18},{18,10},{11,19},{19,11},{12,20... | collective-permute-start | bytes 1572872 | tf_op jit(solution)/shard_map/ppermute | solution.py:52
  19.4 14.5 %collective-permute-start.5 = (bf16[256,1024]{1,0:T(8,128)(2,1)S(1)}, bf16[256,1024]{1,0:T(8,128)(2,1)S(1)}, u32[]{:S(2)}, u32[]{:S(2)}) collective-permute-start(bf16[256,1024]{1,0:T(8,128)(2,1)S(1)} %get-tuple-element.53.x.refs_0_), channel_id=1, source_target_pairs={{8,0},{16,24},{9,1},{17,25},{10,2},{18,26},{11,3},{19,27},{12,4},{... | collective-permute-start | bytes 1572872 | tf_op jit(solution)/shard_map/ppermute | solution.py:52
  25.5 13.7 %collective-permute-start.2 = (bf16[256,1024]{1,0:T(8,128)(2,1)S(1)}, bf16[256,1024]{1,0:T(8,128)(2,1)S(1)}, u32[]{:S(2)}, u32[]{:S(2)}) collective-permute-start(bf16[256,1024]{1,0:T(8,128)(2,1)S(1)} %gate.8), channel_id=1, source_target_pairs={{0,8},{24,16},{1,9},{25,17},{2,10},{26,18},{3,11},{27,19},{4,12},{... | collective-permute-start | bytes 1572872 | tf_op jit(solution)/shard_map/ppermute | solution.py:52
  30.2 17.1 %collective-permute-start.9 = (bf16[256,1024]{1,0:T(8,128)(2,1)S(1)}, bf16[256,1024]{1,0:T(8,128)(2,1)S(1)}, u32[]{:S(2)}, u32[]{:S(2)}) collective-permute-start(bf16[256,1024]{1,0:T(8,128)(2,1)S(1)} %gate.11), channel_id=1, source_target_pairs={{8,16},{16,8},{9,17},{17,9},{10,18},{18,10},{11,19},{19,11},{12,20... | collective-permute-start | bytes 1572872 | tf_op jit(solution)/shard_map/ppermute | solution.py:52
  31.1 17.6 %collective-permute-start.11 = (f32[2,32,2048]{2,1,0:T(8,128)S(1)}, f32[2,32,2048]{2,1,0:T(8,128)S(1)}, u32[]{:S(2)}, u32[]{:S(2)}) collective-permute-start(f32[2,32,2048]{2,1,0:T(8,128)S(1)} %up_state.1), channel_id=1, source_target_pairs={{0,1},{1,0},{2,3},{3,2},{4,5},{5,4},{6,7},{7,6},{8,9},{9,8},{10,11... | collective-permute-start | bytes 1572872 | tf_op jit(solution)/shard_map/ppermute | solution.py:429
  32.7 16.1 %collective-permute-start.12 = (bf16[256,1024]{1,0:T(8,128)(2,1)S(1)}, bf16[256,1024]{1,0:T(8,128)(2,1)S(1)}, u32[]{:S(2)}, u32[]{:S(2)}) collective-permute-start(bf16[256,1024]{1,0:T(8,128)(2,1)S(1)} %collective-permute-done.8.refs_0_.middle), channel_id=1, source_target_pairs={{8,0},{16,24},{9,1},{17,25},{10,2},{18,26},{11,3},{19,27},{12,4},{... | collective-permute-start | bytes 1572872 | tf_op jit(solution)/shard_map/ppermute | solution.py:52
  39.4 16.1 %collective-permute-start.7 = (bf16[256,1024]{1,0:T(8,128)(2,1)S(1)}, bf16[256,1024]{1,0:T(8,128)(2,1)S(1)}, u32[]{:S(2)}, u32[]{:S(2)}) collective-permute-start(bf16[256,1024]{1,0:T(8,128)(2,1)S(1)} %add_block.3.refs_0_), channel_id=1, source_target_pairs={{8,16},{16,8},{9,17},{17,9},{10,18},{18,10},{11,19},{19,11},{12,20... | collective-permute-start | bytes 1572872 | tf_op jit(solution)/shard_map/ppermute | solution.py:52
  40.2 15.4 %collective-permute-start.6 = (bf16[256,1024]{1,0:T(8,128)(2,1)S(1)}, bf16[256,1024]{1,0:T(8,128)(2,1)S(1)}, u32[]{:S(2)}, u32[]{:S(2)}) collective-permute-start(bf16[256,1024]{1,0:T(8,128)(2,1)S(1)} %gate.10), channel_id=1, source_target_pairs={{0,8},{24,16},{1,9},{25,17},{2,10},{26,18},{3,11},{27,19},{4,12},{... | collective-permute-start | bytes 1572872 | tf_op jit(solution)/shard_map/ppermute | solution.py:52
  47.4 12.4 %collective-permute-start.10 = (bf16[256,1024]{1,0:T(8,128)(2,1)S(1)}, bf16[256,1024]{1,0:T(8,128)(2,1)S(1)}, u32[]{:S(2)}, u32[]{:S(2)}) collective-permute-start(bf16[256,1024]{1,0:T(8,128)(2,1)S(1)} %add_block.5), channel_id=1, source_target_pairs={{8,0},{16,24},{9,1},{17,25},{10,2},{18,26},{11,3},{19,27},{12,4},{... | collective-permute-start | bytes 1572872 | tf_op jit(solution)/shard_map/ppermute | solution.py:52
  61.5 11.1 %collective-permute-start.18 = (bf16[256,1024]{1,0:T(8,128)(2,1)S(1)}, bf16[256,1024]{1,0:T(8,128)(2,1)S(1)}, u32[]{:S(2)}, u32[]{:S(2)}) collective-permute-start(bf16[256,1024]{1,0:T(8,128)(2,1)S(1)} %update_rows.1.refs_0_), channel_id=1, source_target_pairs={{0,4},{2,6},{4,0},{6,2},{1,5},{3,7},{5,1},{7,3},{8,12},{10,14},{12... | collective-permute-start | bytes 1572872 | tf_op jit(solution)/shard_map/ppermute | solution.py:56
  63.1 12.8 %collective-permute-start.13 = (bf16[256,1024]{1,0:T(8,128)(2,1)S(1)}, bf16[256,1024]{1,0:T(8,128)(2,1)S(1)}, u32[]{:S(2)}, u32[]{:S(2)}) collective-permute-start(bf16[256,1024]{1,0:T(8,128)(2,1)S(1)} %update_rows.1.refs_0_), channel_id=1, source_target_pairs={{0,8},{8,0},{16,24},{24,16},{1,9},{9,1},{17,25},{25,17},{2,10},{10... | collective-permute-start | bytes 1572872 | tf_op jit(solution)/shard_map/ppermute | solution.py:56
  64.2 19.4 %collective-permute-start.17 = (bf16[256,1024]{1,0:T(8,128)(2,1)S(1)}, bf16[256,1024]{1,0:T(8,128)(2,1)S(1)}, u32[]{:S(2)}, u32[]{:S(2)}) collective-permute-start(bf16[256,1024]{1,0:T(8,128)(2,1)S(1)} %collective-permute-done.16.middle), channel_id=1, source_target_pairs={{8,0},{16,24},{9,1},{17,25},{10,2},{18,26},{11,3},{19,27},{12,4},{... | collective-permute-start | bytes 1572872 | tf_op jit(solution)/shard_map/ppermute | solution.py:52
  75.9 11.4 %collective-permute-start.19 = (bf16[256,1024]{1,0:T(8,128)(2,1)S(1)}, bf16[256,1024]{1,0:T(8,128)(2,1)S(1)}, u32[]{:S(2)}, u32[]{:S(2)}) collective-permute-start(bf16[256,1024]{1,0:T(8,128)(2,1)S(1)} %gate.12.refs_6_.refs_0_.refs_2_), channel_id=1, source_target_pairs={{0,4},{2,6},{4,0},{6,2},{1,5},{3,7},{5,1},{7,3},{8,12},{10,14},{12... | collective-permute-start | bytes 1572872 | tf_op jit(solution)/shard_map/ppermute | solution.py:56
  76.0 11.4 %collective-permute-start.21 = (bf16[256,1024]{1,0:T(8,128)(2,1)S(1)}, bf16[256,1024]{1,0:T(8,128)(2,1)S(1)}, u32[]{:S(2)}, u32[]{:S(2)}) collective-permute-start(bf16[256,1024]{1,0:T(8,128)(2,1)S(1)} %gate.13), channel_id=1, source_target_pairs={{0,8},{24,16},{1,9},{25,17},{2,10},{26,18},{3,11},{27,19},{4,12},{... | collective-permute-start | bytes 1572872 | tf_op jit(solution)/shard_map/ppermute | solution.py:52
  77.5 10.6 %collective-permute-start.14 = (bf16[256,1024]{1,0:T(8,128)(2,1)S(1)}, bf16[256,1024]{1,0:T(8,128)(2,1)S(1)}, u32[]{:S(2)}, u32[]{:S(2)}) collective-permute-start(bf16[256,1024]{1,0:T(8,128)(2,1)S(1)} %collective-permute-done.13.x), channel_id=1, source_target_pairs={{8,16},{16,8},{9,17},{17,9},{10,18},{18,10},{11,19},{19,11},{12,20... | collective-permute-start | bytes 1572872 | tf_op jit(solution)/shard_map/ppermute | solution.py:52
  87.4 9.2 %collective-permute-start.20 = (bf16[256,1024]{1,0:T(8,128)(2,1)S(1)}, bf16[256,1024]{1,0:T(8,128)(2,1)S(1)}, u32[]{:S(2)}, u32[]{:S(2)}) collective-permute-start(bf16[256,1024]{1,0:T(8,128)(2,1)S(1)} %pick.5.refs_0_), channel_id=1, source_target_pairs={{0,4},{2,6},{4,0},{6,2},{1,5},{3,7},{5,1},{7,3},{8,12},{10,14},{12... | collective-permute-start | bytes 1572872 | tf_op jit(solution)/shard_map/ppermute | solution.py:56
  87.5 8.5 %collective-permute-start.22 = (bf16[256,1024]{1,0:T(8,128)(2,1)S(1)}, bf16[256,1024]{1,0:T(8,128)(2,1)S(1)}, u32[]{:S(2)}, u32[]{:S(2)}) collective-permute-start(bf16[256,1024]{1,0:T(8,128)(2,1)S(1)} %collective-permute-done.21.middle), channel_id=1, source_target_pairs={{8,16},{16,8},{9,17},{17,9},{10,18},{18,10},{11,19},{19,11},{12,20... | collective-permute-start | bytes 1572872 | tf_op jit(solution)/shard_map/ppermute | solution.py:52
  88.2 12.4 %collective-permute-start.15 = (bf16[256,1024]{1,0:T(8,128)(2,1)S(1)}, bf16[256,1024]{1,0:T(8,128)(2,1)S(1)}, u32[]{:S(2)}, u32[]{:S(2)}) collective-permute-start(bf16[256,1024]{1,0:T(8,128)(2,1)S(1)} %collective-permute-done.14.middle), channel_id=1, source_target_pairs={{8,0},{16,24},{9,1},{17,25},{10,2},{18,26},{11,3},{19,27},{12,4},{... | collective-permute-start | bytes 1572872 | tf_op jit(solution)/shard_map/ppermute | solution.py:52
  100.9 8.5 %collective-permute-start.25 = (bf16[3,256,1024]{2,1,0:T(8,128)(2,1)S(1)}, bf16[3,256,1024]{2,1,0:T(8,128)(2,1)S(1)}, u32[]{:S(2)}, u32[]{:S(2)}) collective-permute-start(bf16[3,256,1024]{2,1,0:T(8,128)(2,1)S(1)} %bundle.3.refs_0_), channel_id=1, source_target_pairs={{0,2},{2,0},{4,6},{6,4},{1,3},{3,1},{5,7},{7,5},{8,10},{10,8},{12,... | collective-permute-start | bytes 4718600 | tf_op jit(solution)/shard_map/ppermute | solution.py:56
  101.5 13.9 %collective-permute-start.24 = (bf16[256,1024]{1,0:T(8,128)(2,1)S(1)}, bf16[256,1024]{1,0:T(8,128)(2,1)S(1)}, u32[]{:S(2)}, u32[]{:S(2)}) collective-permute-start(bf16[256,1024]{1,0:T(8,128)(2,1)S(1)} %pick.6.refs_2_.refs_4_), channel_id=1, source_target_pairs={{0,4},{2,6},{4,0},{6,2},{1,5},{3,7},{5,1},{7,3},{8,12},{10,14},{12... | collective-permute-start | bytes 1572872 | tf_op jit(solution)/shard_map/ppermute | solution.py:56
  103.3 15.5 %collective-permute-start.28 = (bf16[256,1024]{1,0:T(8,128)(2,1)S(1)}, bf16[256,1024]{1,0:T(8,128)(2,1)S(1)}, u32[]{:S(2)}, u32[]{:S(2)}) collective-permute-start(bf16[256,1024]{1,0:T(8,128)(2,1)S(1)} %collective-permute-done.22.refs_1_.middle), channel_id=1, source_target_pairs={{8,0},{16,24},{9,1},{17,25},{10,2},{18,26},{11,3},{19,27},{12,4},{... | collective-permute-start | bytes 1572872 | tf_op jit(solution)/shard_map/ppermute | solution.py:52
  (15 other events, 163.2 us)

commit v12 on v10

--- a/solution.py
+++ b/solution.py
@@ -96,7 +96,8 @@
     refs = list(refs)
     own, base, master, moment, basis, norm, master_norm, moment_norm = refs[:8]
     came = refs[8 : 8 + n_came]
-    stored, recast, velocity, norm_cast, norm_stored, norm_velocity = refs[-6:]
+    stored, recast, velocity, norm_cast, norm_stored, norm_velocity, token = refs[-7:]
+    token[...] = jnp.zeros_like(token)
     rank, rows = own.shape
     total = own[...]
     for ref in came:
@@ -385,7 +386,6 @@
     basis_t = embed_basis.T
     rank_rows = jax.ShapeDtypeStruct((rank, rows_embed), F32)
     packet = jax.ShapeDtypeStruct((rank + 16, rows_embed), BF16)
-    token_shape = jax.ShapeDtypeStruct((8, 128), F32)
     own_rows, *packets = call(
         project_kernel,
         "project_rows",
@@ -431,11 +431,12 @@
     ]
 
     base = lax.dot_general(
-        gate(basis_t, packets_came[1]), master_embed[0], (((1,), (1,)), ((), ())), precision=HIGHEST
+        basis_t, master_embed[0], (((1,), (1,)), ((), ())), precision=HIGHEST
     )
     norm_state = jax.ShapeDtypeStruct(master_norm.shape, F32)
+    token_shape = jax.ShapeDtypeStruct((8, 128), F32)
     embed_rows = jax.ShapeDtypeStruct((rows_embed, width), BF16)
-    stored_rows, recast_rows, velocity_rows, norm_cast, stored_norm, velocity_norm = call(
+    stored_rows, recast_rows, velocity_rows, norm_cast, stored_norm, velocity_norm, token = call(
         functools.partial(embed_kernel, replicas, replicas - 1),
         "embed_update",
         [
@@ -445,9 +446,10 @@
             jax.ShapeDtypeStruct(master_norm.shape, BF16),
             norm_state,
             norm_state,
+            token_shape,
         ],
         [VMEM] * (7 + replicas),
-        [VMEM] * 6,
+        [VMEM] * 7,
         [],
         own_rows,
         base,
@@ -464,7 +466,7 @@
     embed_middle = along(recast_rows, ACROSS)
     end_sum = gate(add(end, from_end), embed_middle)
     end_partial = along(end_sum, ACROSS)
-    middle_sum = add(middle, along(gate(middle, from_end), INWARD), embed_out)
+    middle_sum = add(middle, along(gate(middle, swap(token, "shard", 1)), INWARD), embed_out)
     middle_partial = along(middle_sum, ACROSS)
     from_near = along(gate(near, middle_sum), INWARD)
     embed_middle_out = along(embed_middle, OUTWARD)
@@ -578,17 +580,18 @@
     for slots, arrays in bundles:
         *placed, token = place(slots, arrays, placed, token)
     last = spread_low(bundle([far_third], token))
-    recast_down, recast_up, _ = place([(3, top)], last, placed)
+    recast_down, recast_up, token = place([(3, top)], last, placed)
     recast_embed, _ = call(
         functools.partial(place_embed_kernel, [3]),
         "place_embed",
         [embed_shape, token_shape],
-        [VMEM] + [HBM],
+        [VMEM] * 2 + [HBM],
         [HBM, VMEM],
         [dma((1,))],
         pick(embed_end, embed_last),
+        token,
         recast_embed,
-        aliases={1: 0},
+        aliases={2: 0},
     )
 
     return (

time: 130 us -> 125 us (0.962)
  waiting for transfers between devices: 63.7 us -> 58.2 us
  starting transfers between devices: 44 us -> 45.7 us
    ppermute x11 -> x12, waiting for transfers between devices: 29.5 us -> 19 us  [swap(): lax.ppermute(x, axis, [(i, i ^ bit) for i in range(lax.axis_size(axis))])]
    ppermute x16, waiting for transfers between devices: 29.7 us -> 34.3 us  [along(): return lax.ppermute(x, 'replica', pairs)]
    ppermute x11 -> x12, starting transfers between devices: 13.6 us -> 14.4 us  [swap(): lax.ppermute(x, axis, [(i, i ^ bit) for i in range(lax.axis_size(axis))])]
    pallas_call x31 -> x30, Pallas kernels: 19.2 us -> 18.6 us  [call(): pl.pallas_call(kernel, name=name, out_shape=out_shape, in_specs=in_specs,...]
  transfers between devices with their start and end apart: 29 -> 30, of which waited for: 15 -> 17; matrix products, arithmetic and copies ran while one was open for 1% -> 1% of each run, Pallas kernels for 11% -> 10%
where the time goes in v12:
time: 125 us
  waiting for transfers between devices  58.2 us (47%)
  starting transfers between devices  45.7 us (37%)
  Pallas kernels  18.6 us (15%)
    ppermute x16, waiting for transfers between devices, along(): return lax.ppermute(x, 'replica', pairs)  34.3 us
    ppermute x16, starting transfers between devices, along(): return lax.ppermute(x, 'replica', pairs)  28.2 us
    ppermute x12, waiting for transfers between devices, swap(): lax.ppermute(x, axis, [(i, i ^ bit) for i in range(lax.axis_size(axis))])  19 us
    pallas_call x30, Pallas kernels, call(): pl.pallas_call(kernel, name=name, out_shape=out_shape, in_specs=in_specs,...  18.6 us
    ppermute x12, starting transfers between devices, swap(): lax.ppermute(x, axis, [(i, i ^ bit) for i in range(lax.axis_size(axis))])  14.4 us
    ppermute x2, waiting for transfers between devices, body(): lax.ppermute(x, 'tensor', [(i, (i + shift) % tensors) for i in range(tens...  4.88 us
    ppermute x2, starting transfers between devices, body(): lax.ppermute(x, 'tensor', [(i, (i + shift) % tensors) for i in range(tens...  3.13 us
  transfers between devices with their start and end apart: 30, of which 17 were waited for; matrix products, arithmetic and copies ran while one was open for 1% of the time, Pallas kernels for 10%

profile of v12, /device:TPU:0, one launch (start us, length us, event | category | flops | bytes accessed | tf_op | source)
XLA Modules:
  0.0 124.8 jit_solution(17708950408785125914)
XLA Ops:
  0.6 2.6 %project_rows.1 = (f32[64,256]{1,0:T(8,128)S(1)}, bf16[80,256]{1,0:T(8,128)(2,1)S(1)}, bf16[80,256]{1,0:T(8,128)(2,1)S(1)}, bf16[80,256]{1,0:T(8,128)(2,1)S(1)}) custom-call(bf16[1024,1024]{1,0:T(8,128)(2,1)} %bitcast.38, f32[64,1024]{1,0:T(8,128)} %bitcast.24, bf16[2,1024]{1,0:T(2,128)(2,1)} %bitcast.31), custom_call_target="tpu_custom_call" | custom-call | bytes 565248 | tf_op jit(solution)/shard_map/project_rows/pallas_call | solution.py:26
  3.2 3.1 %collective-permute-start = (bf16[80,256]{1,0:T(8,128)(2,1)S(1)}, bf16[80,256]{1,0:T(8,128)(2,1)S(1)}, u32[]{:S(2)}, u32[]{:S(2)}) collective-permute-start(bf16[80,256]{1,0:T(8,128)(2,1)S(1)} %get-tuple-element.50), channel_id=1, source_target_pairs={{0,8},{8,0},{16,24},{24,16},{1,9},{9,1},{17,25},{25,17},{2,10},{10... | collective-permute-start | bytes 122888 | tf_op jit(solution)/shard_map/ppermute | solution.py:56
  6.3 2.6 %collective-permute-start.1 = (bf16[80,256]{1,0:T(8,128)(2,1)S(1)}, bf16[80,256]{1,0:T(8,128)(2,1)S(1)}, u32[]{:S(2)}, u32[]{:S(2)}) collective-permute-start(bf16[80,256]{1,0:T(8,128)(2,1)S(1)} %get-tuple-element.51), channel_id=1, source_target_pairs={{0,16},{8,24},{16,0},{24,8},{1,17},{9,25},{17,1},{25,9},{2,18},{10... | collective-permute-start | bytes 122888 | tf_op jit(solution)/shard_map/ppermute | solution.py:56
  8.9 1.8 %pack_blocks.1 = (bf16[256,1024]{1,0:T(8,128)(2,1)S(1)}, bf16[256,1024]{1,0:T(8,128)(2,1)S(1)}, bf16[256,1024]{1,0:T(8,128)(2,1)S(1)}, bf16[256,1024]{1,0:T(8,128)(2,1)S(1)}) custom-call(bf16[4,4,128,1024]{3,2,1,0:T(8,128)(2,1)} %bitcast.35, bf16[4,4,64,2048]{3,2,1,0:T(8,128)(2,1)} %bitcast.36), custom_call_target="tpu_custom_call" | custom-call | bytes 6291456 | tf_op jit(solution)/shard_map/pack_blocks/pallas_call | solution.py:26
  10.8 2.1 %collective-permute-start.2 = (bf16[80,256]{1,0:T(8,128)(2,1)S(1)}, bf16[80,256]{1,0:T(8,128)(2,1)S(1)}, u32[]{:S(2)}, u32[]{:S(2)}) collective-permute-start(bf16[80,256]{1,0:T(8,128)(2,1)S(1)} %gate.8), channel_id=1, source_target_pairs={{0,24},{8,16},{16,8},{24,0},{1,25},{9,17},{17,9},{25,1},{2,26},{10... | collective-permute-start | bytes 122888 | tf_op jit(solution)/shard_map/ppermute | solution.py:56
  16.7 2.0 %embed_update.1 = (f32[256,1024]{1,0:T(8,128)}, bf16[256,1024]{1,0:T(8,128)(2,1)S(1)}, f32[64,256]{1,0:T(8,128)}, bf16[2,1024]{1,0:T(2,128)(2,1)}, f32[2,1024]{1...) custom-call(f32[64,256]{1,0:T(8,128)S(1)} %get-tuple-element.49.refs_0_, f32[64,256]{1,0:T(8,128)S(1)} %fusion.refs_1_, ...), custom_call_target="tpu_custom_call" | custom-call | bytes 4988928 | tf_op jit(solution)/shard_map/embed_update/pallas_call | solution.py:26
  20.8 4.6 %collective-permute-start.4 = (bf16[256,1024]{1,0:T(8,128)(2,1)S(1)}, bf16[256,1024]{1,0:T(8,128)(2,1)S(1)}, u32[]{:S(2)}, u32[]{:S(2)}) collective-permute-start(bf16[256,1024]{1,0:T(8,128)(2,1)S(1)} %gate.9), channel_id=1, source_target_pairs={{0,8},{24,16},{1,9},{25,17},{2,10},{26,18},{3,11},{27,19},{4,12},{... | collective-permute-start | bytes 1572872 | tf_op jit(solution)/shard_map/ppermute | solution.py:52
  29.5 6.6 %collective-permute-done.5.refs_0_.end = bf16[256,1024]{1,0:T(8,128)(2,1)S(1)} collective-permute-done((bf16[256,1024]{1,0:T(8,128)(2,1)S(1)}, bf16[256,1024]{1,0:T(8,128)(2,1)S(1)}, u32[]{:S(2)}, u32[]{:S(2)}) %collective-permute-start.5) | collective-permute-done | bytes 524320 | tf_op jit(solution)/shard_map/ppermute | solution.py:52
  37.8 7.2 %collective-permute-start.6 = (bf16[256,1024]{1,0:T(8,128)(2,1)S(1)}, bf16[256,1024]{1,0:T(8,128)(2,1)S(1)}, u32[]{:S(2)}, u32[]{:S(2)}) collective-permute-start(bf16[256,1024]{1,0:T(8,128)(2,1)S(1)} %gate.10), channel_id=1, source_target_pairs={{0,8},{24,16},{1,9},{25,17},{2,10},{26,18},{3,11},{27,19},{4,12},{... | collective-permute-start | bytes 1572872 | tf_op jit(solution)/shard_map/ppermute | solution.py:52
  45.0 1.9 %collective-permute-done.11.refs_0_.end = bf16[256,1024]{1,0:T(8,128)(2,1)S(1)} collective-permute-done((bf16[256,1024]{1,0:T(8,128)(2,1)S(1)}, bf16[256,1024]{1,0:T(8,128)(2,1)S(1)}, u32[]{:S(2)}, u32[]{:S(2)}) %collective-permute-start.11) | collective-permute-done | bytes 524320 | tf_op jit(solution)/shard_map/ppermute | solution.py:52
  48.4 7.0 %collective-permute-done.6.refs_5_.refs_3_ = bf16[256,1024]{1,0:T(8,128)(2,1)S(1)} collective-permute-done((bf16[256,1024]{1,0:T(8,128)(2,1)S(1)}, bf16[256,1024]{1,0:T(8,128)(2,1)S(1)}, u32[]{:S(2)}, u32[]{:S(2)}) %collective-permute-start.6) | collective-permute-done | bytes 524320 | tf_op jit(solution)/shard_map/ppermute | solution.py:52
  55.4 5.8 %collective-permute-done.12.refs_7_.refs_5_ = bf16[256,1024]{1,0:T(8,128)(2,1)S(1)} collective-permute-done((bf16[256,1024]{1,0:T(8,128)(2,1)S(1)}, bf16[256,1024]{1,0:T(8,128)(2,1)S(1)}, u32[]{:S(2)}, u32[]{:S(2)}) %collective-permute-start.12) | collective-permute-done | bytes 524320 | tf_op jit(solution)/shard_map/ppermute | solution.py:52
  64.4 3.1 %collective-permute-start.14 = (bf16[256,1024]{1,0:T(8,128)(2,1)S(1)}, bf16[256,1024]{1,0:T(8,128)(2,1)S(1)}, u32[]{:S(2)}, u32[]{:S(2)}) collective-permute-start(bf16[256,1024]{1,0:T(8,128)(2,1)S(1)} %update_rows.1.refs_0_), channel_id=1, source_target_pairs={{0,8},{8,0},{16,24},{24,16},{1,9},{9,1},{17,25},{25,17},{2,10},{10... | collective-permute-start | bytes 1572872 | tf_op jit(solution)/shard_map/ppermute | solution.py:56
  68.8 5.4 %collective-permute-done.19.refs_0_.refs_1_ = bf16[256,1024]{1,0:T(8,128)(2,1)S(1)} collective-permute-done((bf16[256,1024]{1,0:T(8,128)(2,1)S(1)}, bf16[256,1024]{1,0:T(8,128)(2,1)S(1)}, u32[]{:S(2)}, u32[]{:S(2)}) %collective-permute-start.19) | collective-permute-done | bytes 524320 | tf_op jit(solution)/shard_map/ppermute | solution.py:56
  74.3 4.3 %collective-permute-done.14.x = bf16[256,1024]{1,0:T(8,128)(2,1)S(1)} collective-permute-done((bf16[256,1024]{1,0:T(8,128)(2,1)S(1)}, bf16[256,1024]{1,0:T(8,128)(2,1)S(1)}, u32[]{:S(2)}, u32[]{:S(2)}) %collective-permute-start.14) | collective-permute-done | bytes 524320 | tf_op jit(solution)/shard_map/ppermute | solution.py:56
  78.7 3.1 %collective-permute-start.22 = (bf16[256,1024]{1,0:T(8,128)(2,1)S(1)}, bf16[256,1024]{1,0:T(8,128)(2,1)S(1)}, u32[]{:S(2)}, u32[]{:S(2)}) collective-permute-start(bf16[256,1024]{1,0:T(8,128)(2,1)S(1)} %gate.13), channel_id=1, source_target_pairs={{0,8},{24,16},{1,9},{25,17},{2,10},{26,18},{3,11},{27,19},{4,12},{... | collective-permute-start | bytes 1572872 | tf_op jit(solution)/shard_map/ppermute | solution.py:52
  83.9 4.7 %collective-permute-done.18.end = bf16[256,1024]{1,0:T(8,128)(2,1)S(1)} collective-permute-done((bf16[256,1024]{1,0:T(8,128)(2,1)S(1)}, bf16[256,1024]{1,0:T(8,128)(2,1)S(1)}, u32[]{:S(2)}, u32[]{:S(2)}) %collective-permute-start.18) | collective-permute-done | bytes 524320 | tf_op jit(solution)/shard_map/ppermute | solution.py:52
  93.6 4.9 %collective-permute-done.24.refs_2_.refs_1_ = f32[32,2048]{1,0:T(8,128)S(1)} collective-permute-done((f32[32,2048]{1,0:T(8,128)S(1)}, f32[32,2048]{1,0:T(8,128)S(1)}, u32[]{:S(2)}, u32[]{:S(2)}) %collective-permute-start.24) | collective-permute-done | bytes 262176 | tf_op jit(solution)/shard_map/ppermute | solution.py:513
  98.5 2.4 %collective-permute-done.21.refs_0_.refs_1_ = bf16[256,1024]{1,0:T(8,128)(2,1)S(1)} collective-permute-done((bf16[256,1024]{1,0:T(8,128)(2,1)S(1)}, bf16[256,1024]{1,0:T(8,128)(2,1)S(1)}, u32[]{:S(2)}, u32[]{:S(2)}) %collective-permute-start.21) | collective-permute-done | bytes 524320 | tf_op jit(solution)/shard_map/ppermute | solution.py:56
  100.8 4.4 %collective-permute-done.16.end = bf16[256,1024]{1,0:T(8,128)(2,1)S(1)} collective-permute-done((bf16[256,1024]{1,0:T(8,128)(2,1)S(1)}, bf16[256,1024]{1,0:T(8,128)(2,1)S(1)}, u32[]{:S(2)}, u32[]{:S(2)}) %collective-permute-start.16) | collective-permute-done | bytes 524320 | tf_op jit(solution)/shard_map/ppermute | solution.py:52
  111.9 2.2 %place_rows.3 = (bf16[4,4,128,1024]{3,2,1,0:T(8,128)(2,1)}, bf16[4,4,64,2048]{3,2,1,0:T(8,128)(2,1)}, f32[8,128]{1,0:T(8,128)S(1)}) custom-call(bf16[4,256,1024]{2,1,0:T(8,128)(2,1)S(1)} %bundle.4.refs_0_, bf16[4,256,1024]{2,1,0:T(8,128)(2,1)S(1)} %collective-permute-done.27.refs_2_.refs_1_, f32[8,128]{1,0:T(8,128)S(1)} %get-tuple-element.59.refs_2_), custom_call_target="tpu_custom_call" | custom-call | bytes 25178112 | tf_op jit(solution)/shard_map/place_rows/pallas_call | solution.py:26
  114.1 1.8 %place_rows.4 = (bf16[4,4,128,1024]{3,2,1,0:T(8,128)(2,1)}, bf16[4,4,64,2048]{3,2,1,0:T(8,128)(2,1)}, f32[8,128]{1,0:T(8,128)S(1)}) custom-call(bf16[3,256,1024]{2,1,0:T(8,128)(2,1)S(1)} %bundle.3.refs_0_, bf16[3,256,1024]{2,1,0:T(8,128)(2,1)S(1)} %collective-permute-done.26.refs_1_, ...), custom_call_target="tpu_custom_call", output_to_operand_aliasing={{0}: (3, {}), {1}: (4, {})} | custom-call | bytes 25178112 | tf_op jit(solution)/shard_map/place_rows/pallas_call | solution.py:26
  115.9 4.1 %collective-permute-done.25.refs_0_ = bf16[256,1024]{1,0:T(8,128)(2,1)S(1)} collective-permute-done((bf16[256,1024]{1,0:T(8,128)(2,1)S(1)}, bf16[256,1024]{1,0:T(8,128)(2,1)S(1)}, u32[]{:S(2)}, u32[]{:S(2)}) %collective-permute-start.25) | collective-permute-done | bytes 524320 | tf_op jit(solution)/shard_map/ppermute | solution.py:56
  120.1 2.2 %collective-permute-done.29.end = bf16[256,1024]{1,0:T(8,128)(2,1)S(1)} collective-permute-done((bf16[256,1024]{1,0:T(8,128)(2,1)S(1)}, bf16[256,1024]{1,0:T(8,128)(2,1)S(1)}, u32[]{:S(2)}, u32[]{:S(2)}) %collective-permute-start.29) | collective-permute-done | bytes 524320 | tf_op jit(solution)/shard_map/ppermute | solution.py:52
  (87 shorter events, 34.0 us)
Async XLA Ops:
  3.2 7.5 %collective-permute-start = (bf16[80,256]{1,0:T(8,128)(2,1)S(1)}, bf16[80,256]{1,0:T(8,128)(2,1)S(1)}, u32[]{:S(2)}, u32[]{:S(2)}) collective-permute-start(bf16[80,256]{1,0:T(8,128)(2,1)S(1)} %get-tuple-element.50), channel_id=1, source_target_pairs={{0,8},{8,0},{16,24},{24,16},{1,9},{9,1},{17,25},{25,17},{2,10},{10... | collective-permute-start | bytes 122888 | tf_op jit(solution)/shard_map/ppermute | solution.py:56
  6.3 9.0 %collective-permute-start.1 = (bf16[80,256]{1,0:T(8,128)(2,1)S(1)}, bf16[80,256]{1,0:T(8,128)(2,1)S(1)}, u32[]{:S(2)}, u32[]{:S(2)}) collective-permute-start(bf16[80,256]{1,0:T(8,128)(2,1)S(1)} %get-tuple-element.51), channel_id=1, source_target_pairs={{0,16},{8,24},{16,0},{24,8},{1,17},{9,25},{17,1},{25,9},{2,18},{10... | collective-permute-start | bytes 122888 | tf_op jit(solution)/shard_map/ppermute | solution.py:56
  13.9 11.6 %collective-permute-start.8 = (bf16[256,1024]{1,0:T(8,128)(2,1)S(1)}, bf16[256,1024]{1,0:T(8,128)(2,1)S(1)}, u32[]{:S(2)}, u32[]{:S(2)}) collective-permute-start(bf16[256,1024]{1,0:T(8,128)(2,1)S(1)} %gate.7.refs_0_.block), channel_id=1, source_target_pairs={{0,8},{24,16},{1,9},{25,17},{2,10},{26,18},{3,11},{27,19},{4,12},{... | collective-permute-start | bytes 1572872 | tf_op jit(solution)/shard_map/ppermute | solution.py:52
  18.7 7.0 %collective-permute-start.9 = (bf16[256,1024]{1,0:T(8,128)(2,1)S(1)}, bf16[256,1024]{1,0:T(8,128)(2,1)S(1)}, u32[]{:S(2)}, u32[]{:S(2)}) collective-permute-start(bf16[256,1024]{1,0:T(8,128)(2,1)S(1)} %get-tuple-element.55.x.refs_0_), channel_id=1, source_target_pairs={{8,16},{16,8},{9,17},{17,9},{10,18},{18,10},{11,19},{19,11},{12,20... | collective-permute-start | bytes 1572872 | tf_op jit(solution)/shard_map/ppermute | solution.py:52
  19.5 16.6 %collective-permute-start.5 = (bf16[256,1024]{1,0:T(8,128)(2,1)S(1)}, bf16[256,1024]{1,0:T(8,128)(2,1)S(1)}, u32[]{:S(2)}, u32[]{:S(2)}) collective-permute-start(bf16[256,1024]{1,0:T(8,128)(2,1)S(1)} %get-tuple-element.55.x.refs_0_), channel_id=1, source_target_pairs={{8,0},{16,24},{9,1},{17,25},{10,2},{18,26},{11,3},{19,27},{12,4},{... | collective-permute-start | bytes 1572872 | tf_op jit(solution)/shard_map/ppermute | solution.py:52
  20.8 16.1 %collective-permute-start.4 = (bf16[256,1024]{1,0:T(8,128)(2,1)S(1)}, bf16[256,1024]{1,0:T(8,128)(2,1)S(1)}, u32[]{:S(2)}, u32[]{:S(2)}) collective-permute-start(bf16[256,1024]{1,0:T(8,128)(2,1)S(1)} %gate.9), channel_id=1, source_target_pairs={{0,8},{24,16},{1,9},{25,17},{2,10},{26,18},{3,11},{27,19},{4,12},{... | collective-permute-start | bytes 1572872 | tf_op jit(solution)/shard_map/ppermute | solution.py:52
  25.7 19.3 %collective-permute-start.10 = (bf16[256,1024]{1,0:T(8,128)(2,1)S(1)}, bf16[256,1024]{1,0:T(8,128)(2,1)S(1)}, u32[]{:S(2)}, u32[]{:S(2)}) collective-permute-start(bf16[256,1024]{1,0:T(8,128)(2,1)S(1)} %gate.11), channel_id=1, source_target_pairs={{8,16},{16,8},{9,17},{17,9},{10,18},{18,10},{11,19},{19,11},{12,20... | collective-permute-start | bytes 1572872 | tf_op jit(solution)/shard_map/ppermute | solution.py:52
  26.5 20.4 %collective-permute-start.11 = (bf16[256,1024]{1,0:T(8,128)(2,1)S(1)}, bf16[256,1024]{1,0:T(8,128)(2,1)S(1)}, u32[]{:S(2)}, u32[]{:S(2)}) collective-permute-start(bf16[256,1024]{1,0:T(8,128)(2,1)S(1)} %collective-permute-done.9.refs_0_.middle), channel_id=1, source_target_pairs={{8,0},{16,24},{9,1},{17,25},{10,2},{18,26},{11,3},{19,27},{12,4},{... | collective-permute-start | bytes 1572872 | tf_op jit(solution)/shard_map/ppermute | solution.py:52
  27.9 20.4 %collective-permute-start.13 = (f32[2,32,2048]{2,1,0:T(8,128)S(1)}, f32[2,32,2048]{2,1,0:T(8,128)S(1)}, u32[]{:S(2)}, u32[]{:S(2)}) collective-permute-start(f32[2,32,2048]{2,1,0:T(8,128)S(1)} %up_state.1), channel_id=1, source_target_pairs={{0,1},{1,0},{2,3},{3,2},{4,5},{5,4},{6,7},{7,6},{8,9},{9,8},{10,11... | collective-permute-start | bytes 1572872 | tf_op jit(solution)/shard_map/ppermute | solution.py:429
  37.1 18.3 %collective-permute-start.7 = (bf16[256,1024]{1,0:T(8,128)(2,1)S(1)}, bf16[256,1024]{1,0:T(8,128)(2,1)S(1)}, u32[]{:S(2)}, u32[]{:S(2)}) collective-permute-start(bf16[256,1024]{1,0:T(8,128)(2,1)S(1)} %add_block.3.refs_0_), channel_id=1, source_target_pairs={{8,16},{16,8},{9,17},{17,9},{10,18},{18,10},{11,19},{19,11},{12,20... | collective-permute-start | bytes 1572872 | tf_op jit(solution)/shard_map/ppermute | solution.py:52
  37.8 17.6 %collective-permute-start.6 = (bf16[256,1024]{1,0:T(8,128)(2,1)S(1)}, bf16[256,1024]{1,0:T(8,128)(2,1)S(1)}, u32[]{:S(2)}, u32[]{:S(2)}) collective-permute-start(bf16[256,1024]{1,0:T(8,128)(2,1)S(1)} %gate.10), channel_id=1, source_target_pairs={{0,8},{24,16},{1,9},{25,17},{2,10},{26,18},{3,11},{27,19},{4,12},{... | collective-permute-start | bytes 1572872 | tf_op jit(solution)/shard_map/ppermute | solution.py:52
  47.0 14.2 %collective-permute-start.12 = (bf16[256,1024]{1,0:T(8,128)(2,1)S(1)}, bf16[256,1024]{1,0:T(8,128)(2,1)S(1)}, u32[]{:S(2)}, u32[]{:S(2)}) collective-permute-start(bf16[256,1024]{1,0:T(8,128)(2,1)S(1)} %add_block.5), channel_id=1, source_target_pairs={{8,0},{16,24},{9,1},{17,25},{10,2},{18,26},{11,3},{19,27},{12,4},{... | collective-permute-start | bytes 1572872 | tf_op jit(solution)/shard_map/ppermute | solution.py:52
  62.8 11.4 %collective-permute-start.19 = (bf16[256,1024]{1,0:T(8,128)(2,1)S(1)}, bf16[256,1024]{1,0:T(8,128)(2,1)S(1)}, u32[]{:S(2)}, u32[]{:S(2)}) collective-permute-start(bf16[256,1024]{1,0:T(8,128)(2,1)S(1)} %update_rows.1.refs_0_), channel_id=1, source_target_pairs={{0,4},{2,6},{4,0},{6,2},{1,5},{3,7},{5,1},{7,3},{8,12},{10,14},{12... | collective-permute-start | bytes 1572872 | tf_op jit(solution)/shard_map/ppermute | solution.py:56
  64.4 14.1 %collective-permute-start.14 = (bf16[256,1024]{1,0:T(8,128)(2,1)S(1)}, bf16[256,1024]{1,0:T(8,128)(2,1)S(1)}, u32[]{:S(2)}, u32[]{:S(2)}) collective-permute-start(bf16[256,1024]{1,0:T(8,128)(2,1)S(1)} %update_rows.1.refs_0_), channel_id=1, source_target_pairs={{0,8},{8,0},{16,24},{24,16},{1,9},{9,1},{17,25},{25,17},{2,10},{10... | collective-permute-start | bytes 1572872 | tf_op jit(solution)/shard_map/ppermute | solution.py:56
  67.5 21.1 %collective-permute-start.18 = (bf16[256,1024]{1,0:T(8,128)(2,1)S(1)}, bf16[256,1024]{1,0:T(8,128)(2,1)S(1)}, u32[]{:S(2)}, u32[]{:S(2)}) collective-permute-start(bf16[256,1024]{1,0:T(8,128)(2,1)S(1)} %collective-permute-done.17.middle), channel_id=1, source_target_pairs={{8,0},{16,24},{9,1},{17,25},{10,2},{18,26},{11,3},{19,27},{12,4},{... | collective-permute-start | bytes 1572872 | tf_op jit(solution)/shard_map/ppermute | solution.py:52
  78.6 10.1 %collective-permute-start.20 = (bf16[256,1024]{1,0:T(8,128)(2,1)S(1)}, bf16[256,1024]{1,0:T(8,128)(2,1)S(1)}, u32[]{:S(2)}, u32[]{:S(2)}) collective-permute-start(bf16[256,1024]{1,0:T(8,128)(2,1)S(1)} %gate.12.refs_6_.refs_0_.refs_2_), channel_id=1, source_target_pairs={{0,4},{2,6},{4,0},{6,2},{1,5},{3,7},{5,1},{7,3},{8,12},{10,14},{12... | collective-permute-start | bytes 1572872 | tf_op jit(solution)/shard_map/ppermute | solution.py:56
  78.7 11.4 %collective-permute-start.22 = (bf16[256,1024]{1,0:T(8,128)(2,1)S(1)}, bf16[256,1024]{1,0:T(8,128)(2,1)S(1)}, u32[]{:S(2)}, u32[]{:S(2)}) collective-permute-start(bf16[256,1024]{1,0:T(8,128)(2,1)S(1)} %gate.13), channel_id=1, source_target_pairs={{0,8},{24,16},{1,9},{25,17},{2,10},{26,18},{3,11},{27,19},{4,12},{... | collective-permute-start | bytes 1572872 | tf_op jit(solution)/shard_map/ppermute | solution.py:52
  81.8 9.0 %collective-permute-start.15 = (bf16[256,1024]{1,0:T(8,128)(2,1)S(1)}, bf16[256,1024]{1,0:T(8,128)(2,1)S(1)}, u32[]{:S(2)}, u32[]{:S(2)}) collective-permute-start(bf16[256,1024]{1,0:T(8,128)(2,1)S(1)} %collective-permute-done.14.x), channel_id=1, source_target_pairs={{8,16},{16,8},{9,17},{17,9},{10,18},{18,10},{11,19},{19,11},{12,20... | collective-permute-start | bytes 1572872 | tf_op jit(solution)/shard_map/ppermute | solution.py:52
  88.7 12.1 %collective-permute-start.21 = (bf16[256,1024]{1,0:T(8,128)(2,1)S(1)}, bf16[256,1024]{1,0:T(8,128)(2,1)S(1)}, u32[]{:S(2)}, u32[]{:S(2)}) collective-permute-start(bf16[256,1024]{1,0:T(8,128)(2,1)S(1)} %pick.5.refs_0_), channel_id=1, source_target_pairs={{0,4},{2,6},{4,0},{6,2},{1,5},{3,7},{5,1},{7,3},{8,12},{10,14},{12... | collective-permute-start | bytes 1572872 | tf_op jit(solution)/shard_map/ppermute | solution.py:56
  90.0 8.4 %collective-permute-start.23 = (bf16[256,1024]{1,0:T(8,128)(2,1)S(1)}, bf16[256,1024]{1,0:T(8,128)(2,1)S(1)}, u32[]{:S(2)}, u32[]{:S(2)}) collective-permute-start(bf16[256,1024]{1,0:T(8,128)(2,1)S(1)} %collective-permute-done.22.middle), channel_id=1, source_target_pairs={{8,16},{16,8},{9,17},{17,9},{10,18},{18,10},{11,19},{19,11},{12,20... | collective-permute-start | bytes 1572872 | tf_op jit(solution)/shard_map/ppermute | solution.py:52
  90.7 14.5 %collective-permute-start.16 = (bf16[256,1024]{1,0:T(8,128)(2,1)S(1)}, bf16[256,1024]{1,0:T(8,128)(2,1)S(1)}, u32[]{:S(2)}, u32[]{:S(2)}) collective-permute-start(bf16[256,1024]{1,0:T(8,128)(2,1)S(1)} %collective-permute-done.15.middle), channel_id=1, source_target_pairs={{8,0},{16,24},{9,1},{17,25},{10,2},{18,26},{11,3},{19,27},{12,4},{... | collective-permute-start | bytes 1572872 | tf_op jit(solution)/shard_map/ppermute | solution.py:52
  105.6 8.5 %collective-permute-start.26 = (bf16[3,256,1024]{2,1,0:T(8,128)(2,1)S(1)}, bf16[3,256,1024]{2,1,0:T(8,128)(2,1)S(1)}, u32[]{:S(2)}, u32[]{:S(2)}) collective-permute-start(bf16[3,256,1024]{2,1,0:T(8,128)(2,1)S(1)} %bundle.3.refs_0_), channel_id=1, source_target_pairs={{0,2},{2,0},{4,6},{6,4},{1,3},{3,1},{5,7},{7,5},{8,10},{10,8},{12,... | collective-permute-start | bytes 4718600 | tf_op jit(solution)/shard_map/ppermute | solution.py:56
  106.1 13.9 %collective-permute-start.25 = (bf16[256,1024]{1,0:T(8,128)(2,1)S(1)}, bf16[256,1024]{1,0:T(8,128)(2,1)S(1)}, u32[]{:S(2)}, u32[]{:S(2)}) collective-permute-start(bf16[256,1024]{1,0:T(8,128)(2,1)S(1)} %pick.6.refs_2_.refs_4_), channel_id=1, source_target_pairs={{0,4},{2,6},{4,0},{6,2},{1,5},{3,7},{5,1},{7,3},{8,12},{10,14},{12... | collective-permute-start | bytes 1572872 | tf_op jit(solution)/shard_map/ppermute | solution.py:56
  106.8 15.5 %collective-permute-start.29 = (bf16[256,1024]{1,0:T(8,128)(2,1)S(1)}, bf16[256,1024]{1,0:T(8,128)(2,1)S(1)}, u32[]{:S(2)}, u32[]{:S(2)}) collective-permute-start(bf16[256,1024]{1,0:T(8,128)(2,1)S(1)} %collective-permute-done.23.refs_1_.middle), channel_id=1, source_target_pairs={{8,0},{16,24},{9,1},{17,25},{10,2},{18,26},{11,3},{19,27},{12,4},{... | collective-permute-start | bytes 1572872 | tf_op jit(solution)/shard_map/ppermute | solution.py:52
  (16 other events, 169.8 us)

commit v13 on v11

--- a/solution.py
+++ b/solution.py
@@ -64,17 +64,26 @@
 
 
 def project_kernel(trained, basis, norm, own, *refs):
-    *outs, projected = refs
+    *outs, projected, held, sems = refs
     rank, rows = basis.shape[0], own.shape[1]
+    spans = [slice(i * rows, (i + 1) * rows) for i in range(len(outs) + 1)]
+    loads = [
+        pltpu.make_async_copy(trained.at[span], held.at[span], sems.at[i])
+        for i, span in enumerate(spans)
+    ]
+    for load in loads:
+        load.start()
     high = basis[...].astype(BF16)
     rest = basis[...] - high.astype(F32)
     middle = rest.astype(BF16)
     low = (rest - middle.astype(F32)).astype(BF16)
     split = jnp.concatenate([high, middle, low], axis=0)
-    product = lax.dot_general(
-        split, trained[...], (((1,), (1,)), ((), ())), preferred_element_type=F32
-    )
-    projected[...] = product[:rank] + (product[rank : 2 * rank] + product[2 * rank :])
+    for load, span in zip(loads, spans):
+        load.wait()
+        product = lax.dot_general(
+            split, held[span, :], (((1,), (1,)), ((), ())), preferred_element_type=F32
+        )
+        projected[:, span] = product[:rank] + (product[rank : 2 * rank] + product[2 * rank :])
     pos = lax.axis_index("replica")
     values = norm[...].astype(F32)
     per = norm.shape[1] // rows
@@ -390,9 +399,13 @@
         project_kernel,
         "project_rows",
         [rank_rows] + [packet] * (replicas - 1),
-        [VMEM] * 3,
+        [HBM] + [VMEM] * 2,
         [VMEM] * replicas,
-        [pltpu.VMEM((rank, replicas * rows_embed), F32)],
+        [
+            pltpu.VMEM((rank, replicas * rows_embed), F32),
+            pltpu.VMEM((replicas * rows_embed, width), BF16),
+            dma((replicas,)),
+        ],
         pltpu.with_memory_space_constraint(trained_embed[0], pltpu.HBM),
         pltpu.with_memory_space_constraint(basis_t, pltpu.HBM),
         pltpu.with_memory_space_constraint(trained_norm[0], pltpu.HBM),

time: 122 us -> 123 us (level)
  Pallas kernels: 18.6 us -> 19.9 us
    pallas_call x30, Pallas kernels: 18.6 us -> 19.9 us  [call(): pl.pallas_call(kernel, name=name, out_shape=out_shape, in_specs=in_specs,...]
where the time goes in v13:
time: 123 us
  waiting for transfers between devices  58 us (47%)
  starting transfers between devices  42.5 us (35%)
  Pallas kernels  19.9 us (16%)
    ppermute x16, waiting for transfers between devices, along(): return lax.ppermute(x, 'replica', pairs)  32.5 us
    ppermute x16, starting transfers between devices, along(): return lax.ppermute(x, 'replica', pairs)  26.3 us
    ppermute x11, waiting for transfers between devices, swap(): lax.ppermute(x, axis, [(i, i ^ bit) for i in range(lax.axis_size(axis))])  20.7 us
    pallas_call x30, Pallas kernels, call(): pl.pallas_call(kernel, name=name, out_shape=out_shape, in_specs=in_specs,...  19.9 us
    ppermute x11, starting transfers between devices, swap(): lax.ppermute(x, axis, [(i, i ^ bit) for i in range(lax.axis_size(axis))])  13.1 us
    ppermute x2, waiting for transfers between devices, body(): lax.ppermute(x, 'tensor', [(i, (i + shift) % tensors) for i in range(tens...  4.9 us
    ppermute x2, starting transfers between devices, body(): lax.ppermute(x, 'tensor', [(i, (i + shift) % tensors) for i in range(tens...  3.1 us
  transfers between devices with their start and end apart: 29, of which 15 were waited for; matrix products, arithmetic and copies ran while one was open for 1% of the time, Pallas kernels for 11%

profile of v13, /device:TPU:0, one launch (start us, length us, event | category | flops | bytes accessed | tf_op | source)
XLA Modules:
  0.0 122.7 jit_solution(2698445117158342541)
XLA Ops:
  0.6 3.8 %project_rows.1 = (f32[64,256]{1,0:T(8,128)S(1)}, bf16[80,256]{1,0:T(8,128)(2,1)S(1)}, bf16[80,256]{1,0:T(8,128)(2,1)S(1)}, bf16[80,256]{1,0:T(8,128)(2,1)S(1)}) custom-call(bf16[1024,1024]{1,0:T(8,128)(2,1)} %bitcast.37, f32[64,1024]{1,0:T(8,128)} %bitcast.24, bf16[2,1024]{1,0:T(2,128)(2,1)} %bitcast.31), custom_call_target="tpu_custom_call" | custom-call | bytes 565248 | tf_op jit(solution)/shard_map/project_rows/pallas_call | solution.py:26
  4.5 3.1 %collective-permute-start = (bf16[80,256]{1,0:T(8,128)(2,1)S(1)}, bf16[80,256]{1,0:T(8,128)(2,1)S(1)}, u32[]{:S(2)}, u32[]{:S(2)}) collective-permute-start(bf16[80,256]{1,0:T(8,128)(2,1)S(1)} %get-tuple-element.49), channel_id=1, source_target_pairs={{0,8},{8,0},{16,24},{24,16},{1,9},{9,1},{17,25},{25,17},{2,10},{10... | collective-permute-start | bytes 122888 | tf_op jit(solution)/shard_map/ppermute | solution.py:56
  7.6 2.6 %collective-permute-start.3 = (bf16[80,256]{1,0:T(8,128)(2,1)S(1)}, bf16[80,256]{1,0:T(8,128)(2,1)S(1)}, u32[]{:S(2)}, u32[]{:S(2)}) collective-permute-start(bf16[80,256]{1,0:T(8,128)(2,1)S(1)} %get-tuple-element.51), channel_id=1, source_target_pairs={{0,16},{8,24},{16,0},{24,8},{1,17},{9,25},{17,1},{25,9},{2,18},{10... | collective-permute-start | bytes 122888 | tf_op jit(solution)/shard_map/ppermute | solution.py:56
  10.2 1.8 %pack_blocks.1 = (bf16[256,1024]{1,0:T(8,128)(2,1)S(1)}, bf16[256,1024]{1,0:T(8,128)(2,1)S(1)}, bf16[256,1024]{1,0:T(8,128)(2,1)S(1)}, bf16[256,1024]{1,0:T(8,128)(2,1)S(1)}) custom-call(bf16[4,4,128,1024]{3,2,1,0:T(8,128)(2,1)} %bitcast.35, bf16[4,4,64,2048]{3,2,1,0:T(8,128)(2,1)} %bitcast.36), custom_call_target="tpu_custom_call" | custom-call | bytes 6291456 | tf_op jit(solution)/shard_map/pack_blocks/pallas_call | solution.py:26
  12.1 2.0 %collective-permute-start.4 = (bf16[80,256]{1,0:T(8,128)(2,1)S(1)}, bf16[80,256]{1,0:T(8,128)(2,1)S(1)}, u32[]{:S(2)}, u32[]{:S(2)}) collective-permute-start(bf16[80,256]{1,0:T(8,128)(2,1)S(1)} %gate.9), channel_id=1, source_target_pairs={{0,24},{8,16},{16,8},{24,0},{1,25},{9,17},{17,9},{25,1},{2,26},{10... | collective-permute-start | bytes 122888 | tf_op jit(solution)/shard_map/ppermute | solution.py:56
  18.0 2.0 %embed_update.1 = (f32[256,1024]{1,0:T(8,128)}, bf16[256,1024]{1,0:T(8,128)(2,1)S(1)}, f32[64,256]{1,0:T(8,128)}, bf16[2,1024]{1,0:T(2,128)(2,1)}, f32[2,1024]{1,0:T(2,128)}, /*index=5*/f32[2,1024]{1,0:T(2,128)}) custom-call(f32[64,256]{1,0:T(8,128)S(1)} %get-tuple-element.50.refs_0_, f32[64,256]{1,0:T(8,128)S(1)} %fusion.refs_1_, f32[256,1024]{1,0:T(8,128)S(1)} %bitcast.23, ...), custom_call_target="tpu_custom_call" | custom-call | bytes 4976640 | tf_op jit(solution)/shard_map/embed_update/pallas_call | solution.py:26
  22.0 4.8 %collective-permute-done.1.refs_0_.came = bf16[256,1024]{1,0:T(8,128)(2,1)S(1)} collective-permute-done((bf16[256,1024]{1,0:T(8,128)(2,1)S(1)}, bf16[256,1024]{1,0:T(8,128)(2,1)S(1)}, u32[]{:S(2)}, u32[]{:S(2)}) %collective-permute-start.1) | collective-permute-done | bytes 524320 | tf_op jit(solution)/shard_map/ppermute | solution.py:52
  26.8 4.4 %collective-permute-start.2 = (bf16[256,1024]{1,0:T(8,128)(2,1)S(1)}, bf16[256,1024]{1,0:T(8,128)(2,1)S(1)}, u32[]{:S(2)}, u32[]{:S(2)}) collective-permute-start(bf16[256,1024]{1,0:T(8,128)(2,1)S(1)} %gate.8), channel_id=1, source_target_pairs={{0,8},{24,16},{1,9},{25,17},{2,10},{26,18},{3,11},{27,19},{4,12},{... | collective-permute-start | bytes 1572872 | tf_op jit(solution)/shard_map/ppermute | solution.py:52
  35.2 5.4 %collective-permute-done.2.came = bf16[256,1024]{1,0:T(8,128)(2,1)S(1)} collective-permute-done((bf16[256,1024]{1,0:T(8,128)(2,1)S(1)}, bf16[256,1024]{1,0:T(8,128)(2,1)S(1)}, u32[]{:S(2)}, u32[]{:S(2)}) %collective-permute-start.2) | collective-permute-done | bytes 524320 | tf_op jit(solution)/shard_map/ppermute | solution.py:52
  41.5 7.1 %collective-permute-start.6 = (bf16[256,1024]{1,0:T(8,128)(2,1)S(1)}, bf16[256,1024]{1,0:T(8,128)(2,1)S(1)}, u32[]{:S(2)}, u32[]{:S(2)}) collective-permute-start(bf16[256,1024]{1,0:T(8,128)(2,1)S(1)} %gate.10), channel_id=1, source_target_pairs={{0,8},{24,16},{1,9},{25,17},{2,10},{26,18},{3,11},{27,19},{4,12},{... | collective-permute-start | bytes 1572872 | tf_op jit(solution)/shard_map/ppermute | solution.py:52
  50.0 6.8 %collective-permute-done.6.refs_5_.refs_3_ = bf16[256,1024]{1,0:T(8,128)(2,1)S(1)} collective-permute-done((bf16[256,1024]{1,0:T(8,128)(2,1)S(1)}, bf16[256,1024]{1,0:T(8,128)(2,1)S(1)}, u32[]{:S(2)}, u32[]{:S(2)}) %collective-permute-start.6) | collective-permute-done | bytes 524320 | tf_op jit(solution)/shard_map/ppermute | solution.py:52
  56.8 4.3 %collective-permute-done.10.refs_7_.refs_5_ = bf16[256,1024]{1,0:T(8,128)(2,1)S(1)} collective-permute-done((bf16[256,1024]{1,0:T(8,128)(2,1)S(1)}, bf16[256,1024]{1,0:T(8,128)(2,1)S(1)}, u32[]{:S(2)}, u32[]{:S(2)}) %collective-permute-start.10) | collective-permute-done | bytes 524320 | tf_op jit(solution)/shard_map/ppermute | solution.py:52
  66.8 7.0 %collective-permute-done.18.refs_0_.refs_1_ = bf16[256,1024]{1,0:T(8,128)(2,1)S(1)} collective-permute-done((bf16[256,1024]{1,0:T(8,128)(2,1)S(1)}, bf16[256,1024]{1,0:T(8,128)(2,1)S(1)}, u32[]{:S(2)}, u32[]{:S(2)}) %collective-permute-start.18) | collective-permute-done | bytes 524320 | tf_op jit(solution)/shard_map/ppermute | solution.py:56
  73.8 3.4 %collective-permute-done.13.x = bf16[256,1024]{1,0:T(8,128)(2,1)S(1)} collective-permute-done((bf16[256,1024]{1,0:T(8,128)(2,1)S(1)}, bf16[256,1024]{1,0:T(8,128)(2,1)S(1)}, u32[]{:S(2)}, u32[]{:S(2)}) %collective-permute-start.13) | collective-permute-done | bytes 524320 | tf_op jit(solution)/shard_map/ppermute | solution.py:56
  81.0 3.9 %collective-permute-done.17.end = bf16[256,1024]{1,0:T(8,128)(2,1)S(1)} collective-permute-done((bf16[256,1024]{1,0:T(8,128)(2,1)S(1)}, bf16[256,1024]{1,0:T(8,128)(2,1)S(1)}, u32[]{:S(2)}, u32[]{:S(2)}) %collective-permute-start.17) | collective-permute-done | bytes 524320 | tf_op jit(solution)/shard_map/ppermute | solution.py:52
  84.9 3.8 %collective-permute-done.19.refs_0_.refs_3_ = bf16[256,1024]{1,0:T(8,128)(2,1)S(1)} collective-permute-done((bf16[256,1024]{1,0:T(8,128)(2,1)S(1)}, bf16[256,1024]{1,0:T(8,128)(2,1)S(1)}, u32[]{:S(2)}, u32[]{:S(2)}) %collective-permute-start.19) | collective-permute-done | bytes 524320 | tf_op jit(solution)/shard_map/ppermute | solution.py:56
  92.4 4.9 %collective-permute-done.23.refs_2_.refs_1_ = f32[32,2048]{1,0:T(8,128)S(1)} collective-permute-done((f32[32,2048]{1,0:T(8,128)S(1)}, f32[32,2048]{1,0:T(8,128)S(1)}, u32[]{:S(2)}, u32[]{:S(2)}) %collective-permute-start.23) | collective-permute-done | bytes 262176 | tf_op jit(solution)/shard_map/ppermute | solution.py:525
  98.0 3.9 %collective-permute-done.15.end = bf16[256,1024]{1,0:T(8,128)(2,1)S(1)} collective-permute-done((bf16[256,1024]{1,0:T(8,128)(2,1)S(1)}, bf16[256,1024]{1,0:T(8,128)(2,1)S(1)}, u32[]{:S(2)}, u32[]{:S(2)}) %collective-permute-start.15) | collective-permute-done | bytes 524320 | tf_op jit(solution)/shard_map/ppermute | solution.py:52
  102.8 1.7 %collective-permute-start.24 = (bf16[256,1024]{1,0:T(8,128)(2,1)S(1)}, bf16[256,1024]{1,0:T(8,128)(2,1)S(1)}, u32[]{:S(2)}, u32[]{:S(2)}) collective-permute-start(bf16[256,1024]{1,0:T(8,128)(2,1)S(1)} %pick.6.refs_2_.refs_4_), channel_id=1, source_target_pairs={{0,4},{2,6},{4,0},{6,2},{1,5},{3,7},{5,1},{7,3},{8,12},{10,14},{12... | collective-permute-start | bytes 1572872 | tf_op jit(solution)/shard_map/ppermute | solution.py:56
  108.6 2.2 %place_rows.3 = (bf16[4,4,128,1024]{3,2,1,0:T(8,128)(2,1)}, bf16[4,4,64,2048]{3,2,1,0:T(8,128)(2,1)}, f32[8,128]{1,0:T(8,128)S(1)}) custom-call(bf16[4,256,1024]{2,1,0:T(8,128)(2,1)S(1)} %bundle.4.refs_0_, bf16[4,256,1024]{2,1,0:T(8,128)(2,1)S(1)} %collective-permute-done.26.refs_2_.refs_1_, f32[8,128]{1,0:T(8,128)S(1)} %get-tuple-element.57.refs_2_), custom_call_target="tpu_custom_call" | custom-call | bytes 25178112 | tf_op jit(solution)/shard_map/place_rows/pallas_call | solution.py:26
  110.8 1.8 %place_rows.4 = (bf16[4,4,128,1024]{3,2,1,0:T(8,128)(2,1)}, bf16[4,4,64,2048]{3,2,1,0:T(8,128)(2,1)}, f32[8,128]{1,0:T(8,128)S(1)}) custom-call(bf16[3,256,1024]{2,1,0:T(8,128)(2,1)S(1)} %bundle.3.refs_0_, bf16[3,256,1024]{2,1,0:T(8,128)(2,1)S(1)} %collective-permute-done.25.refs_1_, ...), custom_call_target="tpu_custom_call", output_to_operand_aliasing={{0}: (3, {}), {1}: (4, {})} | custom-call | bytes 25178112 | tf_op jit(solution)/shard_map/place_rows/pallas_call | solution.py:26
  112.6 4.1 %collective-permute-done.24.refs_0_ = bf16[256,1024]{1,0:T(8,128)(2,1)S(1)} collective-permute-done((bf16[256,1024]{1,0:T(8,128)(2,1)S(1)}, bf16[256,1024]{1,0:T(8,128)(2,1)S(1)}, u32[]{:S(2)}, u32[]{:S(2)}) %collective-permute-start.24) | collective-permute-done | bytes 524320 | tf_op jit(solution)/shard_map/ppermute | solution.py:56
  116.9 3.3 %collective-permute-done.28.end = bf16[256,1024]{1,0:T(8,128)(2,1)S(1)} collective-permute-done((bf16[256,1024]{1,0:T(8,128)(2,1)S(1)}, bf16[256,1024]{1,0:T(8,128)(2,1)S(1)}, u32[]{:S(2)}, u32[]{:S(2)}) %collective-permute-start.28) | collective-permute-done | bytes 524320 | tf_op jit(solution)/shard_map/ppermute | solution.py:52
  121.1 1.6 %place_rows.5 = (bf16[4,4,128,1024]{3,2,1,0:T(8,128)(2,1)}, bf16[4,4,64,2048]{3,2,1,0:T(8,128)(2,1)}, f32[8,128]{1,0:T(8,128)}) custom-call(bf16[1,256,1024]{2,1,0:T(8,128)(2,1)S(1)} %bundle.5.refs_1_.refs_0_, bf16[1,256,1024]{2,1,0:T(8,128)(2,1)S(1)} %collective-permute-done.27.refs_1_, ...), custom_call_target="tpu_custom_call", output_to_operand_aliasing={{0}: (3, {}), {1}: (4, {})} | custom-call | bytes 25178112 | tf_op jit(solution)/shard_map/place_rows/pallas_call | solution.py:26
  (85 shorter events, 31.7 us)
Async XLA Ops:
  4.5 7.5 %collective-permute-start = (bf16[80,256]{1,0:T(8,128)(2,1)S(1)}, bf16[80,256]{1,0:T(8,128)(2,1)S(1)}, u32[]{:S(2)}, u32[]{:S(2)}) collective-permute-start(bf16[80,256]{1,0:T(8,128)(2,1)S(1)} %get-tuple-element.49), channel_id=1, source_target_pairs={{0,8},{8,0},{16,24},{24,16},{1,9},{9,1},{17,25},{25,17},{2,10},{10... | collective-permute-start | bytes 122888 | tf_op jit(solution)/shard_map/ppermute | solution.py:56
  7.6 9.0 %collective-permute-start.3 = (bf16[80,256]{1,0:T(8,128)(2,1)S(1)}, bf16[80,256]{1,0:T(8,128)(2,1)S(1)}, u32[]{:S(2)}, u32[]{:S(2)}) collective-permute-start(bf16[80,256]{1,0:T(8,128)(2,1)S(1)} %get-tuple-element.51), channel_id=1, source_target_pairs={{0,16},{8,24},{16,0},{24,8},{1,17},{9,25},{17,1},{25,9},{2,18},{10... | collective-permute-start | bytes 122888 | tf_op jit(solution)/shard_map/ppermute | solution.py:56
  15.2 11.6 %collective-permute-start.1 = (bf16[256,1024]{1,0:T(8,128)(2,1)S(1)}, bf16[256,1024]{1,0:T(8,128)(2,1)S(1)}, u32[]{:S(2)}, u32[]{:S(2)}) collective-permute-start(bf16[256,1024]{1,0:T(8,128)(2,1)S(1)} %gate.7.refs_0_.block), channel_id=1, source_target_pairs={{0,8},{24,16},{1,9},{25,17},{2,10},{26,18},{3,11},{27,19},{4,12},{... | collective-permute-start | bytes 1572872 | tf_op jit(solution)/shard_map/ppermute | solution.py:52
  20.0 11.4 %collective-permute-start.8 = (bf16[256,1024]{1,0:T(8,128)(2,1)S(1)}, bf16[256,1024]{1,0:T(8,128)(2,1)S(1)}, u32[]{:S(2)}, u32[]{:S(2)}) collective-permute-start(bf16[256,1024]{1,0:T(8,128)(2,1)S(1)} %get-tuple-element.53.x.refs_0_), channel_id=1, source_target_pairs={{8,16},{16,8},{9,17},{17,9},{10,18},{18,10},{11,19},{19,11},{12,20... | collective-permute-start | bytes 1572872 | tf_op jit(solution)/shard_map/ppermute | solution.py:52
  20.7 14.5 %collective-permute-start.5 = (bf16[256,1024]{1,0:T(8,128)(2,1)S(1)}, bf16[256,1024]{1,0:T(8,128)(2,1)S(1)}, u32[]{:S(2)}, u32[]{:S(2)}) collective-permute-start(bf16[256,1024]{1,0:T(8,128)(2,1)S(1)} %get-tuple-element.53.x.refs_0_), channel_id=1, source_target_pairs={{8,0},{16,24},{9,1},{17,25},{10,2},{18,26},{11,3},{19,27},{12,4},{... | collective-permute-start | bytes 1572872 | tf_op jit(solution)/shard_map/ppermute | solution.py:52
  26.8 13.8 %collective-permute-start.2 = (bf16[256,1024]{1,0:T(8,128)(2,1)S(1)}, bf16[256,1024]{1,0:T(8,128)(2,1)S(1)}, u32[]{:S(2)}, u32[]{:S(2)}) collective-permute-start(bf16[256,1024]{1,0:T(8,128)(2,1)S(1)} %gate.8), channel_id=1, source_target_pairs={{0,8},{24,16},{1,9},{25,17},{2,10},{26,18},{3,11},{27,19},{4,12},{... | collective-permute-start | bytes 1572872 | tf_op jit(solution)/shard_map/ppermute | solution.py:52
  31.5 17.1 %collective-permute-start.9 = (bf16[256,1024]{1,0:T(8,128)(2,1)S(1)}, bf16[256,1024]{1,0:T(8,128)(2,1)S(1)}, u32[]{:S(2)}, u32[]{:S(2)}) collective-permute-start(bf16[256,1024]{1,0:T(8,128)(2,1)S(1)} %gate.11), channel_id=1, source_target_pairs={{8,16},{16,8},{9,17},{17,9},{10,18},{18,10},{11,19},{19,11},{12,20... | collective-permute-start | bytes 1572872 | tf_op jit(solution)/shard_map/ppermute | solution.py:52
  32.4 17.6 %collective-permute-start.11 = (f32[2,32,2048]{2,1,0:T(8,128)S(1)}, f32[2,32,2048]{2,1,0:T(8,128)S(1)}, u32[]{:S(2)}, u32[]{:S(2)}) collective-permute-start(f32[2,32,2048]{2,1,0:T(8,128)S(1)} %up_state.1), channel_id=1, source_target_pairs={{0,1},{1,0},{2,3},{3,2},{4,5},{5,4},{6,7},{7,6},{8,9},{9,8},{10,11... | collective-permute-start | bytes 1572872 | tf_op jit(solution)/shard_map/ppermute | solution.py:442
  33.9 16.1 %collective-permute-start.12 = (bf16[256,1024]{1,0:T(8,128)(2,1)S(1)}, bf16[256,1024]{1,0:T(8,128)(2,1)S(1)}, u32[]{:S(2)}, u32[]{:S(2)}) collective-permute-start(bf16[256,1024]{1,0:T(8,128)(2,1)S(1)} %collective-permute-done.8.refs_0_.middle), channel_id=1, source_target_pairs={{8,0},{16,24},{9,1},{17,25},{10,2},{18,26},{11,3},{19,27},{12,4},{... | collective-permute-start | bytes 1572872 | tf_op jit(solution)/shard_map/ppermute | solution.py:52
  40.7 16.1 %collective-permute-start.7 = (bf16[256,1024]{1,0:T(8,128)(2,1)S(1)}, bf16[256,1024]{1,0:T(8,128)(2,1)S(1)}, u32[]{:S(2)}, u32[]{:S(2)}) collective-permute-start(bf16[256,1024]{1,0:T(8,128)(2,1)S(1)} %add_block.3.refs_0_), channel_id=1, source_target_pairs={{8,16},{16,8},{9,17},{17,9},{10,18},{18,10},{11,19},{19,11},{12,20... | collective-permute-start | bytes 1572872 | tf_op jit(solution)/shard_map/ppermute | solution.py:52
  41.5 15.4 %collective-permute-start.6 = (bf16[256,1024]{1,0:T(8,128)(2,1)S(1)}, bf16[256,1024]{1,0:T(8,128)(2,1)S(1)}, u32[]{:S(2)}, u32[]{:S(2)}) collective-permute-start(bf16[256,1024]{1,0:T(8,128)(2,1)S(1)} %gate.10), channel_id=1, source_target_pairs={{0,8},{24,16},{1,9},{25,17},{2,10},{26,18},{3,11},{27,19},{4,12},{... | collective-permute-start | bytes 1572872 | tf_op jit(solution)/shard_map/ppermute | solution.py:52
  48.7 12.4 %collective-permute-start.10 = (bf16[256,1024]{1,0:T(8,128)(2,1)S(1)}, bf16[256,1024]{1,0:T(8,128)(2,1)S(1)}, u32[]{:S(2)}, u32[]{:S(2)}) collective-permute-start(bf16[256,1024]{1,0:T(8,128)(2,1)S(1)} %add_block.5), channel_id=1, source_target_pairs={{8,0},{16,24},{9,1},{17,25},{10,2},{18,26},{11,3},{19,27},{12,4},{... | collective-permute-start | bytes 1572872 | tf_op jit(solution)/shard_map/ppermute | solution.py:52
  62.7 11.1 %collective-permute-start.18 = (bf16[256,1024]{1,0:T(8,128)(2,1)S(1)}, bf16[256,1024]{1,0:T(8,128)(2,1)S(1)}, u32[]{:S(2)}, u32[]{:S(2)}) collective-permute-start(bf16[256,1024]{1,0:T(8,128)(2,1)S(1)} %update_rows.1.refs_0_), channel_id=1, source_target_pairs={{0,4},{2,6},{4,0},{6,2},{1,5},{3,7},{5,1},{7,3},{8,12},{10,14},{12... | collective-permute-start | bytes 1572872 | tf_op jit(solution)/shard_map/ppermute | solution.py:56
  64.3 12.9 %collective-permute-start.13 = (bf16[256,1024]{1,0:T(8,128)(2,1)S(1)}, bf16[256,1024]{1,0:T(8,128)(2,1)S(1)}, u32[]{:S(2)}, u32[]{:S(2)}) collective-permute-start(bf16[256,1024]{1,0:T(8,128)(2,1)S(1)} %update_rows.1.refs_0_), channel_id=1, source_target_pairs={{0,8},{8,0},{16,24},{24,16},{1,9},{9,1},{17,25},{25,17},{2,10},{10... | collective-permute-start | bytes 1572872 | tf_op jit(solution)/shard_map/ppermute | solution.py:56
  65.5 19.4 %collective-permute-start.17 = (bf16[256,1024]{1,0:T(8,128)(2,1)S(1)}, bf16[256,1024]{1,0:T(8,128)(2,1)S(1)}, u32[]{:S(2)}, u32[]{:S(2)}) collective-permute-start(bf16[256,1024]{1,0:T(8,128)(2,1)S(1)} %collective-permute-done.16.middle), channel_id=1, source_target_pairs={{8,0},{16,24},{9,1},{17,25},{10,2},{18,26},{11,3},{19,27},{12,4},{... | collective-permute-start | bytes 1572872 | tf_op jit(solution)/shard_map/ppermute | solution.py:52
  77.2 11.4 %collective-permute-start.19 = (bf16[256,1024]{1,0:T(8,128)(2,1)S(1)}, bf16[256,1024]{1,0:T(8,128)(2,1)S(1)}, u32[]{:S(2)}, u32[]{:S(2)}) collective-permute-start(bf16[256,1024]{1,0:T(8,128)(2,1)S(1)} %gate.12.refs_6_.refs_0_.refs_2_), channel_id=1, source_target_pairs={{0,4},{2,6},{4,0},{6,2},{1,5},{3,7},{5,1},{7,3},{8,12},{10,14},{12... | collective-permute-start | bytes 1572872 | tf_op jit(solution)/shard_map/ppermute | solution.py:56
  77.4 11.4 %collective-permute-start.21 = (bf16[256,1024]{1,0:T(8,128)(2,1)S(1)}, bf16[256,1024]{1,0:T(8,128)(2,1)S(1)}, u32[]{:S(2)}, u32[]{:S(2)}) collective-permute-start(bf16[256,1024]{1,0:T(8,128)(2,1)S(1)} %gate.13), channel_id=1, source_target_pairs={{0,8},{24,16},{1,9},{25,17},{2,10},{26,18},{3,11},{27,19},{4,12},{... | collective-permute-start | bytes 1572872 | tf_op jit(solution)/shard_map/ppermute | solution.py:52
  78.8 10.7 %collective-permute-start.14 = (bf16[256,1024]{1,0:T(8,128)(2,1)S(1)}, bf16[256,1024]{1,0:T(8,128)(2,1)S(1)}, u32[]{:S(2)}, u32[]{:S(2)}) collective-permute-start(bf16[256,1024]{1,0:T(8,128)(2,1)S(1)} %collective-permute-done.13.x), channel_id=1, source_target_pairs={{8,16},{16,8},{9,17},{17,9},{10,18},{18,10},{11,19},{19,11},{12,20... | collective-permute-start | bytes 1572872 | tf_op jit(solution)/shard_map/ppermute | solution.py:52
  88.7 9.2 %collective-permute-start.20 = (bf16[256,1024]{1,0:T(8,128)(2,1)S(1)}, bf16[256,1024]{1,0:T(8,128)(2,1)S(1)}, u32[]{:S(2)}, u32[]{:S(2)}) collective-permute-start(bf16[256,1024]{1,0:T(8,128)(2,1)S(1)} %pick.5.refs_0_), channel_id=1, source_target_pairs={{0,4},{2,6},{4,0},{6,2},{1,5},{3,7},{5,1},{7,3},{8,12},{10,14},{12... | collective-permute-start | bytes 1572872 | tf_op jit(solution)/shard_map/ppermute | solution.py:56
  88.8 8.5 %collective-permute-start.22 = (bf16[256,1024]{1,0:T(8,128)(2,1)S(1)}, bf16[256,1024]{1,0:T(8,128)(2,1)S(1)}, u32[]{:S(2)}, u32[]{:S(2)}) collective-permute-start(bf16[256,1024]{1,0:T(8,128)(2,1)S(1)} %collective-permute-done.21.middle), channel_id=1, source_target_pairs={{8,16},{16,8},{9,17},{17,9},{10,18},{18,10},{11,19},{19,11},{12,20... | collective-permute-start | bytes 1572872 | tf_op jit(solution)/shard_map/ppermute | solution.py:52
  89.5 12.4 %collective-permute-start.15 = (bf16[256,1024]{1,0:T(8,128)(2,1)S(1)}, bf16[256,1024]{1,0:T(8,128)(2,1)S(1)}, u32[]{:S(2)}, u32[]{:S(2)}) collective-permute-start(bf16[256,1024]{1,0:T(8,128)(2,1)S(1)} %collective-permute-done.14.middle), channel_id=1, source_target_pairs={{8,0},{16,24},{9,1},{17,25},{10,2},{18,26},{11,3},{19,27},{12,4},{... | collective-permute-start | bytes 1572872 | tf_op jit(solution)/shard_map/ppermute | solution.py:52
  102.3 8.5 %collective-permute-start.25 = (bf16[3,256,1024]{2,1,0:T(8,128)(2,1)S(1)}, bf16[3,256,1024]{2,1,0:T(8,128)(2,1)S(1)}, u32[]{:S(2)}, u32[]{:S(2)}) collective-permute-start(bf16[3,256,1024]{2,1,0:T(8,128)(2,1)S(1)} %bundle.3.refs_0_), channel_id=1, source_target_pairs={{0,2},{2,0},{4,6},{6,4},{1,3},{3,1},{5,7},{7,5},{8,10},{10,8},{12,... | collective-permute-start | bytes 4718600 | tf_op jit(solution)/shard_map/ppermute | solution.py:56
  102.8 13.9 %collective-permute-start.24 = (bf16[256,1024]{1,0:T(8,128)(2,1)S(1)}, bf16[256,1024]{1,0:T(8,128)(2,1)S(1)}, u32[]{:S(2)}, u32[]{:S(2)}) collective-permute-start(bf16[256,1024]{1,0:T(8,128)(2,1)S(1)} %pick.6.refs_2_.refs_4_), channel_id=1, source_target_pairs={{0,4},{2,6},{4,0},{6,2},{1,5},{3,7},{5,1},{7,3},{8,12},{10,14},{12... | collective-permute-start | bytes 1572872 | tf_op jit(solution)/shard_map/ppermute | solution.py:56
  104.7 15.5 %collective-permute-start.28 = (bf16[256,1024]{1,0:T(8,128)(2,1)S(1)}, bf16[256,1024]{1,0:T(8,128)(2,1)S(1)}, u32[]{:S(2)}, u32[]{:S(2)}) collective-permute-start(bf16[256,1024]{1,0:T(8,128)(2,1)S(1)} %collective-permute-done.22.refs_1_.middle), channel_id=1, source_target_pairs={{8,0},{16,24},{9,1},{17,25},{10,2},{18,26},{11,3},{19,27},{12,4},{... | collective-permute-start | bytes 1572872 | tf_op jit(solution)/shard_map/ppermute | solution.py:52
  (15 other events, 163.2 us)

commit v14 on v11

--- a/solution.py
+++ b/solution.py
@@ -521,12 +521,10 @@
     embed_last = along(embed_end, OUTWARD)
     bundles = [
         (
-            [(0, 0), (0, top), (1, 0), (1, top)],
-            spread_low(bundle([piece, far_piece, near_piece, far_near], third)),
-        ),
-        (
-            [(2, 0), (2, top), (3, 0)],
-            spread_low(bundle([second, far_second, third])),
+            [(0, 0), (0, top), (1, 0), (1, top), (2, 0), (2, top), (3, 0)],
+            spread_low(
+                bundle([piece, far_piece, near_piece, far_near, second, far_second, third])
+            ),
         ),
     ]
 

time: 122 us -> 122 us (level)
    ppermute x11 -> x10, waiting for transfers between devices: 20.6 us -> 21.7 us  [swap(): lax.ppermute(x, axis, [(i, i ^ bit) for i in range(lax.axis_size(axis))])]
    pallas_call x30 -> x28, Pallas kernels: 18.6 us -> 17.9 us  [call(): pl.pallas_call(kernel, name=name, out_shape=out_shape, in_specs=in_specs,...]
    ppermute x11 -> x10, starting transfers between devices: 13 us -> 12.5 us  [swap(): lax.ppermute(x, axis, [(i, i ^ bit) for i in range(lax.axis_size(axis))])]
  transfers between devices with their start and end apart: 29 -> 28, of which waited for: 15 -> 15; matrix products, arithmetic and copies ran while one was open for 1% -> 1% of each run, Pallas kernels for 11% -> 10%
where the time goes in v14:
time: 122 us; the launch traced here: 121 us
  waiting for transfers between devices  59 us (48%)
  starting transfers between devices  42 us (34%)
  Pallas kernels  17.9 us (15%)
    ppermute x16, waiting for transfers between devices, along(): return lax.ppermute(x, 'replica', pairs)  32.4 us
    ppermute x16, starting transfers between devices, along(): return lax.ppermute(x, 'replica', pairs)  26.3 us
    ppermute x10, waiting for transfers between devices, swap(): lax.ppermute(x, axis, [(i, i ^ bit) for i in range(lax.axis_size(axis))])  21.7 us
    pallas_call x28, Pallas kernels, call(): pl.pallas_call(kernel, name=name, out_shape=out_shape, in_specs=in_specs,...  17.9 us
    ppermute x10, starting transfers between devices, swap(): lax.ppermute(x, axis, [(i, i ^ bit) for i in range(lax.axis_size(axis))])  12.5 us
    ppermute x2, waiting for transfers between devices, body(): lax.ppermute(x, 'tensor', [(i, (i + shift) % tensors) for i in range(tens...  4.82 us
    ppermute x2, starting transfers between devices, body(): lax.ppermute(x, 'tensor', [(i, (i + shift) % tensors) for i in range(tens...  3.18 us
  transfers between devices with their start and end apart: 28, of which 15 were waited for; matrix products, arithmetic and copies ran while one was open for 1% of the time, Pallas kernels for 10%

profile of v14, /device:TPU:0, one launch (start us, length us, event | category | flops | bytes accessed | tf_op | source)
XLA Modules:
  0.0 121.2 jit_solution(11330603400110955923)
XLA Ops:
  0.6 2.6 %project_rows.1 = (f32[64,256]{1,0:T(8,128)S(1)}, bf16[80,256]{1,0:T(8,128)(2,1)S(1)}, bf16[80,256]{1,0:T(8,128)(2,1)S(1)}, bf16[80,256]{1,0:T(8,128)(2,1)S(1)}) custom-call(bf16[1024,1024]{1,0:T(8,128)(2,1)} %bitcast.37, f32[64,1024]{1,0:T(8,128)} %bitcast.24, bf16[2,1024]{1,0:T(2,128)(2,1)} %bitcast.31), custom_call_target="tpu_custom_call" | custom-call | bytes 565248 | tf_op jit(solution)/shard_map/project_rows/pallas_call | solution.py:26
  3.2 3.1 %collective-permute-start = (bf16[80,256]{1,0:T(8,128)(2,1)S(1)}, bf16[80,256]{1,0:T(8,128)(2,1)S(1)}, u32[]{:S(2)}, u32[]{:S(2)}) collective-permute-start(bf16[80,256]{1,0:T(8,128)(2,1)S(1)} %get-tuple-element.46), channel_id=1, source_target_pairs={{0,8},{8,0},{16,24},{24,16},{1,9},{9,1},{17,25},{25,17},{2,10},{10... | collective-permute-start | bytes 122888 | tf_op jit(solution)/shard_map/ppermute | solution.py:56
  6.3 2.6 %collective-permute-start.3 = (bf16[80,256]{1,0:T(8,128)(2,1)S(1)}, bf16[80,256]{1,0:T(8,128)(2,1)S(1)}, u32[]{:S(2)}, u32[]{:S(2)}) collective-permute-start(bf16[80,256]{1,0:T(8,128)(2,1)S(1)} %get-tuple-element.48), channel_id=1, source_target_pairs={{0,16},{8,24},{16,0},{24,8},{1,17},{9,25},{17,1},{25,9},{2,18},{10... | collective-permute-start | bytes 122888 | tf_op jit(solution)/shard_map/ppermute | solution.py:56
  8.9 1.8 %pack_blocks.1 = (bf16[256,1024]{1,0:T(8,128)(2,1)S(1)}, bf16[256,1024]{1,0:T(8,128)(2,1)S(1)}, bf16[256,1024]{1,0:T(8,128)(2,1)S(1)}, bf16[256,1024]{1,0:T(8,128)(2,1)S(1)}) custom-call(bf16[4,4,128,1024]{3,2,1,0:T(8,128)(2,1)} %bitcast.33, bf16[4,4,64,2048]{3,2,1,0:T(8,128)(2,1)} %bitcast.34), custom_call_target="tpu_custom_call" | custom-call | bytes 6291456 | tf_op jit(solution)/shard_map/pack_blocks/pallas_call | solution.py:26
  10.8 2.1 %collective-permute-start.4 = (bf16[80,256]{1,0:T(8,128)(2,1)S(1)}, bf16[80,256]{1,0:T(8,128)(2,1)S(1)}, u32[]{:S(2)}, u32[]{:S(2)}) collective-permute-start(bf16[80,256]{1,0:T(8,128)(2,1)S(1)} %gate.9), channel_id=1, source_target_pairs={{0,24},{8,16},{16,8},{24,0},{1,25},{9,17},{17,9},{25,1},{2,26},{10... | collective-permute-start | bytes 122888 | tf_op jit(solution)/shard_map/ppermute | solution.py:56
  16.7 2.0 %embed_update.1 = (f32[256,1024]{1,0:T(8,128)}, bf16[256,1024]{1,0:T(8,128)(2,1)S(1)}, f32[64,256]{1,0:T(8,128)}, bf16[2,1024]{1,0:T(2,128)(2,1)}, f32[2,1024]{1,0:T(2,128)}, /*index=5*/f32[2,1024]{1,0:T(2,128)}) custom-call(f32[64,256]{1,0:T(8,128)S(1)} %get-tuple-element.47.refs_0_, f32[64,256]{1,0:T(8,128)S(1)} %fusion.refs_1_, f32[256,1024]{1,0:T(8,128)S(1)} %bitcast.23, ...), custom_call_target="tpu_custom_call" | custom-call | bytes 4976640 | tf_op jit(solution)/shard_map/embed_update/pallas_call | solution.py:26
  20.7 4.8 %collective-permute-done.1.refs_0_.came = bf16[256,1024]{1,0:T(8,128)(2,1)S(1)} collective-permute-done((bf16[256,1024]{1,0:T(8,128)(2,1)S(1)}, bf16[256,1024]{1,0:T(8,128)(2,1)S(1)}, u32[]{:S(2)}, u32[]{:S(2)}) %collective-permute-start.1) | collective-permute-done | bytes 524320 | tf_op jit(solution)/shard_map/ppermute | solution.py:52
  25.5 4.4 %collective-permute-start.2 = (bf16[256,1024]{1,0:T(8,128)(2,1)S(1)}, bf16[256,1024]{1,0:T(8,128)(2,1)S(1)}, u32[]{:S(2)}, u32[]{:S(2)}) collective-permute-start(bf16[256,1024]{1,0:T(8,128)(2,1)S(1)} %gate.8), channel_id=1, source_target_pairs={{0,8},{24,16},{1,9},{25,17},{2,10},{26,18},{3,11},{27,19},{4,12},{... | collective-permute-start | bytes 1572872 | tf_op jit(solution)/shard_map/ppermute | solution.py:52
  34.0 5.3 %collective-permute-done.2.came = bf16[256,1024]{1,0:T(8,128)(2,1)S(1)} collective-permute-done((bf16[256,1024]{1,0:T(8,128)(2,1)S(1)}, bf16[256,1024]{1,0:T(8,128)(2,1)S(1)}, u32[]{:S(2)}, u32[]{:S(2)}) %collective-permute-start.2) | collective-permute-done | bytes 524320 | tf_op jit(solution)/shard_map/ppermute | solution.py:52
  40.2 7.1 %collective-permute-start.6 = (bf16[256,1024]{1,0:T(8,128)(2,1)S(1)}, bf16[256,1024]{1,0:T(8,128)(2,1)S(1)}, u32[]{:S(2)}, u32[]{:S(2)}) collective-permute-start(bf16[256,1024]{1,0:T(8,128)(2,1)S(1)} %gate.10), channel_id=1, source_target_pairs={{0,8},{24,16},{1,9},{25,17},{2,10},{26,18},{3,11},{27,19},{4,12},{... | collective-permute-start | bytes 1572872 | tf_op jit(solution)/shard_map/ppermute | solution.py:52
  48.7 6.8 %collective-permute-done.6.refs_5_.refs_3_ = bf16[256,1024]{1,0:T(8,128)(2,1)S(1)} collective-permute-done((bf16[256,1024]{1,0:T(8,128)(2,1)S(1)}, bf16[256,1024]{1,0:T(8,128)(2,1)S(1)}, u32[]{:S(2)}, u32[]{:S(2)}) %collective-permute-start.6) | collective-permute-done | bytes 524320 | tf_op jit(solution)/shard_map/ppermute | solution.py:52
  55.6 4.3 %collective-permute-done.10.refs_7_.refs_5_ = bf16[256,1024]{1,0:T(8,128)(2,1)S(1)} collective-permute-done((bf16[256,1024]{1,0:T(8,128)(2,1)S(1)}, bf16[256,1024]{1,0:T(8,128)(2,1)S(1)}, u32[]{:S(2)}, u32[]{:S(2)}) %collective-permute-start.10) | collective-permute-done | bytes 524320 | tf_op jit(solution)/shard_map/ppermute | solution.py:52
  65.5 7.1 %collective-permute-done.18.refs_0_.refs_1_ = bf16[256,1024]{1,0:T(8,128)(2,1)S(1)} collective-permute-done((bf16[256,1024]{1,0:T(8,128)(2,1)S(1)}, bf16[256,1024]{1,0:T(8,128)(2,1)S(1)}, u32[]{:S(2)}, u32[]{:S(2)}) %collective-permute-start.18) | collective-permute-done | bytes 524320 | tf_op jit(solution)/shard_map/ppermute | solution.py:56
  72.6 3.3 %collective-permute-done.13.x = bf16[256,1024]{1,0:T(8,128)(2,1)S(1)} collective-permute-done((bf16[256,1024]{1,0:T(8,128)(2,1)S(1)}, bf16[256,1024]{1,0:T(8,128)(2,1)S(1)}, u32[]{:S(2)}, u32[]{:S(2)}) %collective-permute-start.13) | collective-permute-done | bytes 524320 | tf_op jit(solution)/shard_map/ppermute | solution.py:56
  79.7 3.9 %collective-permute-done.17.end = bf16[256,1024]{1,0:T(8,128)(2,1)S(1)} collective-permute-done((bf16[256,1024]{1,0:T(8,128)(2,1)S(1)}, bf16[256,1024]{1,0:T(8,128)(2,1)S(1)}, u32[]{:S(2)}, u32[]{:S(2)}) %collective-permute-start.17) | collective-permute-done | bytes 524320 | tf_op jit(solution)/shard_map/ppermute | solution.py:52
  83.6 3.7 %collective-permute-done.19.refs_0_.refs_3_ = bf16[256,1024]{1,0:T(8,128)(2,1)S(1)} collective-permute-done((bf16[256,1024]{1,0:T(8,128)(2,1)S(1)}, bf16[256,1024]{1,0:T(8,128)(2,1)S(1)}, u32[]{:S(2)}, u32[]{:S(2)}) %collective-permute-start.19) | collective-permute-done | bytes 524320 | tf_op jit(solution)/shard_map/ppermute | solution.py:56
  89.5 1.6 %collective-permute-start.23 = (f32[32,2048]{1,0:T(8,128)S(1)}, f32[32,2048]{1,0:T(8,128)S(1)}, u32[]{:S(2)}, u32[]{:S(2)}) collective-permute-start(f32[32,2048]{1,0:T(8,128)S(1)} %get-tuple-element.52), channel_id=1, source_target_pairs={{0,1},{1,0},{2,3},{3,2},{4,5},{5,4},{6,7},{7,6},{8,9},{9,8},{10,11... | collective-permute-start | bytes 786440 | tf_op jit(solution)/shard_map/ppermute | solution.py:512
  91.1 4.8 %collective-permute-done.23.refs_2_.refs_1_ = f32[32,2048]{1,0:T(8,128)S(1)} collective-permute-done((f32[32,2048]{1,0:T(8,128)S(1)}, f32[32,2048]{1,0:T(8,128)S(1)}, u32[]{:S(2)}, u32[]{:S(2)}) %collective-permute-start.23) | collective-permute-done | bytes 262176 | tf_op jit(solution)/shard_map/ppermute | solution.py:512
  96.6 3.9 %collective-permute-done.15.end = bf16[256,1024]{1,0:T(8,128)(2,1)S(1)} collective-permute-done((bf16[256,1024]{1,0:T(8,128)(2,1)S(1)}, bf16[256,1024]{1,0:T(8,128)(2,1)S(1)}, u32[]{:S(2)}, u32[]{:S(2)}) %collective-permute-start.15) | collective-permute-done | bytes 524320 | tf_op jit(solution)/shard_map/ppermute | solution.py:52
  100.9 1.7 %collective-permute-start.24 = (bf16[256,1024]{1,0:T(8,128)(2,1)S(1)}, bf16[256,1024]{1,0:T(8,128)(2,1)S(1)}, u32[]{:S(2)}, u32[]{:S(2)}) collective-permute-start(bf16[256,1024]{1,0:T(8,128)(2,1)S(1)} %pick.6.refs_6_), channel_id=1, source_target_pairs={{0,4},{2,6},{4,0},{6,2},{1,5},{3,7},{5,1},{7,3},{8,12},{10,14},{12... | collective-permute-start | bytes 1572872 | tf_op jit(solution)/shard_map/ppermute | solution.py:56
  104.1 3.2 %collective-permute-done.25.refs_2_.refs_1_ = bf16[7,256,1024]{2,1,0:T(8,128)(2,1)S(1)} collective-permute-done((bf16[7,256,1024]{2,1,0:T(8,128)(2,1)S(1)}, bf16[7,256,1024]{2,1,0:T(8,128)(2,1)S(1)}, u32[]{:S(2)}, u32[]{:S(2)}) %collective-permute-start.25) | collective-permute-done | bytes 3670048 | tf_op jit(solution)/shard_map/ppermute | solution.py:56
  109.6 3.3 %place_rows.2 = (bf16[4,4,128,1024]{3,2,1,0:T(8,128)(2,1)}, bf16[4,4,64,2048]{3,2,1,0:T(8,128)(2,1)}, f32[8,128]{1,0:T(8,128)S(1)}) custom-call(bf16[7,256,1024]{2,1,0:T(8,128)(2,1)S(1)} %bundle.2.refs_0_, bf16[7,256,1024]{2,1,0:T(8,128)(2,1)S(1)} %collective-permute-done.25.refs_2_.refs_1_, f32[8,128]{1,0:T(8,128)S(1)} %get-tuple-element.54.refs_2_), custom_call_target="tpu_custom_call" | custom-call | bytes 25178112 | tf_op jit(solution)/shard_map/place_rows/pallas_call | solution.py:26
  112.9 2.3 %collective-permute-done.24.refs_0_ = bf16[256,1024]{1,0:T(8,128)(2,1)S(1)} collective-permute-done((bf16[256,1024]{1,0:T(8,128)(2,1)S(1)}, bf16[256,1024]{1,0:T(8,128)(2,1)S(1)}, u32[]{:S(2)}, u32[]{:S(2)}) %collective-permute-start.24) | collective-permute-done | bytes 524320 | tf_op jit(solution)/shard_map/ppermute | solution.py:56
  115.4 3.3 %collective-permute-done.27.end = bf16[256,1024]{1,0:T(8,128)(2,1)S(1)} collective-permute-done((bf16[256,1024]{1,0:T(8,128)(2,1)S(1)}, bf16[256,1024]{1,0:T(8,128)(2,1)S(1)}, u32[]{:S(2)}, u32[]{:S(2)}) %collective-permute-start.27) | collective-permute-done | bytes 524320 | tf_op jit(solution)/shard_map/ppermute | solution.py:52
  (81 shorter events, 30.9 us)
Async XLA Ops:
  3.2 7.5 %collective-permute-start = (bf16[80,256]{1,0:T(8,128)(2,1)S(1)}, bf16[80,256]{1,0:T(8,128)(2,1)S(1)}, u32[]{:S(2)}, u32[]{:S(2)}) collective-permute-start(bf16[80,256]{1,0:T(8,128)(2,1)S(1)} %get-tuple-element.46), channel_id=1, source_target_pairs={{0,8},{8,0},{16,24},{24,16},{1,9},{9,1},{17,25},{25,17},{2,10},{10... | collective-permute-start | bytes 122888 | tf_op jit(solution)/shard_map/ppermute | solution.py:56
  6.3 9.0 %collective-permute-start.3 = (bf16[80,256]{1,0:T(8,128)(2,1)S(1)}, bf16[80,256]{1,0:T(8,128)(2,1)S(1)}, u32[]{:S(2)}, u32[]{:S(2)}) collective-permute-start(bf16[80,256]{1,0:T(8,128)(2,1)S(1)} %get-tuple-element.48), channel_id=1, source_target_pairs={{0,16},{8,24},{16,0},{24,8},{1,17},{9,25},{17,1},{25,9},{2,18},{10... | collective-permute-start | bytes 122888 | tf_op jit(solution)/shard_map/ppermute | solution.py:56
  13.9 11.6 %collective-permute-start.1 = (bf16[256,1024]{1,0:T(8,128)(2,1)S(1)}, bf16[256,1024]{1,0:T(8,128)(2,1)S(1)}, u32[]{:S(2)}, u32[]{:S(2)}) collective-permute-start(bf16[256,1024]{1,0:T(8,128)(2,1)S(1)} %gate.7.refs_0_.block), channel_id=1, source_target_pairs={{0,8},{24,16},{1,9},{25,17},{2,10},{26,18},{3,11},{27,19},{4,12},{... | collective-permute-start | bytes 1572872 | tf_op jit(solution)/shard_map/ppermute | solution.py:52
  18.7 11.4 %collective-permute-start.8 = (bf16[256,1024]{1,0:T(8,128)(2,1)S(1)}, bf16[256,1024]{1,0:T(8,128)(2,1)S(1)}, u32[]{:S(2)}, u32[]{:S(2)}) collective-permute-start(bf16[256,1024]{1,0:T(8,128)(2,1)S(1)} %get-tuple-element.50.x.refs_0_), channel_id=1, source_target_pairs={{8,16},{16,8},{9,17},{17,9},{10,18},{18,10},{11,19},{19,11},{12,20... | collective-permute-start | bytes 1572872 | tf_op jit(solution)/shard_map/ppermute | solution.py:52
  19.4 14.5 %collective-permute-start.5 = (bf16[256,1024]{1,0:T(8,128)(2,1)S(1)}, bf16[256,1024]{1,0:T(8,128)(2,1)S(1)}, u32[]{:S(2)}, u32[]{:S(2)}) collective-permute-start(bf16[256,1024]{1,0:T(8,128)(2,1)S(1)} %get-tuple-element.50.x.refs_0_), channel_id=1, source_target_pairs={{8,0},{16,24},{9,1},{17,25},{10,2},{18,26},{11,3},{19,27},{12,4},{... | collective-permute-start | bytes 1572872 | tf_op jit(solution)/shard_map/ppermute | solution.py:52
  25.5 13.7 %collective-permute-start.2 = (bf16[256,1024]{1,0:T(8,128)(2,1)S(1)}, bf16[256,1024]{1,0:T(8,128)(2,1)S(1)}, u32[]{:S(2)}, u32[]{:S(2)}) collective-permute-start(bf16[256,1024]{1,0:T(8,128)(2,1)S(1)} %gate.8), channel_id=1, source_target_pairs={{0,8},{24,16},{1,9},{25,17},{2,10},{26,18},{3,11},{27,19},{4,12},{... | collective-permute-start | bytes 1572872 | tf_op jit(solution)/shard_map/ppermute | solution.py:52
  30.2 17.1 %collective-permute-start.9 = (bf16[256,1024]{1,0:T(8,128)(2,1)S(1)}, bf16[256,1024]{1,0:T(8,128)(2,1)S(1)}, u32[]{:S(2)}, u32[]{:S(2)}) collective-permute-start(bf16[256,1024]{1,0:T(8,128)(2,1)S(1)} %gate.11), channel_id=1, source_target_pairs={{8,16},{16,8},{9,17},{17,9},{10,18},{18,10},{11,19},{19,11},{12,20... | collective-permute-start | bytes 1572872 | tf_op jit(solution)/shard_map/ppermute | solution.py:52
  31.1 17.6 %collective-permute-start.11 = (f32[2,32,2048]{2,1,0:T(8,128)S(1)}, f32[2,32,2048]{2,1,0:T(8,128)S(1)}, u32[]{:S(2)}, u32[]{:S(2)}) collective-permute-start(f32[2,32,2048]{2,1,0:T(8,128)S(1)} %up_state.1), channel_id=1, source_target_pairs={{0,1},{1,0},{2,3},{3,2},{4,5},{5,4},{6,7},{7,6},{8,9},{9,8},{10,11... | collective-permute-start | bytes 1572872 | tf_op jit(solution)/shard_map/ppermute | solution.py:429
  32.7 16.1 %collective-permute-start.12 = (bf16[256,1024]{1,0:T(8,128)(2,1)S(1)}, bf16[256,1024]{1,0:T(8,128)(2,1)S(1)}, u32[]{:S(2)}, u32[]{:S(2)}) collective-permute-start(bf16[256,1024]{1,0:T(8,128)(2,1)S(1)} %collective-permute-done.8.refs_0_.middle), channel_id=1, source_target_pairs={{8,0},{16,24},{9,1},{17,25},{10,2},{18,26},{11,3},{19,27},{12,4},{... | collective-permute-start | bytes 1572872 | tf_op jit(solution)/shard_map/ppermute | solution.py:52
  39.4 16.1 %collective-permute-start.7 = (bf16[256,1024]{1,0:T(8,128)(2,1)S(1)}, bf16[256,1024]{1,0:T(8,128)(2,1)S(1)}, u32[]{:S(2)}, u32[]{:S(2)}) collective-permute-start(bf16[256,1024]{1,0:T(8,128)(2,1)S(1)} %add_block.3.refs_0_), channel_id=1, source_target_pairs={{8,16},{16,8},{9,17},{17,9},{10,18},{18,10},{11,19},{19,11},{12,20... | collective-permute-start | bytes 1572872 | tf_op jit(solution)/shard_map/ppermute | solution.py:52
  40.2 15.4 %collective-permute-start.6 = (bf16[256,1024]{1,0:T(8,128)(2,1)S(1)}, bf16[256,1024]{1,0:T(8,128)(2,1)S(1)}, u32[]{:S(2)}, u32[]{:S(2)}) collective-permute-start(bf16[256,1024]{1,0:T(8,128)(2,1)S(1)} %gate.10), channel_id=1, source_target_pairs={{0,8},{24,16},{1,9},{25,17},{2,10},{26,18},{3,11},{27,19},{4,12},{... | collective-permute-start | bytes 1572872 | tf_op jit(solution)/shard_map/ppermute | solution.py:52
  47.4 12.4 %collective-permute-start.10 = (bf16[256,1024]{1,0:T(8,128)(2,1)S(1)}, bf16[256,1024]{1,0:T(8,128)(2,1)S(1)}, u32[]{:S(2)}, u32[]{:S(2)}) collective-permute-start(bf16[256,1024]{1,0:T(8,128)(2,1)S(1)} %add_block.5), channel_id=1, source_target_pairs={{8,0},{16,24},{9,1},{17,25},{10,2},{18,26},{11,3},{19,27},{12,4},{... | collective-permute-start | bytes 1572872 | tf_op jit(solution)/shard_map/ppermute | solution.py:52
  61.5 11.1 %collective-permute-start.18 = (bf16[256,1024]{1,0:T(8,128)(2,1)S(1)}, bf16[256,1024]{1,0:T(8,128)(2,1)S(1)}, u32[]{:S(2)}, u32[]{:S(2)}) collective-permute-start(bf16[256,1024]{1,0:T(8,128)(2,1)S(1)} %update_rows.1.refs_0_), channel_id=1, source_target_pairs={{0,4},{2,6},{4,0},{6,2},{1,5},{3,7},{5,1},{7,3},{8,12},{10,14},{12... | collective-permute-start | bytes 1572872 | tf_op jit(solution)/shard_map/ppermute | solution.py:56
  63.1 12.8 %collective-permute-start.13 = (bf16[256,1024]{1,0:T(8,128)(2,1)S(1)}, bf16[256,1024]{1,0:T(8,128)(2,1)S(1)}, u32[]{:S(2)}, u32[]{:S(2)}) collective-permute-start(bf16[256,1024]{1,0:T(8,128)(2,1)S(1)} %update_rows.1.refs_0_), channel_id=1, source_target_pairs={{0,8},{8,0},{16,24},{24,16},{1,9},{9,1},{17,25},{25,17},{2,10},{10... | collective-permute-start | bytes 1572872 | tf_op jit(solution)/shard_map/ppermute | solution.py:56
  64.3 19.4 %collective-permute-start.17 = (bf16[256,1024]{1,0:T(8,128)(2,1)S(1)}, bf16[256,1024]{1,0:T(8,128)(2,1)S(1)}, u32[]{:S(2)}, u32[]{:S(2)}) collective-permute-start(bf16[256,1024]{1,0:T(8,128)(2,1)S(1)} %collective-permute-done.16.middle), channel_id=1, source_target_pairs={{8,0},{16,24},{9,1},{17,25},{10,2},{18,26},{11,3},{19,27},{12,4},{... | collective-permute-start | bytes 1572872 | tf_op jit(solution)/shard_map/ppermute | solution.py:52
  75.9 11.4 %collective-permute-start.19 = (bf16[256,1024]{1,0:T(8,128)(2,1)S(1)}, bf16[256,1024]{1,0:T(8,128)(2,1)S(1)}, u32[]{:S(2)}, u32[]{:S(2)}) collective-permute-start(bf16[256,1024]{1,0:T(8,128)(2,1)S(1)} %gate.12.refs_6_.refs_0_.refs_2_), channel_id=1, source_target_pairs={{0,4},{2,6},{4,0},{6,2},{1,5},{3,7},{5,1},{7,3},{8,12},{10,14},{12... | collective-permute-start | bytes 1572872 | tf_op jit(solution)/shard_map/ppermute | solution.py:56
  76.1 11.4 %collective-permute-start.21 = (bf16[256,1024]{1,0:T(8,128)(2,1)S(1)}, bf16[256,1024]{1,0:T(8,128)(2,1)S(1)}, u32[]{:S(2)}, u32[]{:S(2)}) collective-permute-start(bf16[256,1024]{1,0:T(8,128)(2,1)S(1)} %gate.13), channel_id=1, source_target_pairs={{0,8},{24,16},{1,9},{25,17},{2,10},{26,18},{3,11},{27,19},{4,12},{... | collective-permute-start | bytes 1572872 | tf_op jit(solution)/shard_map/ppermute | solution.py:52
  77.5 10.6 %collective-permute-start.14 = (bf16[256,1024]{1,0:T(8,128)(2,1)S(1)}, bf16[256,1024]{1,0:T(8,128)(2,1)S(1)}, u32[]{:S(2)}, u32[]{:S(2)}) collective-permute-start(bf16[256,1024]{1,0:T(8,128)(2,1)S(1)} %collective-permute-done.13.x), channel_id=1, source_target_pairs={{8,16},{16,8},{9,17},{17,9},{10,18},{18,10},{11,19},{19,11},{12,20... | collective-permute-start | bytes 1572872 | tf_op jit(solution)/shard_map/ppermute | solution.py:52
  87.4 9.2 %collective-permute-start.20 = (bf16[256,1024]{1,0:T(8,128)(2,1)S(1)}, bf16[256,1024]{1,0:T(8,128)(2,1)S(1)}, u32[]{:S(2)}, u32[]{:S(2)}) collective-permute-start(bf16[256,1024]{1,0:T(8,128)(2,1)S(1)} %pick.5.refs_4_), channel_id=1, source_target_pairs={{0,4},{2,6},{4,0},{6,2},{1,5},{3,7},{5,1},{7,3},{8,12},{10,14},{12... | collective-permute-start | bytes 1572872 | tf_op jit(solution)/shard_map/ppermute | solution.py:56
  87.5 8.5 %collective-permute-start.22 = (bf16[256,1024]{1,0:T(8,128)(2,1)S(1)}, bf16[256,1024]{1,0:T(8,128)(2,1)S(1)}, u32[]{:S(2)}, u32[]{:S(2)}) collective-permute-start(bf16[256,1024]{1,0:T(8,128)(2,1)S(1)} %collective-permute-done.21.middle), channel_id=1, source_target_pairs={{8,16},{16,8},{9,17},{17,9},{10,18},{18,10},{11,19},{19,11},{12,20... | collective-permute-start | bytes 1572872 | tf_op jit(solution)/shard_map/ppermute | solution.py:52
  88.2 12.4 %collective-permute-start.15 = (bf16[256,1024]{1,0:T(8,128)(2,1)S(1)}, bf16[256,1024]{1,0:T(8,128)(2,1)S(1)}, u32[]{:S(2)}, u32[]{:S(2)}) collective-permute-start(bf16[256,1024]{1,0:T(8,128)(2,1)S(1)} %collective-permute-done.14.middle), channel_id=1, source_target_pairs={{8,0},{16,24},{9,1},{17,25},{10,2},{18,26},{11,3},{19,27},{12,4},{... | collective-permute-start | bytes 1572872 | tf_op jit(solution)/shard_map/ppermute | solution.py:52
  100.8 6.5 %collective-permute-start.25 = (bf16[7,256,1024]{2,1,0:T(8,128)(2,1)S(1)}, bf16[7,256,1024]{2,1,0:T(8,128)(2,1)S(1)}, u32[]{:S(2)}, u32[]{:S(2)}) collective-permute-start(bf16[7,256,1024]{2,1,0:T(8,128)(2,1)S(1)} %bundle.2.refs_0_), channel_id=1, source_target_pairs={{0,2},{2,0},{4,6},{6,4},{1,3},{3,1},{5,7},{7,5},{8,10},{10,8},{12,... | collective-permute-start | bytes 11010056 | tf_op jit(solution)/shard_map/ppermute | solution.py:56
  100.9 14.3 %collective-permute-start.24 = (bf16[256,1024]{1,0:T(8,128)(2,1)S(1)}, bf16[256,1024]{1,0:T(8,128)(2,1)S(1)}, u32[]{:S(2)}, u32[]{:S(2)}) collective-permute-start(bf16[256,1024]{1,0:T(8,128)(2,1)S(1)} %pick.6.refs_6_), channel_id=1, source_target_pairs={{0,4},{2,6},{4,0},{6,2},{1,5},{3,7},{5,1},{7,3},{8,12},{10,14},{12... | collective-permute-start | bytes 1572872 | tf_op jit(solution)/shard_map/ppermute | solution.py:56
  102.8 15.9 %collective-permute-start.27 = (bf16[256,1024]{1,0:T(8,128)(2,1)S(1)}, bf16[256,1024]{1,0:T(8,128)(2,1)S(1)}, u32[]{:S(2)}, u32[]{:S(2)}) collective-permute-start(bf16[256,1024]{1,0:T(8,128)(2,1)S(1)} %collective-permute-done.22.refs_1_.middle), channel_id=1, source_target_pairs={{8,0},{16,24},{9,1},{17,25},{10,2},{18,26},{11,3},{19,27},{12,4},{... | collective-permute-start | bytes 1572872 | tf_op jit(solution)/shard_map/ppermute | solution.py:52
  (14 other events, 158.9 us)

commit v15 on v14

--- a/solution.py
+++ b/solution.py
@@ -464,9 +464,10 @@
     embed_middle = along(recast_rows, ACROSS)
     end_sum = gate(add(end, from_end), embed_middle)
     end_partial = along(end_sum, ACROSS)
-    middle_sum = add(middle, along(gate(middle, from_end), INWARD), embed_out)
+    from_middle = along(gate(middle, from_end), INWARD)
+    middle_sum = add(middle, from_middle, embed_out)
     middle_partial = along(middle_sum, ACROSS)
-    from_near = along(gate(near, middle_sum), INWARD)
+    from_near = along(gate(near, embed_out, from_middle), INWARD)
     embed_middle_out = along(embed_middle, OUTWARD)
     to_end = along(add(near, end_partial), OUTWARD)
     came0 = [own, from_near, middle_partial, to_end]

time: 122 us -> 119 us (0.975)
  waiting for transfers between devices: 59 us -> 56.5 us
    ppermute x16, starting transfers between devices: 26.3 us -> 23.7 us  [along(): return lax.ppermute(x, 'replica', pairs)]
    ppermute x2, starting transfers between devices: 3.18 us -> 5.38 us  [body(): lax.ppermute(x, 'tensor', [(i, (i + shift) % tensors) for i in range(tens...]
    ppermute x10, waiting for transfers between devices: 21.7 us -> 19.5 us  [swap(): lax.ppermute(x, axis, [(i, i ^ bit) for i in range(lax.axis_size(axis))])]
  transfers between devices with their start and end apart: 28 -> 28, of which waited for: 15 -> 16; matrix products, arithmetic and copies ran while one was open for 1% -> 1% of each run, Pallas kernels for 10% -> 11%
where the time goes in v15:
time: 119 us; the launch traced here: 118 us
  waiting for transfers between devices  56.5 us (47%)
  starting transfers between devices  41.2 us (35%)
  Pallas kernels  17.9 us (15%)
    ppermute x16, waiting for transfers between devices, along(): return lax.ppermute(x, 'replica', pairs)  32.6 us
    ppermute x16, starting transfers between devices, along(): return lax.ppermute(x, 'replica', pairs)  23.7 us
    ppermute x10, waiting for transfers between devices, swap(): lax.ppermute(x, axis, [(i, i ^ bit) for i in range(lax.axis_size(axis))])  19.5 us
    pallas_call x28, Pallas kernels, call(): pl.pallas_call(kernel, name=name, out_shape=out_shape, in_specs=in_specs,...  17.9 us
    ppermute x10, starting transfers between devices, swap(): lax.ppermute(x, axis, [(i, i ^ bit) for i in range(lax.axis_size(axis))])  12.2 us
    ppermute x2, starting transfers between devices, body(): lax.ppermute(x, 'tensor', [(i, (i + shift) % tensors) for i in range(tens...  5.38 us
    ppermute x2, waiting for transfers between devices, body(): lax.ppermute(x, 'tensor', [(i, (i + shift) % tensors) for i in range(tens...  4.35 us
  transfers between devices with their start and end apart: 28, of which 16 were waited for; matrix products, arithmetic and copies ran while one was open for 1% of the time, Pallas kernels for 11%

profile of v15, /device:TPU:0, one launch (start us, length us, event | category | flops | bytes accessed | tf_op | source)
XLA Modules:
  0.0 117.9 jit_solution(1074016106293311437)
XLA Ops:
  0.6 2.6 %project_rows.1 = (f32[64,256]{1,0:T(8,128)S(1)}, bf16[80,256]{1,0:T(8,128)(2,1)S(1)}, bf16[80,256]{1,0:T(8,128)(2,1)S(1)}, bf16[80,256]{1,0:T(8,128)(2,1)S(1)}) custom-call(bf16[1024,1024]{1,0:T(8,128)(2,1)} %bitcast.37, f32[64,1024]{1,0:T(8,128)} %bitcast.24, bf16[2,1024]{1,0:T(2,128)(2,1)} %bitcast.31), custom_call_target="tpu_custom_call" | custom-call | bytes 565248 | tf_op jit(solution)/shard_map/project_rows/pallas_call | solution.py:26
  3.2 3.1 %collective-permute-start = (bf16[80,256]{1,0:T(8,128)(2,1)S(1)}, bf16[80,256]{1,0:T(8,128)(2,1)S(1)}, u32[]{:S(2)}, u32[]{:S(2)}) collective-permute-start(bf16[80,256]{1,0:T(8,128)(2,1)S(1)} %get-tuple-element.45), channel_id=1, source_target_pairs={{0,8},{8,0},{16,24},{24,16},{1,9},{9,1},{17,25},{25,17},{2,10},{10... | collective-permute-start | bytes 122888 | tf_op jit(solution)/shard_map/ppermute | solution.py:56
  6.3 2.6 %collective-permute-start.1 = (bf16[80,256]{1,0:T(8,128)(2,1)S(1)}, bf16[80,256]{1,0:T(8,128)(2,1)S(1)}, u32[]{:S(2)}, u32[]{:S(2)}) collective-permute-start(bf16[80,256]{1,0:T(8,128)(2,1)S(1)} %get-tuple-element.46), channel_id=1, source_target_pairs={{0,16},{8,24},{16,0},{24,8},{1,17},{9,25},{17,1},{25,9},{2,18},{10... | collective-permute-start | bytes 122888 | tf_op jit(solution)/shard_map/ppermute | solution.py:56
  8.9 1.8 %pack_blocks.1 = (bf16[256,1024]{1,0:T(8,128)(2,1)S(1)}, bf16[256,1024]{1,0:T(8,128)(2,1)S(1)}, bf16[256,1024]{1,0:T(8,128)(2,1)S(1)}, bf16[256,1024]{1,0:T(8,128)(2,1)S(1)}) custom-call(bf16[4,4,128,1024]{3,2,1,0:T(8,128)(2,1)} %bitcast.33, bf16[4,4,64,2048]{3,2,1,0:T(8,128)(2,1)} %bitcast.34), custom_call_target="tpu_custom_call" | custom-call | bytes 6291456 | tf_op jit(solution)/shard_map/pack_blocks/pallas_call | solution.py:26
  10.8 2.1 %collective-permute-start.2 = (bf16[80,256]{1,0:T(8,128)(2,1)S(1)}, bf16[80,256]{1,0:T(8,128)(2,1)S(1)}, u32[]{:S(2)}, u32[]{:S(2)}) collective-permute-start(bf16[80,256]{1,0:T(8,128)(2,1)S(1)} %gate.8), channel_id=1, source_target_pairs={{0,24},{8,16},{16,8},{24,0},{1,25},{9,17},{17,9},{25,1},{2,26},{10... | collective-permute-start | bytes 122888 | tf_op jit(solution)/shard_map/ppermute | solution.py:56
  16.7 2.0 %embed_update.1 = (f32[256,1024]{1,0:T(8,128)}, bf16[256,1024]{1,0:T(8,128)(2,1)S(1)}, f32[64,256]{1,0:T(8,128)}, bf16[2,1024]{1,0:T(2,128)(2,1)}, f32[2,1024]{1,0:T(2,128)}, /*index=5*/f32[2,1024]{1,0:T(2,128)}) custom-call(f32[64,256]{1,0:T(8,128)S(1)} %get-tuple-element.44.refs_0_, f32[64,256]{1,0:T(8,128)S(1)} %fusion.refs_1_, f32[256,1024]{1,0:T(8,128)S(1)} %bitcast.23, ...), custom_call_target="tpu_custom_call" | custom-call | bytes 4976640 | tf_op jit(solution)/shard_map/embed_update/pallas_call | solution.py:26
  20.7 4.8 %collective-permute-done.4.refs_0_.came = bf16[256,1024]{1,0:T(8,128)(2,1)S(1)} collective-permute-done((bf16[256,1024]{1,0:T(8,128)(2,1)S(1)}, bf16[256,1024]{1,0:T(8,128)(2,1)S(1)}, u32[]{:S(2)}, u32[]{:S(2)}) %collective-permute-start.4) | collective-permute-done | bytes 524320 | tf_op jit(solution)/shard_map/ppermute | solution.py:52
  25.5 4.4 %collective-permute-start.5 = (bf16[256,1024]{1,0:T(8,128)(2,1)S(1)}, bf16[256,1024]{1,0:T(8,128)(2,1)S(1)}, u32[]{:S(2)}, u32[]{:S(2)}) collective-permute-start(bf16[256,1024]{1,0:T(8,128)(2,1)S(1)} %gate.9), channel_id=1, source_target_pairs={{0,8},{24,16},{1,9},{25,17},{2,10},{26,18},{3,11},{27,19},{4,12},{... | collective-permute-start | bytes 1572872 | tf_op jit(solution)/shard_map/ppermute | solution.py:52
  34.0 5.3 %collective-permute-done.5.refs_1_.came = bf16[256,1024]{1,0:T(8,128)(2,1)S(1)} collective-permute-done((bf16[256,1024]{1,0:T(8,128)(2,1)S(1)}, bf16[256,1024]{1,0:T(8,128)(2,1)S(1)}, u32[]{:S(2)}, u32[]{:S(2)}) %collective-permute-start.5) | collective-permute-done | bytes 524320 | tf_op jit(solution)/shard_map/ppermute | solution.py:52
  39.3 4.4 %collective-permute-start.6 = (bf16[256,1024]{1,0:T(8,128)(2,1)S(1)}, bf16[256,1024]{1,0:T(8,128)(2,1)S(1)}, u32[]{:S(2)}, u32[]{:S(2)}) collective-permute-start(bf16[256,1024]{1,0:T(8,128)(2,1)S(1)} %gate.10), channel_id=1, source_target_pairs={{0,8},{24,16},{1,9},{25,17},{2,10},{26,18},{3,11},{27,19},{4,12},{... | collective-permute-start | bytes 1572872 | tf_op jit(solution)/shard_map/ppermute | solution.py:52
  47.1 5.0 %collective-permute-done.6.refs_5_.refs_3_ = bf16[256,1024]{1,0:T(8,128)(2,1)S(1)} collective-permute-done((bf16[256,1024]{1,0:T(8,128)(2,1)S(1)}, bf16[256,1024]{1,0:T(8,128)(2,1)S(1)}, u32[]{:S(2)}, u32[]{:S(2)}) %collective-permute-start.6) | collective-permute-done | bytes 524320 | tf_op jit(solution)/shard_map/ppermute | solution.py:52
  52.2 5.7 %collective-permute-done.10.refs_7_.refs_5_ = bf16[256,1024]{1,0:T(8,128)(2,1)S(1)} collective-permute-done((bf16[256,1024]{1,0:T(8,128)(2,1)S(1)}, bf16[256,1024]{1,0:T(8,128)(2,1)S(1)}, u32[]{:S(2)}, u32[]{:S(2)}) %collective-permute-start.10) | collective-permute-done | bytes 524320 | tf_op jit(solution)/shard_map/ppermute | solution.py:52
  61.1 1.8 %collective-permute-start.13 = (bf16[256,1024]{1,0:T(8,128)(2,1)S(1)}, bf16[256,1024]{1,0:T(8,128)(2,1)S(1)}, u32[]{:S(2)}, u32[]{:S(2)}) collective-permute-start(bf16[256,1024]{1,0:T(8,128)(2,1)S(1)} %update_rows.1.refs_0_), channel_id=1, source_target_pairs={{0,8},{8,0},{16,24},{24,16},{1,9},{9,1},{17,25},{25,17},{2,10},{10... | collective-permute-start | bytes 1572872 | tf_op jit(solution)/shard_map/ppermute | solution.py:56
  64.2 6.4 %collective-permute-done.18.refs_0_.refs_1_ = bf16[256,1024]{1,0:T(8,128)(2,1)S(1)} collective-permute-done((bf16[256,1024]{1,0:T(8,128)(2,1)S(1)}, bf16[256,1024]{1,0:T(8,128)(2,1)S(1)}, u32[]{:S(2)}, u32[]{:S(2)}) %collective-permute-start.18) | collective-permute-done | bytes 524320 | tf_op jit(solution)/shard_map/ppermute | solution.py:56
  70.6 3.4 %collective-permute-done.13.x = bf16[256,1024]{1,0:T(8,128)(2,1)S(1)} collective-permute-done((bf16[256,1024]{1,0:T(8,128)(2,1)S(1)}, bf16[256,1024]{1,0:T(8,128)(2,1)S(1)}, u32[]{:S(2)}, u32[]{:S(2)}) %collective-permute-start.13) | collective-permute-done | bytes 524320 | tf_op jit(solution)/shard_map/ppermute | solution.py:56
  77.8 4.6 %collective-permute-done.17.end = bf16[256,1024]{1,0:T(8,128)(2,1)S(1)} collective-permute-done((bf16[256,1024]{1,0:T(8,128)(2,1)S(1)}, bf16[256,1024]{1,0:T(8,128)(2,1)S(1)}, u32[]{:S(2)}, u32[]{:S(2)}) %collective-permute-start.17) | collective-permute-done | bytes 524320 | tf_op jit(solution)/shard_map/ppermute | solution.py:52
  82.4 1.8 %collective-permute-done.19.refs_0_.refs_3_ = bf16[256,1024]{1,0:T(8,128)(2,1)S(1)} collective-permute-done((bf16[256,1024]{1,0:T(8,128)(2,1)S(1)}, bf16[256,1024]{1,0:T(8,128)(2,1)S(1)}, u32[]{:S(2)}, u32[]{:S(2)}) %collective-permute-start.19) | collective-permute-done | bytes 524320 | tf_op jit(solution)/shard_map/ppermute | solution.py:56
  86.3 3.8 %collective-permute-start.23 = (f32[32,2048]{1,0:T(8,128)S(1)}, f32[32,2048]{1,0:T(8,128)S(1)}, u32[]{:S(2)}, u32[]{:S(2)}) collective-permute-start(f32[32,2048]{1,0:T(8,128)S(1)} %get-tuple-element.52), channel_id=1, source_target_pairs={{0,1},{1,0},{2,3},{3,2},{4,5},{5,4},{6,7},{7,6},{8,9},{9,8},{10,11... | collective-permute-start | bytes 786440 | tf_op jit(solution)/shard_map/ppermute | solution.py:513
  90.1 4.4 %collective-permute-done.23.refs_2_.refs_1_ = f32[32,2048]{1,0:T(8,128)S(1)} collective-permute-done((f32[32,2048]{1,0:T(8,128)S(1)}, f32[32,2048]{1,0:T(8,128)S(1)}, u32[]{:S(2)}, u32[]{:S(2)}) %collective-permute-start.23) | collective-permute-done | bytes 262176 | tf_op jit(solution)/shard_map/ppermute | solution.py:513
  94.5 3.8 %collective-permute-done.15.end = bf16[256,1024]{1,0:T(8,128)(2,1)S(1)} collective-permute-done((bf16[256,1024]{1,0:T(8,128)(2,1)S(1)}, bf16[256,1024]{1,0:T(8,128)(2,1)S(1)}, u32[]{:S(2)}, u32[]{:S(2)}) %collective-permute-start.15) | collective-permute-done | bytes 524320 | tf_op jit(solution)/shard_map/ppermute | solution.py:52
  100.8 4.2 %collective-permute-done.25.refs_2_.refs_1_ = bf16[7,256,1024]{2,1,0:T(8,128)(2,1)S(1)} collective-permute-done((bf16[7,256,1024]{2,1,0:T(8,128)(2,1)S(1)}, bf16[7,256,1024]{2,1,0:T(8,128)(2,1)S(1)}, u32[]{:S(2)}, u32[]{:S(2)}) %collective-permute-start.25) | collective-permute-done | bytes 3670048 | tf_op jit(solution)/shard_map/ppermute | solution.py:56
  107.3 3.3 %place_rows.2 = (bf16[4,4,128,1024]{3,2,1,0:T(8,128)(2,1)}, bf16[4,4,64,2048]{3,2,1,0:T(8,128)(2,1)}, f32[8,128]{1,0:T(8,128)S(1)}) custom-call(bf16[7,256,1024]{2,1,0:T(8,128)(2,1)S(1)} %bundle.2.refs_0_, bf16[7,256,1024]{2,1,0:T(8,128)(2,1)S(1)} %collective-permute-done.25.refs_2_.refs_1_, f32[8,128]{1,0:T(8,128)S(1)} %get-tuple-element.54.refs_2_), custom_call_target="tpu_custom_call" | custom-call | bytes 25178112 | tf_op jit(solution)/shard_map/place_rows/pallas_call | solution.py:26
  110.6 2.3 %collective-permute-done.24.refs_0_ = bf16[256,1024]{1,0:T(8,128)(2,1)S(1)} collective-permute-done((bf16[256,1024]{1,0:T(8,128)(2,1)S(1)}, bf16[256,1024]{1,0:T(8,128)(2,1)S(1)}, u32[]{:S(2)}, u32[]{:S(2)}) %collective-permute-start.24) | collective-permute-done | bytes 524320 | tf_op jit(solution)/shard_map/ppermute | solution.py:56
  113.1 2.3 %collective-permute-done.27.end = bf16[256,1024]{1,0:T(8,128)(2,1)S(1)} collective-permute-done((bf16[256,1024]{1,0:T(8,128)(2,1)S(1)}, bf16[256,1024]{1,0:T(8,128)(2,1)S(1)}, u32[]{:S(2)}, u32[]{:S(2)}) %collective-permute-start.27) | collective-permute-done | bytes 524320 | tf_op jit(solution)/shard_map/ppermute | solution.py:52
  (81 shorter events, 31.0 us)
Async XLA Ops:
  3.2 7.5 %collective-permute-start = (bf16[80,256]{1,0:T(8,128)(2,1)S(1)}, bf16[80,256]{1,0:T(8,128)(2,1)S(1)}, u32[]{:S(2)}, u32[]{:S(2)}) collective-permute-start(bf16[80,256]{1,0:T(8,128)(2,1)S(1)} %get-tuple-element.45), channel_id=1, source_target_pairs={{0,8},{8,0},{16,24},{24,16},{1,9},{9,1},{17,25},{25,17},{2,10},{10... | collective-permute-start | bytes 122888 | tf_op jit(solution)/shard_map/ppermute | solution.py:56
  6.3 9.0 %collective-permute-start.1 = (bf16[80,256]{1,0:T(8,128)(2,1)S(1)}, bf16[80,256]{1,0:T(8,128)(2,1)S(1)}, u32[]{:S(2)}, u32[]{:S(2)}) collective-permute-start(bf16[80,256]{1,0:T(8,128)(2,1)S(1)} %get-tuple-element.46), channel_id=1, source_target_pairs={{0,16},{8,24},{16,0},{24,8},{1,17},{9,25},{17,1},{25,9},{2,18},{10... | collective-permute-start | bytes 122888 | tf_op jit(solution)/shard_map/ppermute | solution.py:56
  13.9 11.6 %collective-permute-start.4 = (bf16[256,1024]{1,0:T(8,128)(2,1)S(1)}, bf16[256,1024]{1,0:T(8,128)(2,1)S(1)}, u32[]{:S(2)}, u32[]{:S(2)}) collective-permute-start(bf16[256,1024]{1,0:T(8,128)(2,1)S(1)} %gate.7.refs_0_.block), channel_id=1, source_target_pairs={{0,8},{24,16},{1,9},{25,17},{2,10},{26,18},{3,11},{27,19},{4,12},{... | collective-permute-start | bytes 1572872 | tf_op jit(solution)/shard_map/ppermute | solution.py:52
  18.7 11.4 %collective-permute-start.8 = (bf16[256,1024]{1,0:T(8,128)(2,1)S(1)}, bf16[256,1024]{1,0:T(8,128)(2,1)S(1)}, u32[]{:S(2)}, u32[]{:S(2)}) collective-permute-start(bf16[256,1024]{1,0:T(8,128)(2,1)S(1)} %get-tuple-element.49.x.refs_0_), channel_id=1, source_target_pairs={{8,16},{16,8},{9,17},{17,9},{10,18},{18,10},{11,19},{19,11},{12,20... | collective-permute-start | bytes 1572872 | tf_op jit(solution)/shard_map/ppermute | solution.py:52
  19.4 14.5 %collective-permute-start.3 = (bf16[256,1024]{1,0:T(8,128)(2,1)S(1)}, bf16[256,1024]{1,0:T(8,128)(2,1)S(1)}, u32[]{:S(2)}, u32[]{:S(2)}) collective-permute-start(bf16[256,1024]{1,0:T(8,128)(2,1)S(1)} %get-tuple-element.49.x.refs_0_), channel_id=1, source_target_pairs={{8,0},{16,24},{9,1},{17,25},{10,2},{18,26},{11,3},{19,27},{12,4},{... | collective-permute-start | bytes 1572872 | tf_op jit(solution)/shard_map/ppermute | solution.py:52
  25.5 13.7 %collective-permute-start.5 = (bf16[256,1024]{1,0:T(8,128)(2,1)S(1)}, bf16[256,1024]{1,0:T(8,128)(2,1)S(1)}, u32[]{:S(2)}, u32[]{:S(2)}) collective-permute-start(bf16[256,1024]{1,0:T(8,128)(2,1)S(1)} %gate.9), channel_id=1, source_target_pairs={{0,8},{24,16},{1,9},{25,17},{2,10},{26,18},{3,11},{27,19},{4,12},{... | collective-permute-start | bytes 1572872 | tf_op jit(solution)/shard_map/ppermute | solution.py:52
  30.2 14.4 %collective-permute-start.9 = (bf16[256,1024]{1,0:T(8,128)(2,1)S(1)}, bf16[256,1024]{1,0:T(8,128)(2,1)S(1)}, u32[]{:S(2)}, u32[]{:S(2)}) collective-permute-start(bf16[256,1024]{1,0:T(8,128)(2,1)S(1)} %gate.11), channel_id=1, source_target_pairs={{8,16},{16,8},{9,17},{17,9},{10,18},{18,10},{11,19},{19,11},{12,20... | collective-permute-start | bytes 1572872 | tf_op jit(solution)/shard_map/ppermute | solution.py:52
  31.1 15.0 %collective-permute-start.11 = (f32[2,32,2048]{2,1,0:T(8,128)S(1)}, f32[2,32,2048]{2,1,0:T(8,128)S(1)}, u32[]{:S(2)}, u32[]{:S(2)}) collective-permute-start(f32[2,32,2048]{2,1,0:T(8,128)S(1)} %up_state.1), channel_id=1, source_target_pairs={{0,1},{1,0},{2,3},{3,2},{4,5},{5,4},{6,7},{7,6},{8,9},{9,8},{10,11... | collective-permute-start | bytes 1572872 | tf_op jit(solution)/shard_map/ppermute | solution.py:429
  32.7 14.5 %collective-permute-start.12 = (bf16[256,1024]{1,0:T(8,128)(2,1)S(1)}, bf16[256,1024]{1,0:T(8,128)(2,1)S(1)}, u32[]{:S(2)}, u32[]{:S(2)}) collective-permute-start(bf16[256,1024]{1,0:T(8,128)(2,1)S(1)} %collective-permute-done.8.refs_0_.middle), channel_id=1, source_target_pairs={{8,0},{16,24},{9,1},{17,25},{10,2},{18,26},{11,3},{19,27},{12,4},{... | collective-permute-start | bytes 1572872 | tf_op jit(solution)/shard_map/ppermute | solution.py:52
  39.3 12.8 %collective-permute-start.6 = (bf16[256,1024]{1,0:T(8,128)(2,1)S(1)}, bf16[256,1024]{1,0:T(8,128)(2,1)S(1)}, u32[]{:S(2)}, u32[]{:S(2)}) collective-permute-start(bf16[256,1024]{1,0:T(8,128)(2,1)S(1)} %gate.10), channel_id=1, source_target_pairs={{0,8},{24,16},{1,9},{25,17},{2,10},{26,18},{3,11},{27,19},{4,12},{... | collective-permute-start | bytes 1572872 | tf_op jit(solution)/shard_map/ppermute | solution.py:52
  43.9 8.3 %collective-permute-start.7 = (bf16[256,1024]{1,0:T(8,128)(2,1)S(1)}, bf16[256,1024]{1,0:T(8,128)(2,1)S(1)}, u32[]{:S(2)}, u32[]{:S(2)}) collective-permute-start(bf16[256,1024]{1,0:T(8,128)(2,1)S(1)} %add_block.3), channel_id=1, source_target_pairs={{8,16},{16,8},{9,17},{17,9},{10,18},{18,10},{11,19},{19,11},{12,20... | collective-permute-start | bytes 1572872 | tf_op jit(solution)/shard_map/ppermute | solution.py:52
  44.7 13.1 %collective-permute-start.10 = (bf16[256,1024]{1,0:T(8,128)(2,1)S(1)}, bf16[256,1024]{1,0:T(8,128)(2,1)S(1)}, u32[]{:S(2)}, u32[]{:S(2)}) collective-permute-start(bf16[256,1024]{1,0:T(8,128)(2,1)S(1)} %add_block.5), channel_id=1, source_target_pairs={{8,0},{16,24},{9,1},{17,25},{10,2},{18,26},{11,3},{19,27},{12,4},{... | collective-permute-start | bytes 1572872 | tf_op jit(solution)/shard_map/ppermute | solution.py:52
  59.5 11.1 %collective-permute-start.18 = (bf16[256,1024]{1,0:T(8,128)(2,1)S(1)}, bf16[256,1024]{1,0:T(8,128)(2,1)S(1)}, u32[]{:S(2)}, u32[]{:S(2)}) collective-permute-start(bf16[256,1024]{1,0:T(8,128)(2,1)S(1)} %update_rows.1.refs_0_), channel_id=1, source_target_pairs={{0,4},{2,6},{4,0},{6,2},{1,5},{3,7},{5,1},{7,3},{8,12},{10,14},{12... | collective-permute-start | bytes 1572872 | tf_op jit(solution)/shard_map/ppermute | solution.py:56
  61.1 12.9 %collective-permute-start.13 = (bf16[256,1024]{1,0:T(8,128)(2,1)S(1)}, bf16[256,1024]{1,0:T(8,128)(2,1)S(1)}, u32[]{:S(2)}, u32[]{:S(2)}) collective-permute-start(bf16[256,1024]{1,0:T(8,128)(2,1)S(1)} %update_rows.1.refs_0_), channel_id=1, source_target_pairs={{0,8},{8,0},{16,24},{24,16},{1,9},{9,1},{17,25},{25,17},{2,10},{10... | collective-permute-start | bytes 1572872 | tf_op jit(solution)/shard_map/ppermute | solution.py:56
  62.9 19.5 %collective-permute-start.17 = (bf16[256,1024]{1,0:T(8,128)(2,1)S(1)}, bf16[256,1024]{1,0:T(8,128)(2,1)S(1)}, u32[]{:S(2)}, u32[]{:S(2)}) collective-permute-start(bf16[256,1024]{1,0:T(8,128)(2,1)S(1)} %collective-permute-done.16.middle), channel_id=1, source_target_pairs={{8,0},{16,24},{9,1},{17,25},{10,2},{18,26},{11,3},{19,27},{12,4},{... | collective-permute-start | bytes 1572872 | tf_op jit(solution)/shard_map/ppermute | solution.py:52
  74.0 10.1 %collective-permute-start.19 = (bf16[256,1024]{1,0:T(8,128)(2,1)S(1)}, bf16[256,1024]{1,0:T(8,128)(2,1)S(1)}, u32[]{:S(2)}, u32[]{:S(2)}) collective-permute-start(bf16[256,1024]{1,0:T(8,128)(2,1)S(1)} %gate.12.refs_6_.refs_0_.refs_2_), channel_id=1, source_target_pairs={{0,4},{2,6},{4,0},{6,2},{1,5},{3,7},{5,1},{7,3},{8,12},{10,14},{12... | collective-permute-start | bytes 1572872 | tf_op jit(solution)/shard_map/ppermute | solution.py:56
  74.1 10.1 %collective-permute-start.21 = (bf16[256,1024]{1,0:T(8,128)(2,1)S(1)}, bf16[256,1024]{1,0:T(8,128)(2,1)S(1)}, u32[]{:S(2)}, u32[]{:S(2)}) collective-permute-start(bf16[256,1024]{1,0:T(8,128)(2,1)S(1)} %gate.13), channel_id=1, source_target_pairs={{0,8},{24,16},{1,9},{25,17},{2,10},{26,18},{3,11},{27,19},{4,12},{... | collective-permute-start | bytes 1572872 | tf_op jit(solution)/shard_map/ppermute | solution.py:52
  75.6 9.3 %collective-permute-start.14 = (bf16[256,1024]{1,0:T(8,128)(2,1)S(1)}, bf16[256,1024]{1,0:T(8,128)(2,1)S(1)}, u32[]{:S(2)}, u32[]{:S(2)}) collective-permute-start(bf16[256,1024]{1,0:T(8,128)(2,1)S(1)} %collective-permute-done.13.x), channel_id=1, source_target_pairs={{8,16},{16,8},{9,17},{17,9},{10,18},{18,10},{11,19},{19,11},{12,20... | collective-permute-start | bytes 1572872 | tf_op jit(solution)/shard_map/ppermute | solution.py:52
  84.2 10.3 %collective-permute-start.20 = (bf16[256,1024]{1,0:T(8,128)(2,1)S(1)}, bf16[256,1024]{1,0:T(8,128)(2,1)S(1)}, u32[]{:S(2)}, u32[]{:S(2)}) collective-permute-start(bf16[256,1024]{1,0:T(8,128)(2,1)S(1)} %pick.5.refs_4_), channel_id=1, source_target_pairs={{0,4},{2,6},{4,0},{6,2},{1,5},{3,7},{5,1},{7,3},{8,12},{10,14},{12... | collective-permute-start | bytes 1572872 | tf_op jit(solution)/shard_map/ppermute | solution.py:56
  84.3 10.2 %collective-permute-start.22 = (bf16[256,1024]{1,0:T(8,128)(2,1)S(1)}, bf16[256,1024]{1,0:T(8,128)(2,1)S(1)}, u32[]{:S(2)}, u32[]{:S(2)}) collective-permute-start(bf16[256,1024]{1,0:T(8,128)(2,1)S(1)} %collective-permute-done.21.middle), channel_id=1, source_target_pairs={{8,16},{16,8},{9,17},{17,9},{10,18},{18,10},{11,19},{19,11},{12,20... | collective-permute-start | bytes 1572872 | tf_op jit(solution)/shard_map/ppermute | solution.py:52
  85.0 13.3 %collective-permute-start.15 = (bf16[256,1024]{1,0:T(8,128)(2,1)S(1)}, bf16[256,1024]{1,0:T(8,128)(2,1)S(1)}, u32[]{:S(2)}, u32[]{:S(2)}) collective-permute-start(bf16[256,1024]{1,0:T(8,128)(2,1)S(1)} %collective-permute-done.14.middle), channel_id=1, source_target_pairs={{8,0},{16,24},{9,1},{17,25},{10,2},{18,26},{11,3},{19,27},{12,4},{... | collective-permute-start | bytes 1572872 | tf_op jit(solution)/shard_map/ppermute | solution.py:52
  86.3 8.2 %collective-permute-start.23 = (f32[32,2048]{1,0:T(8,128)S(1)}, f32[32,2048]{1,0:T(8,128)S(1)}, u32[]{:S(2)}, u32[]{:S(2)}) collective-permute-start(f32[32,2048]{1,0:T(8,128)S(1)} %get-tuple-element.52), channel_id=1, source_target_pairs={{0,1},{1,0},{2,3},{3,2},{4,5},{5,4},{6,7},{7,6},{8,9},{9,8},{10,11... | collective-permute-start | bytes 786440 | tf_op jit(solution)/shard_map/ppermute | solution.py:513
  98.6 14.3 %collective-permute-start.24 = (bf16[256,1024]{1,0:T(8,128)(2,1)S(1)}, bf16[256,1024]{1,0:T(8,128)(2,1)S(1)}, u32[]{:S(2)}, u32[]{:S(2)}) collective-permute-start(bf16[256,1024]{1,0:T(8,128)(2,1)S(1)} %pick.6.refs_6_), channel_id=1, source_target_pairs={{0,4},{2,6},{4,0},{6,2},{1,5},{3,7},{5,1},{7,3},{8,12},{10,14},{12... | collective-permute-start | bytes 1572872 | tf_op jit(solution)/shard_map/ppermute | solution.py:56
  99.5 15.9 %collective-permute-start.27 = (bf16[256,1024]{1,0:T(8,128)(2,1)S(1)}, bf16[256,1024]{1,0:T(8,128)(2,1)S(1)}, u32[]{:S(2)}, u32[]{:S(2)}) collective-permute-start(bf16[256,1024]{1,0:T(8,128)(2,1)S(1)} %collective-permute-done.22.refs_1_.middle), channel_id=1, source_target_pairs={{8,0},{16,24},{9,1},{17,25},{10,2},{18,26},{11,3},{19,27},{12,4},{... | collective-permute-start | bytes 1572872 | tf_op jit(solution)/shard_map/ppermute | solution.py:52
  (14 other events, 154.7 us)
